TPU v7x, 32 devices: a whole 2x2x4 slice. The times are simulated.
32 devices in a mesh: dp: 4 (over y, x), seq: 8 (over z, core).
Axes of the slice: x: 2, y: 2, z: 4, core: 2. Of those that a mesh axis runs over, the one named last changes fastest.
Arguments:
- history: bfloat16 [9, 4, 3072, 1024], P(None, 'dp', 'seq'), may hold values from -6 to 6
- documents: int32 [4, 3072], P('dp'), may hold values from 0 to 4, as said below
- cotangent: bfloat16 [4, 3072, 1024], P('dp', 'seq'), may hold values from -6 to 6
- mixer_gain: bfloat16 [1024], replicated, may hold values from 0.25 to 1.75
- mixer_inner: bfloat16 [1024, 36], replicated, may hold values from -0.1875 to 0.1875
- mixer_outer: bfloat16 [36, 36], replicated, may hold values from -0.5 to 0.5
- mixer_bias: bfloat16 [36], replicated, may hold values from -1.5 to 1.5
- stream_gain: bfloat16 [4, 1024], replicated, may hold values from 0.25 to 1.75
- stream_bias: bfloat16 [4, 1024], replicated, may hold values from -1.5 to 1.5
- inbound_weight: bfloat16 [1024, 3072], P(('dp', 'seq')), may hold values from -0.1875 to 0.1875
- inbound_bias: bfloat16 [3072], replicated, may hold values from -1.5 to 1.5
- outbound_weight: bfloat16 [1024, 1024], P(('dp', 'seq')), may hold values from -1.5 to 1.5
- outbound_bias: bfloat16 [1024], replicated, may hold values from -1.5 to 1.5
- expand: bfloat16 [1024, 4096], P(('dp', 'seq')), may hold values from -0.1875 to 0.1875
- expand_bias: bfloat16 [4096], replicated, may hold values from -1.5 to 1.5
- contract: bfloat16 [1024, 4096], P(('dp', 'seq')), may hold values from -0.09375 to 0.09375
- contract_bias: bfloat16 [1024], replicated, may hold values from -1.5 to 1.5
Outputs:
- layer_out: bfloat16 [4, 3072, 1024], P('dp', 'seq')
- history_grad: float32 [9, 4, 3072, 1024], P(None, 'dp', 'seq')
- mixer_gain_grad: float32 [1024], replicated
- mixer_inner_grad: float32 [1024, 36], replicated
- mixer_outer_grad: float32 [36, 36], replicated
- mixer_bias_grad: float32 [36], replicated
- stream_gain_grad: float32 [4, 1024], replicated
- stream_bias_grad: float32 [4, 1024], replicated
- inbound_weight_grad: float32 [1024, 3072], P(('dp', 'seq'))
- inbound_bias_grad: float32 [3072], replicated
- outbound_weight_grad: float32 [1024, 1024], P(('dp', 'seq'))
- outbound_bias_grad: float32 [1024], replicated
- expand_grad: float32 [1024, 4096], P(('dp', 'seq'))
- expand_bias_grad: float32 [4096], replicated
- contract_grad: float32 [1024, 4096], P(('dp', 'seq'))
- contract_bias_grad: float32 [1024], replicated
Inputs may be any that keep to these rules, and one draw needn't show every extreme that they name: Along each sequence the ids never fall and rise by one at each of four document starts, so there are five documents; document 2 begins within the first 384 positions and ends within the last 384 positions.
All inputs are finite; a program needn't handle non-finite values.
Results may differ from a plain program's by a relative error of at most 0.012.
The roundings to bfloat16 on the way count: a program that leaves them out, or rounds other values in their place, can miss the bound.
Values may be sent and summed in bfloat16 or wider, within the bound.
A program may use at most 256 MiB of HBM per device.

v0:
```python
import math

import jax
import jax.numpy as jnp
from jax import lax
from jax.sharding import PartitionSpec as P

HEADS = 16
HEAD_DIM = 64
ROT_DIMS = 16


EPS = 1e-05
HIGHEST = lax.Precision.HIGHEST
NEG = -1e30


def inner(left, right):
    return lax.dot_general(
        left, right, (((0,), (0,)), ((), ())), preferred_element_type=jnp.float32
    )


def against(left, right):
    return lax.dot_general(
        left, right, (((1,), (1,)), ((), ())), preferred_element_type=jnp.float32
    )


def product(left, right):
    return jnp.dot(left, right, preferred_element_type=jnp.float32)


def exact_gelu(value):
    return jax.nn.gelu(value, approximate=False)


def rms_scale(last, gain):
    return last * lax.rsqrt(jnp.mean(last * last, axis=-1, keepdims=True) + EPS) * gain


def layer_norm(streams, gains, biases):
    center = jnp.mean(streams, axis=-1, keepdims=True)
    centered = streams - center
    spread = jnp.mean(centered * centered, axis=-1, keepdims=True)
    return centered * lax.rsqrt(spread + EPS) * gains[:, None, :] + biases[:, None, :]


def rotary_tables(positions):
    half = ROT_DIMS // 2
    freq = 10000.0 ** (-jnp.arange(half).astype(jnp.float32) * 2.0 / ROT_DIMS)
    angles = positions.astype(jnp.float32)[:, None] * freq[None, :]
    angles = jnp.concatenate([angles, angles], axis=-1)
    return (jnp.cos(angles)[:, None, :], jnp.sin(angles)[:, None, :])


def rotate(value, cosine, sine):
    half = ROT_DIMS // 2
    part = value[..., :ROT_DIMS]
    turned = jnp.concatenate([-part[..., half:], part[..., :half]], axis=-1)
    return jnp.concatenate([part * cosine + turned * sine, value[..., ROT_DIMS:]], axis=-1)


def on_device(
    history,
    documents,
    cotangent,
    mixer_gain,
    mixer_inner,
    mixer_outer,
    mixer_bias,
    stream_gain,
    stream_bias,
    inbound_weight,
    inbound_bias,
    outbound_weight,
    outbound_bias,
    expand,
    expand_bias,
    contract,
    contract_bias,
):
    tokens = history.shape[2]
    width = history.shape[3]
    scale = 1.0 / math.sqrt(HEAD_DIM)
    history_full = history[:, 0].astype(jnp.float32)
    offset = lax.axis_index("seq") * tokens
    positions = offset + jnp.arange(tokens, dtype=jnp.int32)
    key_docs = documents[0]
    query_docs = lax.dynamic_slice_in_dim(key_docs, offset, tokens)
    key_places = jnp.arange(key_docs.shape[0], dtype=jnp.int32)
    allowed = (query_docs[:, None] == key_docs[None, :]) & (
        key_places[None, :] <= positions[:, None]
    )
    last = history_full[-1]
    scaled, rms_pull = jax.vjp(rms_scale, last, mixer_gain.astype(jnp.float32))
    scaled_low = scaled.astype(jnp.bfloat16)
    mix_pre = product(scaled_low, mixer_inner)
    mix_value, mix_pull = jax.vjp(exact_gelu, mix_pre)
    mix_hidden = mix_value.astype(jnp.bfloat16)
    coeffs = (product(mix_hidden, mixer_outer) + mixer_bias.astype(jnp.float32)).reshape(
        tokens, 4, -1
    )
    streams = jnp.einsum("tcj,jtd->ctd", coeffs, history_full, precision=HIGHEST)
    normed, norm_pull = jax.vjp(
        layer_norm, streams, stream_gain.astype(jnp.float32), stream_bias.astype(jnp.float32)
    )
    lowered = normed.astype(jnp.bfloat16)
    full_in, full_out, full_expand, full_contract = (
        lax.all_gather(inbound_weight, ("dp", "seq"), axis=0, tiled=True),
        lax.all_gather(outbound_weight, ("dp", "seq"), axis=0, tiled=True),
        lax.all_gather(expand, ("dp", "seq"), axis=0, tiled=True),
        lax.all_gather(contract, ("dp", "seq"), axis=0, tiled=True),
    )
    bias_in = inbound_bias.astype(jnp.float32)
    query_pre = product(lowered[0], full_in[:, :width]) + bias_in[:width]
    key_pre = product(lowered[1], full_in[:, width : 2 * width]) + bias_in[width : 2 * width]
    value_pre = product(lowered[2], full_in[:, 2 * width :]) + bias_in[2 * width :]
    cosine, sine = rotary_tables(positions)
    query_turned = rotate(query_pre.reshape(tokens, HEADS, HEAD_DIM), cosine, sine)
    key_turned = rotate(key_pre.reshape(tokens, HEADS, HEAD_DIM), cosine, sine)
    query_low = jnp.transpose(query_turned, (1, 0, 2)).astype(jnp.bfloat16)
    pair_low = jnp.concatenate(
        [
            jnp.transpose(key_turned, (1, 0, 2)),
            jnp.transpose(value_pre.reshape(tokens, HEADS, HEAD_DIM), (1, 0, 2)),
        ],
        axis=-1,
    ).astype(jnp.bfloat16)
    pair_all = lax.all_gather(pair_low, "seq", axis=1, tiled=True)

    def head_forward(args):
        query_head, pair_head = args
        scores = against(query_head, pair_head[:, :HEAD_DIM]) * scale
        scores = jnp.where(allowed, scores, NEG)
        top = jnp.max(scores, axis=-1, keepdims=True)
        weights = jnp.exp(scores - top)
        totals = jnp.sum(weights, axis=-1, keepdims=True)
        probs_low = (weights / totals).astype(jnp.bfloat16)
        return (product(probs_low, pair_head[:, HEAD_DIM:]), (top + jnp.log(totals))[:, 0])

    attended, log_totals = lax.map(head_forward, (query_low, pair_all))
    attended_low = jnp.transpose(attended, (1, 0, 2)).reshape(tokens, width).astype(jnp.bfloat16)
    attention = against(attended_low, full_out) + outbound_bias.astype(jnp.float32)
    expanded = product(lowered[3], full_expand) + expand_bias.astype(jnp.float32)
    hidden_value, hidden_pull = jax.vjp(exact_gelu, expanded)
    hidden_low = hidden_value.astype(jnp.bfloat16)
    feed = against(hidden_low, full_contract) + contract_bias.astype(jnp.float32)
    layer_out = (streams[3] + attention + feed).astype(jnp.bfloat16)
    grad_low = cotangent[0]
    grad_full = grad_low.astype(jnp.float32)
    full_in, full_out, full_expand, full_contract = (
        lax.all_gather(inbound_weight, ("dp", "seq"), axis=0, tiled=True),
        lax.all_gather(outbound_weight, ("dp", "seq"), axis=0, tiled=True),
        lax.all_gather(expand, ("dp", "seq"), axis=0, tiled=True),
        lax.all_gather(contract, ("dp", "seq"), axis=0, tiled=True),
    )
    attended_grad = product(grad_low, full_out).astype(jnp.bfloat16)
    attended_grad = jnp.transpose(attended_grad.reshape(tokens, HEADS, HEAD_DIM), (1, 0, 2))
    expanded_grad = hidden_pull(product(grad_low, full_contract))[0]
    expanded_grad_low = expanded_grad.astype(jnp.bfloat16)

    def query_backward(query_head, pair_head, grad_head, log_total):
        keys_head = pair_head[:, :HEAD_DIM]
        scores = against(query_head, keys_head) * scale
        probs = jnp.exp(jnp.where(allowed, scores - log_total[:, None], NEG))
        probs_grad = against(grad_head, pair_head[:, HEAD_DIM:])
        delta = jnp.sum(probs * probs_grad, axis=-1, keepdims=True)
        scores_grad = (probs * (probs_grad - delta)).astype(jnp.bfloat16)
        query_grad = product(scores_grad, keys_head) * scale
        return (probs, scores_grad, query_grad, delta[:, 0])

    def head_backward(args):
        query_head, pair_head, grad_head, log_total = args
        probs, scores_grad, query_grad, delta = query_backward(
            query_head, pair_head, grad_head, log_total
        )
        key_grad = inner(scores_grad, query_head) * scale
        value_grad = inner(probs.astype(jnp.bfloat16), grad_head)
        return (query_grad, jnp.concatenate([key_grad, value_grad], axis=-1))

    query_grads, pair_grads = lax.map(
        head_backward, (query_low, pair_all, attended_grad, log_totals)
    )
    pair_own = lax.psum_scatter(
        pair_grads.astype(jnp.bfloat16), "seq", scatter_dimension=1, tiled=True
    ).astype(jnp.float32)
    query_turned_grad = jnp.transpose(query_grads, (1, 0, 2))
    key_turned_grad = jnp.transpose(pair_own[..., :HEAD_DIM], (1, 0, 2))
    value_grad = jnp.transpose(pair_own[..., HEAD_DIM:], (1, 0, 2)).reshape(tokens, width)
    query_grad = rotate(query_turned_grad, cosine, -sine).reshape(tokens, width)
    key_grad = rotate(key_turned_grad, cosine, -sine).reshape(tokens, width)
    proj_grad = jnp.concatenate([query_grad, key_grad, value_grad], axis=-1)
    proj_grad_low = proj_grad.astype(jnp.bfloat16)
    normed_grad = jnp.stack(
        [
            against(proj_grad_low[:, :width], full_in[:, :width]),
            against(proj_grad_low[:, width : 2 * width], full_in[:, width : 2 * width]),
            against(proj_grad_low[:, 2 * width :], full_in[:, 2 * width :]),
            against(expanded_grad_low, full_expand),
        ]
    )
    streams_grad, stream_gain_grad, stream_bias_grad = norm_pull(normed_grad)
    streams_grad = streams_grad.at[3].add(grad_full)
    history_grad = jnp.einsum("tcj,ctd->jtd", coeffs, streams_grad, precision=HIGHEST)
    coeffs_grad = jnp.einsum("ctd,jtd->tcj", streams_grad, history_full, precision=HIGHEST).reshape(
        tokens, -1
    )
    mixer_bias_grad = jnp.sum(coeffs_grad, axis=0)
    coeffs_grad_low = coeffs_grad.astype(jnp.bfloat16)
    mixer_outer_grad = inner(mix_hidden, coeffs_grad_low)
    mix_pre_grad_low = mix_pull(against(coeffs_grad_low, mixer_outer))[0].astype(jnp.bfloat16)
    mixer_inner_grad = inner(scaled_low, mix_pre_grad_low)
    last_grad, mixer_gain_grad = rms_pull(against(mix_pre_grad_low, mixer_inner))
    history_grad = history_grad.at[-1].add(last_grad)
    owned = lax.psum_scatter(
        jnp.concatenate(
            [
                inner(lowered[0], proj_grad_low[:, :width]),
                inner(lowered[1], proj_grad_low[:, width : 2 * width]),
                inner(lowered[2], proj_grad_low[:, 2 * width :]),
                inner(grad_low, attended_low),
                inner(lowered[3], expanded_grad_low),
                inner(grad_low, hidden_low),
            ],
            axis=1,
        ),
        ("dp", "seq"),
        scatter_dimension=0,
        tiled=True,
    )
    hidden_width = expand.shape[1]
    small = lax.psum(
        (
            mixer_gain_grad,
            mixer_inner_grad,
            mixer_outer_grad,
            mixer_bias_grad,
            stream_gain_grad,
            stream_bias_grad,
            jnp.sum(proj_grad, axis=0),
            jnp.sum(grad_full, axis=0),
            jnp.sum(expanded_grad, axis=0),
        ),
        ("dp", "seq"),
    )
    inbound_weight_grad = owned[:, : 3 * width]
    outbound_weight_grad = owned[:, 3 * width : 4 * width]
    expand_grad = owned[:, 4 * width : 4 * width + hidden_width]
    contract_grad = owned[:, 4 * width + hidden_width :]
    return (
        layer_out[None],
        history_grad[:, None],
        small[0],
        small[1],
        small[2],
        small[3],
        small[4],
        small[5],
        inbound_weight_grad,
        small[6],
        outbound_weight_grad,
        small[7],
        expand_grad,
        small[8],
        contract_grad,
        small[7],
    )


def solution(mesh):
    placed = (
        P(None, "dp", "seq", None),
        P("dp", None),
        P("dp", "seq", None),
        P(),
        P(),
        P(),
        P(),
        P(),
        P(),
        P(("dp", "seq"), None),
        P(),
        P(("dp", "seq"), None),
        P(),
        P(("dp", "seq"), None),
        P(),
        P(("dp", "seq"), None),
        P(),
    )
    return jax.shard_map(
        on_device,
        mesh=mesh,
        in_specs=placed,
        out_specs=(
            P("dp", "seq", None),
            P(None, "dp", "seq", None),
            P(),
            P(),
            P(),
            P(),
            P(),
            P(),
            P(("dp", "seq"), None),
            P(),
            P(("dp", "seq"), None),
            P(),
            P(("dp", "seq"), None),
            P(),
            P(("dp", "seq"), None),
            P(),
        ),
        check_vma=False,
    )
```

profile of v0, /device:TPU:0, one launch (start us, length us, event | category | flops | bytes accessed | tf_op | source)
XLA Modules:
  0.0 1525.2 jit_solution(5996638936083155253)
XLA Ops:
  16.5 17.0 %fusion.39 = f32[384,4,1024]{2,1,0:T(4,128)S(1)} fusion(f32[384,4,9]{2,1,0:T(4,128)S(1)} %copy.101, bf16[9,384,1024]{2,1,0:T(8,128)(2,1)} %bitcast.230), kind=kOutput, calls=%fused_computation.53 | convolution fusion | flops 169869312 | bytes 13424640 | tf_op jit(solution)/shard_map/tcj,jtd->ctd/dot_general | solution.py:104
  34.4 3.4 fusion.136
  37.9 3.5 multiply_reduce_fusion.3
  41.5 3.7 add_convert_fusion
  45.2 38.0 %all-gather.6.cloned.1.call-done = bf16[1024,3072]{1,0:T(8,128)(2,1)} async-done(((bf16[32,3072]{1,0:T(8,128)(2,1)}), bf16[1024,3072]{1,0:T(8,128)(2,1)}) %all-gather.6.cloned.1.call-update) | async-done | bytes 6291472 | tf_op jit(solution)/shard_map/all_gather | solution.py:110
  83.2 3.7 fusion.91
  86.9 3.1 copy.104
  90.0 3.7 fusion.94
  93.7 3.1 copy.105
  96.7 3.5 add_convert_fusion.1
  110.1 31.1 %all-gather.10.cloned.1.call-done = bf16[1024,1024]{1,0:T(8,128)(2,1)} async-done(((bf16[32,1024]{1,0:T(8,128)(2,1)}), bf16[1024,1024]{1,0:T(8,128)(2,1)}) %all-gather.10.cloned.1.call-update) | async-done | bytes 2097168 | tf_op jit(solution)/shard_map/all_gather | solution.py:111
  141.2 3.7 convolution_convert_fusion
  149.5 3.0 copy.107
  152.5 106.4 %all-gather.8.cloned.1.call-done = bf16[16,3072,128]{1,2,0:T(8,128)(2,1)} async-done(((bf16[16,384,128]{1,2,0:T(8,128)(2,1)}), bf16[16,3072,128]{1,2,0:T(8,128)(2,1)}) %all-gather.8.cloned.1.call-update) | async-done | bytes 12582928 | tf_op jit(solution)/shard_map/all_gather | solution.py:130
  258.9 16.6 %copy.108 = bf16[16,3072,128]{2,1,0:T(8,128)(2,1)} copy(bf16[16,3072,128]{1,2,0:T(8,128)(2,1)} %all-gather.8.cloned.1.call-done) | data formatting | bytes 25165824
  275.5 103.4 %while.30 = (s32[]{:T(128)}, bf16[16,384,64]{1,2,0:T(8,128)(2,1)}, f32[16,384]{1,0:T(8,128)S(1)}, bf16[16,384,64]{2,1,0:T(8,128)(2,1)}, bf16[16,3072,128]{2,1,0:...) while((s32[]{:T(128)}, bf16[16,384,64]{1,2,0:T(8,128)(2,1)}, ...), condition=%wide.region_6.7_spmd.clone.clone, body=%wide.region_3.6_spmd.clone.sunk.clone | while | flops 314965632 | bytes 17532012 | solution.py:142
  347.9 2.3 fusion.208
  378.9 197.7 %while.31 = (s32[]{:T(128)}, f32[16,384,64]{1,2,0:T(8,128)}, bf16[16,3072,128]{1,2,0:T(8,128)(2,1)}, bf16[16,384,64]{2,1,0:T(8,128)(2,1)}, bf16[16,3072,128]{2,1...) while((s32[]{:T(128)}, f32[16,384,64]{1,2,0:T(8,128)}, ...), condition=%wide.region_9.10_spmd.clone.clone, body=%wide.region_7.9_spmd.clone.sunk.clone | while | flops 771120768 | bytes 42097292 | solution.py:182
  381.8 3.0 multiply_reduce_fusion.6
  394.2 3.0 multiply_reduce_fusion.6
  406.5 3.0 multiply_reduce_fusion.6
  418.8 3.0 multiply_reduce_fusion.6
  431.2 3.0 multiply_reduce_fusion.6
  443.6 3.0 multiply_reduce_fusion.6
  455.9 3.0 multiply_reduce_fusion.6
  468.3 3.0 multiply_reduce_fusion.6
  480.7 3.0 multiply_reduce_fusion.6
  493.0 3.0 multiply_reduce_fusion.6
  505.3 3.0 multiply_reduce_fusion.6
  517.7 3.0 multiply_reduce_fusion.6
  530.1 3.0 multiply_reduce_fusion.6
  542.4 3.0 multiply_reduce_fusion.6
  554.8 3.0 multiply_reduce_fusion.6
  567.1 3.0 multiply_reduce_fusion.6
  576.6 16.6 %copy.129 = bf16[16,3072,128]{2,0,1:T(8,128)(2,1)} copy(bf16[16,3072,128]{1,2,0:T(8,128)(2,1)} %get-tuple-element.119) | data formatting | bytes 25165824
  593.2 13.2 copy.164
  609.0 20.3 %multiply_convert_fusion.1 = (bf16[384,4096]{1,0:T(8,128)(2,1)}, f32[384,4096]{1,0:T(8,128)}, f32[384,4096]{1,0:T(8,128)}) fusion(f32[4096]{0:T(1024)S(1)} %convert_element_type.124, bf16[1024,4096]{1,0:T(8,128)(2,1)} %all-gather.12.cloned.1.call-done, bf16[4,384,1024]{2,1,0:T(8,128)(2,1)S(1)} %add_convert_fusion), kind=kOutput, calls=%fused_computation.65 | convolution fusion | flops 3325034496 | bytes 24920064 | tf_op jit(solution)/shard_map/dot_general | solution.py:31
  629.3 11.2 fusion.144
  640.6 4.6 fusion.79
  646.3 3.3 convolution_bitcast_fusion
  649.6 5.4 copy.123
  656.7 77.3 %reduce-scatter.7.cloned.1.call-done = bf16[384,2048]{1,0:T(8,128)(2,1)} async-done(((bf16[3072,2048]{1,0:T(8,128)(2,1)}), bf16[384,2048]{1,0:T(8,128)(2,1)}) %reduce-scatter.7.cloned.1.call-update) | async-done | bytes 1572880
  734.0 3.0 copy.134
  737.0 3.0 copy.130
  746.4 3.4 convolution_dynamic-update-slice_fusion.3
  753.5 4.3 multiply_reduce_fusion.2
  757.8 6.0 multiply_reduce_fusion.1
  763.8 5.4 broadcast_add_fusion
  769.8 20.2 %fusion.142 = (f32[4,9]{1,0:T(4,128)S(1)}, bf16[384,4,9]{2,1,0:T(4,128)(2,1)}) fusion(bf16[9,384,1024]{2,1,0:T(8,128)(2,1)S(1)} %bitcast.233, f32[4,384,1024]{2,1,0:T(8,128)S(1)} %fusion.72), kind=kOutput, calls=%fused_computation.221 | convolution fusion | flops 169896928 | bytes 13397136 | tf_op jit(solution)/shard_map/ctd,jtd->tcj/dot_general | solution.py:206
  792.3 3.4 fusion.67
  796.3 4.4 convolution_dynamic-update-slice_fusion.2
  800.8 4.7 convolution_dynamic-update-slice_fusion.1
  805.4 2.4 constant_dynamic-update-slice_fusion
  808.8 8.2 convolution_dynamic-update-slice_fusion
  817.3 12.5 bitcast_dynamic-update-slice_fusion
  829.9 6.6 copy.165
  836.6 6.3 fusion.145
  844.9 24.9 %fusion.48 = f32[384,1024,9]{1,2,0:T(8,128)} fusion(f32[384,4,9]{2,1,0:T(4,128)S(1)} %copy-done.6, f32[4,384,1024]{2,1,0:T(8,128)S(1)} %bitcast.237), kind=kOutput, calls=%fused_computation.83 | convolution fusion | flops 169869312 | bytes 20502528 | tf_op jit(solution)/shard_map/tcj,ctd->jtd/dot_general | solution.py:205
  869.9 6.1 slice.269
  879.4 30.6 %scatter-add.9 = f32[9,1,384,1024]{3,0,2,1:T(8,128)} dynamic-update-slice(f32[9,1,384,1024]{3,0,2,1:T(8,128)} %bitcast.229, f32[1,1,384,1024]{3,0,2,1:T(1,128)S(1)} %copy.118, s32[]{:T(128)} %constant.228.clone.1, s32[]{:T(128)} %constant.219.clone.1, s32[]{:T(128)} %constant.219.clone.1, s32[]{:T(128)} %constant.219.clone.1) | dynamic-update-slice | bytes 3145732 | tf_op jit(solution)/shard_map/scatter-add | solution.py:215
  910.0 17.8 %copy.124 = f32[9,1,384,1024]{3,2,1,0:T(8,128)} copy(f32[9,1,384,1024]{3,0,2,1:T(8,128)} %scatter-add.9) | data formatting | bytes 28311552
  930.1 8.8 all-reduce.6.cloned.1.call-done
  938.9 439.2 %reduce-scatter.5.cloned.1.call-done = f32[32,12288]{1,0:T(8,128)} async-done(((f32[1024,12288]{1,0:T(8,128)}), f32[32,12288]{1,0:T(8,128)}) %reduce-scatter.5.cloned.1.call-update) | async-done | bytes 1572880 | tf_op jit(solution)/shard_map/reduce_scatter | solution.py:216
  1383.7 121.4 %all-reduce.4.cloned.1.call-done = f32[1024,36]{0,1:T(8,128)} async-done(((f32[1024,36]{0,1:T(8,128)}), f32[1024,36]{0,1:T(8,128)}) %all-reduce.4.cloned.1.call-update) | async-done | bytes 147472 | tf_op jit(solution)/shard_map/psum | solution.py:233
  (454 shorter events, 320.6 us)
Async XLA Ops:
  7.2 5.7 copy-start
  7.2 76.0 %all-gather.6.cloned.1.call-start = ((), (), s32[]{:S(2)}) async-start(), calls=%async_computation.2 | async-start | bytes 6488064 | tf_op jit(solution)/shard_map/all_gather | solution.py:110
  7.9 133.3 %all-gather.10.cloned.1.call-start = ((), (), s32[]{:S(2)}) async-start(), calls=%async_computation.4 | async-start | bytes 2162688 | tf_op jit(solution)/shard_map/all_gather | solution.py:111
  8.7 250.2 %all-gather.8.cloned.1.call-start = ((), (), s32[]{:S(2)}) async-start(), calls=%async_computation.3 | async-start | bytes 14155776 | tf_op jit(solution)/shard_map/all_gather | solution.py:130
  10.1 31.3 %copy-start.20 = (f32[4,1024]{1,0:T(4,128)}, f32[4,1024]{1,0:T(4,128)S(1)}, u32[]{:S(2)}) copy-start(f32[4,1024]{1,0:T(4,128)S(1)} %convert_element_type.113) | copy-start | bytes 49156
  10.8 5.7 copy-start.36
  12.2 4.3 copy-start.34
  12.2 4.3 copy-start.38
  16.5 17.0 %copy-start.5 = (f32[384,4,9]{2,1,0:T(4,128)}, f32[384,4,9]{2,1,0:T(4,128)S(1)}, u32[]{:S(2)}) copy-start(f32[384,4,9]{2,1,0:T(4,128)S(1)} %copy.101) | copy-start | bytes 165892
  33.5 7.9 copy-start.1
  34.4 70.7 %copy-start.22 = (f32[384,16]{0,1:T(8,128)}, f32[384,16]{0,1:T(8,128)S(1)}, u32[]{:S(2)}) copy-start(f32[384,16]{0,1:T(8,128)S(1)} %get-tuple-element.359) | copy-start | bytes 73732
  37.9 3.5 copy-start.33
  37.9 7.3 copy-start.24
  41.4 3.8 copy-start.29
  41.4 3.8 copy-start.26
  102.5 4.1 copy-start.16
  105.2 4.9 copy-start.43
  107.9 501.1 %all-gather.12.cloned.1.call-start = ((), (), s32[]{:S(2)}) async-start(), calls=%async_computation.5 | async-start | bytes 8650752 | tf_op jit(solution)/shard_map/all_gather | solution.py:112
  108.5 520.9 %all-gather.14.cloned.1.call-start = ((), (), s32[]{:S(2)}) async-start(), calls=%async_computation.6 | async-start | bytes 8650752 | tf_op jit(solution)/shard_map/all_gather | solution.py:113
  109.1 625.0 %reduce-scatter.7.cloned.1.call-start = ((), (), s32[]{:S(2)}) async-start(), calls=%async_computation.9 | async-start | bytes 14155776
  606.5 332.4 %all-reduce.6.cloned.1.call-start = ((), (), s32[]{:S(2)}) async-start(), calls=%async_computation.10 | async-start | bytes 181248 | tf_op jit(solution)/shard_map/psum | solution.py:233
  629.3 11.2 copy-start.44
  640.6 4.6 copy-start.14
  640.6 4.6 copy-start.17
  640.6 5.7 copy-start.7
  640.6 5.7 copy-start.11
  741.3 2.1 copy-start.19
  741.4 2.1 copy-start.23
  741.4 2.1 copy-start.28
  743.3 1.5 copy-start.13
  745.3 6.6 copy-start.9
  745.3 4.5 slice-start.6
  746.4 3.5 slice-start.7
  749.8 3.1 slice-start
  750.9 2.1 slice-start.1
  751.9 1.6 copy-start.4
  751.9 1.6 copy-start.21
  751.9 1.6 copy-start.25
  753.5 4.3 copy-start.30
  753.5 4.3 copy-start.27
  757.8 11.9 slice-start.2
  763.8 5.4 copy-start.8
  763.8 5.9 slice-start.3
  769.7 20.3 %copy-start.2 = (f32[4,384,1024]{2,1,0:T(8,128)}, f32[4,384,1024]{2,1,0:T(8,128)S(1)}, u32[]{:S(2)}) copy-start(f32[4,384,1024]{2,1,0:T(8,128)S(1)} %fusion.72) | copy-start | bytes 18874372
  769.7 21.6 %copy-start.32 = (bf16[384,36]{0,1:T(8,128)(2,1)S(1)}, bf16[384,36]{0,1:T(8,128)(2,1)}, u32[]{:S(2)}) copy-start(bf16[384,36]{0,1:T(8,128)(2,1)} %copy-done.31) | copy-start | bytes 82948
  769.7 22.4 %copy-start.46 = (bf16[36,36]{1,0:T(8,128)(2,1)S(1)}, bf16[36,36]{1,0:T(8,128)(2,1)}, u32[]{:S(2)}) copy-start(bf16[36,36]{1,0:T(8,128)(2,1)} %param.30) | copy-start | bytes 7780
  769.8 22.4 %copy-start.47 = (f32[384,36]{0,1:T(8,128)S(1)}, f32[384,36]{0,1:T(8,128)}, u32[]{:S(2)}) copy-start(f32[384,36]{0,1:T(8,128)} %get-tuple-element.336) | copy-start | bytes 165892
  769.8 22.4 %copy-start.48 = (f32[384,36]{0,1:T(8,128)S(1)}, f32[384,36]{0,1:T(8,128)}, u32[]{:S(2)}) copy-start(f32[384,36]{0,1:T(8,128)} %get-tuple-element.363) | copy-start | bytes 165892
  769.8 22.5 %copy-start.37 = (f32[1024]{0:T(1024)S(1)}, f32[1024]{0:T(1024)}, u32[]{:S(2)}) copy-start(f32[1024]{0:T(1024)} %copy-done.36) | copy-start | bytes 12292
  769.8 22.5 %copy-start.39 = (f32[384]{0:T(512)S(1)}, f32[384]{0:T(512)}, u32[]{:S(2)}) copy-start(f32[384]{0:T(512)} %copy-done.38) | copy-start | bytes 4612
  800.7 4.7 copy-start.3
  805.4 3.4 copy-start.15
  817.1 561.0 %reduce-scatter.5.cloned.1.call-start = ((), (), s32[]{:S(2)}) async-start(), calls=%async_computation.8 | async-start | bytes 51904512 | tf_op jit(solution)/shard_map/reduce_scatter | solution.py:216
  829.8 6.7 copy-start.41
  829.8 6.7 copy-start.42
  829.8 6.7 copy-start.10
  829.8 675.2 %all-reduce.4.cloned.1.call-start = ((), (), s32[]{:S(2)}) async-start(), calls=%async_computation.7 | async-start | bytes 327680 | tf_op jit(solution)/shard_map/psum | solution.py:233
  836.5 8.4 slice-start.4
  836.6 6.4 copy-start.12
  836.6 6.4 copy-start.45
  836.6 8.3 slice-start.5
  842.9 2.0 copy-start.6
  844.9 31.1 %copy-start.35 = (f32[384]{0:T(512)S(1)}, f32[384]{0:T(512)}, u32[]{:S(2)}) copy-start(f32[384]{0:T(512)} %copy-done.34) | copy-start | bytes 4612
  844.9 31.1 %copy-start.18 = (f32[384,1024]{1,0:T(8,128)S(1)}, f32[384,1024]{1,0:T(8,128)}, u32[]{:S(2)}) copy-start(f32[384,1024]{1,0:T(8,128)} %get-tuple-element.366) | copy-start | bytes 4718596
  (2 other events, 1.6 us)
Sparse Core Ops, SparseCore 0:
  11.0 72.1 all-gather.5
  86.2 54.9 all-gather.9
  143.4 115.4 all-gather.7
  261.8 75.6 all-gather.11
  340.3 75.9 all-gather.13
  606.6 127.4 reduce-scatter.6
  817.2 121.6 all-reduce.5
  945.3 432.7 reduce-scatter.4
  1384.2 120.8 all-reduce.3
where the time goes:
time: 1540 us; the launch traced here: 1530 us
  waiting for transfers between devices  825 us (54%)
  matrix products  384 us (25%)
  local copies, waits for them, and re-layouts  205 us (13%)
  other arithmetic  95 us (6%)
    reduce_scatter x1, waiting for transfers between devices, on_device(): lax.psum_scatter(jnp.concatenate([inner(lowered[0], proj_grad_low[:, :wid...  439 us
    dot_general x56, matrix products, against(): lax.dot_general(left, right, (((1,), (1,)), ((), ())), preferred_element_...  131 us
    psum x2, waiting for transfers between devices, on_device(): lax.psum((mixer_gain_grad, mixer_inner_grad, mixer_outer_grad, mixer_bias...  130 us
    all_gather x1, waiting for transfers between devices, on_device(): pair_all = lax.all_gather(pair_low, 'seq', axis=1, tiled=True)  106 us
    dot_general x40, matrix products, product(): return jnp.dot(left, right, preferred_element_type=jnp.float32)  106 us
    unnamed x132, local copies, waits for them, and re-layouts  91.2 us
    dot_general x40, matrix products, inner(): lax.dot_general(left, right, (((0,), (0,)), ((), ())), preferred_element_...  84.2 us
    unnamed x10, waiting for transfers between devices  79.8 us
  transfers between devices with their start and end apart: 9, of which 7 were waited for; matrix products, arithmetic and copies ran while one was open for 38% of the time, Pallas kernels for 0%

commit v1 on v0

v1 whole, which is shorter than its diff:
```python
import functools
import math

import jax
import jax.numpy as jnp
from jax import lax
from jax.experimental import pallas as pl
from jax.experimental.pallas import tpu as pltpu
from jax.sharding import PartitionSpec as P

HEADS = 16
HEAD_DIM = 64
ROT_DIMS = 16
EPS = 1e-05
HIGHEST = lax.Precision.HIGHEST
NEG = -1e30
MESH = pl.DeviceIdType.MESH
F32 = jnp.float32
BF16 = jnp.bfloat16
VMEM_LIMIT = 56 * 1024 * 1024


def inner(left, right):
    return lax.dot_general(left, right, (((0,), (0,)), ((), ())), preferred_element_type=F32)


def against(left, right):
    return lax.dot_general(left, right, (((1,), (1,)), ((), ())), preferred_element_type=F32)


def product(left, right):
    return jnp.dot(left, right, preferred_element_type=F32)


def exact_gelu(value):
    return jax.nn.gelu(value, approximate=False)


def rms_scale(last, gain):
    return last * lax.rsqrt(jnp.mean(last * last, axis=-1, keepdims=True) + EPS) * gain


def layer_norm(streams, gains, biases):
    center = jnp.mean(streams, axis=-1, keepdims=True)
    centered = streams - center
    spread = jnp.mean(centered * centered, axis=-1, keepdims=True)
    return centered * lax.rsqrt(spread + EPS) * gains[:, None, :] + biases[:, None, :]


def rotary_tables(positions, width):
    half = ROT_DIMS // 2
    place = jnp.arange(width) % HEAD_DIM
    freq = 10000.0 ** (-(place % half).astype(F32) * 2.0 / ROT_DIMS)
    angles = positions.astype(F32)[:, None] * freq[None, :]
    turned = (place < ROT_DIMS)[None, :]
    cosine = jnp.where(turned, jnp.cos(angles), 1.0)
    sine = jnp.where(turned, jnp.sin(angles), 0.0)
    above = jnp.where((place < half)[None, :], -sine, 0.0)
    below = jnp.where((place < half)[None, :], 0.0, sine)
    return cosine, above, below


def rotate(value, tables, sign):
    half = ROT_DIMS // 2
    cosine, above, below = tables
    up = jnp.roll(value, -half, axis=-1)
    down = jnp.roll(value, half, axis=-1)
    return value * cosine + sign * (up * above + down * below)


class Grid:
    def __init__(self, n_dp, n_seq):
        self.n_dp, self.n_seq = n_dp, n_seq
        self.na, self.nb, self.nz = 2, n_dp // 2, n_seq // 2

    def here(self):
        dp, seq = lax.axis_index("dp"), lax.axis_index("seq")
        return dp // self.nb, lax.rem(dp, self.nb), seq // 2, lax.rem(seq, 2)

    def device(self, a, b, z, c):
        return (a * self.nb + b, z * 2 + c)

    def peers(self, a, b, z, c):
        found = [self.device(a, b, z, 1 - c), self.device(1 - a, b, z, c)]
        found += [self.device(a, lax.rem(b + k, self.nb), z, c) for k in range(1, self.nb)]
        found += [self.device(a, b, lax.rem(z + k, self.nz), c) for k in range(1, self.nz)]
        return found

    def greet(self, a, b, z, c):
        barrier = pltpu.get_barrier_semaphore()
        found = self.peers(a, b, z, c)
        for peer in found:
            pl.semaphore_signal(barrier, inc=1, device_id=peer, device_id_type=MESH)
        pl.semaphore_wait(barrier, len(found))


def remote(src, dst, send, recv, device):
    return pltpu.make_async_remote_copy(
        src_ref=src, dst_ref=dst, send_sem=send, recv_sem=recv, device_id=device, device_id_type=MESH
    )


def gather_kernel(grid, rows, chunks, n_in, n_out, *refs):
    ins, outs = refs[:n_in], refs[n_in : n_in + n_out]
    local_sem, send_sem, recv_sem = refs[n_in + n_out :]
    a, b, z, c = grid.here()
    nz, nb = grid.nz, grid.nb
    grid.greet(a, b, z, c)
    slots = {"pair": 0, "z": 1, "b": nz, "a": nz + nb - 1}

    def begin(t, stage):
        src_i, base, dst_i, col, n, order = chunks[t]
        out = outs[dst_i]
        cols = pl.ds(col, n)
        copies = []
        if stage == 0:
            mine = ins[src_i].at[:, pl.ds(pl.multiple_of(base(c), 128), n)]
            theirs = ins[src_i].at[:, pl.ds(pl.multiple_of(base(1 - c), 128), n)]
            spot = out.at[a, b, z, pl.ds(pl.multiple_of(c * rows, rows), rows), cols]
            copies.append(pltpu.make_async_copy(mine, spot, local_sem.at[t]))
            copies.append(remote(theirs, spot, send_sem.at[t, 0], recv_sem.at[t, 0], grid.device(a, b, z, 1 - c)))
        elif stage == 1:
            block = out.at[a, b, z, :, cols]
            for k in range(1, nz):
                s = slots["z"] + k - 1
                copies.append(remote(block, block, send_sem.at[t, s], recv_sem.at[t, s], grid.device(a, b, lax.rem(z + k, nz), c)))
        else:
            axis = order[stage - 2]
            if axis == "b":
                block = out.at[a, b, :, :, cols] if stage == 2 else out.at[:, b, :, :, cols]
                for k in range(1, nb):
                    s = slots["b"] + k - 1
                    copies.append(remote(block, block, send_sem.at[t, s], recv_sem.at[t, s], grid.device(a, lax.rem(b + k, nb), z, c)))
            else:
                block = out.at[a, b, :, :, cols] if stage == 2 else out.at[a, :, :, :, cols]
                s = slots["a"]
                copies.append(remote(block, block, send_sem.at[t, s], recv_sem.at[t, s], grid.device(1 - a, b, z, c)))
        for copy in copies:
            copy.start()
        return copies

    started = {}
    count = len(chunks)
    for turn in range(count + 4):
        for stage in (4, 3, 2, 1, 0):
            t = turn - stage
            if 0 <= t < count:
                if stage > 0:
                    for copy in started[t, stage - 1]:
                        copy.wait()
                if stage < 4:
                    started[t, stage] = begin(t, stage)


def gather(grid, arrays, chunks, widths, collective_id, name):
    rows = arrays[0].shape[0]
    slots = grid.nz + grid.nb
    outs = [jax.ShapeDtypeStruct((grid.na, grid.nb, grid.nz, 2 * rows, w), BF16) for w in widths]
    moved = sum(w for w in widths) * 2 * rows * grid.na * grid.nb * grid.nz * 2
    results = pl.pallas_call(
        functools.partial(gather_kernel, grid, rows, chunks, len(arrays), len(outs)),
        out_shape=outs,
        in_specs=[pl.BlockSpec(memory_space=pl.ANY)] * len(arrays),
        out_specs=[pl.BlockSpec(memory_space=pl.ANY)] * len(outs),
        scratch_shapes=[
            pltpu.SemaphoreType.DMA((len(chunks),)),
            pltpu.SemaphoreType.DMA((len(chunks), slots)),
            pltpu.SemaphoreType.DMA((len(chunks), slots)),
        ],
        compiler_params=pltpu.CompilerParams(collective_id=collective_id, has_side_effects=True),
        cost_estimate=pl.CostEstimate(flops=0, bytes_accessed=moved * 20, transcendentals=0),
        name=name,
    )(*arrays)
    return [r.reshape(-1, r.shape[-1]) for r in results]


def scatter_kernel(grid, orders, *refs):
    count = len(orders)
    parts, outs = refs[:count], refs[count : 2 * count]
    scratch = refs[2 * count :]
    first, second, third, final, theirs = (scratch[i * count : (i + 1) * count] for i in range(5))
    send_sem, recv_sem = scratch[5 * count :]
    a, b, z, c = grid.here()
    na, nb, nz = grid.na, grid.nb, grid.nz
    rows = parts[0].shape[3] // 2
    grid.greet(a, b, z, c)
    slots = {"pair": 0, "z": 1, "b": nz, "a": nz + nb - 1}

    def launch(copies):
        for copy in copies:
            copy.start()
        return copies

    def to_b(t, src, dst):
        return [
            remote(src(lax.rem(b + k, nb)), dst(k - 1), send_sem.at[t, slots["b"] + k - 1], recv_sem.at[t, slots["b"] + k - 1],
                   grid.device(a, lax.rem(b + k, nb), z, c))
            for k in range(1, nb)
        ]

    def to_a(t, src, dst):
        return [remote(src(1 - a), dst(0), send_sem.at[t, slots["a"]], recv_sem.at[t, slots["a"]], grid.device(1 - a, b, z, c))]

    def begin(t, stage):
        part, order = parts[t], orders[t]
        n = part.shape[-1]
        if stage == 0:
            if order == "ab":
                return launch(to_a(t, lambda o: part.at[o], lambda k: first[t].at[k]))
            return launch(to_b(t, lambda o: part.at[:, o], lambda k: first[t].at[k]))
        if stage == 1:
            peers, length = first[t].shape[0], first[t].shape[1]

            def add(i, carry):
                o, j = i // nz, lax.rem(i, nz)
                own = part[a, o, j] if order == "ab" else part[o, b, j]
                total = own.astype(F32)
                for k in range(peers):
                    total = total + first[t][k, o, j].astype(F32)
                first[t][0, o, j] = total.astype(BF16)
                return carry

            lax.fori_loop(0, length * nz, add, 0)
            if order == "ab":
                return launch(to_b(t, lambda o: first[t].at[0, o], lambda k: second[t].at[k]))
            return launch(to_a(t, lambda o: first[t].at[0, o], lambda k: second[t].at[k]))
        if stage == 2:
            peers = second[t].shape[0]
            mine = b if order == "ab" else a

            def add(j, carry):
                total = first[t][0, mine, j].astype(F32)
                for k in range(peers):
                    total = total + second[t][k, j].astype(F32)
                second[t][0, j] = total.astype(BF16)
                return carry

            lax.fori_loop(0, nz, add, 0)
            return launch([
                remote(second[t].at[0, lax.rem(z + k, nz)], third[t].at[k - 1], send_sem.at[t, k], recv_sem.at[t, k],
                       grid.device(a, b, lax.rem(z + k, nz), c))
                for k in range(1, nz)
            ])
        total = second[t][0, z].astype(F32)
        for k in range(nz - 1):
            total = total + third[t][k].astype(F32)
        final[t][...] = total.reshape(2, rows, n)
        return launch([remote(final[t].at[1 - c], theirs[t], send_sem.at[t, 0], recv_sem.at[t, 0], grid.device(a, b, z, 1 - c))])

    started = {}
    for turn in range(count + 4):
        for stage in (4, 3, 2, 1, 0):
            t = turn - stage
            if 0 <= t < count:
                if stage > 0:
                    for copy in started[t, stage - 1]:
                        copy.wait()
                if stage < 4:
                    started[t, stage] = begin(t, stage)
                else:
                    n = parts[t].shape[-1]
                    outs[t][c] = final[t][c]
                    outs[t][1 - c] = theirs[t][...]


def scatter(grid, parts, orders, collective_id, name):
    rows = parts[0].shape[0] // (grid.na * grid.nb * grid.nz)
    na, nb, nz = grid.na, grid.nb, grid.nz
    shaped = [p.reshape(na, nb, nz, rows, p.shape[1]) for p in parts]
    widths = [p.shape[1] for p in parts]
    first = [pltpu.VMEM((1, nb, nz, rows, w) if o == "ab" else (nb - 1, na, nz, rows, w), BF16) for o, w in zip(orders, widths)]
    second = [pltpu.VMEM((nb - 1, nz, rows, w) if o == "ab" else (1, nz, rows, w), BF16) for o, w in zip(orders, widths)]
    third = [pltpu.VMEM((nz - 1, rows, w), BF16) for w in widths]
    final = [pltpu.VMEM((2, rows // 2, w), F32) for w in widths]
    theirs = [pltpu.VMEM((rows // 2, w), F32) for w in widths]
    moved = sum(widths) * rows * na * nb * nz * 2
    return pl.pallas_call(
        functools.partial(scatter_kernel, grid, orders),
        out_shape=[jax.ShapeDtypeStruct((2, rows // 2, w), F32) for w in widths],
        in_specs=[pl.BlockSpec(memory_space=pltpu.VMEM)] * len(parts),
        out_specs=[pl.BlockSpec(memory_space=pltpu.VMEM)] * len(parts),
        scratch_shapes=first + second + third + final + theirs + [
            pltpu.SemaphoreType.DMA((len(parts), nz + nb)),
            pltpu.SemaphoreType.DMA((len(parts), nz + nb)),
        ],
        compiler_params=pltpu.CompilerParams(collective_id=collective_id, has_side_effects=True, vmem_limit_bytes=VMEM_LIMIT),
        cost_estimate=pl.CostEstimate(flops=0, bytes_accessed=moved * 20, transcendentals=0),
        name=name,
    )(*shaped)


def small_kernel(n_dp, n_seq, x_ref, out_ref, held, total, send_sem, recv_sem):
    count = n_dp * n_seq
    me = lax.axis_index("dp") * n_seq + lax.axis_index("seq")

    def device(k):
        other = lax.rem(me + k, count)
        return other, (other // n_seq, lax.rem(other, n_seq))

    barrier = pltpu.get_barrier_semaphore()

    def greet(k, carry):
        pl.semaphore_signal(barrier, inc=1, device_id=device(k)[1], device_id_type=MESH)
        return carry

    lax.fori_loop(1, count, greet, 0)
    pl.semaphore_wait(barrier, count - 1)

    def deal(k, carry):
        other, place = device(k)
        remote(x_ref.at[other], held.at[me], send_sem.at[0], recv_sem.at[0], place).start()
        return carry

    lax.fori_loop(1, count, deal, 0)
    held[me] = x_ref[me]
    most = pl.ds(0, count - 1)
    everyone = device(1)[1]
    remote(x_ref.at[most], held.at[most], send_sem.at[0], recv_sem.at[0], everyone).wait()
    total[...] = lax.fori_loop(1, count, lambda k, s: s + held[k], held[0])

    def tell(k, carry):
        place = device(k)[1]
        remote(total, out_ref.at[me], send_sem.at[1], recv_sem.at[1], place).start()
        return carry

    lax.fori_loop(1, count, tell, 0)
    out_ref[me] = total[...]
    remote(x_ref.at[most], out_ref.at[most], send_sem.at[1], recv_sem.at[1], everyone).wait()


def small_sum(n_dp, n_seq, arrays, collective_id):
    count = n_dp * n_seq
    flat = jnp.concatenate([x.reshape(-1) for x in arrays])
    rows = -(-flat.shape[0] // (count * 128 * 8)) * 8
    padded = jnp.pad(flat, (0, count * rows * 128 - flat.shape[0])).reshape(count, rows, 128)
    summed = pl.pallas_call(
        functools.partial(small_kernel, n_dp, n_seq),
        out_shape=jax.ShapeDtypeStruct(padded.shape, F32),
        in_specs=[pl.BlockSpec(memory_space=pltpu.VMEM)],
        out_specs=pl.BlockSpec(memory_space=pltpu.VMEM),
        scratch_shapes=[
            pltpu.VMEM(padded.shape, F32),
            pltpu.VMEM((rows, 128), F32),
            pltpu.SemaphoreType.DMA((2,)),
            pltpu.SemaphoreType.DMA((2,)),
        ],
        compiler_params=pltpu.CompilerParams(collective_id=collective_id, has_side_effects=True),
        name="small_sum",
    )(padded).reshape(-1)
    results, at = [], 0
    for x in arrays:
        results.append(summed[at : at + x.size].reshape(x.shape))
        at += x.size
    return results


def pair_kernel(n_in, *refs):
    ins, outs = refs[:n_in], refs[n_in : 2 * n_in]
    local_sem, send_sem, recv_sem = refs[2 * n_in :]
    dp, seq = lax.axis_index("dp"), lax.axis_index("seq")
    c = lax.rem(seq, 2)
    other = (dp, seq + 1 - 2 * c)
    barrier = pltpu.get_barrier_semaphore()
    pl.semaphore_signal(barrier, inc=1, device_id=other, device_id_type=MESH)
    pl.semaphore_wait(barrier, 1)
    copies = []
    for i in range(n_in):
        copies.append(remote(ins[i], outs[i].at[:, c], send_sem.at[i], recv_sem.at[i], other))
        copies.append(pltpu.make_async_copy(ins[i], outs[i].at[:, c], local_sem.at[i]))
    for copy in copies:
        copy.start()
    for copy in copies:
        copy.wait()


def pair_gather(arrays, collective_id):
    n = len(arrays)
    return pl.pallas_call(
        functools.partial(pair_kernel, n),
        out_shape=[jax.ShapeDtypeStruct((x.shape[0], 2, *x.shape[1:]), x.dtype) for x in arrays],
        in_specs=[pl.BlockSpec(memory_space=pl.ANY)] * n,
        out_specs=[pl.BlockSpec(memory_space=pl.ANY)] * n,
        scratch_shapes=[pltpu.SemaphoreType.DMA((n,))] * 3,
        compiler_params=pltpu.CompilerParams(collective_id=collective_id, has_side_effects=True),
        name="pair_gather",
    )(*arrays)


def attention_kernel(width, heads, tile, edge, length, x_ref, kdoc_ref, qdoc_ref, o_ref, dq_ref, dk_ref, dv_ref,
                     s_ref, kt_ref, vt_ref, ot_ref, dqt_ref):
    i = pl.program_id(0)
    tiles = length // tile
    scale = 1.0 / math.sqrt(HEAD_DIM)

    @pl.when(i == 0)
    def _():
        dk_ref[...] = jnp.zeros_like(dk_ref)
        dv_ref[...] = jnp.zeros_like(dv_ref)

        def turn(j, carry):
            at = pl.ds(pl.multiple_of(j * tile, tile), tile)
            kt_ref[:, at] = x_ref[at, width : 2 * width].T
            vt_ref[:, at] = x_ref[at, 2 * width : 3 * width].T
            return carry

        lax.fori_loop(0, tiles, turn, 0)

    rows = pl.ds(pl.multiple_of(i * tile, tile), tile)
    lanes = lax.broadcasted_iota(jnp.int32, (tile, width), 1) // HEAD_DIM
    query = x_ref[rows, 0:width] * jnp.asarray(scale, BF16)
    grad = x_ref[rows, 3 * width : 4 * width]
    queries = [jnp.where(lanes == h, query, jnp.zeros_like(query)) for h in range(heads)]
    grads = [jnp.where(lanes == h, grad, jnp.zeros_like(grad)) for h in range(heads)]
    all_queries = jnp.concatenate(queries, axis=0)
    all_grads = jnp.concatenate(grads, axis=0)
    qdoc = qdoc_ref[:, rows]
    qpos = i * tile + lax.broadcasted_iota(jnp.int32, (tile, tile), 1)
    head_edge = -(-edge // tile)
    tail_edge = (length - edge) // tile

    def scores(j, tops):
        at = pl.ds(pl.multiple_of(j * tile, tile), tile)
        keys = x_ref[at, width : 2 * width]
        found = [against(keys, queries[h]) for h in range(heads)]
        checked = (j == i) | (j < head_edge) | (i >= tail_edge)

        def masked():
            kdoc = jnp.concatenate([kdoc_ref[at, :]] * (tile // 128), axis=1)
            kpos = j * tile + lax.broadcasted_iota(jnp.int32, (tile, tile), 0)
            allowed = (kdoc == qdoc) & (kpos <= qpos)
            return [jnp.where(allowed, s, NEG) for s in found]

        found = lax.cond(checked, masked, lambda: found)
        for h in range(heads):
            s_ref[h, at, :] = found[h]
        return [jnp.maximum(t, jnp.max(s.reshape(tile // 8, 8, tile), axis=0)) for t, s in zip(tops, found)]

    tops = lax.fori_loop(0, i + 1, scores, [jnp.full((8, tile), NEG, F32)] * heads)
    tops = [jnp.max(t, axis=0, keepdims=True) for t in tops]
    ot_ref[...] = jnp.zeros_like(ot_ref)
    dqt_ref[...] = jnp.zeros_like(dqt_ref)

    def weigh(j, totals):
        at = pl.ds(pl.multiple_of(j * tile, tile), tile)
        new = []
        for h in range(heads):
            own = slice(h * HEAD_DIM, (h + 1) * HEAD_DIM)
            weights = jnp.exp(s_ref[h, at, :] - tops[h])
            s_ref[h, at, :] = weights
            new.append(totals[h] + jnp.sum(weights.reshape(tile // 8, 8, tile), axis=0))
            ot_ref[own, :] += product(vt_ref[own, at], weights.astype(BF16))
        return new

    totals = lax.fori_loop(0, i + 1, weigh, [jnp.zeros((8, tile), F32)] * heads)
    inverse = [1.0 / jnp.sum(t, axis=0, keepdims=True) for t in totals]
    grad_t = grad.astype(F32).T
    deltas = []
    for h in range(heads):
        own = slice(h * HEAD_DIM, (h + 1) * HEAD_DIM)
        value = ot_ref[own, :] * inverse[h]
        ot_ref[own, :] = value
        deltas.append(jnp.sum(value * grad_t[own], axis=0, keepdims=True))
    o_ref[...] = ot_ref[...].T.astype(BF16)

    def back(j, carry):
        at = pl.ds(pl.multiple_of(j * tile, tile), tile)
        values = x_ref[at, 2 * width : 3 * width]
        probs_low, grads_low = [], []
        for h in range(heads):
            own = slice(h * HEAD_DIM, (h + 1) * HEAD_DIM)
            probs = s_ref[h, at, :] * inverse[h]
            probs_grad = against(values, grads[h])
            scores_grad = (probs * (probs_grad - deltas[h])).astype(BF16)
            probs_low.append(probs.astype(BF16))
            grads_low.append(scores_grad)
            dqt_ref[own, :] += product(kt_ref[own, at], scores_grad)
        dv_ref[at, :] += product(jnp.concatenate(probs_low, axis=1), all_grads)
        dk_ref[at, :] += product(jnp.concatenate(grads_low, axis=1), all_queries)
        return carry

    lax.fori_loop(0, i + 1, back, 0)
    dq_ref[...] = dqt_ref[...].T * scale


def attention(dealt, documents, heads, edge):
    length = dealt.shape[0]
    width = heads * HEAD_DIM
    tile = 256
    kdoc = jnp.broadcast_to(documents[:, None], (length, 128))
    qdoc = documents[None, :]
    whole = lambda i: (0, 0)
    part = lambda i: (i, 0)
    pairs = length * length // 2 * heads
    return pl.pallas_call(
        functools.partial(attention_kernel, width, heads, tile, edge, length),
        grid=(length // tile,),
        out_shape=[jax.ShapeDtypeStruct((length, width), BF16)] + [jax.ShapeDtypeStruct((length, width), F32)] * 3,
        in_specs=[
            pl.BlockSpec((length, 4 * width), whole),
            pl.BlockSpec((length, 128), whole),
            pl.BlockSpec((1, length), whole),
        ],
        out_specs=[
            pl.BlockSpec((tile, width), part),
            pl.BlockSpec((tile, width), part),
            pl.BlockSpec((length, width), whole),
            pl.BlockSpec((length, width), whole),
        ],
        scratch_shapes=[
            pltpu.VMEM((heads, length, tile), F32),
            pltpu.VMEM((width, length), BF16),
            pltpu.VMEM((width, length), BF16),
            pltpu.VMEM((width, tile), F32),
            pltpu.VMEM((width, tile), F32),
        ],
        compiler_params=pltpu.CompilerParams(vmem_limit_bytes=VMEM_LIMIT),
        cost_estimate=pl.CostEstimate(flops=pairs * 64 * 2 * 6 * 4, bytes_accessed=length * width * 20, transcendentals=pairs),
        name="attention",
    )(dealt, kdoc, qdoc)


def on_device(
    grid,
    history,
    documents,
    cotangent,
    mixer_gain,
    mixer_inner,
    mixer_outer,
    mixer_bias,
    stream_gain,
    stream_bias,
    inbound_weight,
    inbound_bias,
    outbound_weight,
    outbound_bias,
    expand,
    expand_bias,
    contract,
    contract_bias,
):
    n_dp, n_seq, nz = grid.n_dp, grid.n_seq, grid.nz
    tokens, width = history.shape[2], history.shape[3]
    hidden_width = expand.shape[1]
    half, hidden_half = width // 2, hidden_width // 2
    both = 2 * tokens
    length = documents.shape[1]
    heads = HEADS // n_seq
    own_width = heads * HEAD_DIM
    seq = lax.axis_index("seq")
    z, c = seq // 2, lax.rem(seq, 2)

    def take(array, start, size, axis=0):
        return lax.dynamic_slice_in_dim(array, start, size, axis)

    pick = lambda base: (lambda core: base + core * half)
    weight_k, weight_v, weight_q, weight_o = gather(
        grid,
        [inbound_weight, outbound_weight],
        [
            (0, pick(width), 0, 0, half, "ba"),
            (0, pick(2 * width), 1, 0, half, "ab"),
            (0, pick(0), 2, 0, half, "ba"),
            (1, pick(0), 3, 0, half, "ab"),
        ],
        [half] * 4,
        1,
        "gather_attention",
    )

    history_full = history[:, 0].astype(F32)
    last = history_full[-1]
    scaled, rms_pull = jax.vjp(rms_scale, last, mixer_gain.astype(F32))
    scaled_low = scaled.astype(BF16)
    mix_pre = product(scaled_low, mixer_inner)
    mix_value, mix_pull = jax.vjp(exact_gelu, mix_pre)
    mix_hidden = mix_value.astype(BF16)
    coeffs = (product(mix_hidden, mixer_outer) + mixer_bias.astype(F32)).reshape(tokens, 4, -1)
    streams = jnp.einsum("tcj,jtd->ctd", coeffs, history_full, precision=HIGHEST)
    normed, norm_pull = jax.vjp(layer_norm, streams, stream_gain.astype(F32), stream_bias.astype(F32))
    lowered_own = normed.astype(BF16)
    grad_own = cotangent[0]

    lowered, grad_low = pair_gather([lowered_own, cotangent], 2)
    lowered = lowered.reshape(4, both, width)
    grad_low = grad_low.reshape(both, width)

    bias_in = inbound_bias.astype(F32)
    positions = z * both + jnp.arange(both, dtype=jnp.int32)
    tables = rotary_tables(positions, half)
    query = product(lowered[0], weight_q) + take(bias_in, c * half, half)
    key = product(lowered[1], weight_k) + take(bias_in, width + c * half, half)
    value = product(lowered[2], weight_v) + take(bias_in, 2 * width + c * half, half)
    attended_grad = product(grad_low, weight_o)
    sent = [rotate(query, tables, 1.0), rotate(key, tables, 1.0), value, attended_grad]
    sent = jnp.concatenate([x.astype(BF16).reshape(both, nz, own_width) for x in sent], axis=-1)
    sent = jnp.transpose(sent, (1, 0, 2))
    groups = [[2 * k + core for k in range(nz)] for core in range(2)]
    dealt = lax.all_to_all(sent, "seq", 0, 0, axis_index_groups=groups, tiled=True)

    expand_in, contract_in, sent_seen = lax.optimization_barrier((expand, contract, sent[0, 0]))
    quarter = hidden_half // 2
    chunks = []
    for part in range(2):
        chunks.append((0, (lambda core, part=part: core * hidden_half + part * quarter), 0, part * quarter, quarter, "ba"))
        chunks.append((1, (lambda core, part=part: core * hidden_half + part * quarter), 1, part * quarter, quarter, "ab"))
    weight_e, weight_c = gather(grid, [expand_in, contract_in], chunks, [hidden_half] * 2, 3, "gather_feed")

    expanded = product(lowered[3], weight_e) + take(expand_bias.astype(F32), c * hidden_half, hidden_half)
    hidden_value, hidden_pull = jax.vjp(exact_gelu, expanded)
    hidden_low = hidden_value.astype(BF16)
    feed = against(hidden_low, weight_c)

    attended, dq, dk, dv = attention(dealt.reshape(length, 4 * own_width), documents[0], heads, tokens)
    back_tables = rotary_tables(jnp.arange(length, dtype=jnp.int32), own_width)
    dq = rotate(dq, back_tables, -1.0)
    dk = rotate(dk, back_tables, -1.0)
    head_bias_grads = [jnp.sum(x, axis=0) for x in (dq, dk, dv)]
    returned = jnp.concatenate([attended, dq.astype(BF16), dk.astype(BF16), dv.astype(BF16)], axis=-1)
    returned = returned.reshape(nz, both, 4 * own_width)
    collected = lax.all_to_all(returned, "seq", 0, 0, axis_index_groups=groups, tiled=True)

    expanded_grad = hidden_pull(product(grad_low, weight_c))[0]
    expanded_grad_low = expanded_grad.astype(BF16)
    expand_part = inner(lowered[3], expanded_grad_low).astype(BF16)
    contract_part = inner(grad_low, hidden_low).astype(BF16)
    expand_own, contract_own = scatter(grid, [expand_part, contract_part], ["ab", "ba"], 4, "scatter_feed")

    pieces = [
        jnp.transpose(collected[:, :, k * own_width : (k + 1) * own_width], (1, 0, 2)).reshape(both, half) for k in range(4)
    ]
    attended_low, dq_low, dk_low, dv_low = pieces

    out_part = against(attended_low, weight_o) + feed
    swap = [(s, s + 1 - 2 * (s % 2)) for s in range(n_seq)]
    out_theirs = lax.ppermute(take(out_part, (1 - c) * tokens, tokens), "seq", swap)
    out_own = take(out_part, c * tokens, tokens) + out_theirs
    layer_out = (streams[3] + (out_own + outbound_bias.astype(F32) + contract_bias.astype(F32))).astype(BF16)

    normed_part = jnp.stack(
        [
            against(dq_low, weight_q),
            against(dk_low, weight_k),
            against(dv_low, weight_v),
            against(expanded_grad_low, weight_e),
        ]
    )
    normed_theirs = lax.ppermute(take(normed_part, (1 - c) * tokens, tokens, 1).astype(BF16), "seq", swap)
    normed_grad = take(normed_part, c * tokens, tokens, 1) + normed_theirs.astype(F32)

    owned_q, owned_k, owned_v, owned_o = scatter(
        grid,
        [
            inner(lowered[0], dq_low).astype(BF16),
            inner(lowered[1], dk_low).astype(BF16),
            inner(lowered[2], dv_low).astype(BF16),
            inner(grad_low, attended_low).astype(BF16),
        ],
        ["ab", "ba", "ab", "ba"],
        5,
        "scatter_attention",
    )

    grad_full = grad_own.astype(F32)
    streams_grad, stream_gain_grad, stream_bias_grad = norm_pull(normed_grad)
    streams_grad = jnp.concatenate([streams_grad[:3], streams_grad[3:] + grad_full[None]], axis=0)
    history_grad = jnp.einsum("tcj,ctd->jtd", coeffs, streams_grad, precision=HIGHEST)
    coeffs_grad = jnp.einsum("ctd,jtd->tcj", streams_grad, history_full, precision=HIGHEST).reshape(tokens, -1)
    mixer_bias_grad = jnp.sum(coeffs_grad, axis=0)
    coeffs_grad_low = coeffs_grad.astype(BF16)
    mixer_outer_grad = inner(mix_hidden, coeffs_grad_low)
    mix_pre_grad_low = mix_pull(against(coeffs_grad_low, mixer_outer))[0].astype(BF16)
    mixer_inner_grad = inner(scaled_low, mix_pre_grad_low)
    last_grad, mixer_gain_grad = rms_pull(against(mix_pre_grad_low, mixer_inner))
    history_grad = jnp.concatenate([history_grad[:-1], history_grad[-1:] + last_grad[None]], axis=0)

    first = c * half + z * own_width
    inbound_bias_grad = jnp.zeros((3 * width,), F32)
    for k in range(3):
        inbound_bias_grad = lax.dynamic_update_slice_in_dim(inbound_bias_grad, head_bias_grads[k], k * width + first, 0)
    expand_bias_grad = lax.dynamic_update_slice_in_dim(
        jnp.zeros((hidden_width,), F32), jnp.sum(expanded_grad, axis=0), c * hidden_half, 0
    )
    small = small_sum(
        n_dp,
        n_seq,
        [
            mixer_gain_grad,
            mixer_inner_grad,
            mixer_outer_grad,
            mixer_bias_grad,
            stream_gain_grad,
            stream_bias_grad,
            inbound_bias_grad,
            jnp.sum(grad_full, axis=0),
            expand_bias_grad,
        ],
        6,
    )

    def side(x):
        return jnp.concatenate([x[0], x[1]], axis=-1)

    return (
        layer_out[None],
        history_grad[:, None],
        small[0],
        small[1],
        small[2],
        small[3],
        small[4],
        small[5],
        jnp.concatenate([owned_q[0], owned_q[1], owned_k[0], owned_k[1], owned_v[0], owned_v[1]], axis=-1),
        small[6],
        side(owned_o),
        small[7],
        side(expand_own),
        small[8],
        side(contract_own),
        small[7],
    )


def solution(mesh):
    rows = P(("dp", "seq"), None)
    placed = (
        P(None, "dp", "seq", None),
        P("dp", None),
        P("dp", "seq", None),
        P(),
        P(),
        P(),
        P(),
        P(),
        P(),
        rows,
        P(),
        rows,
        P(),
        rows,
        P(),
        rows,
        P(),
    )
    grid = Grid(mesh.shape["dp"], mesh.shape["seq"])
    return jax.shard_map(
        functools.partial(on_device, grid),
        mesh=mesh,
        in_specs=placed,
        out_specs=(
            P("dp", "seq", None),
            P(None, "dp", "seq", None),
            P(),
            P(),
            P(),
            P(),
            P(),
            P(),
            rows,
            P(),
            rows,
            P(),
            rows,
            P(),
            rows,
            P(),
        ),
        check_vma=False,
    )
```

time: 1540 us -> 1140 us (0.74)
  waiting for transfers between devices: 825 us -> 0.01 us
  Pallas kernels: 0 us -> 787 us
  matrix products: 384 us -> 143 us
  local copies, waits for them, and re-layouts: 205 us -> 98.7 us
  starting transfers between devices: 0.57 us -> 17.3 us
    pallas_call x0 -> x7, Pallas kernels: none -> 787 us  [the longest x2 281 us: gather(): pl.pallas_call(functools.partial(gather_kernel, grid, rows, chunks, len(a...]
    reduce_scatter x1 -> x0, waiting for transfers between devices: 439 us -> none  [on_device(): lax.psum_scatter(jnp.concatenate([inner(lowered[0], proj_grad_low[:, :wid...]
    all_gather x5 -> x0, waiting for transfers between devices: 175 us -> none  [the longest x1 106 us: on_device(): pair_all = lax.all_gather(pair_low, 'seq', axis=1, tiled=True)]
    psum x2 -> x0, waiting for transfers between devices: 130 us -> none  [on_device(): lax.psum((mixer_gain_grad, mixer_inner_grad, mixer_outer_grad, mixer_bias...]
    dot_general x56 -> x8, matrix products: 131 us -> 16.4 us  [against(): lax.dot_general(left, right, (((1,), (1,)), ((), ())), preferred_element_...]
    unnamed x10 -> x0, waiting for transfers between devices: 79.8 us -> none
    dot_general x40 -> x8, matrix products: 84.2 us -> 20.3 us  [inner(): lax.dot_general(left, right, (((0,), (0,)), ((), ())), preferred_element_...]
    unnamed x132 -> x140, local copies, waits for them, and re-layouts: 91.2 us -> 28 us
  transfers between devices with their start and end apart: 9 -> 4, of which waited for: 7 -> 0; matrix products, arithmetic and copies ran while one was open for 38% -> 9% of each run, Pallas kernels for 0% -> 39%
where the time goes in v1:
time: 1140 us; the launch traced here: 1130 us
  Pallas kernels  787 us (69%)
  matrix products  143 us (13%)
  local copies, waits for them, and re-layouts  98.7 us (9%)
  other arithmetic  85.9 us (8%)
  starting transfers between devices  17.3 us (2%)
    pallas_call x2, Pallas kernels, gather(): pl.pallas_call(functools.partial(gather_kernel, grid, rows, chunks, len(a...  281 us
    pallas_call x2, Pallas kernels, scatter(): pl.pallas_call(functools.partial(scatter_kernel, grid, orders), out_shape...  248 us
    pallas_call x1, Pallas kernels, pair_gather(): pl.pallas_call(functools.partial(pair_kernel, n), out_shape=[jax.ShapeDty...  121 us
    pallas_call x1, Pallas kernels, attention(): pl.pallas_call(functools.partial(attention_kernel, width, heads, tile, ed...  115 us
    dot_general x8, matrix products, product(): return jnp.dot(left, right, preferred_element_type=F32)  44.6 us
    unnamed x140, local copies, waits for them, and re-layouts  28 us
    dot_general x1, matrix products, on_device(): jnp.einsum('tcj,ctd->jtd', coeffs, streams_grad, precision=HIGHEST)  25.1 us
    pallas_call x1, Pallas kernels, small_sum(): pl.pallas_call(functools.partial(small_kernel, n_dp, n_seq), out_shape=ja...  23 us
  transfers between devices with their start and end apart: 4, of which 0 were waited for; matrix products, arithmetic and copies ran while one was open for 9% of the time, Pallas kernels for 39%

profile of v1, /device:TPU:0, one launch (start us, length us, event | category | flops | bytes accessed | tf_op | source)
XLA Modules:
  0.0 1134.3 jit_solution(17322414267068952198)
XLA Ops:
  2.8 1.4 fusion.50
  5.4 2.3 multiply_convert_fusion.1
  8.8 17.1 %fusion.2 = f32[384,4,1024]{2,1,0:T(4,128)S(1)} fusion(f32[384,4,9]{2,1,0:T(4,128)S(1)} %copy.45, bf16[9,384,1024]{2,1,0:T(8,128)(2,1)} %bitcast.177), kind=kOutput, calls=%fused_computation.3 | convolution fusion | flops 169869312 | bytes 13424640 | tf_op jit(solution)/shard_map/tcj,jtd->ctd/dot_general | solution.py:579
  26.0 3.4 fusion.85
  29.4 3.5 multiply_reduce_fusion.2
  33.5 5.4 add_convert_fusion.refs_0_
  38.9 120.8 %pair_gather.1 = (bf16[4,2,384,1024]{3,2,1,0:T(8,128)(2,1)}, bf16[1,2,384,1024]{3,2,1,0:T(8,128)(2,1)}) custom-call(bf16[4,384,1024]{2,1,0:T(8,128)(2,1)} %add_convert_fusion.refs_0_, bf16[1,384,1024]{2,1,0:T(8,128)(2,1)} %refs_1_.2), custom_call_target="tpu_custom_call" | custom-call | tf_op jit(solution)/shard_map/pair_gather/pallas_call | solution.py:378
  159.7 5.4 fusion.94
  165.1 85.5 %gather_attention.1 = (bf16[2,2,4,64,512]{4,3,2,1,0:T(8,128)(2,1)}, bf16[2,2,4,64,512]{4,3,2,1,0:T(8,128)(2,1)}, bf16[2,2,4,64,512]{4,3,2,1,0:T(8,128)(2,1)}, bf16[2,2,4,64,512]{4,3,2,1,0:T(8,128)(2,1)}) custom-call(bf16[32,3072]{1,0:T(8,128)(2,1)} %refs_0_.1, bf16[32,1024]{1,0:T(8,128)(2,1)} %refs_1_.3), custom_call_target="tpu_custom_call" | custom-call | bytes 83886080 | tf_op jit(solution)/shard_map/gather_attention/pallas_call | solution.py:160
  250.7 2.3 convolution_add_fusion.2
  253.1 2.4 convolution_add_fusion.1
  255.6 2.8 fusion.102
  258.4 3.6 convolution_convert_fusion.6
  262.0 2.3 copy.51
  264.3 3.6 add_convert_fusion.1
  267.9 2.3 copy.50
  270.2 10.4 fusion.20
  280.6 1.6 copy.49
  282.3 1.5 copy.48
  283.8 1.9 maximum_bitcast_fusion.1
  285.7 4.3 all-to-all-start
  290.0 9.1 copy.93
  300.3 195.2 %gather_feed.1 = (bf16[2,2,4,64,2048]{4,3,2,1,0:T(8,128)(2,1)}, bf16[2,2,4,64,2048]{4,3,2,1,0:T(8,128)(2,1)}) custom-call(bf16[32,4096]{1,0:T(8,128)(2,1)} %refs_0_.2, bf16[32,4096]{1,0:T(8,128)(2,1)} %refs_1_.4), custom_call_target="tpu_custom_call" | custom-call | bytes 167772160 | tf_op jit(solution)/shard_map/gather_feed/pallas_call | solution.py:160
  495.5 8.8 fusion.109
  504.3 21.3 %fusion.87 = (f32[2048]{0:T(1024)S(1)}, bf16[768,2048]{1,0:T(8,128)(2,1)S(1)}, f32[768,2048]{1,0:T(8,128)}) fusion(f32[768,2048]{1,0:T(8,128)} %fusion.109, f32[2048]{0:T(1024)S(1)} %dynamic-slice_convert_fusion.1, bf16[768,1024]{1,0:T(8,128)(2,1)} %bitcast.229, bf16[1024,2048]{1,0:T(8,128)(2,1)} %bitcast.226), kind=kOutput, calls=%fused_computation.189 | convolution fusion | flops 3337615360 | bytes 21512192 | tf_op jit(solution)/shard_map/dot_general | solution.py:32
  526.3 1.5 dynamic_update_slice.15
  527.9 5.3 convolution_convert_fusion.1
  533.1 2.3 broadcast_in_dim.144.kdoc_ref
  535.4 115.3 %attention.1 = (bf16[3072,128]{1,0:T(8,128)(2,1)}, f32[3072,128]{1,0:T(8,128)}, f32[3072,128]{1,0:T(8,128)}, f32[3072,128]{1,0:T(8,128)}) custom-call(bf16[3072,512]{1,0:T(8,128)(2,1)} %bitcast.187, s32[3072,128]{1,0:T(8,128)} %broadcast_in_dim.144.kdoc_ref, s32[1,3072]{1,0:T(1,128)} %qdoc_ref.1), custom_call_target="tpu_custom_call" | custom-call | flops 28991029248 | bytes 7864320 | tf_op jit(solution)/shard_map/attention/pallas_call | solution.py:494
  650.7 2.5 fusion.97
  657.0 8.7 fusion.91
  666.1 2.8 copy.52
  668.9 12.3 %all-to-all-start.1 = ((bf16[4,768,512]{1,2,0:T(8,128)(2,1)}), bf16[4,768,512]{1,2,0:T(8,128)(2,1)S(1)}, u32[]{:S(2)}, u32[]{:S(2)}) async-start(bf16[4,768,512]{1,2,0:T(8,128)(2,1)} %copy.52), calls=%async_computation.1 | async-start | bytes 6291456 | tf_op jit(solution)/shard_map/all_to_all | solution.py:621
  681.2 6.3 multiply_convert_fusion
  687.6 5.0 convolution_convert_fusion
  692.6 163.4 %scatter_feed.1 = (f32[2,32,2048]{2,1,0:T(8,128)}, f32[2,32,2048]{2,1,0:T(8,128)}) custom-call(bf16[2,2,4,64,2048]{4,3,2,1,0:T(8,128)(2,1)} %bitcast.183, bf16[2,2,4,64,2048]{4,3,2,1,0:T(8,128)(2,1)} %bitcast.184), custom_call_target="tpu_custom_call" | custom-call | bytes 167772160 | tf_op jit(solution)/shard_map/scatter_feed/pallas_call | solution.py:277
  856.0 1.4 slice_bitcast_fusion.2
  859.1 5.2 fusion.110
  864.3 5.1 convolution_bitcast_fusion.1
  870.5 1.7 copy-done.12
  879.9 1.3 pad_maximum_fusion
  881.2 2.2 dynamic-slice_convert_fusion
  883.8 2.1 convolution_convert_fusion.5
  886.1 2.1 convolution_convert_fusion.4
  888.7 2.0 convolution_convert_fusion.3
  890.7 2.0 convolution_convert_fusion.2
  892.7 84.4 %scatter_attention.1 = (f32[2,32,512]{2,1,0:T(8,128)}, f32[2,32,512]{2,1,0:T(8,128)}, f32[2,32,512]{2,1,0:T(8,128)}, f32[2,32,512]{2,1,0:T(8,128)}) custom-call(bf16[2,2,4,64,512]{4,3,2,1,0:T(8,128)(2,1)} %bitcast.199, bf16[2,2,4,64,512]{4,3,2,1,0:T(8,128)(2,1)} %bitcast.200, bf16[2,2,4,64,512]{4,3,2,1,0:T(8,128)(2,1)} %bitcast.201, ...), custom_call_target="tpu_custom_call" | custom-call | bytes 83886080 | tf_op jit(solution)/shard_map/scatter_attention/pallas_call | solution.py:277
  984.5 3.3 fusion.57
  987.9 7.2 fusion.86
  995.1 5.0 multiply_reduce_fusion
  1000.2 4.8 broadcast_add_fusion
  1007.0 25.1 %convolution_bitcast_fusion = f32[9,384,1024]{2,0,1:T(8,128)} fusion(f32[384,4,9]{2,1,0:T(4,128)S(1)} %copy-done.6, f32[4,384,1024]{2,1,0:T(8,128)S(1)} %pad_maximum_fusion.1), kind=kOutput, calls=%fused_computation.8 | convolution fusion | flops 169869312 | bytes 20502528 | tf_op jit(solution)/shard_map/tcj,ctd->jtd/dot_general | solution.py:667
  1032.1 19.4 %fusion.105 = (f32[4,9]{1,0:T(4,128)S(1)}, bf16[384,4,9]{2,1,0:T(4,128)(2,1)S(1)}) fusion(bf16[9,384,1024]{2,1,0:T(8,128)(2,1)S(1)} %bitcast.180, f32[4,384,1024]{2,1,0:T(8,128)S(1)} %pad_maximum_fusion.1), kind=kOutput, calls=%fused_computation.203 | convolution fusion | flops 169896928 | bytes 13397136 | tf_op jit(solution)/shard_map/ctd,jtd->tcj/dot_general | solution.py:668
  1052.1 1.8 fusion.15
  1053.9 1.7 fusion.58
  1056.3 2.4 concatenate.67
  1059.4 23.0 %small_sum.1 = f32[32,16,128]{2,1,0:T(8,128)} custom-call(f32[32,16,128]{2,1,0:T(8,128)} %bitcast.198), custom_call_target="tpu_custom_call" | custom-call | tf_op jit(solution)/shard_map/small_sum/pallas_call | solution.py:336
  1086.6 1.5 fusion.106
  1088.1 1.4 slice.246
  1089.5 12.1 %slice.238 = f32[8,384,1024]{2,0,1:T(8,128)} slice(f32[9,384,1024]{2,0,1:T(8,128)} %convolution_bitcast_fusion), slice={[0:8], [0:384], [0:1024]} | slice | bytes 25165824 | tf_op jit(solution)/shard_map/slice | solution.py:675
  1101.6 1.5 add_add_fusion.1
  1103.1 5.9 slice_add_fusion
  1109.0 7.5 maximum_bitcast_fusion
  1116.5 13.5 %copy.59 = f32[9,1,384,1024]{3,2,1,0:T(8,128)} copy(f32[9,1,384,1024]{3,0,2,1:T(8,128)S(1)} %maximum_bitcast_fusion) | data formatting | bytes 28311552
  (210 shorter events, 42.3 us)
Async XLA Ops:
  0.6 4.7 copy-start
  0.7 7.6 copy-start.55
  2.1 30.8 %copy-start.22 = (f32[4,1024]{1,0:T(4,128)}, f32[4,1024]{1,0:T(4,128)S(1)}, u32[]{:S(2)}) copy-start(f32[4,1024]{1,0:T(4,128)S(1)} %convert_element_type.156) | copy-start | bytes 49156
  2.8 4.9 copy-start.35
  4.7 3.0 copy-start.41
  8.8 17.1 %copy-start.5 = (f32[384,4,9]{2,1,0:T(4,128)}, f32[384,4,9]{2,1,0:T(4,128)S(1)}, u32[]{:S(2)}) copy-start(f32[384,4,9]{2,1,0:T(4,128)S(1)} %copy.45) | copy-start | bytes 165892
  26.0 7.0 copy-start.1
  29.4 3.5 copy-start.24
  32.9 6.0 copy-start.28
  159.7 91.0 %copy-start.43 = (bf16[3072]{0:T(1024)(128)(2,1)S(1)}, bf16[3072]{0:T(1024)(128)(2,1)}, u32[]{:S(2)}) copy-start(bf16[3072]{0:T(1024)(128)(2,1)} %param.27) | copy-start | bytes 18436
  165.1 87.9 %copy-start.16 = (bf16[1,2,384,1024]{3,2,1,0:T(8,128)(2,1)}, bf16[1,2,384,1024]{3,2,1,0:T(8,128)(2,1)S(1)}, u32[]{:S(2)}) copy-start(bf16[1,2,384,1024]{3,2,1,0:T(8,128)(2,1)S(1)} %get-tuple-element.104) | copy-start | bytes 4718596
  250.6 2.4 copy-start.52
  280.6 3.2 copy-start.9
  280.6 3.2 copy-start.10
  285.7 247.4 %all-to-all-start = ((bf16[4,768,512]{2,1,0:T(8,128)(2,1)}), bf16[4,768,512]{2,1,0:T(8,128)(2,1)S(1)}, u32[]{:S(2)}, u32[]{:S(2)}) async-start(bf16[4,768,512]{2,1,0:T(8,128)(2,1)} %maximum_bitcast_fusion.1), calls=%async_computation | async-start | bytes 6291456 | tf_op jit(solution)/shard_map/all_to_all | solution.py:599
  290.0 9.2 copy-start.45
  290.0 9.7 copy-start.46
  495.5 8.8 copy-start.44
  504.3 23.5 %copy-start.18 = (bf16[1,2,384,1024]{3,2,1,0:T(8,128)(2,1)S(1)}, bf16[1,2,384,1024]{3,2,1,0:T(8,128)(2,1)}, u32[]{:S(2)}) copy-start(bf16[1,2,384,1024]{3,2,1,0:T(8,128)(2,1)} %get-tuple-element.105) | copy-start | bytes 4718596
  525.7 2.2 copy-start.59
  527.8 5.3 copy-start.39
  533.1 2.3 copy-start.11
  650.7 2.5 copy-start.2
  653.2 1.4 copy-start.3
  655.2 1.4 copy-start.19
  657.0 8.7 copy-start.21
  668.9 201.3 %all-to-all-start.1 = ((bf16[4,768,512]{1,2,0:T(8,128)(2,1)}), bf16[4,768,512]{1,2,0:T(8,128)(2,1)S(1)}, u32[]{:S(2)}, u32[]{:S(2)}) async-start(bf16[4,768,512]{1,2,0:T(8,128)(2,1)} %copy.52), calls=%async_computation.1 | async-start | bytes 6291456 | tf_op jit(solution)/shard_map/all_to_all | solution.py:621
  681.2 6.3 copy-start.49
  856.0 3.1 copy-start.48
  859.1 5.2 copy-start.47
  859.1 5.2 copy-start.60
  870.3 1.9 copy-start.12
  870.3 2.2 copy-start.20
  873.5 3.1 copy-start.7
  873.5 2.0 copy-start.54
  874.8 109.0 %collective-permute-start = (f32[384,1024]{1,0:T(8,128)}, f32[384,1024]{1,0:T(8,128)S(1)}, u32[]{:S(2)}, u32[]{:S(2)}) collective-permute-start(f32[384,1024]{1,0:T(8,128)} %constant_dynamic-slice_fusion), channel_id=1, source_target_pairs={{0,1},{1,0},{2,3},{3,2},{4,5},{5,4},{6,7},{7,6},{8,9},{9,8},{10,11... | collective-permute-start | bytes 4718600 | tf_op jit(solution)/shard_map/ppermute | solution.py:636
  875.5 1.2 copy-start.53
  876.7 1.2 copy-start.51
  878.0 1.9 copy-start.8
  881.2 7.5 copy-start.4
  881.2 2.6 copy-start.17
  883.4 2.6 copy-start.15
  883.4 104.4 %collective-permute-start.1 = (bf16[4,384,1024]{2,1,0:T(8,128)(2,1)}, bf16[4,384,1024]{2,1,0:T(8,128)(2,1)}, u32[]{:S(2)}, u32[]{:S(2)}) collective-permute-start(bf16[4,384,1024]{2,1,0:T(8,128)(2,1)} %dynamic-slice_convert_fusion), channel_id=1, source_target_pairs={{0,1},{1,0},{2,3},{3,2},{4,5},{5,4},{6,7},{7,6},{8,9},{9,8},{10,11... | collective-permute-start | bytes 9437192 | tf_op jit(solution)/shard_map/ppermute | solution.py:648
  886.1 2.6 copy-start.14
  888.7 2.0 copy-start.50
  890.7 97.1 %slice-start = ((s8[6291456]{0:T(1024)(128)(4,1)}), s8[4194304]{0:T(1024)(128)(4,1)S(1)}, s32[]{:S(2)}) async-start(s8[6291456]{0:T(1024)(128)(4,1)} %bitcast.175), calls=%async_computation.2 | async-start | bytes 8388608
  892.7 91.8 %copy-start.37 = (f32[1024]{0:T(1024)S(1)}, f32[1024]{0:T(1024)}, u32[]{:S(2)}) copy-start(f32[1024]{0:T(1024)} %convert_element_type.174) | copy-start | bytes 12292
  892.7 91.8 %copy-start.38 = (f32[1024]{0:T(1024)S(1)}, f32[1024]{0:T(1024)}, u32[]{:S(2)}) copy-start(f32[1024]{0:T(1024)} %convert_element_type.173) | copy-start | bytes 12292
  892.7 95.1 %slice-start.1 = ((s8[6291456]{0:T(1024)(128)(4,1)}), s8[2097152]{0:T(1024)(128)(4,1)S(1)}, s32[]{:S(2)}) async-start(s8[6291456]{0:T(1024)(128)(4,1)} %bitcast.175), calls=%async_computation.3 | async-start | bytes 4194304
  978.7 9.2 copy-start.23
  978.7 9.2 copy-start.25
  987.9 7.2 copy-start.29
  987.9 7.3 copy-start.27
  1000.1 4.8 copy-start.13
  1005.9 26.2 %slice-start.2 = ((s8[7077888]{0:T(1024)(128)(4,1)}), s8[4194304]{0:T(1024)(128)(4,1)S(1)}, s32[]{:S(2)}) async-start(s8[7077888]{0:T(1024)(128)(4,1)} %bitcast.178), calls=%async_computation.4 | async-start | bytes 8388608
  1007.0 25.1 %slice-start.3 = ((s8[7077888]{0:T(1024)(128)(4,1)}), s8[2883584]{0:T(1024)(128)(4,1)S(1)}, s32[]{:S(2)}) async-start(s8[7077888]{0:T(1024)(128)(4,1)} %bitcast.178), calls=%async_computation.5 | async-start | bytes 5767168
  1032.1 19.8 %copy-start.56 = (bf16[36,36]{1,0:T(8,128)(2,1)S(1)}, bf16[36,36]{1,0:T(8,128)(2,1)}, u32[]{:S(2)}) copy-start(bf16[36,36]{1,0:T(8,128)(2,1)} %param.22) | copy-start | bytes 7780
  1032.1 19.8 %copy-start.57 = (f32[384,36]{0,1:T(8,128)S(1)}, f32[384,36]{0,1:T(8,128)}, u32[]{:S(2)}) copy-start(f32[384,36]{0,1:T(8,128)} %get-tuple-element.103) | copy-start | bytes 165892
  1032.1 19.8 %copy-start.58 = (f32[384,36]{0,1:T(8,128)S(1)}, f32[384,36]{0,1:T(8,128)}, u32[]{:S(2)}) copy-start(f32[384,36]{0,1:T(8,128)} %get-tuple-element.152) | copy-start | bytes 165892
  1032.1 19.9 %copy-start.36 = (f32[1024]{0:T(1024)S(1)}, f32[1024]{0:T(1024)}, u32[]{:S(2)}) copy-start(f32[1024]{0:T(1024)} %copy-done.35) | copy-start | bytes 12292
  1032.1 19.9 %copy-start.42 = (f32[384]{0:T(512)S(1)}, f32[384]{0:T(512)}, u32[]{:S(2)}) copy-start(f32[384]{0:T(512)} %copy-done.41) | copy-start | bytes 4612
  1051.6 4.0 copy-start.31
  1053.9 35.7 %copy-start.33 = (f32[384]{0:T(512)S(1)}, f32[384]{0:T(512)}, u32[]{:S(2)}) copy-start(f32[384]{0:T(512)} %copy-done.32) | copy-start | bytes 4612
  1083.8 49.7 %copy-start.34 = (f32[1024]{0:T(1024)}, f32[1024]{0:T(1024)S(1)}, u32[]{:S(2)}) copy-start(f32[1024]{0:T(1024)S(1)} %get-tuple-element.203) | copy-start | bytes 12292
  (5 other events, 3.6 us)

commit v2 on v1

v2 whole, which is shorter than its diff:
```python
import functools
import math

import jax
import jax.numpy as jnp
from jax import lax
from jax.experimental import pallas as pl
from jax.experimental.pallas import tpu as pltpu
from jax.sharding import PartitionSpec as P

HEADS = 16
HEAD_DIM = 64
ROT_DIMS = 16
EPS = 1e-05
HIGHEST = lax.Precision.HIGHEST
NEG = -1e30
MESH = pl.DeviceIdType.MESH
F32 = jnp.float32
BF16 = jnp.bfloat16
VMEM_LIMIT = 56 * 1024 * 1024


def inner(left, right):
    return lax.dot_general(left, right, (((0,), (0,)), ((), ())), preferred_element_type=F32)


def against(left, right):
    return lax.dot_general(left, right, (((1,), (1,)), ((), ())), preferred_element_type=F32)


def product(left, right):
    return jnp.dot(left, right, preferred_element_type=F32)


def exact_gelu(value):
    return jax.nn.gelu(value, approximate=False)


def phi(value):
    return 0.5 * (1.0 + lax.erf(value * (1.0 / math.sqrt(2.0))))


def gelu_slope(value):
    return phi(value) + value * jnp.exp(-0.5 * value * value) * (1.0 / math.sqrt(2.0 * math.pi))


def rotary_tables(positions, width):
    half = ROT_DIMS // 2
    place = jnp.arange(width) % HEAD_DIM
    freq = 10000.0 ** (-jnp.arange(half).astype(F32) * 2.0 / ROT_DIMS)
    angles = positions.astype(F32)[:, None] * freq[None, :]
    spread = lambda x: jnp.tile(x, (1, width // half))
    turned = (place < ROT_DIMS)[None, :]
    cosine = jnp.where(turned, spread(jnp.cos(angles)), 1.0)
    sine = jnp.where(turned, spread(jnp.sin(angles)), 0.0)
    above = jnp.where((place < half)[None, :], -sine, 0.0)
    below = jnp.where((place < half)[None, :], 0.0, sine)
    return cosine, above, below


def rotate(value, tables, sign):
    half = ROT_DIMS // 2
    cosine, above, below = tables
    width = value.shape[-1]
    up = pltpu.roll(value, width - half, 1)
    down = pltpu.roll(value, half, 1)
    return value * cosine + sign * (up * above + down * below)


class Grid:
    def __init__(self, n_dp, n_seq):
        self.n_dp, self.n_seq = n_dp, n_seq
        self.na, self.nb, self.nz = 2, n_dp // 2, n_seq // 2

    def here(self):
        dp, seq = lax.axis_index("dp"), lax.axis_index("seq")
        return dp // self.nb, lax.rem(dp, self.nb), seq // 2, lax.rem(seq, 2)

    def device(self, a, b, z, c):
        return (a * self.nb + b, z * 2 + c)

    def peers(self, a, b, z, c):
        found = [self.device(a, b, z, 1 - c), self.device(1 - a, b, z, c)]
        found += [self.device(a, lax.rem(b + k, self.nb), z, c) for k in range(1, self.nb)]
        found += [self.device(a, b, lax.rem(z + k, self.nz), c) for k in range(1, self.nz)]
        return found

    def greet(self, a, b, z, c):
        barrier = pltpu.get_barrier_semaphore()
        found = self.peers(a, b, z, c)
        for peer in found:
            pl.semaphore_signal(barrier, inc=1, device_id=peer, device_id_type=MESH)
        pl.semaphore_wait(barrier, len(found))


def remote(src, dst, send, recv, device):
    return pltpu.make_async_remote_copy(
        src_ref=src, dst_ref=dst, send_sem=send, recv_sem=recv, device_id=device, device_id_type=MESH
    )


def remote(src, dst, send, recv, device):
    return pltpu.make_async_remote_copy(
        src_ref=src, dst_ref=dst, send_sem=send, recv_sem=recv, device_id=device, device_id_type=MESH
    )


def start(copies):
    for copy in copies:
        copy.start()


def finish(copies):
    for copy in copies:
        copy.wait()


class Gathering:
    def __init__(self, grid, place, rows, chunks, ins, outs, local_sem, send_sem, recv_sem):
        self.grid, self.place, self.rows, self.chunks = grid, place, rows, chunks
        self.ins, self.outs = ins, outs
        self.local_sem, self.send_sem, self.recv_sem = local_sem, send_sem, recv_sem

    def copies(self, t, stage):
        a, b, z, c = self.place
        grid, rows = self.grid, self.rows
        nz, nb = grid.nz, grid.nb
        source, base, result, col, n, order = self.chunks[t]
        out, cols = self.outs[result], pl.ds(col, n)

        def send(src, dst, slot, device):
            return remote(src, dst, self.send_sem.at[t, slot], self.recv_sem.at[t, slot], device)

        if stage == 0:
            mine = self.ins[source].at[:, pl.ds(pl.multiple_of(base(c), 128), n)]
            theirs = self.ins[source].at[:, pl.ds(pl.multiple_of(base(1 - c), 128), n)]
            spot = out.at[a, b, z, pl.ds(pl.multiple_of(c * rows, rows), rows), cols]
            return [pltpu.make_async_copy(mine, spot, self.local_sem.at[t]), send(theirs, spot, 0, grid.device(a, b, z, 1 - c))]
        if stage == 1:
            block = out.at[a, b, z, :, cols]
            return [send(block, block, k, grid.device(a, b, lax.rem(z + k, nz), c)) for k in range(1, nz)]
        if order[stage - 2] == "b":
            block = out.at[a, b, :, :, cols] if stage == 2 else out.at[:, b, :, :, cols]
            return [send(block, block, nz + k - 1, grid.device(a, lax.rem(b + k, nb), z, c)) for k in range(1, nb)]
        block = out.at[a, b, :, :, cols] if stage == 2 else out.at[a, :, :, :, cols]
        return [send(block, block, nz + nb - 1, grid.device(1 - a, b, z, c))]

    def events(self, groups):
        def begin(u, stage):
            for t in groups[u]:
                start(self.copies(t, stage))

        def end(u, stage):
            for t in groups[u]:
                finish(self.copies(t, stage))

        def first():
            for u in range(len(groups)):
                begin(u, 0)

        def second():
            end(0, 0)
            begin(0, 1)

        found = [first, second]

        def turn(u):
            if u < len(groups):
                end(u, 1)
                begin(u, 2)
                if u + 1 < len(groups):
                    end(u + 1, 0)
                    begin(u + 1, 1)
            if 0 <= u - 1 < len(groups):
                end(u - 1, 2)
                begin(u - 1, 3)
            if 0 <= u - 2 < len(groups):
                end(u - 2, 3)

        return found + [functools.partial(turn, u) for u in range(len(groups) + 2)]


def gather_kernel(grid, rows, chunks, groups, n_in, n_out, *refs):
    ins, outs = refs[:n_in], refs[n_in : n_in + n_out]
    place = grid.here()
    grid.greet(*place)
    for event in Gathering(grid, place, rows, chunks, ins, outs, *refs[n_in + n_out :]).events(groups):
        event()


def gather_sems(grid, chunks):
    slots = grid.nz + grid.nb
    return [
        pltpu.SemaphoreType.DMA((len(chunks),)),
        pltpu.SemaphoreType.DMA((len(chunks), slots)),
        pltpu.SemaphoreType.DMA((len(chunks), slots)),
    ]


def gather(grid, arrays, chunks, groups, widths, collective_id, name):
    rows = arrays[0].shape[0]
    outs = [jax.ShapeDtypeStruct((grid.na, grid.nb, grid.nz, 2 * rows, w), BF16) for w in widths]
    moved = sum(w for w in widths) * 2 * rows * grid.na * grid.nb * grid.nz * 2
    results = pl.pallas_call(
        functools.partial(gather_kernel, grid, rows, chunks, groups, len(arrays), len(outs)),
        out_shape=outs,
        in_specs=[pl.BlockSpec(memory_space=pltpu.VMEM)] * len(arrays),
        out_specs=[pl.BlockSpec(memory_space=pl.ANY)] * len(outs),
        scratch_shapes=gather_sems(grid, chunks),
        compiler_params=pltpu.CompilerParams(collective_id=collective_id, has_side_effects=True),
        cost_estimate=pl.CostEstimate(flops=0, bytes_accessed=moved * 20, transcendentals=0),
        name=name,
    )(*arrays)
    return [r.reshape(-1, r.shape[-1]) for r in results]


class Scattering:
    def __init__(self, grid, place, chunks, parts, outs, scratch):
        self.grid, self.place, self.chunks, self.parts, self.outs = grid, place, chunks, parts, outs
        count = len(chunks)
        self.first, self.second, self.third, self.final = (scratch[i * count : (i + 1) * count] for i in range(4))
        self.local_sem, self.send_sem, self.recv_sem = scratch[4 * count :]

    def copies(self, t, stage):
        a, b, z, c = self.place
        grid = self.grid
        nz, nb = grid.nz, grid.nb
        source, col, n, order, result, base = self.chunks[t]
        part, cols = self.parts[source], pl.ds(col, n)
        first, second, third, final = self.first[t], self.second[t], self.third[t], self.final[t]

        def send(src, dst, slot, device):
            return remote(src, dst, self.send_sem.at[t, slot], self.recv_sem.at[t, slot], device)

        def over_a(src, dst):
            return [send(src(1 - a), dst(0), nz + nb - 1, grid.device(1 - a, b, z, c))]

        def over_b(src, dst):
            return [send(src(lax.rem(b + k, nb)), dst(k - 1), nz + k - 1, grid.device(a, lax.rem(b + k, nb), z, c)) for k in range(1, nb)]

        if stage == 0:
            if order == "ab":
                return over_a(lambda o: part.at[o, :, :, :, cols], lambda k: first.at[k])
            return over_b(lambda o: part.at[:, o, :, :, cols], lambda k: first.at[k])
        if stage == 1:
            return (over_b if order == "ab" else over_a)(lambda o: first.at[0, o], lambda k: second.at[k])
        if stage == 2:
            return [
                send(second.at[0, lax.rem(z + k, nz)], third.at[k - 1], k, grid.device(a, b, lax.rem(z + k, nz), c))
                for k in range(1, nz)
            ]
        spot = self.outs[result].at[:, pl.ds(pl.multiple_of(base(c), 128), n)]
        return [
            send(final.at[1 - c], spot, 0, grid.device(a, b, z, 1 - c)),
            pltpu.make_async_copy(final.at[c], spot, self.local_sem.at[t]),
        ]

    def add(self, t, stage):
        a, b, z, c = self.place
        nz = self.grid.nz
        source, col, n, order, result, base = self.chunks[t]
        part, cols = self.parts[source], pl.ds(col, n)
        first, second, third, final = self.first[t], self.second[t], self.third[t], self.final[t]
        if stage == 0:

            def step(i, carry):
                o, j = i // nz, lax.rem(i, nz)
                own = part[a, o, j, :, cols] if order == "ab" else part[o, b, j, :, cols]
                total = own.astype(F32)
                for k in range(first.shape[0]):
                    total = total + first[k, o, j].astype(F32)
                first[0, o, j] = total.astype(BF16)
                return carry

            lax.fori_loop(0, first.shape[1] * nz, step, 0)
        elif stage == 1:
            mine = b if order == "ab" else a

            def step(j, carry):
                total = first[0, mine, j].astype(F32)
                for k in range(second.shape[0]):
                    total = total + second[k, j].astype(F32)
                second[0, j] = total.astype(BF16)
                return carry

            lax.fori_loop(0, nz, step, 0)
        else:
            total = second[0, z].astype(F32)
            for k in range(nz - 1):
                total = total + third[k].astype(F32)
            final[...] = total.reshape(final.shape)

    def events(self, groups):
        def begin(u, stage):
            for t in groups[u]:
                start(self.copies(t, stage))

        def end(u, stage):
            for t in groups[u]:
                finish(self.copies(t, stage))
                if stage < 3:
                    self.add(t, stage)
                    start(self.copies(t, stage + 1))

        def first():
            for u in range(min(2, len(groups))):
                begin(u, 0)

        def turn(u):
            if u < len(groups):
                end(u, 0)
                if u + 2 < len(groups):
                    begin(u + 2, 0)
            for stage in (1, 2, 3):
                if 0 <= u - stage < len(groups):
                    end(u - stage, stage)

        return [first] + [functools.partial(turn, u) for u in range(len(groups) + 3)]


def scatter_kernel(grid, chunks, groups, n_in, n_out, *refs):
    place = grid.here()
    grid.greet(*place)
    work = Scattering(grid, place, chunks, refs[:n_in], refs[n_in : n_in + n_out], refs[n_in + n_out :])
    for event in work.events(groups):
        event()


def scatter_scratch(grid, chunks, rows):
    na, nb, nz = grid.na, grid.nb, grid.nz
    first = [pltpu.VMEM((1, nb, nz, rows, n) if o == "ab" else (nb - 1, na, nz, rows, n), BF16) for _, _, n, o, _, _ in chunks]
    second = [pltpu.VMEM((nb - 1, nz, rows, n) if o == "ab" else (1, nz, rows, n), BF16) for _, _, n, o, _, _ in chunks]
    third = [pltpu.VMEM((nz - 1, rows, n), BF16) for _, _, n, _, _, _ in chunks]
    final = [pltpu.VMEM((2, rows // 2, n), F32) for _, _, n, _, _, _ in chunks]
    return first + second + third + final + gather_sems(grid, chunks)


def scatter(grid, parts, chunks, groups, widths, collective_id, name):
    na, nb, nz = grid.na, grid.nb, grid.nz
    rows = parts[0].shape[0] // (na * nb * nz)
    shaped = [p.reshape(na, nb, nz, rows, p.shape[1]) for p in parts]
    moved = sum(p.size for p in parts) * 2
    return pl.pallas_call(
        functools.partial(scatter_kernel, grid, chunks, groups, len(parts), len(widths)),
        out_shape=[jax.ShapeDtypeStruct((rows // 2, w), F32) for w in widths],
        in_specs=[pl.BlockSpec(memory_space=pltpu.VMEM)] * len(parts),
        out_specs=[pl.BlockSpec(memory_space=pl.ANY)] * len(widths),
        scratch_shapes=scatter_scratch(grid, chunks, rows),
        compiler_params=pltpu.CompilerParams(collective_id=collective_id, has_side_effects=True, vmem_limit_bytes=VMEM_LIMIT),
        cost_estimate=pl.CostEstimate(flops=0, bytes_accessed=moved * 20, transcendentals=0),
        name=name,
    )(*shaped)


def small_kernel(n_dp, n_seq, x_ref, out_ref, held, total, send_sem, recv_sem):
    count = n_dp * n_seq
    me = lax.axis_index("dp") * n_seq + lax.axis_index("seq")

    def device(k):
        other = lax.rem(me + k, count)
        return other, (other // n_seq, lax.rem(other, n_seq))

    barrier = pltpu.get_barrier_semaphore()

    def greet(k, carry):
        pl.semaphore_signal(barrier, inc=1, device_id=device(k)[1], device_id_type=MESH)
        return carry

    lax.fori_loop(1, count, greet, 0)
    pl.semaphore_wait(barrier, count - 1)

    def deal(k, carry):
        other, place = device(k)
        remote(x_ref.at[other], held.at[me], send_sem.at[0], recv_sem.at[0], place).start()
        return carry

    lax.fori_loop(1, count, deal, 0)
    held[me] = x_ref[me]
    most = pl.ds(0, count - 1)
    everyone = device(1)[1]
    remote(x_ref.at[most], held.at[most], send_sem.at[0], recv_sem.at[0], everyone).wait()
    total[...] = lax.fori_loop(1, count, lambda k, s: s + held[k], held[0])

    def tell(k, carry):
        place = device(k)[1]
        remote(total, out_ref.at[me], send_sem.at[1], recv_sem.at[1], place).start()
        return carry

    lax.fori_loop(1, count, tell, 0)
    out_ref[me] = total[...]
    remote(x_ref.at[most], out_ref.at[most], send_sem.at[1], recv_sem.at[1], everyone).wait()


def small_sum(n_dp, n_seq, arrays, collective_id):
    count = n_dp * n_seq
    flat = jnp.concatenate([x.reshape(-1) for x in arrays])
    rows = -(-flat.shape[0] // (count * 128 * 8)) * 8
    padded = jnp.pad(flat, (0, count * rows * 128 - flat.shape[0])).reshape(count, rows, 128)
    summed = pl.pallas_call(
        functools.partial(small_kernel, n_dp, n_seq),
        out_shape=jax.ShapeDtypeStruct(padded.shape, F32),
        in_specs=[pl.BlockSpec(memory_space=pltpu.VMEM)],
        out_specs=pl.BlockSpec(memory_space=pltpu.VMEM),
        scratch_shapes=[
            pltpu.VMEM(padded.shape, F32),
            pltpu.VMEM((rows, 128), F32),
            pltpu.SemaphoreType.DMA((2,)),
            pltpu.SemaphoreType.DMA((2,)),
        ],
        compiler_params=pltpu.CompilerParams(collective_id=collective_id, has_side_effects=True),
        name="small_sum",
    )(padded).reshape(-1)
    results, at = [], 0
    for x in arrays:
        results.append(summed[at : at + x.size].reshape(x.shape))
        at += x.size
    return results


def blend(h_ref, coeffs, streams_ref):
    hist, block, width = h_ref.shape[0], h_ref.shape[2], h_ref.shape[3]
    spread = [jnp.broadcast_to(coeffs[:, k : k + 1], (block, 128)) for k in range(4 * hist)]
    for at in range(0, width, 128):
        lanes = slice(at, at + 128)
        inputs = [h_ref[j, 0, :, lanes].astype(F32) for j in range(hist)]
        for c in range(4):
            total = spread[c * hist] * inputs[0]
            for j in range(1, hist):
                total = total + spread[c * hist + j] * inputs[j]
            streams_ref[c, :, lanes] = total
    return spread


def mix_kernel(grid, rows, chunks, groups, h_ref, g_ref, gain_ref, inner_ref, outer_ref, bias_ref, sgain_ref, sbias_ref, in_ref, out_ref,
               lowered_ref, gpair_ref, last_ref, pre_ref, coeffs_ref, wk_ref, wv_ref, wq_ref, wo_ref,
               streams_ref, held_ref, local_sem, send_sem, recv_sem, pair_local, pair_send, pair_recv):
    i, steps = pl.program_id(0), pl.num_programs(0)
    a, b, z, c = place = grid.here()
    block = h_ref.shape[2]
    work = Gathering(grid, place, rows, chunks, [in_ref, out_ref], [wk_ref, wv_ref, wq_ref, wo_ref], local_sem, send_sem, recv_sem)
    events = work.events(groups)
    other = grid.device(a, b, z, 1 - c)

    def pair(k, src, dst):
        return [
            pltpu.make_async_copy(src, dst, pair_local.at[k]),
            remote(src, dst, pair_send.at[k], pair_recv.at[k], other),
        ]

    grads = lambda: pair(0, g_ref.at[0], gpair_ref.at[c])
    lowereds = lambda: pair(1, held_ref, lowered_ref.at[:, c])

    @pl.when(i == 0)
    def _():
        grid.greet(*place)
        events[0]()
        start(grads())

    @pl.when(i == 1)
    def _():
        events[1]()

    last = h_ref[h_ref.shape[0] - 1, 0].astype(F32)
    r = lax.rsqrt(jnp.mean(last * last, axis=1, keepdims=True) + EPS)
    scaled_low = (last * r * gain_ref[...]).astype(BF16)
    pre = product(scaled_low, inner_ref[...])
    pre_ref[...] = pre
    coeffs = product((pre * phi(pre)).astype(BF16), outer_ref[...]) + bias_ref[...]
    coeffs_ref[...] = coeffs
    blend(h_ref, coeffs, streams_ref)
    at = pl.ds(pl.multiple_of(i * block, block), block)
    for k in range(4):
        stream = streams_ref[k]
        centered = stream - jnp.mean(stream, axis=1, keepdims=True)
        rs = lax.rsqrt(jnp.mean(centered * centered, axis=1, keepdims=True) + EPS)
        held_ref[k, at, :] = (centered * rs * sgain_ref[k : k + 1, :] + sbias_ref[k : k + 1, :]).astype(BF16)
    last_ref[...] = streams_ref[3]

    @pl.when(i == steps - 1)
    def _():
        start(lowereds())
        for event in events[2:]:
            event()
        finish(grads())
        finish(lowereds())


def mix_forward(grid, history, cotangent, params, weights, chunks, groups, widths, collective_id):
    hist, _, tokens, width = history.shape
    mix = params[1].shape[1]
    block = 32
    rows = weights[0].shape[0]
    whole = pl.BlockSpec(memory_space=pltpu.VMEM)
    anywhere = pl.BlockSpec(memory_space=pl.ANY)
    part = lambda n: pl.BlockSpec((block, n), lambda i: (i, 0))
    results = pl.pallas_call(
        functools.partial(mix_kernel, grid, rows, chunks, groups),
        grid=(tokens // block,),
        out_shape=[
            jax.ShapeDtypeStruct((4, 2, tokens, width), BF16),
            jax.ShapeDtypeStruct((2, tokens, width), BF16),
            jax.ShapeDtypeStruct((tokens, width), F32),
            jax.ShapeDtypeStruct((tokens, mix), F32),
            jax.ShapeDtypeStruct((tokens, mix), F32),
        ]
        + [jax.ShapeDtypeStruct((grid.na, grid.nb, grid.nz, 2 * rows, w), BF16) for w in widths],
        in_specs=[pl.BlockSpec((hist, 1, block, width), lambda i: (0, 0, i, 0))] + [whole] * 9,
        out_specs=[anywhere, anywhere, part(width), part(mix), part(mix)] + [anywhere] * len(widths),
        scratch_shapes=[
            pltpu.VMEM((4, block, width), F32),
            pltpu.VMEM((4, tokens, width), BF16),
            *gather_sems(grid, chunks),
            pltpu.SemaphoreType.DMA((2,)),
            pltpu.SemaphoreType.DMA((2,)),
            pltpu.SemaphoreType.DMA((2,)),
        ],
        compiler_params=pltpu.CompilerParams(collective_id=collective_id, has_side_effects=True, vmem_limit_bytes=VMEM_LIMIT),
        cost_estimate=pl.CostEstimate(flops=tokens * width * 80, bytes_accessed=history.size * 40, transcendentals=0),
        name="mix_forward",
    )(history, cotangent, *params, *weights)
    lowered, gpair, last, pre, coeffs = results[:5]
    return (
        lowered.reshape(4, 2 * tokens, width),
        gpair.reshape(2 * tokens, width),
        last,
        pre,
        coeffs,
        [w.reshape(-1, w.shape[-1]) for w in results[5:]],
    )


def unmix_kernel(h_ref, own_ref, theirs_ref, g_ref, pre_ref, coeffs_ref, gain_ref, inner_ref, outer_ref, sgain_ref,
                 hist_ref, sgg_ref, sbg_ref, gg_ref, ig_ref, og_ref, bg_ref, ob_ref,
                 streams_ref, sg_ref, scaled_ref, mpg_ref, hidden_ref, cgl_ref):
    i, steps = pl.program_id(0), pl.num_programs(0)
    hist, block, width = h_ref.shape[0], h_ref.shape[2], h_ref.shape[3]
    mix = 4 * hist

    @pl.when(i == 0)
    def _():
        for ref in (sgg_ref, sbg_ref, gg_ref, bg_ref, ob_ref):
            ref[...] = jnp.zeros_like(ref)

    def down(x):
        return jnp.sum(x, axis=0, keepdims=True)

    coeffs = coeffs_ref[...]
    spread = blend(h_ref, coeffs, streams_ref)
    grad = g_ref[0].astype(F32)
    ob_ref[...] += down(grad)
    for c in range(4):
        stream = streams_ref[c]
        centered = stream - jnp.mean(stream, axis=1, keepdims=True)
        rs = lax.rsqrt(jnp.mean(centered * centered, axis=1, keepdims=True) + EPS)
        n = centered * rs
        ng = own_ref[c] + theirs_ref[c].astype(F32)
        sgg_ref[c : c + 1, :] += down(ng * n)
        sbg_ref[c : c + 1, :] += down(ng)
        w = ng * sgain_ref[c : c + 1, :]
        pulled = rs * (w - jnp.mean(w, axis=1, keepdims=True) - n * jnp.mean(w * n, axis=1, keepdims=True))
        sg_ref[c] = pulled + grad if c == 3 else pulled

    lane = lax.broadcasted_iota(jnp.int32, (block, mix), 1)
    cg = jnp.zeros((block, mix), F32)
    for j in range(hist):
        value = h_ref[j, 0].astype(F32)
        for c in range(4):
            cg = jnp.where(lane == c * hist + j, jnp.sum(value * sg_ref[c], axis=1, keepdims=True), cg)
    bg_ref[...] += down(cg)
    cg_low = cg.astype(BF16)
    pre = pre_ref[...]
    at = pl.ds(pl.multiple_of(i * block, block), block)
    mpg = (against(cg_low, outer_ref[...]) * gelu_slope(pre)).astype(BF16)
    last = h_ref[hist - 1, 0].astype(F32)
    r = lax.rsqrt(jnp.mean(last * last, axis=1, keepdims=True) + EPS)
    scaled_ref[at, :] = (last * r * gain_ref[...]).astype(BF16)
    mpg_ref[at, :] = mpg
    hidden_ref[at, :] = (pre * phi(pre)).astype(BF16)
    cgl_ref[at, :] = cg_low
    scaled_grad = against(mpg, inner_ref[...])
    gg_ref[...] += down(scaled_grad * last * r)
    w = scaled_grad * gain_ref[...]
    last_grad = r * (w - last * (r * r) * jnp.mean(w * last, axis=1, keepdims=True))
    for from_ in range(0, width, 128):
        lanes = slice(from_, from_ + 128)
        pulls = [sg_ref[c, :, lanes] for c in range(4)]
        for j in range(hist):
            total = spread[j] * pulls[0]
            for c in range(1, 4):
                total = total + spread[c * hist + j] * pulls[c]
            hist_ref[j, 0, :, lanes] = total + last_grad[:, lanes] if j == hist - 1 else total

    @pl.when(i == steps - 1)
    def _():
        ig_ref[...] = inner(mpg_ref[...], scaled_ref[...])
        og_ref[...] = inner(hidden_ref[...], cgl_ref[...])


def mix_backward(history, own, theirs, cotangent, pre, coeffs, params):
    hist, _, tokens, width = history.shape
    mix = pre.shape[1]
    block = 32
    whole = pl.BlockSpec(memory_space=pltpu.VMEM)
    part = lambda n: pl.BlockSpec((block, n), lambda i: (i, 0))
    four = pl.BlockSpec((4, block, width), lambda i: (0, i, 0))
    story = pl.BlockSpec((hist, 1, block, width), lambda i: (0, 0, i, 0))
    fixed = lambda *shape: pl.BlockSpec(shape, lambda i: (0,) * len(shape))
    return pl.pallas_call(
        unmix_kernel,
        grid=(tokens // block,),
        out_shape=[
            jax.ShapeDtypeStruct(history.shape, F32),
            jax.ShapeDtypeStruct((4, width), F32),
            jax.ShapeDtypeStruct((4, width), F32),
            jax.ShapeDtypeStruct((1, width), F32),
            jax.ShapeDtypeStruct((mix, width), F32),
            jax.ShapeDtypeStruct((mix, mix), F32),
            jax.ShapeDtypeStruct((1, mix), F32),
            jax.ShapeDtypeStruct((1, width), F32),
        ],
        in_specs=[story, four, four, pl.BlockSpec((1, block, width), lambda i: (0, i, 0)), part(mix), part(mix)] + [whole] * 4,
        out_specs=[story, fixed(4, width), fixed(4, width), fixed(1, width), fixed(mix, width), fixed(mix, mix), fixed(1, mix), fixed(1, width)],
        scratch_shapes=[
            pltpu.VMEM((4, block, width), F32),
            pltpu.VMEM((4, block, width), F32),
            pltpu.VMEM((tokens, width), BF16),
            pltpu.VMEM((tokens, mix), BF16),
            pltpu.VMEM((tokens, mix), BF16),
            pltpu.VMEM((tokens, mix), BF16),
        ],
        compiler_params=pltpu.CompilerParams(vmem_limit_bytes=VMEM_LIMIT),
        cost_estimate=pl.CostEstimate(flops=tokens * width * 300, bytes_accessed=history.size * 8, transcendentals=0),
        name="mix_backward",
    )(history, own, theirs, cotangent, pre, coeffs, *params)


def project_kernel(width, low_ref, g_ref, wq_ref, wk_ref, wv_ref, wo_ref, bias_ref, cos_ref, above_ref, below_ref, sent_ref):
    wide = wq_ref.shape[1]
    reps = wide // cos_ref.shape[1] if wide >= cos_ref.shape[1] else 1
    tables = [jnp.concatenate([t[:, :wide]] * reps, axis=1) for t in (cos_ref, above_ref, below_ref)]
    q = rotate(product(low_ref[0], wq_ref[...]) + bias_ref[0:1, :], tables, 1.0)
    k = rotate(product(low_ref[1], wk_ref[...]) + bias_ref[1:2, :], tables, 1.0)
    v = product(low_ref[2], wv_ref[...]) + bias_ref[2:3, :]
    g = product(g_ref[...], wo_ref[...])
    for n, x in enumerate((q, k, v, g)):
        x = x.astype(BF16)
        for m in range(wide // width):
            sent_ref[m, :, n * width : (n + 1) * width] = x[:, m * width : (m + 1) * width]


def project(grid, lowered, grad_low, weights, biases, tables, own_width):
    both = lowered.shape[1]
    nz = grid.nz
    wide = 2 * own_width
    whole = pl.BlockSpec(memory_space=pltpu.VMEM)
    cols = lambda n: pl.BlockSpec((n, wide), lambda i: (0, i))
    return pl.pallas_call(
        functools.partial(project_kernel, own_width),
        grid=(nz // 2,),
        out_shape=jax.ShapeDtypeStruct((nz, both, 4 * own_width), BF16),
        in_specs=[whole, whole] + [cols(weights[0].shape[0])] * 4 + [cols(3)] + [whole] * 3,
        out_specs=pl.BlockSpec((2, both, 4 * own_width), lambda i: (i, 0, 0)),
        compiler_params=pltpu.CompilerParams(vmem_limit_bytes=VMEM_LIMIT),
        cost_estimate=pl.CostEstimate(flops=8 * both * weights[0].size, bytes_accessed=lowered.size * 4, transcendentals=0),
        name="project",
    )(lowered, grad_low, *weights, biases, *tables)


def attention_kernel(width, heads, tile, step, edge, length, x_ref, kdoc_ref, qdoc_ref, o_ref, dq_ref, dk_ref, dv_ref,
                     s_ref, kt_ref, vt_ref, ot_ref, dqt_ref, dka_ref, dva_ref, top_ref):
    i = pl.program_id(0)
    tiles = length // tile
    scale = 1.0 / math.sqrt(HEAD_DIM)
    @pl.when(i == 0)
    def _():
        dka_ref[...] = jnp.zeros_like(dka_ref)
        dva_ref[...] = jnp.zeros_like(dva_ref)
        def turn(j, carry):
            at = pl.ds(pl.multiple_of(j * tile, tile), tile)
            kt_ref[:, at] = x_ref[at, width : 2 * width].T
            vt_ref[:, at] = x_ref[at, 2 * width : 3 * width].T
            return carry
        lax.fori_loop(0, tiles, turn, 0)
    rows = pl.ds(pl.multiple_of(i * tile, tile), tile)
    query = x_ref[rows, 0:width] * jnp.asarray(scale, BF16)
    grad = x_ref[rows, 3 * width : 4 * width]
    query_t, grad_t = query.T, grad.T
    lanes = lax.broadcasted_iota(jnp.int32, (tile, width), 1) // HEAD_DIM
    subs = lax.broadcasted_iota(jnp.int32, (width, tile), 0) // HEAD_DIM
    zero = jnp.zeros((), BF16)
    queries_t = [jnp.where(subs == h, query_t, zero) for h in range(heads)]
    grads_t = [jnp.where(subs == h, grad_t, zero) for h in range(heads)]
    all_queries = jnp.concatenate([jnp.where(lanes == h, query, zero) for h in range(heads)], axis=0)
    all_grads = jnp.concatenate([jnp.where(lanes == h, grad, zero) for h in range(heads)], axis=0)
    qdoc = qdoc_ref[:, rows]
    qpos = i * tile + lax.broadcasted_iota(jnp.int32, (step, tile), 1)
    head_edge = -(-edge // step)
    tail_edge = (length - edge) // tile
    per = tile // step
    count = (i + 1) * per
    ot_ref[...] = jnp.zeros_like(ot_ref)
    dqt_ref[...] = jnp.zeros_like(dqt_ref)
    top_ref[...] = jnp.full_like(top_ref, NEG)

    def fold(x, f):
        return f(x.reshape(step // 8, 8, tile), axis=0)

    def scores(j, carry):
        at = pl.ds(pl.multiple_of(j * step, step), step)
        checked = (j >= i * per) | (j < head_edge) | (i >= tail_edge)
        def run(mask):
            keys = x_ref[at, width : 2 * width]
            if mask:
                kdoc = jnp.concatenate([kdoc_ref[at, :]] * (tile // 128), axis=1)
                kpos = j * step + lax.broadcasted_iota(jnp.int32, (step, tile), 0)
                allowed = (kdoc == qdoc) & (kpos <= qpos)
            for h in range(heads):
                s = product(keys, queries_t[h])
                if mask:
                    s = jnp.where(allowed, s, NEG)
                s_ref[h, at, :] = s
                top_ref[h] = jnp.maximum(top_ref[h], fold(s, jnp.max))
        pl.when(checked)(lambda: run(True))
        pl.when(jnp.logical_not(checked))(lambda: run(False))
        return carry
    lax.fori_loop(0, count, scores, 0)
    tops = [jnp.max(top_ref[h], axis=0, keepdims=True) for h in range(heads)]

    def weigh(j, totals):
        at = pl.ds(pl.multiple_of(j * step, step), step)
        new = []
        for h in range(heads):
            own = slice(h * HEAD_DIM, (h + 1) * HEAD_DIM)
            weights = jnp.exp(s_ref[h, at, :] - tops[h])
            s_ref[h, at, :] = weights
            new.append(totals[h] + fold(weights, jnp.sum))
            ot_ref[own, :] += product(vt_ref[own, at], weights.astype(BF16))
        return new
    totals = lax.fori_loop(0, count, weigh, [jnp.zeros((8, tile), F32)] * heads)
    inverse = [1.0 / jnp.sum(t, axis=0, keepdims=True) for t in totals]
    grad_f = grad_t.astype(F32)
    deltas = []
    for h in range(heads):
        own = slice(h * HEAD_DIM, (h + 1) * HEAD_DIM)
        value = ot_ref[own, :] * inverse[h]
        ot_ref[own, :] = value
        deltas.append(jnp.sum(value * grad_f[own], axis=0, keepdims=True))
    o_ref[...] = ot_ref[...].T.astype(BF16)

    def back(j, carry):
        at = pl.ds(pl.multiple_of(j * step, step), step)
        values = x_ref[at, 2 * width : 3 * width]
        probs_low, grads_low = [], []
        for h in range(heads):
            own = slice(h * HEAD_DIM, (h + 1) * HEAD_DIM)
            probs_grad = product(values, grads_t[h])
            probs = s_ref[h, at, :] * inverse[h]
            scores_grad = (probs * (probs_grad - deltas[h])).astype(BF16)
            probs_low.append(probs.astype(BF16))
            grads_low.append(scores_grad)
            dqt_ref[own, :] += product(kt_ref[own, at], scores_grad)
        dva_ref[at, :] += product(jnp.concatenate(probs_low, axis=1), all_grads)
        dka_ref[at, :] += product(jnp.concatenate(grads_low, axis=1), all_queries)
        return carry
    lax.fori_loop(0, count, back, 0)
    dq_ref[...] = (dqt_ref[...].T * scale).astype(BF16)
    @pl.when(i == tiles - 1)
    def _():
        dk_ref[...] = dka_ref[...].astype(BF16)
        dv_ref[...] = dva_ref[...].astype(BF16)

def attention(dealt, documents, heads, edge):
    length = dealt.shape[0]
    width = heads * HEAD_DIM
    tile = step = 2 * edge
    pairs = length * length // 2 * heads
    kdoc = jnp.broadcast_to(documents[:, None], (length, 128)); qdoc = documents[None, :]
    whole = lambda i: (0, 0)
    part = lambda i: (i, 0)
    return pl.pallas_call(
        functools.partial(attention_kernel, width, heads, tile, step, edge, length),
        grid=(length // tile,),
        out_shape=[jax.ShapeDtypeStruct((length, width), BF16)]*4,
        in_specs=[pl.BlockSpec((length, 4 * width), whole), pl.BlockSpec((length, 128), whole), pl.BlockSpec((1, length), whole)],
        out_specs=[pl.BlockSpec((tile, width), part), pl.BlockSpec((tile, width), part), pl.BlockSpec((length, width), whole), pl.BlockSpec((length, width), whole)],
        scratch_shapes=[
            pltpu.VMEM((heads, length, tile), F32), pltpu.VMEM((width, length), BF16), pltpu.VMEM((width, length), BF16),
            pltpu.VMEM((width, tile), F32), pltpu.VMEM((width, tile), F32), pltpu.VMEM((length, width), F32), pltpu.VMEM((length, width), F32),
            pltpu.VMEM((heads, 8, tile), F32)],
        compiler_params=pltpu.CompilerParams(vmem_limit_bytes=VMEM_LIMIT),
        cost_estimate=pl.CostEstimate(flops=pairs * 64 * 2 * 6 * 4, bytes_accessed=length * width * 20, transcendentals=pairs),
        name="attention",
    )(dealt, kdoc, qdoc)


def on_device(
    grid,
    history,
    documents,
    cotangent,
    mixer_gain,
    mixer_inner,
    mixer_outer,
    mixer_bias,
    stream_gain,
    stream_bias,
    inbound_weight,
    inbound_bias,
    outbound_weight,
    outbound_bias,
    expand,
    expand_bias,
    contract,
    contract_bias,
):
    n_dp, n_seq, nz = grid.n_dp, grid.n_seq, grid.nz
    tokens, width = history.shape[2], history.shape[3]
    hidden_width = expand.shape[1]
    half, hidden_half = width // 2, hidden_width // 2
    both = 2 * tokens
    length = documents.shape[1]
    heads = HEADS // n_seq
    own_width = heads * HEAD_DIM
    seq = lax.axis_index("seq")
    z, c = seq // 2, lax.rem(seq, 2)

    def take(array, start, size, axis=0):
        return lax.dynamic_slice_in_dim(array, start, size, axis)

    gain = mixer_gain.astype(F32)[None]
    stream_gain_full = stream_gain.astype(F32)
    pick = lambda base, n: (lambda core: base + core * n)
    lowered, grad_low, last_stream, mix_pre, coeffs, (weight_k, weight_v, weight_q, weight_o) = mix_forward(
        grid,
        history,
        cotangent,
        [gain, mixer_inner, mixer_outer, mixer_bias.astype(F32)[None], stream_gain_full, stream_bias.astype(F32)],
        [inbound_weight, outbound_weight],
        [
            (0, pick(width, half), 0, 0, half, "ba"),
            (0, pick(2 * width, half), 1, 0, half, "ab"),
            (0, pick(0, half), 2, 0, half, "ba"),
            (1, pick(0, half), 3, 0, half, "ab"),
        ],
        [[0, 1], [2, 3]],
        [half] * 4,
        1,
    )

    bias_in = inbound_bias.astype(F32).reshape(3, width)
    positions = z * both + jnp.arange(both, dtype=jnp.int32)
    tables = rotary_tables(positions, 128)
    sent = project(
        grid, lowered, grad_low, [weight_q, weight_k, weight_v, weight_o], take(bias_in, c * half, half, 1), tables, own_width
    )
    groups = [[2 * k + core for k in range(nz)] for core in range(2)]
    dealt = lax.all_to_all(sent, "seq", 0, 0, axis_index_groups=groups, tiled=True)

    expand_in, contract_in, _ = lax.optimization_barrier((expand, contract, sent[0, 0]))
    parts = 4
    piece = hidden_half // parts
    chunks = []
    for part in range(parts):
        base = lambda core, part=part: core * hidden_half + part * piece
        chunks.append((0, base, 0, part * piece, piece, "ba"))
        chunks.append((1, base, 1, part * piece, piece, "ab"))
    pairs = [[2 * part, 2 * part + 1] for part in range(parts)]
    weight_e, weight_c = gather(grid, [expand_in, contract_in], chunks, pairs, [hidden_half] * 2, 3, "gather_feed")

    expanded = product(lowered[3], weight_e) + take(expand_bias.astype(F32), c * hidden_half, hidden_half)
    hidden_value, hidden_pull = jax.vjp(exact_gelu, expanded)
    hidden_low = hidden_value.astype(BF16)
    feed = against(hidden_low, weight_c)

    results = attention(dealt.reshape(length, 4 * own_width), documents[0], heads, tokens)
    returned = jnp.concatenate(results, axis=-1).reshape(nz, both, 4 * own_width)
    collected = lax.all_to_all(returned, "seq", 0, 0, axis_index_groups=groups, tiled=True)

    expanded_grad = hidden_pull(product(grad_low, weight_c))[0]
    expanded_grad_low = expanded_grad.astype(BF16)
    expand_part = inner(lowered[3], expanded_grad_low).astype(BF16)
    contract_part = inner(grad_low, hidden_low).astype(BF16)
    chunks = []
    for part in range(parts):
        base = lambda core, part=part: core * hidden_half + part * piece
        chunks.append((0, part * piece, piece, "ab", 0, base))
        chunks.append((1, part * piece, piece, "ba", 1, base))
    expand_grad, contract_grad = scatter(grid, [expand_part, contract_part], chunks, pairs, [hidden_width] * 2, 4, "scatter_feed")

    pieces = [
        jnp.concatenate([collected[m, :, k * own_width : (k + 1) * own_width] for m in range(nz)], axis=-1) for k in range(4)
    ]
    attended_low, value_low = pieces[0], pieces[3]
    spread = [jnp.tile(t, (1, half // 128)) for t in tables]

    def unturn(grad):
        grad = grad.astype(F32)
        up = jnp.roll(grad, -(ROT_DIMS // 2), axis=-1)
        down = jnp.roll(grad, ROT_DIMS // 2, axis=-1)
        return grad * spread[0] - (up * spread[1] + down * spread[2])

    dq, dk = unturn(pieces[1]), unturn(pieces[2])
    dq_low, dk_low, dv_low = dq.astype(BF16), dk.astype(BF16), value_low
    head_bias_grads = jnp.stack([jnp.sum(x.astype(F32), axis=0) for x in (dq, dk, value_low)])

    out_part = against(attended_low, weight_o) + feed
    swap = [(s, s + 1 - 2 * (s % 2)) for s in range(n_seq)]
    out_theirs = lax.ppermute(take(out_part, (1 - c) * tokens, tokens), "seq", swap)
    out_own = take(out_part, c * tokens, tokens) + out_theirs
    layer_out = (last_stream + (out_own + outbound_bias.astype(F32) + contract_bias.astype(F32))).astype(BF16)

    normed_part = jnp.stack(
        [
            against(dq_low, weight_q),
            against(dk_low, weight_k),
            against(dv_low, weight_v),
            against(expanded_grad_low, weight_e),
        ]
    )
    normed_theirs = lax.ppermute(take(normed_part, (1 - c) * tokens, tokens, 1).astype(BF16), "seq", swap)
    normed_own = take(normed_part, c * tokens, tokens, 1)

    inbound_grad, outbound_grad = scatter(
        grid,
        [
            inner(lowered[0], dq_low).astype(BF16),
            inner(lowered[1], dk_low).astype(BF16),
            inner(lowered[2], dv_low).astype(BF16),
            inner(grad_low, attended_low).astype(BF16),
        ],
        [
            (0, 0, half, "ab", 0, pick(0, half)),
            (1, 0, half, "ba", 0, pick(width, half)),
            (2, 0, half, "ab", 0, pick(2 * width, half)),
            (3, 0, half, "ba", 1, pick(0, half)),
        ],
        [[0, 1], [2, 3]],
        [3 * width, width],
        5,
        "scatter_attention",
    )

    history_grad, sgg, sbg, gg, ig, og, bg, ob = mix_backward(
        history,
        normed_own,
        normed_theirs,
        cotangent,
        mix_pre,
        coeffs,
        [gain, mixer_inner, mixer_outer, stream_gain_full],
    )
    inbound_bias_grad = lax.dynamic_update_slice_in_dim(jnp.zeros((3, width), F32), head_bias_grads, c * half, 1)
    expand_bias_grad = lax.dynamic_update_slice_in_dim(
        jnp.zeros((hidden_width,), F32), jnp.sum(expanded_grad, axis=0), c * hidden_half, 0
    )
    small = small_sum(n_dp, n_seq, [gg, ig, og, bg, sgg, sbg, inbound_bias_grad, ob, expand_bias_grad], 6)
    return (
        layer_out[None],
        history_grad,
        small[0].reshape(width),
        small[1].T,
        small[2],
        small[3].reshape(-1),
        small[4],
        small[5],
        inbound_grad,
        small[6].reshape(3 * width),
        outbound_grad,
        small[7].reshape(width),
        expand_grad,
        small[8],
        contract_grad,
        small[7].reshape(width),
    )


def solution(mesh):
    rows = P(("dp", "seq"), None)
    placed = (
        P(None, "dp", "seq", None),
        P("dp", None),
        P("dp", "seq", None),
        P(),
        P(),
        P(),
        P(),
        P(),
        P(),
        rows,
        P(),
        rows,
        P(),
        rows,
        P(),
        rows,
        P(),
    )
    grid = Grid(mesh.shape["dp"], mesh.shape["seq"])
    return jax.shard_map(
        functools.partial(on_device, grid),
        mesh=mesh,
        in_specs=placed,
        out_specs=(
            P("dp", "seq", None),
            P(None, "dp", "seq", None),
            P(),
            P(),
            P(),
            P(),
            P(),
            P(),
            rows,
            P(),
            rows,
            P(),
            rows,
            P(),
            rows,
            P(),
        ),
        check_vma=False,
    )
```

time: 1140 us -> 647 us (0.57)
  Pallas kernels: 787 us -> 478 us
  matrix products: 143 us -> 66.1 us
  other arithmetic: 85.9 us -> 23.1 us
  local copies, waits for them, and re-layouts: 98.7 us -> 58.9 us
    pallas_call x6 -> x7, Pallas kernels: 764 us -> 458 us  [the longest x1 157 us: gather(): pl.pallas_call(functools.partial(gather_kernel, grid, rows, chunks, group...]
    dot_general x3 -> x0, matrix products: 61.6 us -> none  [the longest x1 25.1 us: on_device(): jnp.einsum('tcj,ctd->jtd', coeffs, streams_grad, precision=HIGHEST)]
    reduce_sum x8 -> x2, other arithmetic: 29.8 us -> 1.62 us  [on_device(): jnp.sum(x.astype(F32), axis=0)]
    slice x10 -> x3, local copies, waits for them, and re-layouts: 25.1 us -> 5.71 us  [the longest x1 5.31 us: on_device(): lowered[2]]
    dot_general x8 -> x2, matrix products: 44.6 us -> 27.5 us  [product(): return jnp.dot(left, right, preferred_element_type=F32)]
    convert_element_type x5 -> x3, other arithmetic: 17.8 us -> 1.52 us  [the longest x1 1.3 us: on_device(): stream_gain_full = stream_gain.astype(F32)]
    unnamed x140 -> x106, local copies, waits for them, and re-layouts: 28 us -> 12.9 us
  transfers between devices with their start and end apart: 4 -> 4, of which waited for: 0 -> 0; matrix products, arithmetic and copies ran while one was open for 9% -> 15% of each run, Pallas kernels for 39% -> 48%
where the time goes in v2:
time: 647 us; the launch traced here: 641 us
  Pallas kernels  478 us (74%)
  matrix products  66.1 us (10%)
  local copies, waits for them, and re-layouts  58.9 us (9%)
  other arithmetic  23.1 us (4%)
  starting transfers between devices  13.6 us (2%)
    pallas_call x1, Pallas kernels, gather(): pl.pallas_call(functools.partial(gather_kernel, grid, rows, chunks, group...  157 us
    pallas_call x2, Pallas kernels, scatter(): pl.pallas_call(functools.partial(scatter_kernel, grid, chunks, groups, le...  152 us
    pallas_call x1, Pallas kernels, mix_forward(): pl.pallas_call(functools.partial(mix_kernel, grid, rows, chunks, groups),...  60.8 us
    pallas_call x1, Pallas kernels, attention(): pl.pallas_call(functools.partial(attention_kernel, width, heads, tile, st...  50 us
    pallas_call x1, Pallas kernels, mix_backward(): pl.pallas_call(unmix_kernel, grid=(tokens // block,), out_shape=[jax.Shap...  28.3 us
    dot_general x2, matrix products, product(): return jnp.dot(left, right, preferred_element_type=F32)  27.5 us
    dot_general x6, matrix products, inner(): lax.dot_general(left, right, (((0,), (0,)), ((), ())), preferred_element_...  22.8 us
    pallas_call x1, Pallas kernels, small_sum(): pl.pallas_call(functools.partial(small_kernel, n_dp, n_seq), out_shape=ja...  20.5 us
  transfers between devices with their start and end apart: 4, of which 0 were waited for; matrix products, arithmetic and copies ran while one was open for 15% of the time, Pallas kernels for 48%

profile of v2, /device:TPU:0, one launch (start us, length us, event | category | flops | bytes accessed | tf_op | source)
XLA Modules:
  0.0 641.5 jit_solution(4592334817916472350)
XLA Ops:
  0.7 1.3 broadcast_in_dim.83
  2.0 1.8 copy.39.inner_ref
  3.7 1.2 bitcast_convert_fusion.bias_ref
  4.9 1.3 convert_element_type.153.sgain_ref
  6.2 1.3 convert_element_type.154.sbias_ref
  9.4 1.1 select_select_fusion
  10.4 60.8 %mix_forward.1 = (bf16[4,2,384,1024]{3,2,1,0:T(8,128)(2,1)}, bf16[2,384,1024]{2,1,0:T(8,128)(2,1)}, f32[384,1024]{1,0:T(8,128)}, f32[384,36]{1,0:T(8,128)}, f32[...) custom-call(bf16[9,1,384,1024]{3,2,1,0:T(8,128)(2,1)} %h_ref.3, ...), custom_call_target="tpu_custom_call" | custom-call | flops 31457280 | bytes 141557760 | tf_op jit(solution)/shard_map/mix_forward/pallas_call | solution.py:496
  71.2 9.4 %project.1 = bf16[4,768,512]{2,1,0:T(8,128)(2,1)} custom-call(bf16[4,768,1024]{2,1,0:T(8,128)(2,1)} %bitcast.147, bf16[768,1024]{1,0:T(8,128)(2,1)} %bitcast.158, bf16[1024,512]{1,0:T(8,128)(2,1)} %bitcast.174, bf16[1024,512]{1,0:T(8,128)(2,1)} %bitcast.176, bf16[1024,512]{1,0:T(8,128)(2,1)} %bitcast.172, bf16[1024,512]{1,0:T(8,128)(2,1)} %bitcast.155, ...), custom_call_target="tpu_custom_call" | custom-call | flops 3221225472 | bytes 12582912 | tf_op jit(solution)/shard_map/project/pallas_call | solution.py:657
  80.6 7.8 %all-to-all-start = ((bf16[4,768,512]{2,1,0:T(8,128)(2,1)}), bf16[4,768,512]{2,1,0:T(8,128)(2,1)S(1)}, u32[]{:S(2)}, u32[]{:S(2)}) async-start(bf16[4,768,512]{2,1,0:T(8,128)(2,1)} %project.1), calls=%async_computation | async-start | bytes 6291456 | tf_op jit(solution)/shard_map/all_to_all | solution.py:857
  88.4 157.0 %gather_feed.1 = (bf16[2,2,4,64,2048]{4,3,2,1,0:T(8,128)(2,1)}, bf16[2,2,4,64,2048]{4,3,2,1,0:T(8,128)(2,1)}) custom-call(bf16[32,4096]{1,0:T(8,128)(2,1)} %refs_0_, bf16[32,4096]{1,0:T(8,128)(2,1)} %refs_1_), custom_call_target="tpu_custom_call" | custom-call | bytes 167772160 | tf_op jit(solution)/shard_map/gather_feed/pallas_call | solution.py:204
  245.4 5.3 fusion.19
  250.7 1.2 copy-done.14
  251.9 5.3 fusion.24
  257.2 2.3 broadcast_in_dim.79.kdoc_ref
  259.5 50.0 %attention.1 = (bf16[3072,128]{1,0:T(8,128)(2,1)}, bf16[3072,128]{1,0:T(8,128)(2,1)}, bf16[3072,128]{1,0:T(8,128)(2,1)}, bf16[3072,128]{1,0:T(8,128)(2,1)}) custom-call(bf16[3072,512]{1,0:T(8,128)(2,1)} %bitcast.157, s32[3072,128]{1,0:T(8,128)} %broadcast_in_dim.79.kdoc_ref, s32[1,3072]{1,0:T(1,128)} %qdoc_ref.1), custom_call_target="tpu_custom_call" | custom-call | flops 28991029248 | bytes 7864320 | tf_op jit(solution)/shard_map/attention/pallas_call | solution.py:780
  309.5 2.0 pad_maximum_fusion.1
  311.5 2.8 copy.42
  314.4 5.1 all-to-all-start.1
  319.5 22.2 %fusion.13 = (f32[2048]{0:T(1024)}, bf16[768,2048]{1,0:T(8,128)(2,1)}, f32[768,2048]{1,0:T(8,128)}) fusion(f32[768,2048]{1,0:T(8,128)} %fusion.24, f32[2048]{0:T(1024)S(1)} %dynamic-slice_convert_fusion.1, bf16[768,1024]{1,0:T(8,128)(2,1)} %bitcast.159, bf16[1024,2048]{1,0:T(8,128)(2,1)} %bitcast.200), kind=kOutput, calls=%fused_computation.101 | convolution fusion | flops 3337615360 | bytes 21512192 | tf_op jit(solution)/shard_map/dot_general | solution.py:32
  341.8 1.9 copy.45
  343.7 1.9 copy.44
  345.6 0.9 copy.43
  347.7 7.8 %convolution_convert_fusion.1 = bf16[1024,2048]{1,0:T(8,128)(2,1)} fusion(bf16[768,1024]{1,0:T(8,128)(2,1)} %bitcast.166, bf16[768,2048]{1,0:T(8,128)(2,1)} %get-tuple-element.75), kind=kOutput, calls=%fused_computation.20 | convolution fusion | flops 3223322624 | bytes 8912896 | tf_op jit(solution)/shard_map/dot_general | solution.py:24
  355.5 6.3 multiply_convert_fusion
  361.9 5.1 convolution_convert_fusion
  366.9 92.3 %scatter_feed.1 = (f32[32,4096]{1,0:T(8,128)}, f32[32,4096]{1,0:T(8,128)}) custom-call(bf16[2,2,4,64,2048]{4,3,2,1,0:T(8,128)(2,1)} %bitcast.153, bf16[2,2,4,64,2048]{4,3,2,1,0:T(8,128)(2,1)} %bitcast.154), custom_call_target="tpu_custom_call" | custom-call | bytes 167772160 | tf_op jit(solution)/shard_map/scatter_feed/pallas_call | solution.py:343
  459.6 8.3 %convolution_bitcast_fusion = f32[1,768,1024]{2,1,0:T(8,128)} fusion(bf16[1024,2048]{1,0:T(8,128)(2,1)} %bitcast.202, bf16[768,2048]{1,0:T(8,128)(2,1)} %get-tuple-element.75), kind=kOutput, calls=%fused_computation.22 | convolution fusion | flops 3221225472 | bytes 10485760 | tf_op jit(solution)/shard_map/dot_general | solution.py:28
  469.5 0.7 copy-done.7
  470.8 1.4 fusion.15
  472.3 1.0 convolution_bitcast_fusion.2
  474.1 1.0 convolution_bitcast_fusion.3
  475.3 1.0 convolution_bitcast_fusion.1
  476.3 0.9 copy-done.5
  477.2 1.5 pad_maximum_fusion
  478.7 2.1 dynamic-slice_convert_fusion
  481.2 1.8 copy-done.4
  482.9 3.5 fusion.25
  486.4 1.0 convolution_add_fusion
  487.5 1.3 constant_dynamic-slice_fusion.1
  490.5 1.3 reshape.546
  491.8 3.8 convolution_convert_fusion.5
  495.6 2.1 convolution_convert_fusion.4
  497.8 2.0 convolution_convert_fusion.2
  499.8 2.0 convolution_convert_fusion.3
  501.8 60.0 %scatter_attention.1 = (f32[32,3072]{1,0:T(8,128)}, f32[32,1024]{1,0:T(8,128)}) custom-call(bf16[2,2,4,64,512]{4,3,2,1,0:T(8,128)(2,1)} %bitcast.179, bf16[2,2,4,64,512]{4,3,2,1,0:T(8,128)(2,1)} %bitcast.180, bf16[2,2,4,64,512]{4,3,2,1,0:T(8,128)(2,1)} %bitcast.182, bf16[2,2,4,64,512]{4,3,2,1,0:T(8,128)(2,1)} %bitcast.181), custom_call_target="tpu_custom_call" | custom-call | bytes 83886080 | tf_op jit(solution)/shard_map/scatter_attention/pallas_call | solution.py:343
  561.8 6.7 %constant_dynamic-slice_fusion.own_ref = f32[4,384,1024]{2,1,0:T(8,128)} fusion(f32[4,768,1024]{2,1,0:T(8,128)} %copy-done, s32[]{:T(128)S(6)} %select_n.69), kind=kLoop, calls=%fused_computation.92 | loop fusion | bytes 12582916 | tf_op jit(solution)/shard_map/dynamic_slice | solution.py:828
  568.6 2.8 fusion.10
  571.4 28.3 %mix_backward.1 = (f32[9,1,384,1024]{3,2,1,0:T(8,128)}, f32[4,1024]{1,0:T(4,128)}, f32[4,1024]{1,0:T(4,128)}, f32[1,1024]{1,0:T(1,128)}, f32[36,1024]{1,0:T(8,12...) custom-call(bf16[9,1,384,1024]{3,2,1,0:T(8,128)(2,1)} %h_ref.3, ...), custom_call_target="tpu_custom_call" | custom-call | flops 117964800 | bytes 28311552 | tf_op jit(solution)/shard_map/mix_backward/pallas_call | solution.py:608
  599.8 1.1 reshape.541
  600.8 0.8 reshape.542
  601.6 0.7 copy.52
  602.4 0.7 copy.51
  603.1 3.6 concatenate.89
  606.7 0.7 pad.4
  607.4 20.5 %small_sum.1 = f32[32,16,128]{2,1,0:T(8,128)} custom-call(f32[32,16,128]{2,1,0:T(8,128)} %bitcast.178), custom_call_target="tpu_custom_call" | custom-call | tf_op jit(solution)/shard_map/small_sum/pallas_call | solution.py:399
  627.9 1.0 slice.150
  628.9 1.3 fusion.23
  630.9 1.3 slice.185
  632.2 1.5 fusion.22
  633.6 1.4 slice.188
  635.7 0.7 reshape.550
  638.3 0.7 copy.61
  639.7 0.8 copy.63
  640.5 0.8 copy.64
  (135 shorter events, 12.4 us)
Async XLA Ops:
  80.6 164.8 %copy-start.44 = (bf16[4096]{0:T(1024)(128)(2,1)S(1)}, bf16[4096]{0:T(1024)(128)(2,1)}, u32[]{:S(2)}) copy-start(bf16[4096]{0:T(1024)(128)(2,1)} %param.31) | copy-start | bytes 24580
  80.6 176.6 %all-to-all-start = ((bf16[4,768,512]{2,1,0:T(8,128)(2,1)}), bf16[4,768,512]{2,1,0:T(8,128)(2,1)S(1)}, u32[]{:S(2)}, u32[]{:S(2)}) async-start(bf16[4,768,512]{2,1,0:T(8,128)(2,1)} %project.1), calls=%async_computation | async-start | bytes 6291456 | tf_op jit(solution)/shard_map/all_to_all | solution.py:857
  245.4 6.5 %copy-start.48 = (bf16[2,2,4,64,2048]{4,3,2,1,0:T(8,128)(2,1)S(1)}, bf16[2,2,4,64,2048]{4,3,2,1,0:T(8,128)(2,1)}, u32[]{:S(2)}) copy-start(bf16[2,2,4,64,2048]{4,3,2,1,0:T(8,128)(2,1)} %get-tuple-element.58) | copy-start | bytes 12582916
  250.7 1.2 copy-start.14
  251.9 5.3 copy-start.42
  257.2 2.3 copy-start.6
  314.4 153.5 %all-to-all-start.1 = ((bf16[4,768,512]{1,2,0:T(8,128)(2,1)}), bf16[4,768,512]{1,2,0:T(8,128)(2,1)S(1)}, u32[]{:S(2)}, u32[]{:S(2)}) async-start(bf16[4,768,512]{1,2,0:T(8,128)(2,1)} %copy.42), calls=%async_computation.1 | async-start | bytes 6291456 | tf_op jit(solution)/shard_map/all_to_all | solution.py:877
  319.5 26.1 %copy-start.2 = (f32[768,128]{1,0:T(8,128)S(1)}, f32[768,128]{1,0:T(8,128)}, u32[]{:S(2)}) copy-start(f32[768,128]{1,0:T(8,128)} %get-tuple-element.128.cos_ref) | copy-start | bytes 1179652
  319.5 27.0 %copy-start.45 = (bf16[1024]{0:T(1024)(128)(2,1)S(1)}, bf16[1024]{0:T(1024)(128)(2,1)}, u32[]{:S(2)}) copy-start(bf16[1024]{0:T(1024)(128)(2,1)} %param.33) | copy-start | bytes 6148
  319.5 27.6 %copy-start.46 = (bf16[1024]{0:T(1024)(128)(2,1)S(1)}, bf16[1024]{0:T(1024)(128)(2,1)}, u32[]{:S(2)}) copy-start(bf16[1024]{0:T(1024)(128)(2,1)} %param.29) | copy-start | bytes 6148
  355.5 6.3 copy-start.10
  361.8 5.1 copy-start.3
  366.9 92.3 %copy-start.43 = (f32[2048]{0:T(1024)S(1)}, f32[2048]{0:T(1024)}, u32[]{:S(2)}) copy-start(f32[2048]{0:T(1024)} %get-tuple-element.74) | copy-start | bytes 24580
  468.2 20.9 %copy-start.19 = (bf16[768,128]{0,1:T(8,128)(2,1)}, bf16[768,128]{0,1:T(8,128)(2,1)S(1)}, u32[]{:S(2)}) copy-start(bf16[768,128]{0,1:T(8,128)(2,1)S(1)} %get-tuple-element.96) | copy-start | bytes 589828
  468.3 20.8 %copy-start.21 = (bf16[768,128]{0,1:T(8,128)(2,1)}, bf16[768,128]{0,1:T(8,128)(2,1)S(1)}, u32[]{:S(2)}) copy-start(bf16[768,128]{0,1:T(8,128)(2,1)S(1)} %get-tuple-element.97) | copy-start | bytes 589828
  469.3 1.0 copy-start.7
  469.3 1.1 copy-start.8
  469.3 1.5 copy-start.9
  469.5 16.9 %copy-start.26 = (bf16[768,128]{0,1:T(8,128)(2,1)}, bf16[768,128]{0,1:T(8,128)(2,1)S(1)}, u32[]{:S(2)}) copy-start(bf16[768,128]{0,1:T(8,128)(2,1)S(1)} %get-tuple-element.105) | copy-start | bytes 589828
  469.5 16.9 %copy-start.28 = (bf16[768,128]{0,1:T(8,128)(2,1)}, bf16[768,128]{0,1:T(8,128)(2,1)S(1)}, u32[]{:S(2)}) copy-start(bf16[768,128]{0,1:T(8,128)(2,1)S(1)} %get-tuple-element.106) | copy-start | bytes 589828
  469.5 16.9 %copy-start.30 = (bf16[768,128]{0,1:T(8,128)(2,1)}, bf16[768,128]{0,1:T(8,128)(2,1)S(1)}, u32[]{:S(2)}) copy-start(bf16[768,128]{0,1:T(8,128)(2,1)S(1)} %get-tuple-element.107) | copy-start | bytes 589828
  469.5 16.9 %copy-start.32 = (bf16[768,128]{0,1:T(8,128)(2,1)}, bf16[768,128]{0,1:T(8,128)(2,1)S(1)}, u32[]{:S(2)}) copy-start(bf16[768,128]{0,1:T(8,128)(2,1)S(1)} %get-tuple-element.108) | copy-start | bytes 589828
  470.8 1.5 copy-start.18
  472.3 1.1 copy-start.23
  472.3 1.1 copy-start.25
  472.3 1.8 copy-start.17
  474.1 1.2 copy-start.16
  475.3 1.9 copy-start.5
  477.2 4.0 copy-start.47
  478.7 7.7 %copy-start = (f32[4,768,1024]{2,1,0:T(8,128)}, f32[4,768,1024]{2,1,0:T(8,128)S(1)}, u32[]{:S(2)}) copy-start(f32[4,768,1024]{2,1,0:T(8,128)S(1)} %pad_maximum_fusion) | copy-start | bytes 37748740
  478.7 4.2 copy-start.4
  480.9 5.6 copy-start.1
  480.9 90.5 %collective-permute-start.1 = (bf16[4,384,1024]{2,1,0:T(8,128)(2,1)}, bf16[4,384,1024]{2,1,0:T(8,128)(2,1)}, u32[]{:S(2)}, u32[]{:S(2)}) collective-permute-start(bf16[4,384,1024]{2,1,0:T(8,128)(2,1)} %dynamic-slice_convert_fusion), channel_id=1, source_target_pairs={{0,1},{1,0},{2,3},{3,2},{4,5},{5,4},{6,7},{7,6},{8,9},{9,8},{10,11... | collective-permute-start | bytes 9437192 | tf_op jit(solution)/shard_map/ppermute | solution.py:920
  488.8 79.8 %collective-permute-start = (f32[384,1024]{1,0:T(8,128)}, f32[384,1024]{1,0:T(8,128)}, u32[]{:S(2)}, u32[]{:S(2)}) collective-permute-start(f32[384,1024]{1,0:T(8,128)} %constant_dynamic-slice_fusion.1), channel_id=1, source_target_pairs={{0,1},{1,0},{2,3},{3,2},{4,5},{5,4},{6,7},{7,6},{8,9},{9,8},{10,11... | collective-permute-start | bytes 4718600 | tf_op jit(solution)/shard_map/ppermute | solution.py:908
  491.8 3.8 copy-start.13
  491.8 3.8 copy-start.24
  495.6 2.1 copy-start.11
  495.6 2.1 copy-start.27
  495.6 2.1 copy-start.29
  495.6 2.1 copy-start.31
  495.6 2.1 copy-start.33
  497.7 2.1 copy-start.12
  497.7 2.1 copy-start.20
  497.7 2.0 copy-start.22
  561.8 6.7 %copy-start.15 = (f32[384,1024]{1,0:T(8,128)S(1)}, f32[384,1024]{1,0:T(8,128)}, u32[]{:S(2)}) copy-start(f32[384,1024]{1,0:T(8,128)} %get-tuple-element.45) | copy-start | bytes 4718596
  561.8 6.7 %copy-start.40 = (f32[1024]{0:T(1024)S(1)}, f32[1024]{0:T(1024)}, u32[]{:S(2)}) copy-start(f32[1024]{0:T(1024)} %convert_element_type.160) | copy-start | bytes 12292
  561.8 6.7 %copy-start.41 = (f32[1024]{0:T(1024)S(1)}, f32[1024]{0:T(1024)}, u32[]{:S(2)}) copy-start(f32[1024]{0:T(1024)} %convert_element_type.159) | copy-start | bytes 12292
  571.4 31.7 %copy-start.38 = (f32[3072]{0:T(1024)S(1)}, f32[3072]{0:T(1024)}, u32[]{:S(2)}) copy-start(f32[3072]{0:T(1024)} %reshape.546) | copy-start | bytes 36868
  599.7 38.5 %copy-start.36 = (f32[32,3072]{1,0:T(8,128)S(1)}, f32[32,3072]{1,0:T(8,128)}, u32[]{:S(2)}) copy-start(f32[32,3072]{1,0:T(8,128)} %get-tuple-element.196) | copy-start | bytes 1179652
  599.7 39.3 %copy-start.37 = (f32[32,1024]{1,0:T(8,128)S(1)}, f32[32,1024]{1,0:T(8,128)}, u32[]{:S(2)}) copy-start(f32[32,1024]{1,0:T(8,128)} %get-tuple-element.198) | copy-start | bytes 393220
  599.7 39.9 %copy-start.35 = (f32[32,4096]{1,0:T(8,128)S(1)}, f32[32,4096]{1,0:T(8,128)}, u32[]{:S(2)}) copy-start(f32[32,4096]{1,0:T(8,128)} %get-tuple-element.200) | copy-start | bytes 1572868
  599.7 40.7 %copy-start.34 = (f32[32,4096]{1,0:T(8,128)S(1)}, f32[32,4096]{1,0:T(8,128)}, u32[]{:S(2)}) copy-start(f32[32,4096]{1,0:T(8,128)} %get-tuple-element.202) | copy-start | bytes 1572868
  630.2 11.0 %copy-start.39 = (f32[1024]{0:T(1024)}, f32[1024]{0:T(1024)S(1)}, u32[]{:S(2)}) copy-start(f32[1024]{0:T(1024)S(1)} %get-tuple-element.199) | copy-start | bytes 12292

commit v3 on v2

v3 whole, which is shorter than its diff:
```python
import functools
import math

import jax
import jax.numpy as jnp
from jax import lax
from jax.experimental import pallas as pl
from jax.experimental.pallas import tpu as pltpu
from jax.sharding import PartitionSpec as P

HEADS = 16
HEAD_DIM = 64
ROT_DIMS = 16
EPS = 1e-05
HIGHEST = lax.Precision.HIGHEST
NEG = -1e30
MESH = pl.DeviceIdType.MESH
F32 = jnp.float32
BF16 = jnp.bfloat16
VMEM_LIMIT = 56 * 1024 * 1024


def inner(left, right):
    return lax.dot_general(left, right, (((0,), (0,)), ((), ())), preferred_element_type=F32)


def against(left, right):
    return lax.dot_general(left, right, (((1,), (1,)), ((), ())), preferred_element_type=F32)


def product(left, right):
    return jnp.dot(left, right, preferred_element_type=F32)


def exact_gelu(value):
    return jax.nn.gelu(value, approximate=False)


def phi(value):
    return 0.5 * (1.0 + lax.erf(value * (1.0 / math.sqrt(2.0))))


def gelu_slope(value):
    return phi(value) + value * jnp.exp(-0.5 * value * value) * (1.0 / math.sqrt(2.0 * math.pi))


def rotary_tables(positions, width):
    half = ROT_DIMS // 2
    place = jnp.arange(width) % HEAD_DIM
    freq = 10000.0 ** (-jnp.arange(half).astype(F32) * 2.0 / ROT_DIMS)
    angles = positions.astype(F32)[:, None] * freq[None, :]
    spread = lambda x: jnp.tile(x, (1, width // half))
    turned = (place < ROT_DIMS)[None, :]
    cosine = jnp.where(turned, spread(jnp.cos(angles)), 1.0)
    sine = jnp.where(turned, spread(jnp.sin(angles)), 0.0)
    above = jnp.where((place < half)[None, :], -sine, 0.0)
    below = jnp.where((place < half)[None, :], 0.0, sine)
    return cosine, above, below


def rotate(value, tables, sign):
    half = ROT_DIMS // 2
    cosine, above, below = tables
    width = value.shape[-1]
    up = pltpu.roll(value, width - half, 1)
    down = pltpu.roll(value, half, 1)
    return value * cosine + sign * (up * above + down * below)


class Grid:
    def __init__(self, n_dp, n_seq):
        self.n_dp, self.n_seq = n_dp, n_seq
        self.na, self.nb, self.nz = 2, n_dp // 2, n_seq // 2

    def here(self):
        dp, seq = lax.axis_index("dp"), lax.axis_index("seq")
        return dp // self.nb, lax.rem(dp, self.nb), seq // 2, lax.rem(seq, 2)

    def device(self, a, b, z, c):
        return (a * self.nb + b, z * 2 + c)

    def peers(self, a, b, z, c):
        found = [self.device(a, b, z, 1 - c), self.device(1 - a, b, z, c)]
        found += [self.device(a, lax.rem(b + k, self.nb), z, c) for k in range(1, self.nb)]
        found += [self.device(a, b, lax.rem(z + k, self.nz), c) for k in range(1, self.nz)]
        return found

    def greet(self, a, b, z, c):
        barrier = pltpu.get_barrier_semaphore()
        found = self.peers(a, b, z, c)
        for peer in found:
            pl.semaphore_signal(barrier, inc=1, device_id=peer, device_id_type=MESH)
        pl.semaphore_wait(barrier, len(found))


def remote(src, dst, send, recv, device):
    return pltpu.make_async_remote_copy(
        src_ref=src, dst_ref=dst, send_sem=send, recv_sem=recv, device_id=device, device_id_type=MESH
    )


def remote(src, dst, send, recv, device):
    return pltpu.make_async_remote_copy(
        src_ref=src, dst_ref=dst, send_sem=send, recv_sem=recv, device_id=device, device_id_type=MESH
    )


def start(copies):
    for copy in copies:
        copy.start()


def finish(copies):
    for copy in copies:
        copy.wait()


class Gathering:
    def __init__(self, grid, place, rows, chunks, ins, outs, local_sem, send_sem, recv_sem):
        self.grid, self.place, self.rows, self.chunks = grid, place, rows, chunks
        self.ins, self.outs = ins, outs
        self.local_sem, self.send_sem, self.recv_sem = local_sem, send_sem, recv_sem

    def copies(self, t, stage):
        a, b, z, c = self.place
        grid, rows = self.grid, self.rows
        nz, nb = grid.nz, grid.nb
        source, base, result, col, n, order = self.chunks[t]
        out, cols = self.outs[result], pl.ds(col, n)

        def send(src, dst, slot, device):
            return remote(src, dst, self.send_sem.at[t, slot], self.recv_sem.at[t, slot], device)

        if stage == 0:
            mine = self.ins[source].at[:, pl.ds(pl.multiple_of(base(c), 128), n)]
            theirs = self.ins[source].at[:, pl.ds(pl.multiple_of(base(1 - c), 128), n)]
            spot = out.at[a, b, z, pl.ds(pl.multiple_of(c * rows, rows), rows), cols]
            return [pltpu.make_async_copy(mine, spot, self.local_sem.at[t]), send(theirs, spot, 0, grid.device(a, b, z, 1 - c))]
        if stage == 1:
            block = out.at[a, b, z, :, cols]
            return [send(block, block, k, grid.device(a, b, lax.rem(z + k, nz), c)) for k in range(1, nz)]
        if order[stage - 2] == "b":
            block = out.at[a, b, :, :, cols] if stage == 2 else out.at[:, b, :, :, cols]
            return [send(block, block, nz + k - 1, grid.device(a, lax.rem(b + k, nb), z, c)) for k in range(1, nb)]
        block = out.at[a, b, :, :, cols] if stage == 2 else out.at[a, :, :, :, cols]
        return [send(block, block, nz + nb - 1, grid.device(1 - a, b, z, c))]

    def begin(self, group, stage):
        for t in group:
            start(self.copies(t, stage))

    def end(self, group, stage):
        for t in group:
            finish(self.copies(t, stage))

    def events(self, whole, partial):
        groups = whole + partial

        def first():
            for group in groups:
                self.begin(group, 0)

        def second():
            self.end(groups[0], 0)
            self.begin(groups[0], 1)

        def turn(u):
            if u < len(groups):
                self.end(groups[u], 1)
                if u + 1 < len(groups):
                    self.end(groups[u + 1], 0)
                    self.begin(groups[u + 1], 1)
                if u < len(whole):
                    self.begin(groups[u], 2)
            if 0 <= u - 1 < len(whole):
                self.end(groups[u - 1], 2)
                self.begin(groups[u - 1], 3)
            if 0 <= u - 2 < len(whole):
                self.end(groups[u - 2], 3)

        turns = max(len(whole) + 2, len(groups))
        return [first, second] + [functools.partial(turn, u) for u in range(turns)]

    def late_events(self, groups):
        def turn(u):
            if u < len(groups):
                self.begin(groups[u], 2)
            if 0 <= u - 1 < len(groups):
                self.end(groups[u - 1], 2)
                self.begin(groups[u - 1], 3)
            if 0 <= u - 2 < len(groups):
                self.end(groups[u - 2], 3)

        return [functools.partial(turn, u) for u in range(len(groups) + 2)]


def gather_kernel(grid, chunks, groups, n, *refs):
    outs = refs[n : 2 * n]
    place = grid.here()
    grid.greet(*place)
    for event in Gathering(grid, place, None, chunks, None, outs, *refs[2 * n :]).late_events(groups):
        event()


def gather_sems(grid, chunks):
    slots = grid.nz + grid.nb
    return [
        pltpu.SemaphoreType.DMA((len(chunks),)),
        pltpu.SemaphoreType.DMA((len(chunks), slots)),
        pltpu.SemaphoreType.DMA((len(chunks), slots)),
    ]


def gather(grid, arrays, chunks, groups, collective_id, name):
    n = len(arrays)
    moved = sum(x.size for x in arrays) * 2
    results = pl.pallas_call(
        functools.partial(gather_kernel, grid, chunks, groups, n),
        out_shape=[jax.ShapeDtypeStruct(x.shape, x.dtype) for x in arrays],
        in_specs=[pl.BlockSpec(memory_space=pl.ANY)] * n,
        out_specs=[pl.BlockSpec(memory_space=pl.ANY)] * n,
        input_output_aliases={k: k for k in range(n)},
        scratch_shapes=gather_sems(grid, chunks),
        compiler_params=pltpu.CompilerParams(collective_id=collective_id, has_side_effects=True),
        cost_estimate=pl.CostEstimate(flops=0, bytes_accessed=moved * 20, transcendentals=0),
        name=name,
    )(*arrays)
    return [r.reshape(-1, r.shape[-1]) for r in results]


class Scattering:
    def __init__(self, grid, place, chunks, parts, outs, scratch):
        self.grid, self.place, self.chunks, self.parts, self.outs = grid, place, chunks, parts, outs
        count = len(chunks)
        folds = sum(1 for chunk in chunks if chunk[2])
        self.own, scratch = scratch[:count], scratch[count:]
        self.first, self.second, scratch = scratch[:folds], scratch[folds : 2 * folds], scratch[2 * folds :]
        self.third, self.final = scratch[:count], scratch[count : 2 * count]
        self.local_sem, self.send_sem, self.recv_sem = scratch[2 * count :]

    def copies(self, t, stage):
        a, b, z, c = self.place
        grid = self.grid
        nz = grid.nz
        source, n, order, result, base = self.chunks[t]
        part, third, final = self.parts[source], self.third[t], self.final[t]
        sems = (self.send_sem.at[t], self.recv_sem.at[t])

        def send(src, dst, slot, device):
            return remote(src, dst, sems[0].at[slot], sems[1].at[slot], device)

        if stage < 2:
            found = fold_copies(grid, self.place, order, stage, part, self.first[t], self.second[t], sems)
            if stage == 0:
                kept = part.at[a] if order == "ab" else part.at[:, b]
                found.append(pltpu.make_async_copy(kept, self.own[t], self.local_sem.at[t]))
            return found
        if stage == 2:
            source = self.second[t].at[0] if order else part
            found = [send(source.at[lax.rem(z + k, nz)], third.at[k - 1], k, grid.device(a, b, lax.rem(z + k, nz), c)) for k in range(1, nz)]
            if not order:
                found.append(pltpu.make_async_copy(part.at[z], self.own[t], self.local_sem.at[t]))
            return found
        spot = self.outs[result].at[:, pl.ds(pl.multiple_of(base(c), 128), n)]
        return [
            send(final.at[1 - c], spot, 0, grid.device(a, b, z, 1 - c)),
            pltpu.make_async_copy(final.at[c], spot, self.local_sem.at[t]),
        ]

    def add(self, t, stage):
        z = self.place[2]
        order = self.chunks[t][2]
        third, final = self.third[t], self.final[t]
        if stage < 2:
            fold_add(self.grid, self.place, order, stage, self.own[t], self.first[t], self.second[t])
            return
        total = (self.second[t][0, z] if order else self.own[t][...]).astype(F32)
        for k in range(self.grid.nz - 1):
            total = total + third[k].astype(F32)
        final[...] = total.reshape(final.shape)

    def end(self, group, stage):
        for t in group:
            finish(self.copies(t, stage))
            if stage < 3:
                self.add(t, stage)
                start(self.copies(t, stage + 1))

    def events(self, groups):
        late = [t for t, chunk in enumerate(self.chunks) if not chunk[2]]

        def first():
            for group in groups:
                for t in group:
                    start(self.copies(t, 0))
            for t in late:
                start(self.copies(t, 2))

        def turn(u):
            for stage in range(4):
                if 0 <= u - stage < len(groups):
                    self.end(groups[u - stage], stage)

        def last():
            self.end(late, 2)
            self.end(late, 3)

        return [first] + [functools.partial(turn, u) for u in range(len(groups) + 3)] + [last]


def fold_copies(grid, place, order, stage, part, first, second, sems):
    a, b, z, c = place
    nz, nb = grid.nz, grid.nb

    def send(src, dst, slot, device):
        return remote(src, dst, sems[0].at[slot], sems[1].at[slot], device)

    if (order == "ab") == (stage == 0):
        src = part.at[1 - a] if stage == 0 else first.at[0, 1 - a]
        dst = first.at[0] if stage == 0 else second.at[0]
        return [send(src, dst, nz + nb - 1, grid.device(1 - a, b, z, c))]
    found = []
    for k in range(1, nb):
        to = lax.rem(b + k, nb)
        src = part.at[:, to] if stage == 0 else first.at[0, to]
        dst = first.at[k - 1] if stage == 0 else second.at[k - 1]
        found.append(send(src, dst, nz + k - 1, grid.device(a, to, z, c)))
    return found


def fold_add(grid, place, order, stage, own, first, second):
    a, b, z, c = place
    nz = grid.nz
    if stage == 0:

        def step(i, carry):
            o, j = i // nz, lax.rem(i, nz)
            total = own[o, j].astype(F32)
            for k in range(first.shape[0]):
                total = total + first[k, o, j].astype(F32)
            first[0, o, j] = total.astype(BF16)
            return carry

        lax.fori_loop(0, first.shape[1] * nz, step, 0)
        return
    mine = b if order == "ab" else a

    def step(j, carry):
        total = first[0, mine, j].astype(F32)
        for k in range(second.shape[0]):
            total = total + second[k, j].astype(F32)
        second[0, j] = total.astype(BF16)
        return carry

    lax.fori_loop(0, nz, step, 0)


def fold_scratch(grid, order, rows, n):
    na, nb, nz = grid.na, grid.nb, grid.nz
    own = pltpu.VMEM((nb if order == "ab" else na, nz, rows, n), BF16)
    first = pltpu.VMEM((1, nb, nz, rows, n) if order == "ab" else (nb - 1, na, nz, rows, n), BF16)
    second = pltpu.VMEM((nb - 1, nz, rows, n) if order == "ab" else (1, nz, rows, n), BF16)
    return own, first, second


def scatter_scratch(grid, chunks, rows):
    folds = [fold_scratch(grid, order, rows, n) for _, n, order, _, _ in chunks if order]
    own = [fold_scratch(grid, order, rows, n)[0] if order else pltpu.VMEM((rows, n), BF16) for _, n, order, _, _ in chunks]
    third = [pltpu.VMEM((grid.nz - 1, rows, n), BF16) for _, n, _, _, _ in chunks]
    final = [pltpu.VMEM((2, rows // 2, n), F32) for _, n, _, _, _ in chunks]
    return own + [f for _, f, _ in folds] + [s for _, _, s in folds] + third + final + gather_sems(grid, chunks)


class Summing:
    def __init__(self, grid, mine, held, total, done, send_sem, recv_sem):
        self.n_seq, self.count = grid.n_seq, grid.n_dp * grid.n_seq
        self.mine, self.held, self.total, self.done = mine, held, total, done
        self.send_sem, self.recv_sem = send_sem, recv_sem
        self.rows = total.shape[0]
        self.me = lax.axis_index("dp") * grid.n_seq + lax.axis_index("seq")

    def device(self, k):
        other = lax.rem(self.me + k, self.count)
        return other, (other // self.n_seq, lax.rem(other, self.n_seq))

    def part(self, ref, k):
        return ref.at[pl.ds(pl.multiple_of(k * self.rows, self.rows), self.rows)]

    def greet(self):
        barrier = pltpu.get_barrier_semaphore()

        def step(k, carry):
            pl.semaphore_signal(barrier, inc=1, device_id=self.device(k)[1], device_id_type=MESH)
            return carry

        lax.fori_loop(1, self.count, step, 0)
        pl.semaphore_wait(barrier, self.count - 1)

    def settle(self, dst, slot):
        most = pl.ds(0, (self.count - 1) * self.rows)
        remote(self.mine.at[most], dst.at[most], self.send_sem.at[slot], self.recv_sem.at[slot], self.device(1)[1]).wait()

    def deal(self):
        def step(k, carry):
            other, place = self.device(k)
            remote(self.part(self.mine, other), self.part(self.held, self.me), self.send_sem.at[0], self.recv_sem.at[0], place).start()
            return carry

        lax.fori_loop(1, self.count, step, 0)
        at = pl.ds(pl.multiple_of(self.me * self.rows, self.rows), self.rows)
        self.held[at, :] = self.mine[at, :]

    def tell(self):
        self.settle(self.held, 0)

        def add(k, carry):
            return carry + self.held[pl.ds(pl.multiple_of(k * self.rows, self.rows), self.rows), :]

        self.total[...] = lax.fori_loop(0, self.count, add, jnp.zeros(self.total.shape, F32))

        def step(k, carry):
            place = self.device(k)[1]
            remote(self.total, self.part(self.done, self.me), self.send_sem.at[1], self.recv_sem.at[1], place).start()
            return carry

        lax.fori_loop(1, self.count, step, 0)
        self.done[pl.ds(pl.multiple_of(self.me * self.rows, self.rows), self.rows), :] = self.total[...]

    def close(self):
        self.settle(self.done, 1)


def blend(h_ref, coeffs, streams_ref):
    hist, block, width = h_ref.shape[0], h_ref.shape[2], h_ref.shape[3]
    spread = [jnp.broadcast_to(coeffs[:, k : k + 1], (block, 128)) for k in range(4 * hist)]
    for at in range(0, width, 128):
        lanes = slice(at, at + 128)
        inputs = [h_ref[j, 0, :, lanes].astype(F32) for j in range(hist)]
        for c in range(4):
            total = spread[c * hist] * inputs[0]
            for j in range(1, hist):
                total = total + spread[c * hist + j] * inputs[j]
            streams_ref[c, :, lanes] = total
    return spread


def mix_kernel(grid, rows, chunks, whole, partial, h_ref, g_ref, gain_ref, inner_ref, outer_ref, bias_ref, sgain_ref, sbias_ref, *refs):
    ins, (lowered_ref, gpair_ref, last_ref, pre_ref, coeffs_ref), outs = refs[:4], refs[4:9], refs[9:15]
    streams_ref, held_ref, local_sem, send_sem, recv_sem, pair_local, pair_send, pair_recv = refs[15:]
    i, steps = pl.program_id(0), pl.num_programs(0)
    a, b, z, c = place = grid.here()
    block = h_ref.shape[2]
    events = Gathering(grid, place, rows, chunks, ins, outs, local_sem, send_sem, recv_sem).events(whole, partial)
    other = grid.device(a, b, z, 1 - c)

    def pair(k, src, dst):
        return [
            pltpu.make_async_copy(src, dst, pair_local.at[k]),
            remote(src, dst, pair_send.at[k], pair_recv.at[k], other),
        ]

    grads = lambda: pair(0, g_ref.at[0], gpair_ref.at[c])
    lowereds = lambda: pair(1, held_ref, lowered_ref.at[:, c])

    @pl.when(i == 0)
    def _():
        grid.greet(*place)
        events[0]()
        start(grads())

    @pl.when(i == 1)
    def _():
        events[1]()

    last = h_ref[h_ref.shape[0] - 1, 0].astype(F32)
    r = lax.rsqrt(jnp.mean(last * last, axis=1, keepdims=True) + EPS)
    scaled_low = (last * r * gain_ref[...]).astype(BF16)
    pre = product(scaled_low, inner_ref[...])
    pre_ref[...] = pre
    coeffs = product((pre * phi(pre)).astype(BF16), outer_ref[...]) + bias_ref[...]
    coeffs_ref[...] = coeffs
    blend(h_ref, coeffs, streams_ref)
    at = pl.ds(pl.multiple_of(i * block, block), block)
    for k in range(4):
        stream = streams_ref[k]
        centered = stream - jnp.mean(stream, axis=1, keepdims=True)
        rs = lax.rsqrt(jnp.mean(centered * centered, axis=1, keepdims=True) + EPS)
        held_ref[k, at, :] = (centered * rs * sgain_ref[k : k + 1, :] + sbias_ref[k : k + 1, :]).astype(BF16)
    last_ref[...] = streams_ref[3]

    @pl.when(i == steps - 1)
    def _():
        start(lowereds())
        for event in events[2:]:
            event()
        finish(grads())
        finish(lowereds())


def mix_forward(grid, history, cotangent, params, weights, chunks, groups, partial, widths, collective_id):
    hist, _, tokens, width = history.shape
    mix = params[1].shape[1]
    block = 32
    rows = weights[0].shape[0]
    whole = pl.BlockSpec(memory_space=pltpu.VMEM)
    anywhere = pl.BlockSpec(memory_space=pl.ANY)
    part = lambda n: pl.BlockSpec((block, n), lambda i: (i, 0))
    results = pl.pallas_call(
        functools.partial(mix_kernel, grid, rows, chunks, groups, partial),
        grid=(tokens // block,),
        out_shape=[
            jax.ShapeDtypeStruct((4, 2, tokens, width), BF16),
            jax.ShapeDtypeStruct((2, tokens, width), BF16),
            jax.ShapeDtypeStruct((tokens, width), F32),
            jax.ShapeDtypeStruct((tokens, mix), F32),
            jax.ShapeDtypeStruct((tokens, mix), F32),
        ]
        + [jax.ShapeDtypeStruct((grid.na, grid.nb, grid.nz, 2 * rows, w), BF16) for w in widths],
        in_specs=[pl.BlockSpec((hist, 1, block, width), lambda i: (0, 0, i, 0))] + [whole] * 11,
        out_specs=[anywhere, anywhere, part(width), part(mix), part(mix)] + [anywhere] * len(widths),
        scratch_shapes=[
            pltpu.VMEM((4, block, width), F32),
            pltpu.VMEM((4, tokens, width), BF16),
            *gather_sems(grid, chunks),
            pltpu.SemaphoreType.DMA((2,)),
            pltpu.SemaphoreType.DMA((2,)),
            pltpu.SemaphoreType.DMA((2,)),
        ],
        compiler_params=pltpu.CompilerParams(collective_id=collective_id, has_side_effects=True, vmem_limit_bytes=VMEM_LIMIT),
        cost_estimate=pl.CostEstimate(flops=tokens * width * 80, bytes_accessed=history.size * 40, transcendentals=0),
        name="mix_forward",
    )(history, cotangent, *params, *weights)
    lowered, gpair, last, pre, coeffs = results[:5]
    return (
        lowered.reshape(4, 2 * tokens, width),
        gpair.reshape(2 * tokens, width),
        last,
        pre,
        coeffs,
        [w.reshape(-1, w.shape[-1]) for w in results[5:9]],
        results[9:],
    )


def small_rows(width, mix, hidden_width):
    wl, padded = width // 128, -(-mix // 8) * 8
    sizes = [wl, wl * padded, padded, 8, 4 * wl, 4 * wl, 3 * wl, wl, hidden_width // 128]
    firsts = [sum(sizes[:k]) for k in range(len(sizes))]
    return firsts, sum(sizes)


def unmix_kernel(grid, chunks, groups, n_parts, n_outs, h_ref, own_ref, theirs_ref, g_ref, pre_ref, coeffs_ref, gain_ref, inner_ref, outer_ref,
                 sgain_ref, hb_ref, eb_ref, *refs):
    parts, refs = refs[:n_parts], refs[n_parts:]
    hist_ref, small, outs, refs = refs[0], refs[1:10], refs[10 : 10 + n_outs], refs[10 + n_outs :]
    streams_ref, sg_ref, scaled_ref, mpg_ref, hidden_ref, cgl_ref, sgg_ref, sbg_ref, gg_ref, bg_ref, ob_ref = refs[:11]
    i, steps = pl.program_id(0), pl.num_programs(0)
    hist, block, width = h_ref.shape[0], h_ref.shape[2], h_ref.shape[3]
    mix = 4 * hist
    place = grid.here()
    c = place[3]
    sums = Summing(grid, *refs[11:17])
    events = Scattering(grid, place, chunks, parts, outs, refs[17:]).events(groups)

    @pl.when(i == 0)
    def _():
        sums.greet()
        events[0]()
        for ref in (sgg_ref, sbg_ref, gg_ref, bg_ref, ob_ref):
            ref[...] = jnp.zeros_like(ref)

    @pl.when(i == 6)
    def _():
        events[1]()

    def down(x):
        return jnp.sum(x, axis=0, keepdims=True)

    coeffs = coeffs_ref[...]
    spread = blend(h_ref, coeffs, streams_ref)
    grad = g_ref[0].astype(F32)
    ob_ref[...] += down(grad)
    for k in range(4):
        stream = streams_ref[k]
        centered = stream - jnp.mean(stream, axis=1, keepdims=True)
        rs = lax.rsqrt(jnp.mean(centered * centered, axis=1, keepdims=True) + EPS)
        n = centered * rs
        ng = own_ref[k] + theirs_ref[k].astype(F32)
        sgg_ref[k : k + 1, :] += down(ng * n)
        sbg_ref[k : k + 1, :] += down(ng)
        w = ng * sgain_ref[k : k + 1, :]
        pulled = rs * (w - jnp.mean(w, axis=1, keepdims=True) - n * jnp.mean(w * n, axis=1, keepdims=True))
        sg_ref[k] = pulled + grad if k == 3 else pulled

    lane = lax.broadcasted_iota(jnp.int32, (block, mix), 1)
    cg = jnp.zeros((block, mix), F32)
    for j in range(hist):
        value = h_ref[j, 0].astype(F32)
        for k in range(4):
            cg = jnp.where(lane == k * hist + j, jnp.sum(value * sg_ref[k], axis=1, keepdims=True), cg)
    bg_ref[...] += down(cg)
    cg_low = cg.astype(BF16)
    pre = pre_ref[...]
    at = pl.ds(pl.multiple_of(i * block, block), block)
    mpg = (against(cg_low, outer_ref[...]) * gelu_slope(pre)).astype(BF16)
    last = h_ref[hist - 1, 0].astype(F32)
    r = lax.rsqrt(jnp.mean(last * last, axis=1, keepdims=True) + EPS)
    scaled_ref[at, :] = (last * r * gain_ref[...]).astype(BF16)
    mpg_ref[at, :] = mpg
    hidden_ref[at, :] = (pre * phi(pre)).astype(BF16)
    cgl_ref[at, :] = cg_low
    scaled_grad = against(mpg, inner_ref[...])
    gg_ref[...] += down(scaled_grad * last * r)
    w = scaled_grad * gain_ref[...]
    last_grad = r * (w - last * (r * r) * jnp.mean(w * last, axis=1, keepdims=True))
    for from_ in range(0, width, 128):
        lanes = slice(from_, from_ + 128)
        pulls = [sg_ref[k, :, lanes] for k in range(4)]
        for j in range(hist):
            total = spread[j] * pulls[0]
            for k in range(1, 4):
                total = total + spread[k * hist + j] * pulls[k]
            hist_ref[j, 0, :, lanes] = total + last_grad[:, lanes] if j == hist - 1 else total

    @pl.when(i == steps - 1)
    def _():
        mine, done = sums.mine, sums.done
        wl = width // 128
        padded = -(-mix // 8) * 8
        hidden_rows = eb_ref.shape[1] // 128
        firsts, _ = small_rows(width, mix, 2 * eb_ref.shape[1])
        mine[...] = jnp.zeros_like(mine)
        inner_grad = inner(mpg_ref[...], scaled_ref[...])
        for l in range(wl):
            lanes = slice(l * 128, (l + 1) * 128)
            mine[firsts[0] + l : firsts[0] + l + 1, :] = gg_ref[:, lanes]
            mine[firsts[1] + l * padded : firsts[1] + l * padded + mix, :] = inner_grad[:, lanes]
            mine[firsts[4] + 4 * l : firsts[4] + 4 * l + 4, :] = sgg_ref[:, lanes]
            mine[firsts[5] + 4 * l : firsts[5] + 4 * l + 4, :] = sbg_ref[:, lanes]
            mine[firsts[7] + l : firsts[7] + l + 1, :] = ob_ref[:, lanes]
        mine[firsts[2] : firsts[2] + mix, 0:mix] = inner(hidden_ref[...], cgl_ref[...])
        mine[firsts[3] : firsts[3] + 1, 0:mix] = bg_ref[...]
        for k in range(3):
            for l in range(wl // 2):
                mine[pl.ds(firsts[6] + k * wl + c * (wl // 2) + l, 1), :] = hb_ref[k : k + 1, l * 128 : (l + 1) * 128]
        for l in range(hidden_rows):
            mine[pl.ds(firsts[8] + c * hidden_rows + l, 1), :] = eb_ref[:, l * 128 : (l + 1) * 128]
        sums.deal()
        for n, event in enumerate(events[2:]):
            event()
            if n == 0:
                sums.tell()
            if n == 1:
                sums.close()
        for l in range(wl):
            lanes = slice(l * 128, (l + 1) * 128)
            small[0][:, lanes] = done[firsts[0] + l : firsts[0] + l + 1, :]
            small[1][:, lanes] = done[firsts[1] + l * padded : firsts[1] + l * padded + mix, :]
            small[4][:, lanes] = done[firsts[4] + 4 * l : firsts[4] + 4 * l + 4, :]
            small[5][:, lanes] = done[firsts[5] + 4 * l : firsts[5] + 4 * l + 4, :]
            small[7][:, lanes] = done[firsts[7] + l : firsts[7] + l + 1, :]
        small[2][...] = done[firsts[2] : firsts[2] + mix, 0:mix]
        small[3][...] = done[firsts[3] : firsts[3] + 1, 0:mix]
        for l in range(3 * wl):
            small[6][:, l * 128 : (l + 1) * 128] = done[firsts[6] + l : firsts[6] + l + 1, :]
        for l in range(2 * hidden_rows):
            small[8][:, l * 128 : (l + 1) * 128] = done[firsts[8] + l : firsts[8] + l + 1, :]


def mix_backward(grid, history, own, theirs, cotangent, pre, coeffs, params, biases, parts, folded, chunks, groups, widths, collective_id):
    hist, _, tokens, width = history.shape
    mix = pre.shape[1]
    hidden_width = 2 * biases[1].shape[1]
    na, nb, nz = grid.na, grid.nb, grid.nz
    rows = parts[0].shape[0] // (na * nb * nz)
    parts = [p.reshape(na, nb, nz, rows, p.shape[1]) for p in parts] + list(folded)
    devices = grid.n_dp * grid.n_seq
    small_each = -(-small_rows(width, mix, hidden_width)[1] // (devices * 8)) * 8
    block = 32
    whole = pl.BlockSpec(memory_space=pltpu.VMEM)
    anywhere = pl.BlockSpec(memory_space=pl.ANY)
    part = lambda n: pl.BlockSpec((block, n), lambda i: (i, 0))
    four = pl.BlockSpec((4, block, width), lambda i: (0, i, 0))
    story = pl.BlockSpec((hist, 1, block, width), lambda i: (0, 0, i, 0))
    small = [(1, width), (mix, width), (mix, mix), (1, mix), (4, width), (4, width), (1, 3 * width), (1, width), (1, hidden_width)]
    fixed = [pl.BlockSpec(shape, lambda i: (0, 0)) for shape in small]
    moved = sum(p.size for p in parts) * 2
    results = pl.pallas_call(
        functools.partial(unmix_kernel, grid, chunks, groups, len(parts), len(widths)),
        grid=(tokens // block,),
        out_shape=[jax.ShapeDtypeStruct(history.shape, F32)]
        + [jax.ShapeDtypeStruct(shape, F32) for shape in small]
        + [jax.ShapeDtypeStruct((rows // 2, w), F32) for w in widths],
        in_specs=[story, four, four, pl.BlockSpec((1, block, width), lambda i: (0, i, 0)), part(mix), part(mix)]
        + [whole] * 6
        + [anywhere] * len(parts),
        out_specs=[story] + fixed + [anywhere] * len(widths),
        scratch_shapes=[
            pltpu.VMEM((4, block, width), F32),
            pltpu.VMEM((4, block, width), F32),
            pltpu.VMEM((tokens, width), BF16),
            pltpu.VMEM((tokens, mix), BF16),
            pltpu.VMEM((tokens, mix), BF16),
            pltpu.VMEM((tokens, mix), BF16),
            pltpu.VMEM((4, width), F32),
            pltpu.VMEM((4, width), F32),
            pltpu.VMEM((1, width), F32),
            pltpu.VMEM((1, mix), F32),
            pltpu.VMEM((1, width), F32),
            pltpu.VMEM((devices * small_each, 128), F32),
            pltpu.VMEM((devices * small_each, 128), F32),
            pltpu.VMEM((small_each, 128), F32),
            pltpu.VMEM((devices * small_each, 128), F32),
            pltpu.SemaphoreType.DMA((2,)),
            pltpu.SemaphoreType.DMA((2,)),
            *scatter_scratch(grid, chunks, rows),
        ],
        compiler_params=pltpu.CompilerParams(collective_id=collective_id, has_side_effects=True, vmem_limit_bytes=VMEM_LIMIT),
        cost_estimate=pl.CostEstimate(flops=tokens * width * 300, bytes_accessed=moved * 20, transcendentals=0),
        name="mix_backward",
    )(history, own, theirs, cotangent, pre, coeffs, *params, *biases, *parts)
    return results[0], results[10:], results[1:10]


def project_kernel(width, low_ref, g_ref, wq_ref, wk_ref, wv_ref, wo_ref, bias_ref, cos_ref, above_ref, below_ref, sent_ref):
    wide = wq_ref.shape[1]
    reps = wide // cos_ref.shape[1] if wide >= cos_ref.shape[1] else 1
    tables = [jnp.concatenate([t[:, :wide]] * reps, axis=1) for t in (cos_ref, above_ref, below_ref)]
    q = rotate(product(low_ref[0], wq_ref[...]) + bias_ref[0:1, :], tables, 1.0)
    k = rotate(product(low_ref[1], wk_ref[...]) + bias_ref[1:2, :], tables, 1.0)
    v = product(low_ref[2], wv_ref[...]) + bias_ref[2:3, :]
    g = product(g_ref[...], wo_ref[...])
    for n, x in enumerate((q, k, v, g)):
        x = x.astype(BF16)
        for m in range(wide // width):
            sent_ref[m, :, n * width : (n + 1) * width] = x[:, m * width : (m + 1) * width]


def project(grid, lowered, grad_low, weights, biases, tables, own_width):
    both = lowered.shape[1]
    nz = grid.nz
    wide = 2 * own_width
    whole = pl.BlockSpec(memory_space=pltpu.VMEM)
    cols = lambda n: pl.BlockSpec((n, wide), lambda i: (0, i))
    return pl.pallas_call(
        functools.partial(project_kernel, own_width),
        grid=(nz // 2,),
        out_shape=jax.ShapeDtypeStruct((nz, both, 4 * own_width), BF16),
        in_specs=[whole, whole] + [cols(weights[0].shape[0])] * 4 + [cols(3)] + [whole] * 3,
        out_specs=pl.BlockSpec((2, both, 4 * own_width), lambda i: (i, 0, 0)),
        compiler_params=pltpu.CompilerParams(vmem_limit_bytes=VMEM_LIMIT),
        cost_estimate=pl.CostEstimate(flops=8 * both * weights[0].size, bytes_accessed=lowered.size * 4, transcendentals=0),
        name="project",
    )(lowered, grad_low, *weights, biases, *tables)


def feed_kernel(grid, steps, low_ref, g_ref, we_ref, wc_ref, bias_ref, feed_ref, normed_ref, eb_ref, e2_ref, c2_ref, *refs):
    parts, refs = refs[: 2 * steps], refs[2 * steps :]
    first, second, refs = refs[: 2 * steps], refs[2 * steps : 4 * steps], refs[4 * steps :]
    send_sem, recv_sem, out_sem = refs
    i = pl.program_id(0)
    a, b, z, c = place = grid.here()
    orders = ["ab", "ba"] * steps
    outs = (e2_ref, c2_ref)

    def copies(t, stage):
        if stage < 2:
            return fold_copies(grid, place, orders[t], stage, parts[t], first[t], second[t], (send_sem.at[t], recv_sem.at[t]))
        n = parts[t].shape[-1]
        return [pltpu.make_async_copy(second[t].at[0], outs[t % 2].at[:, :, pl.ds((t // 2) * n, n)], out_sem.at[t])]

    def begin(u):
        for t in (2 * u, 2 * u + 1):
            start(copies(t, 0))

    def end(u, stage):
        for t in (2 * u, 2 * u + 1):
            finish(copies(t, stage))
            if stage < 2:
                own = parts[t].at[a] if orders[t] == "ab" else parts[t].at[:, b]
                fold_add(grid, place, orders[t], stage, own, first[t], second[t])
                start(copies(t, stage + 1))

    def turn(u):
        if u < steps:
            end(u, 0)
        if 0 <= u - 1 < steps:
            end(u - 1, 1)

    @pl.when(i == 0)
    def _():
        grid.greet(*place)
        feed_ref[...] = jnp.zeros_like(feed_ref)
        normed_ref[...] = jnp.zeros_like(normed_ref)

    low, grad, expand, contract = low_ref[0], g_ref[...], we_ref[...], wc_ref[...]
    expanded = product(low, expand) + bias_ref[...]
    share = phi(expanded)
    hidden = (expanded * share).astype(BF16)
    slope = share + expanded * jnp.exp(-0.5 * expanded * expanded) * (1.0 / math.sqrt(2.0 * math.pi))
    feed_ref[...] += against(hidden, contract)
    hidden_grad = inner(grad, hidden).astype(BF16)
    pulled = product(grad, contract) * slope
    eb_ref[...] = jnp.sum(pulled, axis=0, keepdims=True)
    pulled_low = pulled.astype(BF16)
    normed_ref[...] += against(pulled_low, expand)
    expand_grad = inner(low, pulled_low).astype(BF16)
    for u in range(steps):

        @pl.when(i == u)
        def _(u=u):
            parts[2 * u][...] = expand_grad.reshape(parts[2 * u].shape)
            parts[2 * u + 1][...] = hidden_grad.reshape(parts[2 * u + 1].shape)
            begin(u)
            if u >= 2:
                turn(u - 2)
            if u == steps - 1:
                for v in range(max(steps - 2, 0), steps + 1):
                    turn(v)
                for v in range(steps):
                    end(v, 2)


def feed_forward(grid, lowered, grad_low, weight_e, weight_c, bias, steps, collective_id):
    both, width = grad_low.shape
    n = weight_e.shape[1] // steps
    na, nb, nz = grid.na, grid.nb, grid.nz
    rows = width // (na * nb * nz)
    whole = lambda *shape: pl.BlockSpec(shape, lambda i: (0,) * len(shape))
    cols = lambda m: pl.BlockSpec((m, n), lambda i: (0, i))
    orders = ["ab", "ba"] * steps
    folds = [fold_scratch(grid, order, rows, n) for order in orders]
    sem = pltpu.SemaphoreType.DMA((2 * steps, nz + nb))
    return pl.pallas_call(
        functools.partial(feed_kernel, grid, steps),
        grid=(steps,),
        out_shape=[
            jax.ShapeDtypeStruct((both, width), F32),
            jax.ShapeDtypeStruct((both, width), F32),
            jax.ShapeDtypeStruct((1, n * steps), F32),
            jax.ShapeDtypeStruct((nz, rows, n * steps), BF16),
            jax.ShapeDtypeStruct((nz, rows, n * steps), BF16),
        ],
        in_specs=[
            pl.BlockSpec((1, both, width), lambda i: (3, 0, 0)),
            whole(both, width),
            cols(width),
            cols(width),
            cols(1),
        ],
        out_specs=[
            whole(both, width),
            whole(both, width),
            cols(1),
            pl.BlockSpec(memory_space=pl.ANY),
            pl.BlockSpec(memory_space=pl.ANY),
        ],
        scratch_shapes=[pltpu.VMEM((na, nb, nz, rows, n), BF16)] * (2 * steps)
        + [f for _, f, _ in folds]
        + [s for _, _, s in folds]
        + [sem, sem, pltpu.SemaphoreType.DMA((2 * steps,))],
        compiler_params=pltpu.CompilerParams(collective_id=collective_id, has_side_effects=True, vmem_limit_bytes=VMEM_LIMIT),
        cost_estimate=pl.CostEstimate(flops=12 * both * width * n * steps * 2, bytes_accessed=width * n * steps * 20, transcendentals=0),
        name="feed_forward",
    )(lowered, grad_low, weight_e, weight_c, bias)


def attention_kernel(width, heads, tile, step, edge, length, x_ref, kdoc_ref, qdoc_ref, out_ref,
                     s_ref, kt_ref, vt_ref, ot_ref, dqt_ref, dka_ref, dva_ref, top_ref):
    i = pl.program_id(0)
    tiles = length // tile
    scale = 1.0 / math.sqrt(HEAD_DIM)
    @pl.when(i == 0)
    def _():
        dka_ref[...] = jnp.zeros_like(dka_ref)
        dva_ref[...] = jnp.zeros_like(dva_ref)
        def turn(j, carry):
            at = pl.ds(pl.multiple_of(j * tile, tile), tile)
            kt_ref[:, at] = x_ref[at, width : 2 * width].T
            vt_ref[:, at] = x_ref[at, 2 * width : 3 * width].T
            return carry
        lax.fori_loop(0, tiles, turn, 0)
    rows = pl.ds(pl.multiple_of(i * tile, tile), tile)
    query = x_ref[rows, 0:width] * jnp.asarray(scale, BF16)
    grad = x_ref[rows, 3 * width : 4 * width]
    query_t, grad_t = query.T, grad.T
    lanes = lax.broadcasted_iota(jnp.int32, (tile, width), 1) // HEAD_DIM
    subs = lax.broadcasted_iota(jnp.int32, (width, tile), 0) // HEAD_DIM
    zero = jnp.zeros((), BF16)
    queries_t = [jnp.where(subs == h, query_t, zero) for h in range(heads)]
    grads_t = [jnp.where(subs == h, grad_t, zero) for h in range(heads)]
    all_queries = jnp.concatenate([jnp.where(lanes == h, query, zero) for h in range(heads)], axis=0)
    all_grads = jnp.concatenate([jnp.where(lanes == h, grad, zero) for h in range(heads)], axis=0)
    qdoc = qdoc_ref[:, rows]
    qpos = i * tile + lax.broadcasted_iota(jnp.int32, (step, tile), 1)
    head_edge = -(-edge // step)
    tail_edge = (length - edge) // tile
    per = tile // step
    count = (i + 1) * per
    ot_ref[...] = jnp.zeros_like(ot_ref)
    dqt_ref[...] = jnp.zeros_like(dqt_ref)
    top_ref[...] = jnp.full_like(top_ref, NEG)

    def fold(x, f):
        return f(x.reshape(step // 8, 8, tile), axis=0)

    def scores(j, carry):
        at = pl.ds(pl.multiple_of(j * step, step), step)
        checked = (j >= i * per) | (j < head_edge) | (i >= tail_edge)
        def run(mask):
            keys = x_ref[at, width : 2 * width]
            if mask:
                kdoc = jnp.concatenate([kdoc_ref[at, :]] * (tile // 128), axis=1)
                kpos = j * step + lax.broadcasted_iota(jnp.int32, (step, tile), 0)
                allowed = (kdoc == qdoc) & (kpos <= qpos)
            for h in range(heads):
                s = product(keys, queries_t[h])
                if mask:
                    s = jnp.where(allowed, s, NEG)
                s_ref[h, at, :] = s
                top_ref[h] = jnp.maximum(top_ref[h], fold(s, jnp.max))
        pl.when(checked)(lambda: run(True))
        pl.when(jnp.logical_not(checked))(lambda: run(False))
        return carry
    lax.fori_loop(0, count, scores, 0)
    tops = [jnp.max(top_ref[h], axis=0, keepdims=True) for h in range(heads)]

    def weigh(j, totals):
        at = pl.ds(pl.multiple_of(j * step, step), step)
        new = []
        for h in range(heads):
            own = slice(h * HEAD_DIM, (h + 1) * HEAD_DIM)
            weights = jnp.exp(s_ref[h, at, :] - tops[h])
            s_ref[h, at, :] = weights
            new.append(totals[h] + fold(weights, jnp.sum))
            ot_ref[own, :] += product(vt_ref[own, at], weights.astype(BF16))
        return new
    totals = lax.fori_loop(0, count, weigh, [jnp.zeros((8, tile), F32)] * heads)
    inverse = [1.0 / jnp.sum(t, axis=0, keepdims=True) for t in totals]
    grad_f = grad_t.astype(F32)
    deltas = []
    for h in range(heads):
        own = slice(h * HEAD_DIM, (h + 1) * HEAD_DIM)
        value = ot_ref[own, :] * inverse[h]
        ot_ref[own, :] = value
        deltas.append(jnp.sum(value * grad_f[own], axis=0, keepdims=True))
    out_ref[rows, 0:width] = ot_ref[...].T.astype(BF16)

    def back(j, carry):
        at = pl.ds(pl.multiple_of(j * step, step), step)
        values = x_ref[at, 2 * width : 3 * width]
        probs_low, grads_low = [], []
        for h in range(heads):
            own = slice(h * HEAD_DIM, (h + 1) * HEAD_DIM)
            probs_grad = product(values, grads_t[h])
            probs = s_ref[h, at, :] * inverse[h]
            scores_grad = (probs * (probs_grad - deltas[h])).astype(BF16)
            probs_low.append(probs.astype(BF16))
            grads_low.append(scores_grad)
            dqt_ref[own, :] += product(kt_ref[own, at], scores_grad)
        dva_ref[at, :] += product(jnp.concatenate(probs_low, axis=1), all_grads)
        dka_ref[at, :] += product(jnp.concatenate(grads_low, axis=1), all_queries)
        return carry
    lax.fori_loop(0, count, back, 0)
    out_ref[rows, width : 2 * width] = (dqt_ref[...].T * scale).astype(BF16)

    @pl.when(i == tiles - 1)
    def _():
        out_ref[:, 2 * width : 3 * width] = dka_ref[...].astype(BF16)
        out_ref[:, 3 * width : 4 * width] = dva_ref[...].astype(BF16)


def attention(dealt, documents, heads, edge):
    length = dealt.shape[0]
    width = heads * HEAD_DIM
    tile = step = 2 * edge
    pairs = length * length // 2 * heads
    kdoc = jnp.broadcast_to(documents[:, None], (length, 128)); qdoc = documents[None, :]
    whole = lambda i: (0, 0)
    return pl.pallas_call(
        functools.partial(attention_kernel, width, heads, tile, step, edge, length),
        grid=(length // tile,),
        out_shape=jax.ShapeDtypeStruct((length, 4 * width), BF16),
        in_specs=[pl.BlockSpec((length, 4 * width), whole), pl.BlockSpec((length, 128), whole), pl.BlockSpec((1, length), whole)],
        out_specs=pl.BlockSpec((length, 4 * width), whole),
        scratch_shapes=[
            pltpu.VMEM((heads, length, tile), F32), pltpu.VMEM((width, length), BF16), pltpu.VMEM((width, length), BF16),
            pltpu.VMEM((width, tile), F32), pltpu.VMEM((width, tile), F32), pltpu.VMEM((length, width), F32), pltpu.VMEM((length, width), F32),
            pltpu.VMEM((heads, 8, tile), F32)],
        compiler_params=pltpu.CompilerParams(vmem_limit_bytes=VMEM_LIMIT),
        cost_estimate=pl.CostEstimate(flops=pairs * 64 * 2 * 6 * 4, bytes_accessed=length * width * 20, transcendentals=pairs),
        name="attention",
    )(dealt, kdoc, qdoc)


def on_device(
    grid,
    history,
    documents,
    cotangent,
    mixer_gain,
    mixer_inner,
    mixer_outer,
    mixer_bias,
    stream_gain,
    stream_bias,
    inbound_weight,
    inbound_bias,
    outbound_weight,
    outbound_bias,
    expand,
    expand_bias,
    contract,
    contract_bias,
):
    n_seq, nz = grid.n_seq, grid.nz
    tokens, width = history.shape[2], history.shape[3]
    hidden_width = expand.shape[1]
    half, hidden_half = width // 2, hidden_width // 2
    both = 2 * tokens
    length = documents.shape[1]
    heads = HEADS // n_seq
    own_width = heads * HEAD_DIM
    seq = lax.axis_index("seq")
    z, c = seq // 2, lax.rem(seq, 2)

    def take(array, start, size, axis=0):
        return lax.dynamic_slice_in_dim(array, start, size, axis)

    gain = mixer_gain.astype(F32)[None]
    stream_gain_full = stream_gain.astype(F32)
    pick = lambda base, n: (lambda core: base + core * n)
    parts = 4
    piece = hidden_half // parts
    feed = []
    for part in range(parts):
        base = lambda core, part=part: core * hidden_half + part * piece
        feed.append((2, base, 4, part * piece, piece, "ba"))
        feed.append((3, base, 5, part * piece, piece, "ab"))
    lowered, grad_low, last_stream, mix_pre, coeffs, (weight_k, weight_v, weight_q, weight_o), started = mix_forward(
        grid,
        history,
        cotangent,
        [gain, mixer_inner, mixer_outer, mixer_bias.astype(F32)[None], stream_gain_full, stream_bias.astype(F32)],
        [inbound_weight, outbound_weight, expand, contract],
        [
            (0, pick(width, half), 0, 0, half, "ba"),
            (0, pick(2 * width, half), 1, 0, half, "ab"),
            (0, pick(0, half), 2, 0, half, "ba"),
            (1, pick(0, half), 3, 0, half, "ab"),
        ]
        + feed,
        [[0, 1], [2, 3]],
        [[4 + 2 * part, 5 + 2 * part] for part in range(parts)],
        [half] * 4 + [hidden_half] * 2,
        1,
    )

    bias_in = inbound_bias.astype(F32).reshape(3, width)
    positions = z * both + jnp.arange(both, dtype=jnp.int32)
    tables = rotary_tables(positions, 128)
    sent = project(
        grid, lowered, grad_low, [weight_q, weight_k, weight_v, weight_o], take(bias_in, c * half, half, 1), tables, own_width
    )
    groups = [[2 * k + core for k in range(nz)] for core in range(2)]
    dealt = lax.all_to_all(sent, "seq", 0, 0, axis_index_groups=groups, tiled=True)

    started_e, started_c, _ = lax.optimization_barrier((*started, sent[0, 0]))
    chunks = [(0, None, n - 4, col, size, order) for _, _, n, col, size, order in feed]
    pairs = [[2 * part, 2 * part + 1] for part in range(parts)]
    weight_e, weight_c = gather(grid, [started_e, started_c], chunks, pairs, 3, "gather_feed")
    dealt, weight_e, weight_c = lax.optimization_barrier((dealt, weight_e, weight_c))

    returned = attention(dealt.reshape(length, 4 * own_width), documents[0], heads, tokens).reshape(nz, both, 4 * own_width)
    collected = lax.all_to_all(returned, "seq", 0, 0, axis_index_groups=groups, tiled=True)

    bias_e = take(expand_bias.astype(F32), c * hidden_half, hidden_half)[None]
    lowered_seen, _ = lax.optimization_barrier((lowered, returned[0, 0]))
    feed_part, normed_feed, expand_bias_part, *folded = feed_forward(
        grid, lowered_seen, grad_low, weight_e, weight_c, bias_e, parts, 5
    )

    pieces = [
        jnp.concatenate([collected[m, :, k * own_width : (k + 1) * own_width] for m in range(nz)], axis=-1) for k in range(4)
    ]
    attended_low, value_low = pieces[0], pieces[3]
    spread = [jnp.tile(t, (1, half // 128)) for t in tables]

    def unturn(grad):
        grad = grad.astype(F32)
        up = jnp.roll(grad, -(ROT_DIMS // 2), axis=-1)
        down = jnp.roll(grad, ROT_DIMS // 2, axis=-1)
        return grad * spread[0] - (up * spread[1] + down * spread[2])

    dq, dk = unturn(pieces[1]), unturn(pieces[2])
    dq_low, dk_low, dv_low = dq.astype(BF16), dk.astype(BF16), value_low
    head_bias_grads = jnp.stack([jnp.sum(x.astype(F32), axis=0) for x in (dq, dk, value_low)])

    out_part = against(attended_low, weight_o) + feed_part
    swap = [(s, s + 1 - 2 * (s % 2)) for s in range(n_seq)]
    out_theirs = lax.ppermute(take(out_part, (1 - c) * tokens, tokens), "seq", swap)
    out_own = take(out_part, c * tokens, tokens) + out_theirs
    layer_out = (last_stream + (out_own + outbound_bias.astype(F32) + contract_bias.astype(F32))).astype(BF16)

    normed_part = jnp.stack(
        [
            against(dq_low, weight_q),
            against(dk_low, weight_k),
            against(dv_low, weight_v),
            normed_feed,
        ]
    )
    normed_theirs = lax.ppermute(take(normed_part, (1 - c) * tokens, tokens, 1).astype(BF16), "seq", swap)
    normed_own = take(normed_part, c * tokens, tokens, 1)

    chunks = [
        (0, half, "ab", 0, pick(0, half)),
        (1, half, "ba", 0, pick(width, half)),
        (2, half, "ab", 0, pick(2 * width, half)),
        (3, half, "ba", 1, pick(0, half)),
        (4, hidden_half, "", 2, pick(0, hidden_half)),
        (5, hidden_half, "", 3, pick(0, hidden_half)),
    ]
    history_grad, owned, small = mix_backward(
        grid,
        history,
        normed_own,
        normed_theirs,
        cotangent,
        mix_pre,
        coeffs,
        [gain, mixer_inner, mixer_outer, stream_gain_full],
        [head_bias_grads, expand_bias_part],
        [
            inner(lowered[0], dq_low).astype(BF16),
            inner(lowered[1], dk_low).astype(BF16),
            inner(lowered[2], dv_low).astype(BF16),
            inner(grad_low, attended_low).astype(BF16),
        ],
        folded,
        chunks,
        [[0, 1], [2, 3]],
        [3 * width, width, hidden_width, hidden_width],
        4,
    )
    gain_grad, inner_grad, outer_grad, bias_grad, stream_gain_grad, stream_bias_grad, in_bias_grad, out_bias_grad, expand_bias_grad = small
    return (
        layer_out[None],
        history_grad,
        gain_grad.reshape(width),
        inner_grad.T,
        outer_grad,
        bias_grad.reshape(-1),
        stream_gain_grad,
        stream_bias_grad,
        owned[0],
        in_bias_grad.reshape(3 * width),
        owned[1],
        out_bias_grad.reshape(width),
        owned[2],
        expand_bias_grad.reshape(hidden_width),
        owned[3],
        out_bias_grad.reshape(width),
    )


def solution(mesh):
    rows = P(("dp", "seq"), None)
    placed = (
        P(None, "dp", "seq", None),
        P("dp", None),
        P("dp", "seq", None),
        P(),
        P(),
        P(),
        P(),
        P(),
        P(),
        rows,
        P(),
        rows,
        P(),
        rows,
        P(),
        rows,
        P(),
    )
    grid = Grid(mesh.shape["dp"], mesh.shape["seq"])
    return jax.shard_map(
        functools.partial(on_device, grid),
        mesh=mesh,
        in_specs=placed,
        out_specs=(
            P("dp", "seq", None),
            P(None, "dp", "seq", None),
            P(),
            P(),
            P(),
            P(),
            P(),
            P(),
            rows,
            P(),
            rows,
            P(),
            rows,
            P(),
            rows,
            P(),
        ),
        check_vma=False,
    )
```

time: 647 us -> 499 us (0.77)
  Pallas kernels: 478 us -> 390 us
  matrix products: 66.1 us -> 14.8 us
    pallas_call x6 -> x4, Pallas kernels: 419 us -> 330 us  [the longest x1 89.5 us: mix_backward(): pl.pallas_call(functools.partial(unmix_kernel, grid, chunks, groups, len(...]
    dot_general x2 -> x0, matrix products: 27.5 us -> none  [product(): return jnp.dot(left, right, preferred_element_type=F32)]
    unnamed x106 -> x94, local copies, waits for them, and re-layouts: 12.9 us -> 32 us
    dot_general x6 -> x4, matrix products: 22.8 us -> 8.12 us  [inner(): lax.dot_general(left, right, (((0,), (0,)), ((), ())), preferred_element_...]
    another operation x1, other arithmetic: 1.51 us -> 10.8 us  [on_device(): jnp.stack([against(dq_low, weight_q), against(dk_low, weight_k), against(...]
    dot_general x6 -> x4, matrix products: 15.8 us -> 6.66 us  [against(): lax.dot_general(left, right, (((1,), (1,)), ((), ())), preferred_element_...]
    slice x6 -> x0, local copies, waits for them, and re-layouts: 7.12 us -> none  [small_sum(): results.append(summed[at:at + x.size].reshape(x.shape))]
  transfers between devices with their start and end apart: 4 -> 4, of which waited for: 0 -> 0; matrix products, arithmetic and copies ran while one was open for 15% -> 5% of each run, Pallas kernels for 48% -> 32%
where the time goes in v3:
time: 499 us; the launch traced here: 494 us
  Pallas kernels  390 us (78%)
  local copies, waits for them, and re-layouts  55.6 us (11%)
  other arithmetic  21.9 us (4%)
  matrix products  14.8 us (3%)
  starting transfers between devices  10.1 us (2%)
    pallas_call x1, Pallas kernels, mix_backward(): pl.pallas_call(functools.partial(unmix_kernel, grid, chunks, groups, len(...  89.5 us
    pallas_call x1, Pallas kernels, feed_forward(): pl.pallas_call(functools.partial(feed_kernel, grid, steps), grid=(steps,)...  88.2 us
    pallas_call x1, Pallas kernels, mix_forward(): pl.pallas_call(functools.partial(mix_kernel, grid, rows, chunks, groups,...  81.5 us
    pallas_call x1, Pallas kernels, gather(): pl.pallas_call(functools.partial(gather_kernel, grid, chunks, groups, n),...  71.3 us
    pallas_call x1, Pallas kernels, attention(): pl.pallas_call(functools.partial(attention_kernel, width, heads, tile, st...  50.5 us
    unnamed x94, local copies, waits for them, and re-layouts  32 us
    another operation x1, other arithmetic, on_device(): jnp.stack([against(dq_low, weight_q), against(dk_low, weight_k), against(...  10.8 us
  transfers between devices with their start and end apart: 4, of which 0 were waited for; matrix products, arithmetic and copies ran while one was open for 5% of the time, Pallas kernels for 32%

profile of v3, /device:TPU:0, one launch (start us, length us, event | category | flops | bytes accessed | tf_op | source)
XLA Modules:
  0.0 494.0 jit_solution(9233386043651766336)
XLA Ops:
  0.7 1.2 bitcast_convert_fusion.bias_ref
  1.9 1.3 broadcast_in_dim.78
  3.1 1.3 convert_element_type.139.sgain_ref
  4.4 1.3 convert_element_type.140.sbias_ref
  5.8 0.7 reshape.517
  6.5 1.8 copy.41.inner_ref
  8.8 0.6 constant_dynamic-slice_fusion.2.bias_ref
  9.4 1.1 select_select_fusion
  10.4 81.5 %mix_forward.1 = (bf16[4,2,384,1024]{3,2,1,0:T(8,128)(2,1)}, bf16[2,384,1024]{2,1,0:T(8,128)(2,1)}, f32[384,1024]{1,0:T(8,128)}, f32[384,36]{1,0:T(8,128)}, f32[...) custom-call(bf16[9,1,384,1024]{3,2,1,0:T(8,128)(2,1)} %h_ref.3, ...), custom_call_target="tpu_custom_call" | custom-call | flops 31457280 | bytes 141557760 | tf_op jit(solution)/shard_map/mix_forward/pallas_call | solution.py:508
  91.9 9.4 %project.1 = bf16[4,768,512]{2,1,0:T(8,128)(2,1)} custom-call(bf16[4,768,1024]{2,1,0:T(8,128)(2,1)} %bitcast.123, bf16[768,1024]{1,0:T(8,128)(2,1)} %bitcast.136, bf16[1024,512]{1,0:T(8,128)(2,1)} %bitcast.146, bf16[1024,512]{1,0:T(8,128)(2,1)} %bitcast.144, bf16[1024,512]{1,0:T(8,128)(2,1)} %bitcast.142, bf16[1024,512]{1,0:T(8,128)(2,1)} %bitcast.131, ...), custom_call_target="tpu_custom_call" | custom-call | flops 3221225472 | bytes 12582912 | tf_op jit(solution)/shard_map/project/pallas_call | solution.py:745
  101.3 4.2 all-to-all-start
  105.5 71.3 %gather_feed.1 = (bf16[2,2,4,64,2048]{4,3,2,1,0:T(8,128)(2,1)}, bf16[2,2,4,64,2048]{4,3,2,1,0:T(8,128)(2,1)}) custom-call(bf16[2,2,4,64,2048]{4,3,2,1,0:T(8,128)(2,1)} %get-tuple-element.62.refs_0_, bf16[2,2,4,64,2048]{4,3,2,1,0:T(8,128)(2,1)} %get-tuple-element.63.refs_1_), custom_call_target="tpu_custom_call", output_to_operand_aliasing={{0}: (0, {}), {1}: (1, {})} | custom-call | bytes 167772160 | tf_op jit(solution)/shard_map/gather_feed/pallas_call | solution.py:217
  176.8 2.2 broadcast_in_dim.75.kdoc_ref
  179.1 50.5 %attention.1 = bf16[3072,512]{1,0:T(8,128)(2,1)} custom-call(bf16[3072,512]{1,0:T(8,128)(2,1)} %bitcast.134, s32[3072,128]{1,0:T(8,128)} %broadcast_in_dim.75.kdoc_ref, s32[1,3072]{1,0:T(1,128)} %qdoc_ref.1), custom_call_target="tpu_custom_call" | custom-call | flops 28991029248 | bytes 7864320 | tf_op jit(solution)/shard_map/attention/pallas_call | solution.py:980
  229.6 4.6 copy.44
  234.2 5.3 %all-to-all-start.1 = ((bf16[4,768,512]{1,2,0:T(8,128)(2,1)}), bf16[4,768,512]{1,2,0:T(8,128)(2,1)S(1)}, u32[]{:S(2)}, u32[]{:S(2)}) async-start(bf16[4,768,512]{1,2,0:T(8,128)(2,1)} %copy.44), calls=%async_computation.1 | async-start | bytes 6291456 | tf_op jit(solution)/shard_map/all_to_all | solution.py:1075
  239.6 2.0 copy.47
  241.5 1.9 copy.46
  243.5 0.9 copy.45
  244.4 0.6 dynamic-slice_convert_fusion.1
  245.0 88.2 %feed_forward.1 = (f32[768,1024]{1,0:T(8,128)}, f32[768,1024]{1,0:T(8,128)}, f32[1,2048]{1,0:T(1,128)}, bf16[4,64,2048]{2,1,0:T(8,128)(2,1)}, bf16[4,64,2048]{2,1,0:T(8,128)(2,1)}) custom-call(bf16[4,768,1024]{2,1,0:T(8,128)(2,1)} %bitcast.124, bf16[768,1024]{1,0:T(8,128)(2,1)} %bitcast.137, bf16[1024,2048]{1,0:T(8,128)(2,1)} %bitcast.129, ...), custom_call_target="tpu_custom_call" | custom-call | flops 38654705664 | bytes 41943040 | tf_op jit(solution)/shard_map/feed_forward/pallas_call | solution.py:834
  333.2 0.4 slice_bitcast_fusion.23
  333.9 0.2 fusion.10
  334.1 0.2 fusion.11
  334.8 0.9 slice_bitcast_fusion.21
  335.7 0.2 copy-done.6
  335.9 0.3 copy-done.7
  336.3 1.3 fusion.5
  337.6 1.0 convolution_bitcast_fusion.2
  338.6 0.2 copy-done.12
  338.8 1.0 convolution_bitcast_fusion.1
  340.0 1.0 convolution_bitcast_fusion
  341.0 0.9 copy-done.4
  341.9 10.8 %pad_maximum_fusion = f32[4,768,1024]{2,1,0:T(8,128)S(1)} fusion(f32[1,768,1024]{2,1,0:T(8,128)S(1)} %bitcast.133, f32[1,768,1024]{2,1,0:T(8,128)S(1)} %convolution_bitcast_fusion, f32[1,768,1024]{2,1,0:T(8,128)S(1)} %convolution_bitcast_fusion.1, f32[1,768,1024]{2,1,0:T(8,128)S(1)} %convolution_bitcast_fusion.2), kind=kLoop, calls=%fused_computation | loop fusion | flops 9437184 | bytes 25165824 | tf_op jit(solution)/shard_map/stack | solution.py:1105
  352.7 4.8 copy-done
  357.5 2.1 dynamic-slice_convert_fusion
  359.7 3.0 fusion.9
  362.8 3.6 convolution_add_fusion
  366.4 0.2 constant_dynamic-slice_fusion.1
  366.5 0.6 collective-permute-start
  367.4 0.2 convert_reduce_fusion
  367.5 0.6 pad_maximum_fusion.9.hb_ref
  368.2 3.3 constant_dynamic-slice_fusion.own_ref
  371.4 2.0 convolution_convert_fusion.2
  373.5 2.0 convolution_convert_fusion.3
  375.5 2.0 convolution_convert_fusion
  377.5 2.0 convolution_convert_fusion.1
  379.6 1.4 fusion.2
  381.0 89.5 %mix_backward.1 = (f32[9,1,384,1024]{3,2,1,0:T(8,128)}, f32[1,1024]{1,0:T(1,128)}, f32[36,1024]{1,0:T(8,128)}, f32[36,36]{1,0:T(8,128)}, f32[1,36]{1,0:T(1,128)}...) custom-call(bf16[9,1,384,1024]{3,2,1,0:T(8,128)(2,1)} %h_ref.3, ...), custom_call_target="tpu_custom_call" | custom-call | flops 117964800 | bytes 125829120 | tf_op jit(solution)/shard_map/mix_backward/pallas_call | solution.py:688
  470.5 1.3 copy.66
  471.8 13.6 %copy.67 = f32[9,1,384,1024]{3,2,1,0:T(8,128)} copy(f32[9,1,384,1024]{3,2,1,0:T(8,128)} %get-tuple-element.193) | data formatting | bytes 28311552
  485.4 0.6 copy.68
  486.0 0.7 copy.69
  486.7 0.6 copy.70
  487.3 0.5 copy.71
  487.8 0.6 copy.72
  488.4 0.6 copy.73
  489.0 0.7 copy.74
  489.8 0.6 copy.75
  490.4 0.7 copy.76
  491.0 0.6 copy.77
  491.6 0.8 copy.78
  492.4 0.6 copy.79
  493.0 0.8 copy.80
  (95 shorter events, 1.9 us)
Async XLA Ops:
  101.3 75.5 %all-to-all-start = ((bf16[4,768,512]{2,1,0:T(8,128)(2,1)}), bf16[4,768,512]{2,1,0:T(8,128)(2,1)S(1)}, u32[]{:S(2)}, u32[]{:S(2)}) async-start(bf16[4,768,512]{2,1,0:T(8,128)(2,1)} %project.1), calls=%async_computation | async-start | bytes 6291456 | tf_op jit(solution)/shard_map/all_to_all | solution.py:1066
  105.5 71.3 %copy-start.32 = (s32[1,3072]{1,0:T(1,128)S(1)}, s32[1,3072]{1,0:T(1,128)}, u32[]{:S(2)}) copy-start(s32[1,3072]{1,0:T(1,128)} %qdoc_ref.1) | copy-start | bytes 36868
  176.8 2.3 copy-start.5
  234.2 99.0 %all-to-all-start.1 = ((bf16[4,768,512]{1,2,0:T(8,128)(2,1)}), bf16[4,768,512]{1,2,0:T(8,128)(2,1)S(1)}, u32[]{:S(2)}, u32[]{:S(2)}) async-start(bf16[4,768,512]{1,2,0:T(8,128)(2,1)} %copy.44), calls=%async_computation.1 | async-start | bytes 6291456 | tf_op jit(solution)/shard_map/all_to_all | solution.py:1075
  239.6 3.9 copy-start.3
  239.6 4.8 copy-start.35
  333.6 6.2 %copy-start.14 = (bf16[768,128]{0,1:T(8,128)(2,1)}, bf16[768,128]{0,1:T(8,128)(2,1)S(1)}, u32[]{:S(2)}) copy-start(bf16[768,128]{0,1:T(8,128)(2,1)S(1)} %get-tuple-element.108) | copy-start | bytes 589828
  333.6 6.2 %copy-start.16 = (bf16[768,128]{0,1:T(8,128)(2,1)}, bf16[768,128]{0,1:T(8,128)(2,1)S(1)}, u32[]{:S(2)}) copy-start(bf16[768,128]{0,1:T(8,128)(2,1)S(1)} %get-tuple-element.109) | copy-start | bytes 589828
  334.7 1.1 copy-start.6
  334.8 1.4 copy-start.7
  334.8 1.5 copy-start.8
  336.3 1.3 copy-start.13
  337.5 1.2 copy-start.12
  338.8 1.2 copy-start.11
  340.0 1.9 copy-start.4
  352.7 4.8 copy-start
  357.5 2.2 copy-start.36
  357.5 2.2 copy-start.37
  357.5 5.2 %copy-start.2 = (bf16[2,2,4,64,512]{4,3,2,1,0:T(8,128)(2,1)S(1)}, bf16[2,2,4,64,512]{4,3,2,1,0:T(8,128)(2,1)}, u32[]{:S(2)}) copy-start(bf16[2,2,4,64,512]{4,3,2,1,0:T(8,128)(2,1)} %get-tuple-element.59) | copy-start | bytes 3145732
  357.5 5.3 %copy-start.18 = (bf16[768,128]{0,1:T(8,128)(2,1)S(1)}, bf16[768,128]{0,1:T(8,128)(2,1)}, u32[]{:S(2)}) copy-start(bf16[768,128]{0,1:T(8,128)(2,1)} %get-tuple-element.117) | copy-start | bytes 589828
  357.5 5.3 %copy-start.19 = (bf16[768,128]{0,1:T(8,128)(2,1)S(1)}, bf16[768,128]{0,1:T(8,128)(2,1)}, u32[]{:S(2)}) copy-start(bf16[768,128]{0,1:T(8,128)(2,1)} %get-tuple-element.118) | copy-start | bytes 589828
  359.6 21.4 %collective-permute-start.1 = (bf16[4,384,1024]{2,1,0:T(8,128)(2,1)}, bf16[4,384,1024]{2,1,0:T(8,128)(2,1)}, u32[]{:S(2)}, u32[]{:S(2)}) collective-permute-start(bf16[4,384,1024]{2,1,0:T(8,128)(2,1)} %dynamic-slice_convert_fusion), channel_id=1, source_target_pairs={{0,1},{1,0},{2,3},{3,2},{4,5},{5,4},{6,7},{7,6},{8,9},{9,8},{10,11... | collective-permute-start | bytes 9437192 | tf_op jit(solution)/shard_map/ppermute | solution.py:1113
  359.7 8.5 %copy-start.1 = (f32[4,768,1024]{2,1,0:T(8,128)S(1)}, f32[4,768,1024]{2,1,0:T(8,128)}, u32[]{:S(2)}) copy-start(f32[4,768,1024]{2,1,0:T(8,128)} %copy-done) | copy-start | bytes 37748740
  366.3 0.9 copy-start.15
  366.4 1.0 copy-start.17
  366.5 13.0 %collective-permute-start = (f32[384,1024]{1,0:T(8,128)S(1)}, f32[384,1024]{1,0:T(8,128)S(1)}, u32[]{:S(2)}, u32[]{:S(2)}) collective-permute-start(f32[384,1024]{1,0:T(8,128)S(1)} %constant_dynamic-slice_fusion.1), channel_id=1, source_target_pairs={{0,1},{1,0},{2,3},{3,2},{4,5},{5,4},{6,7},{7,6},{8,9},{9,8},{10,11... | collective-permute-start | bytes 4718600 | tf_op jit(solution)/shard_map/ppermute | solution.py:1101
  373.4 2.0 copy-start.9
  373.5 2.0 copy-start.20
  373.5 2.0 copy-start.21
  377.5 2.1 copy-start.10
  471.8 13.6 %copy-start.34 = (f32[1,1024]{1,0:T(1,128)S(1)}, f32[1,1024]{1,0:T(1,128)}, u32[]{:S(2)}) copy-start(f32[1,1024]{1,0:T(1,128)} %get-tuple-element.77) | copy-start | bytes 12292
  471.8 14.2 %copy-start.25 = (f32[36,1024]{1,0:T(8,128)S(1)}, f32[36,1024]{1,0:T(8,128)}, u32[]{:S(2)}) copy-start(f32[36,1024]{1,0:T(8,128)} %get-tuple-element.78) | copy-start | bytes 442372
  471.8 14.9 %copy-start.27 = (f32[36,36]{1,0:T(8,128)S(1)}, f32[36,36]{1,0:T(8,128)}, u32[]{:S(2)}) copy-start(f32[36,36]{1,0:T(8,128)} %get-tuple-element.196) | copy-start | bytes 15556
  471.8 15.5 %copy-start.38 = (f32[1,36]{1,0:T(1,128)S(1)}, f32[1,36]{1,0:T(1,128)}, u32[]{:S(2)}) copy-start(f32[1,36]{1,0:T(1,128)} %get-tuple-element.80) | copy-start | bytes 436
  471.8 16.0 %copy-start.30 = (f32[4,1024]{1,0:T(4,128)S(1)}, f32[4,1024]{1,0:T(4,128)}, u32[]{:S(2)}) copy-start(f32[4,1024]{1,0:T(4,128)} %get-tuple-element.198) | copy-start | bytes 49156
  471.8 16.6 %copy-start.29 = (f32[4,1024]{1,0:T(4,128)S(1)}, f32[4,1024]{1,0:T(4,128)}, u32[]{:S(2)}) copy-start(f32[4,1024]{1,0:T(4,128)} %get-tuple-element.199) | copy-start | bytes 49156
  471.8 17.2 %copy-start.24 = (f32[32,3072]{1,0:T(8,128)S(1)}, f32[32,3072]{1,0:T(8,128)}, u32[]{:S(2)}) copy-start(f32[32,3072]{1,0:T(8,128)} %get-tuple-element.200) | copy-start | bytes 1179652
  471.8 18.0 %copy-start.33 = (f32[1,3072]{1,0:T(1,128)S(1)}, f32[1,3072]{1,0:T(1,128)}, u32[]{:S(2)}) copy-start(f32[1,3072]{1,0:T(1,128)} %get-tuple-element.84) | copy-start | bytes 36868
  471.8 18.6 %copy-start.26 = (f32[32,1024]{1,0:T(8,128)S(1)}, f32[32,1024]{1,0:T(8,128)}, u32[]{:S(2)}) copy-start(f32[32,1024]{1,0:T(8,128)} %get-tuple-element.202) | copy-start | bytes 393220
  471.8 19.2 %copy-start.31 = (f32[1,1024]{1,0:T(1,128)S(1)}, f32[1,1024]{1,0:T(1,128)}, u32[]{:S(2)}) copy-start(f32[1,1024]{1,0:T(1,128)} %get-tuple-element.86) | copy-start | bytes 12292
  485.4 6.2 %copy-start.23 = (f32[32,4096]{1,0:T(8,128)S(1)}, f32[32,4096]{1,0:T(8,128)}, u32[]{:S(2)}) copy-start(f32[32,4096]{1,0:T(8,128)} %get-tuple-element.204) | copy-start | bytes 1572868
  485.4 7.0 %copy-start.28 = (f32[1,4096]{1,0:T(1,128)S(1)}, f32[1,4096]{1,0:T(1,128)}, u32[]{:S(2)}) copy-start(f32[1,4096]{1,0:T(1,128)} %get-tuple-element.88) | copy-start | bytes 49156
  485.4 7.6 %copy-start.22 = (f32[32,4096]{1,0:T(8,128)S(1)}, f32[32,4096]{1,0:T(8,128)}, u32[]{:S(2)}) copy-start(f32[32,4096]{1,0:T(8,128)} %get-tuple-element.206) | copy-start | bytes 1572868

commit v4 on v3

--- a/solution.py
+++ b/solution.py
@@ -42,20 +42,6 @@
 
 def gelu_slope(value):
     return phi(value) + value * jnp.exp(-0.5 * value * value) * (1.0 / math.sqrt(2.0 * math.pi))
-
-
-def rotary_tables(positions, width):
-    half = ROT_DIMS // 2
-    place = jnp.arange(width) % HEAD_DIM
-    freq = 10000.0 ** (-jnp.arange(half).astype(F32) * 2.0 / ROT_DIMS)
-    angles = positions.astype(F32)[:, None] * freq[None, :]
-    spread = lambda x: jnp.tile(x, (1, width // half))
-    turned = (place < ROT_DIMS)[None, :]
-    cosine = jnp.where(turned, spread(jnp.cos(angles)), 1.0)
-    sine = jnp.where(turned, spread(jnp.sin(angles)), 0.0)
-    above = jnp.where((place < half)[None, :], -sine, 0.0)
-    below = jnp.where((place < half)[None, :], 0.0, sine)
-    return cosine, above, below
 
 
 def rotate(value, tables, sign):
@@ -228,86 +214,6 @@
     return [r.reshape(-1, r.shape[-1]) for r in results]
 
 
-class Scattering:
-    def __init__(self, grid, place, chunks, parts, outs, scratch):
-        self.grid, self.place, self.chunks, self.parts, self.outs = grid, place, chunks, parts, outs
-        count = len(chunks)
-        folds = sum(1 for chunk in chunks if chunk[2])
-        self.own, scratch = scratch[:count], scratch[count:]
-        self.first, self.second, scratch = scratch[:folds], scratch[folds : 2 * folds], scratch[2 * folds :]
-        self.third, self.final = scratch[:count], scratch[count : 2 * count]
-        self.local_sem, self.send_sem, self.recv_sem = scratch[2 * count :]
-
-    def copies(self, t, stage):
-        a, b, z, c = self.place
-        grid = self.grid
-        nz = grid.nz
-        source, n, order, result, base = self.chunks[t]
-        part, third, final = self.parts[source], self.third[t], self.final[t]
-        sems = (self.send_sem.at[t], self.recv_sem.at[t])
-
-        def send(src, dst, slot, device):
-            return remote(src, dst, sems[0].at[slot], sems[1].at[slot], device)
-
-        if stage < 2:
-            found = fold_copies(grid, self.place, order, stage, part, self.first[t], self.second[t], sems)
-            if stage == 0:
-                kept = part.at[a] if order == "ab" else part.at[:, b]
-                found.append(pltpu.make_async_copy(kept, self.own[t], self.local_sem.at[t]))
-            return found
-        if stage == 2:
-            source = self.second[t].at[0] if order else part
-            found = [send(source.at[lax.rem(z + k, nz)], third.at[k - 1], k, grid.device(a, b, lax.rem(z + k, nz), c)) for k in range(1, nz)]
-            if not order:
-                found.append(pltpu.make_async_copy(part.at[z], self.own[t], self.local_sem.at[t]))
-            return found
-        spot = self.outs[result].at[:, pl.ds(pl.multiple_of(base(c), 128), n)]
-        return [
-            send(final.at[1 - c], spot, 0, grid.device(a, b, z, 1 - c)),
-            pltpu.make_async_copy(final.at[c], spot, self.local_sem.at[t]),
-        ]
-
-    def add(self, t, stage):
-        z = self.place[2]
-        order = self.chunks[t][2]
-        third, final = self.third[t], self.final[t]
-        if stage < 2:
-            fold_add(self.grid, self.place, order, stage, self.own[t], self.first[t], self.second[t])
-            return
-        total = (self.second[t][0, z] if order else self.own[t][...]).astype(F32)
-        for k in range(self.grid.nz - 1):
-            total = total + third[k].astype(F32)
-        final[...] = total.reshape(final.shape)
-
-    def end(self, group, stage):
-        for t in group:
-            finish(self.copies(t, stage))
-            if stage < 3:
-                self.add(t, stage)
-                start(self.copies(t, stage + 1))
-
-    def events(self, groups):
-        late = [t for t, chunk in enumerate(self.chunks) if not chunk[2]]
-
-        def first():
-            for group in groups:
-                for t in group:
-                    start(self.copies(t, 0))
-            for t in late:
-                start(self.copies(t, 2))
-
-        def turn(u):
-            for stage in range(4):
-                if 0 <= u - stage < len(groups):
-                    self.end(groups[u - stage], stage)
-
-        def last():
-            self.end(late, 2)
-            self.end(late, 3)
-
-        return [first] + [functools.partial(turn, u) for u in range(len(groups) + 3)] + [last]
-
-
 def fold_copies(grid, place, order, stage, part, first, second, sems):
     a, b, z, c = place
     nz, nb = grid.nz, grid.nb
@@ -363,14 +269,6 @@
     return own, first, second
 
 
-def scatter_scratch(grid, chunks, rows):
-    folds = [fold_scratch(grid, order, rows, n) for _, n, order, _, _ in chunks if order]
-    own = [fold_scratch(grid, order, rows, n)[0] if order else pltpu.VMEM((rows, n), BF16) for _, n, order, _, _ in chunks]
-    third = [pltpu.VMEM((grid.nz - 1, rows, n), BF16) for _, n, _, _, _ in chunks]
-    final = [pltpu.VMEM((2, rows // 2, n), F32) for _, n, _, _, _ in chunks]
-    return own + [f for _, f, _ in folds] + [s for _, _, s in folds] + third + final + gather_sems(grid, chunks)
-
-
 class Summing:
     def __init__(self, grid, mine, held, total, done, send_sem, recv_sem):
         self.n_seq, self.count = grid.n_seq, grid.n_dp * grid.n_seq
@@ -394,7 +292,6 @@
             return carry
 
         lax.fori_loop(1, self.count, step, 0)
-        pl.semaphore_wait(barrier, self.count - 1)
 
     def settle(self, dst, slot):
         most = pl.ds(0, (self.count - 1) * self.rows)
@@ -445,11 +342,13 @@
 
 
 def mix_kernel(grid, rows, chunks, whole, partial, h_ref, g_ref, gain_ref, inner_ref, outer_ref, bias_ref, sgain_ref, sbias_ref, *refs):
-    ins, (lowered_ref, gpair_ref, last_ref, pre_ref, coeffs_ref), outs = refs[:4], refs[4:9], refs[9:15]
+    ins, (lowered_ref, gpair_ref, last_ref, pre_ref, coeffs_ref, cos_ref, above_ref, below_ref) = refs[:4], refs[4:12]
+    weights_ref, outs = refs[12], refs[13:15]
     streams_ref, held_ref, local_sem, send_sem, recv_sem, pair_local, pair_send, pair_recv = refs[15:]
     i, steps = pl.program_id(0), pl.num_programs(0)
     a, b, z, c = place = grid.here()
     block = h_ref.shape[2]
+    outs = [weights_ref.at[k] for k in range(4)] + list(outs)
     events = Gathering(grid, place, rows, chunks, ins, outs, local_sem, send_sem, recv_sem).events(whole, partial)
     other = grid.device(a, b, z, 1 - c)
 
@@ -472,12 +371,28 @@
     def _():
         events[1]()
 
+    @pl.when(i == 2)
+    def _():
+        both, wide = cos_ref.shape
+        half = ROT_DIMS // 2
+        place_in = lax.rem(lax.broadcasted_iota(jnp.int32, (1, wide), 1), HEAD_DIM)
+        step = lax.rem(place_in, half)
+        freq = jnp.ones((1, wide), F32)
+        for k in range(1, half):
+            freq = jnp.where(step == k, 10000.0 ** (-2.0 * k / ROT_DIMS), freq)
+        angles = (z * both + lax.broadcasted_iota(jnp.int32, (both, wide), 0)).astype(F32) * freq
+        turned = place_in < ROT_DIMS
+        sine = jnp.where(turned, jnp.sin(angles), 0.0)
+        cos_ref[...] = jnp.where(turned, jnp.cos(angles), 1.0)
+        above_ref[...] = jnp.where(place_in < half, -sine, 0.0)
+        below_ref[...] = jnp.where(place_in < half, 0.0, sine)
+
     last = h_ref[h_ref.shape[0] - 1, 0].astype(F32)
     r = lax.rsqrt(jnp.mean(last * last, axis=1, keepdims=True) + EPS)
-    scaled_low = (last * r * gain_ref[...]).astype(BF16)
-    pre = product(scaled_low, inner_ref[...])
+    scaled_low = (last * r * gain_ref[...].astype(F32)).astype(BF16)
+    pre = against(scaled_low, inner_ref[...])
     pre_ref[...] = pre
-    coeffs = product((pre * phi(pre)).astype(BF16), outer_ref[...]) + bias_ref[...]
+    coeffs = product((pre * phi(pre)).astype(BF16), outer_ref[...]) + bias_ref[...].astype(F32)
     coeffs_ref[...] = coeffs
     blend(h_ref, coeffs, streams_ref)
     at = pl.ds(pl.multiple_of(i * block, block), block)
@@ -485,7 +400,8 @@
         stream = streams_ref[k]
         centered = stream - jnp.mean(stream, axis=1, keepdims=True)
         rs = lax.rsqrt(jnp.mean(centered * centered, axis=1, keepdims=True) + EPS)
-        held_ref[k, at, :] = (centered * rs * sgain_ref[k : k + 1, :] + sbias_ref[k : k + 1, :]).astype(BF16)
+        gain, bias = sgain_ref[k : k + 1, :].astype(F32), sbias_ref[k : k + 1, :].astype(F32)
+        held_ref[k, at, :] = (centered * rs * gain + bias).astype(BF16)
     last_ref[...] = streams_ref[3]
 
     @pl.when(i == steps - 1)
@@ -499,12 +415,13 @@
 
 def mix_forward(grid, history, cotangent, params, weights, chunks, groups, partial, widths, collective_id):
     hist, _, tokens, width = history.shape
-    mix = params[1].shape[1]
+    mix = params[1].shape[0]
     block = 32
     rows = weights[0].shape[0]
     whole = pl.BlockSpec(memory_space=pltpu.VMEM)
     anywhere = pl.BlockSpec(memory_space=pl.ANY)
     part = lambda n: pl.BlockSpec((block, n), lambda i: (i, 0))
+    chips = (grid.na, grid.nb, grid.nz, 2 * rows)
     results = pl.pallas_call(
         functools.partial(mix_kernel, grid, rows, chunks, groups, partial),
         grid=(tokens // block,),
@@ -515,9 +432,13 @@
             jax.ShapeDtypeStruct((tokens, mix), F32),
             jax.ShapeDtypeStruct((tokens, mix), F32),
         ]
-        + [jax.ShapeDtypeStruct((grid.na, grid.nb, grid.nz, 2 * rows, w), BF16) for w in widths],
+        + [jax.ShapeDtypeStruct((2 * tokens, 128), F32)] * 3
+        + [jax.ShapeDtypeStruct((4, *chips, width // 2), BF16)]
+        + [jax.ShapeDtypeStruct((*chips, w), BF16) for w in widths],
         in_specs=[pl.BlockSpec((hist, 1, block, width), lambda i: (0, 0, i, 0))] + [whole] * 11,
-        out_specs=[anywhere, anywhere, part(width), part(mix), part(mix)] + [anywhere] * len(widths),
+        out_specs=[anywhere, anywhere, part(width), part(mix), part(mix)]
+        + [pl.BlockSpec((2 * tokens, 128), lambda i: (0, 0))] * 3
+        + [anywhere] * 3,
         scratch_shapes=[
             pltpu.VMEM((4, block, width), F32),
             pltpu.VMEM((4, tokens, width), BF16),
@@ -537,7 +458,8 @@
         last,
         pre,
         coeffs,
-        [w.reshape(-1, w.shape[-1]) for w in results[5:9]],
+        results[5:8],
+        results[8].reshape(4, width, width // 2),
         results[9:],
     )
 
@@ -549,29 +471,17 @@
     return firsts, sum(sizes)
 
 
-def unmix_kernel(grid, chunks, groups, n_parts, n_outs, h_ref, own_ref, theirs_ref, g_ref, pre_ref, coeffs_ref, gain_ref, inner_ref, outer_ref,
-                 sgain_ref, hb_ref, eb_ref, *refs):
-    parts, refs = refs[:n_parts], refs[n_parts:]
-    hist_ref, small, outs, refs = refs[0], refs[1:10], refs[10 : 10 + n_outs], refs[10 + n_outs :]
-    streams_ref, sg_ref, scaled_ref, mpg_ref, hidden_ref, cgl_ref, sgg_ref, sbg_ref, gg_ref, bg_ref, ob_ref = refs[:11]
+def unmix_kernel(h_ref, own_ref, theirs_ref, g_ref, pre_ref, coeffs_ref, gain_ref, inner_ref, outer_ref, sgain_ref,
+                 hist_ref, sgg_ref, sbg_ref, gg_ref, ig_ref, og_ref, bg_ref, ob_ref,
+                 streams_ref, sg_ref, scaled_ref, mpg_ref, hidden_ref, cgl_ref):
     i, steps = pl.program_id(0), pl.num_programs(0)
     hist, block, width = h_ref.shape[0], h_ref.shape[2], h_ref.shape[3]
     mix = 4 * hist
-    place = grid.here()
-    c = place[3]
-    sums = Summing(grid, *refs[11:17])
-    events = Scattering(grid, place, chunks, parts, outs, refs[17:]).events(groups)
 
     @pl.when(i == 0)
     def _():
-        sums.greet()
-        events[0]()
         for ref in (sgg_ref, sbg_ref, gg_ref, bg_ref, ob_ref):
             ref[...] = jnp.zeros_like(ref)
-
-    @pl.when(i == 6)
-    def _():
-        events[1]()
 
     def down(x):
         return jnp.sum(x, axis=0, keepdims=True)
@@ -588,7 +498,7 @@
         ng = own_ref[k] + theirs_ref[k].astype(F32)
         sgg_ref[k : k + 1, :] += down(ng * n)
         sbg_ref[k : k + 1, :] += down(ng)
-        w = ng * sgain_ref[k : k + 1, :]
+        w = ng * sgain_ref[k : k + 1, :].astype(F32)
         pulled = rs * (w - jnp.mean(w, axis=1, keepdims=True) - n * jnp.mean(w * n, axis=1, keepdims=True))
         sg_ref[k] = pulled + grad if k == 3 else pulled
 
@@ -605,13 +515,14 @@
     mpg = (against(cg_low, outer_ref[...]) * gelu_slope(pre)).astype(BF16)
     last = h_ref[hist - 1, 0].astype(F32)
     r = lax.rsqrt(jnp.mean(last * last, axis=1, keepdims=True) + EPS)
-    scaled_ref[at, :] = (last * r * gain_ref[...]).astype(BF16)
+    gain = gain_ref[...].astype(F32)
+    scaled_ref[at, :] = (last * r * gain).astype(BF16)
     mpg_ref[at, :] = mpg
     hidden_ref[at, :] = (pre * phi(pre)).astype(BF16)
     cgl_ref[at, :] = cg_low
-    scaled_grad = against(mpg, inner_ref[...])
+    scaled_grad = product(mpg, inner_ref[...])
     gg_ref[...] += down(scaled_grad * last * r)
-    w = scaled_grad * gain_ref[...]
+    w = scaled_grad * gain
     last_grad = r * (w - last * (r * r) * jnp.mean(w * last, axis=1, keepdims=True))
     for from_ in range(0, width, 128):
         lanes = slice(from_, from_ + 128)
@@ -624,77 +535,25 @@
 
     @pl.when(i == steps - 1)
     def _():
-        mine, done = sums.mine, sums.done
-        wl = width // 128
-        padded = -(-mix // 8) * 8
-        hidden_rows = eb_ref.shape[1] // 128
-        firsts, _ = small_rows(width, mix, 2 * eb_ref.shape[1])
-        mine[...] = jnp.zeros_like(mine)
-        inner_grad = inner(mpg_ref[...], scaled_ref[...])
-        for l in range(wl):
-            lanes = slice(l * 128, (l + 1) * 128)
-            mine[firsts[0] + l : firsts[0] + l + 1, :] = gg_ref[:, lanes]
-            mine[firsts[1] + l * padded : firsts[1] + l * padded + mix, :] = inner_grad[:, lanes]
-            mine[firsts[4] + 4 * l : firsts[4] + 4 * l + 4, :] = sgg_ref[:, lanes]
-            mine[firsts[5] + 4 * l : firsts[5] + 4 * l + 4, :] = sbg_ref[:, lanes]
-            mine[firsts[7] + l : firsts[7] + l + 1, :] = ob_ref[:, lanes]
-        mine[firsts[2] : firsts[2] + mix, 0:mix] = inner(hidden_ref[...], cgl_ref[...])
-        mine[firsts[3] : firsts[3] + 1, 0:mix] = bg_ref[...]
-        for k in range(3):
-            for l in range(wl // 2):
-                mine[pl.ds(firsts[6] + k * wl + c * (wl // 2) + l, 1), :] = hb_ref[k : k + 1, l * 128 : (l + 1) * 128]
-        for l in range(hidden_rows):
-            mine[pl.ds(firsts[8] + c * hidden_rows + l, 1), :] = eb_ref[:, l * 128 : (l + 1) * 128]
-        sums.deal()
-        for n, event in enumerate(events[2:]):
-            event()
-            if n == 0:
-                sums.tell()
-            if n == 1:
-                sums.close()
-        for l in range(wl):
-            lanes = slice(l * 128, (l + 1) * 128)
-            small[0][:, lanes] = done[firsts[0] + l : firsts[0] + l + 1, :]
-            small[1][:, lanes] = done[firsts[1] + l * padded : firsts[1] + l * padded + mix, :]
-            small[4][:, lanes] = done[firsts[4] + 4 * l : firsts[4] + 4 * l + 4, :]
-            small[5][:, lanes] = done[firsts[5] + 4 * l : firsts[5] + 4 * l + 4, :]
-            small[7][:, lanes] = done[firsts[7] + l : firsts[7] + l + 1, :]
-        small[2][...] = done[firsts[2] : firsts[2] + mix, 0:mix]
-        small[3][...] = done[firsts[3] : firsts[3] + 1, 0:mix]
-        for l in range(3 * wl):
-            small[6][:, l * 128 : (l + 1) * 128] = done[firsts[6] + l : firsts[6] + l + 1, :]
-        for l in range(2 * hidden_rows):
-            small[8][:, l * 128 : (l + 1) * 128] = done[firsts[8] + l : firsts[8] + l + 1, :]
-
-
-def mix_backward(grid, history, own, theirs, cotangent, pre, coeffs, params, biases, parts, folded, chunks, groups, widths, collective_id):
+        ig_ref[...] = inner(mpg_ref[...], scaled_ref[...])
+        og_ref[...] = inner(hidden_ref[...], cgl_ref[...])
+
+
+def mix_backward(history, own, theirs, cotangent, pre, coeffs, params):
     hist, _, tokens, width = history.shape
     mix = pre.shape[1]
-    hidden_width = 2 * biases[1].shape[1]
-    na, nb, nz = grid.na, grid.nb, grid.nz
-    rows = parts[0].shape[0] // (na * nb * nz)
-    parts = [p.reshape(na, nb, nz, rows, p.shape[1]) for p in parts] + list(folded)
-    devices = grid.n_dp * grid.n_seq
-    small_each = -(-small_rows(width, mix, hidden_width)[1] // (devices * 8)) * 8
     block = 32
     whole = pl.BlockSpec(memory_space=pltpu.VMEM)
-    anywhere = pl.BlockSpec(memory_space=pl.ANY)
     part = lambda n: pl.BlockSpec((block, n), lambda i: (i, 0))
     four = pl.BlockSpec((4, block, width), lambda i: (0, i, 0))
     story = pl.BlockSpec((hist, 1, block, width), lambda i: (0, 0, i, 0))
-    small = [(1, width), (mix, width), (mix, mix), (1, mix), (4, width), (4, width), (1, 3 * width), (1, width), (1, hidden_width)]
-    fixed = [pl.BlockSpec(shape, lambda i: (0, 0)) for shape in small]
-    moved = sum(p.size for p in parts) * 2
-    results = pl.pallas_call(
-        functools.partial(unmix_kernel, grid, chunks, groups, len(parts), len(widths)),
+    small = [(4, width), (4, width), (1, width), (mix, width), (mix, mix), (1, mix), (1, width)]
+    return pl.pallas_call(
+        unmix_kernel,
         grid=(tokens // block,),
-        out_shape=[jax.ShapeDtypeStruct(history.shape, F32)]
-        + [jax.ShapeDtypeStruct(shape, F32) for shape in small]
-        + [jax.ShapeDtypeStruct((rows // 2, w), F32) for w in widths],
-        in_specs=[story, four, four, pl.BlockSpec((1, block, width), lambda i: (0, i, 0)), part(mix), part(mix)]
-        + [whole] * 6
-        + [anywhere] * len(parts),
-        out_specs=[story] + fixed + [anywhere] * len(widths),
+        out_shape=[jax.ShapeDtypeStruct(history.shape, F32)] + [jax.ShapeDtypeStruct(shape, F32) for shape in small],
+        in_specs=[story, four, four, pl.BlockSpec((1, block, width), lambda i: (0, i, 0)), part(mix), part(mix)] + [whole] * 4,
+        out_specs=[story] + [pl.BlockSpec(shape, lambda i: (0, 0)) for shape in small],
         scratch_shapes=[
             pltpu.VMEM((4, block, width), F32),
             pltpu.VMEM((4, block, width), F32),
@@ -702,34 +561,189 @@
             pltpu.VMEM((tokens, mix), BF16),
             pltpu.VMEM((tokens, mix), BF16),
             pltpu.VMEM((tokens, mix), BF16),
-            pltpu.VMEM((4, width), F32),
-            pltpu.VMEM((4, width), F32),
-            pltpu.VMEM((1, width), F32),
-            pltpu.VMEM((1, mix), F32),
-            pltpu.VMEM((1, width), F32),
-            pltpu.VMEM((devices * small_each, 128), F32),
-            pltpu.VMEM((devices * small_each, 128), F32),
-            pltpu.VMEM((small_each, 128), F32),
-            pltpu.VMEM((devices * small_each, 128), F32),
+        ],
+        compiler_params=pltpu.CompilerParams(vmem_limit_bytes=VMEM_LIMIT),
+        cost_estimate=pl.CostEstimate(flops=tokens * width * 1000, bytes_accessed=history.size * 12, transcendentals=0),
+        name="mix_backward",
+    )(history, own, theirs, cotangent, pre, coeffs, *params)
+
+
+def finish_kernel(grid, orders, n_kept, *refs):
+    nz = grid.nz
+    kept, refs = refs[:n_kept], refs[n_kept:]
+    came_a, came_b, refs = refs[:1], refs[1 : grid.nb], refs[grid.nb :]
+    folded, refs = refs[:nz], refs[nz:]
+    sgg_ref, sbg_ref, gg_ref, ig_ref, og_ref, bg_ref, ob_ref, hb_ref, eb_ref = refs[:9]
+    done_ref, outs, refs = refs[9], refs[10:14], refs[14:]
+    first, second, third, final, refs = refs[:4], refs[4:8], refs[8:12], refs[12:18], refs[18:]
+    sums = Summing(grid, *refs[:3], done_ref, *refs[3:5])
+    local_sem, send_sem, recv_sem = refs[5:]
+    a, b, z, c = place = grid.here()
+    width, mix = gg_ref.shape[1], bg_ref.shape[1]
+    wl, padded, hidden_rows = width // 128, -(-mix // 8) * 8, eb_ref.shape[1] // 128
+    firsts, _ = small_rows(width, mix, 2 * eb_ref.shape[1])
+    half = width // 2
+    spots = [(0, lambda core: core * half), (0, lambda core: width + core * half), (0, lambda core: 2 * width + core * half),
+             (1, lambda core: core * half), (2, lambda core: core * eb_ref.shape[1]), (3, lambda core: core * eb_ref.shape[1])]
+
+    def copies(t, stage):
+        if stage == 1:
+            return fold_copies(grid, place, orders[t], 1, None, first[t], second[t], (send_sem.at[t], recv_sem.at[t]))
+        if stage == 2:
+            return [
+                remote(second[t].at[0, lax.rem(z + k, nz)], third[t].at[k - 1], send_sem.at[t, k], recv_sem.at[t, k],
+                       grid.device(a, b, lax.rem(z + k, nz), c))
+                for k in range(1, nz)
+            ]
+        result, base = spots[t]
+        n = final[t].shape[-1]
+        spot = outs[result].at[:, pl.ds(pl.multiple_of(base(c), 128), n)]
+        return [
+            remote(final[t].at[1 - c], spot, send_sem.at[t, 0], recv_sem.at[t, 0], grid.device(a, b, z, 1 - c)),
+            pltpu.make_async_copy(final[t].at[c], spot, local_sem.at[t]),
+        ]
+
+    sums.greet()
+    for t in range(4):
+
+        def step(i, carry, t=t):
+            o, j = i // nz, lax.rem(i, nz)
+            total = kept[t][o, j].astype(F32)
+            for piece in came_a if orders[t] == "ab" else came_b:
+                total = total + piece[t // 2, o, j].astype(F32)
+            first[t][0, o, j] = total.astype(BF16)
+            return carry
+
+        lax.fori_loop(0, first[t].shape[1] * nz, step, 0)
+    pl.semaphore_wait(pltpu.get_barrier_semaphore(), sums.count - 1)
+    for t in range(4):
+        start(copies(t, 1))
+
+    mine = sums.mine
+    mine[...] = jnp.zeros_like(mine)
+    for l in range(wl):
+        lanes = slice(l * 128, (l + 1) * 128)
+        mine[firsts[0] + l : firsts[0] + l + 1, :] = gg_ref[:, lanes]
+        mine[firsts[1] + l * padded : firsts[1] + l * padded + mix, :] = ig_ref[:, lanes]
+        mine[firsts[4] + 4 * l : firsts[4] + 4 * l + 4, :] = sgg_ref[:, lanes]
+        mine[firsts[5] + 4 * l : firsts[5] + 4 * l + 4, :] = sbg_ref[:, lanes]
+        mine[firsts[7] + l : firsts[7] + l + 1, :] = ob_ref[:, lanes]
+    mine[firsts[2] : firsts[2] + mix, 0:mix] = og_ref[...]
+    mine[firsts[3] : firsts[3] + 1, 0:mix] = bg_ref[...]
+    for k in range(3):
+        for l in range(wl // 2):
+            mine[pl.ds(firsts[6] + k * wl + c * (wl // 2) + l, 1), :] = hb_ref[k : k + 1, l * 128 : (l + 1) * 128]
+    for l in range(hidden_rows):
+        mine[pl.ds(firsts[8] + c * hidden_rows + l, 1), :] = eb_ref[:, l * 128 : (l + 1) * 128]
+    sums.deal()
+
+    for t in range(2):
+        total = folded[0][t].astype(F32)
+        for piece in folded[1:]:
+            total = total + piece[t].astype(F32)
+        final[4 + t][...] = total.reshape(final[4 + t].shape)
+        start(copies(4 + t, 3))
+    for t in range(4):
+        finish(copies(t, 1))
+        fold_add(grid, place, orders[t], 1, None, first[t], second[t])
+        start(copies(t, 2))
+    sums.tell()
+    for t in range(4):
+        finish(copies(t, 2))
+        total = second[t][0, z].astype(F32)
+        for k in range(nz - 1):
+            total = total + third[t][k].astype(F32)
+        final[t][...] = total.reshape(final[t].shape)
+        start(copies(t, 3))
+    sums.close()
+    for t in range(6):
+        finish(copies(t, 3))
+
+
+def finish_sums(grid, orders, kept, came, folded, smalls, collective_id):
+    sgg, _, _, ig, og, bg, _, hb, eb = smalls
+    mix, width = ig.shape
+    hidden_width = 2 * eb.shape[1]
+    nz = grid.nz
+    rows, n = kept[0].shape[-2:]
+    devices = grid.n_dp * grid.n_seq
+    each = -(-small_rows(width, mix, hidden_width)[1] // (devices * 8)) * 8
+    vmem = pl.BlockSpec(memory_space=pltpu.VMEM)
+    owned = [3 * width, width, hidden_width, hidden_width]
+    folds = [fold_scratch(grid, order, rows, n) for order in orders]
+    operands = list(kept) + list(came) + list(folded) + list(smalls)
+    return pl.pallas_call(
+        functools.partial(finish_kernel, grid, orders, len(kept)),
+        out_shape=[jax.ShapeDtypeStruct((devices * each, 128), F32)] + [jax.ShapeDtypeStruct((rows // 2, w), F32) for w in owned],
+        in_specs=[vmem] * len(operands),
+        out_specs=[vmem] + [pl.BlockSpec(memory_space=pl.ANY)] * len(owned),
+        scratch_shapes=[f for _, f, _ in folds]
+        + [s for _, _, s in folds]
+        + [pltpu.VMEM((nz - 1, rows, n), BF16)] * 4
+        + [pltpu.VMEM((2, rows // 2, n), F32)] * 4
+        + [pltpu.VMEM((2, rows // 2, hidden_width // 2), F32)] * 2
+        + [
+            pltpu.VMEM((devices * each, 128), F32),
+            pltpu.VMEM((devices * each, 128), F32),
+            pltpu.VMEM((each, 128), F32),
             pltpu.SemaphoreType.DMA((2,)),
             pltpu.SemaphoreType.DMA((2,)),
-            *scatter_scratch(grid, chunks, rows),
+            pltpu.SemaphoreType.DMA((6,)),
+            pltpu.SemaphoreType.DMA((6, nz + grid.nb)),
+            pltpu.SemaphoreType.DMA((6, nz + grid.nb)),
         ],
         compiler_params=pltpu.CompilerParams(collective_id=collective_id, has_side_effects=True, vmem_limit_bytes=VMEM_LIMIT),
-        cost_estimate=pl.CostEstimate(flops=tokens * width * 300, bytes_accessed=moved * 20, transcendentals=0),
-        name="mix_backward",
-    )(history, own, theirs, cotangent, pre, coeffs, *params, *biases, *parts)
-    return results[0], results[10:], results[1:10]
-
-
-def project_kernel(width, low_ref, g_ref, wq_ref, wk_ref, wv_ref, wo_ref, bias_ref, cos_ref, above_ref, below_ref, sent_ref):
-    wide = wq_ref.shape[1]
-    reps = wide // cos_ref.shape[1] if wide >= cos_ref.shape[1] else 1
-    tables = [jnp.concatenate([t[:, :wide]] * reps, axis=1) for t in (cos_ref, above_ref, below_ref)]
-    q = rotate(product(low_ref[0], wq_ref[...]) + bias_ref[0:1, :], tables, 1.0)
-    k = rotate(product(low_ref[1], wk_ref[...]) + bias_ref[1:2, :], tables, 1.0)
-    v = product(low_ref[2], wv_ref[...]) + bias_ref[2:3, :]
-    g = product(g_ref[...], wo_ref[...])
+        cost_estimate=pl.CostEstimate(flops=0, bytes_accessed=100 * width * width, transcendentals=0),
+        name="finish_sums",
+    )(*operands)
+
+
+def hand_kernel(mix, hidden_width, done, out_ref, *refs):
+    owned, placed_ref, small, outs = refs[:4], refs[4], refs[5:14], refs[14:]
+    width = out_ref.shape[1]
+    wl, padded, hidden_rows = width // 128, -(-mix // 8) * 8, hidden_width // 256
+    firsts, _ = small_rows(width, mix, hidden_width)
+    placed_ref[...] = out_ref[...]
+    for src, dst in zip(owned, outs):
+        dst[...] = src[...]
+    for l in range(wl):
+        lanes = slice(l * 128, (l + 1) * 128)
+        small[0][:, lanes] = done[firsts[0] + l : firsts[0] + l + 1, :]
+        small[1][:, lanes] = done[firsts[1] + l * padded : firsts[1] + l * padded + mix, :]
+        small[4][:, lanes] = done[firsts[4] + 4 * l : firsts[4] + 4 * l + 4, :]
+        small[5][:, lanes] = done[firsts[5] + 4 * l : firsts[5] + 4 * l + 4, :]
+        small[7][:, lanes] = done[firsts[7] + l : firsts[7] + l + 1, :]
+    small[2][...] = done[firsts[2] : firsts[2] + mix, 0:mix]
+    small[3][...] = done[firsts[3] : firsts[3] + 1, 0:mix]
+    for l in range(3 * wl):
+        small[6][:, l * 128 : (l + 1) * 128] = done[firsts[6] + l : firsts[6] + l + 1, :]
+    for l in range(2 * hidden_rows):
+        small[8][:, l * 128 : (l + 1) * 128] = done[firsts[8] + l : firsts[8] + l + 1, :]
+
+
+def hand_over(summed, layer_out, owned, mix, hidden_width):
+    width = layer_out.shape[1]
+    small = [(1, width), (mix, width), (mix, mix), (1, mix), (4, width), (4, width), (1, 3 * width), (1, width), (1, hidden_width)]
+    vmem = pl.BlockSpec(memory_space=pltpu.VMEM)
+    return pl.pallas_call(
+        functools.partial(hand_kernel, mix, hidden_width),
+        out_shape=[jax.ShapeDtypeStruct(layer_out.shape, BF16)]
+        + [jax.ShapeDtypeStruct(shape, F32) for shape in small]
+        + [jax.ShapeDtypeStruct(x.shape, F32) for x in owned],
+        in_specs=[vmem] * 6,
+        out_specs=[vmem] * 14,
+        name="hand_over",
+    )(summed, layer_out, *owned)
+
+
+def project_kernel(width, low_ref, g_ref, w_ref, bias_ref, cos_ref, above_ref, below_ref, sent_ref):
+    wide = w_ref.shape[2]
+    reps = max(wide // 128, 1)
+    tables = [jnp.concatenate([t[...]] * reps, axis=1) for t in (cos_ref, above_ref, below_ref)]
+    q = rotate(product(low_ref[0], w_ref[0]) + bias_ref[0:1, :], tables, 1.0)
+    k = rotate(product(low_ref[1], w_ref[1]) + bias_ref[1:2, :], tables, 1.0)
+    v = product(low_ref[2], w_ref[2]) + bias_ref[2:3, :]
+    g = product(g_ref[...], w_ref[3])
     for n, x in enumerate((q, k, v, g)):
         x = x.astype(BF16)
         for m in range(wide // width):
@@ -741,33 +755,161 @@
     nz = grid.nz
     wide = 2 * own_width
     whole = pl.BlockSpec(memory_space=pltpu.VMEM)
-    cols = lambda n: pl.BlockSpec((n, wide), lambda i: (0, i))
     return pl.pallas_call(
         functools.partial(project_kernel, own_width),
         grid=(nz // 2,),
         out_shape=jax.ShapeDtypeStruct((nz, both, 4 * own_width), BF16),
-        in_specs=[whole, whole] + [cols(weights[0].shape[0])] * 4 + [cols(3)] + [whole] * 3,
+        in_specs=[whole, whole]
+        + [pl.BlockSpec((4, weights.shape[1], wide), lambda i: (0, 0, i)), pl.BlockSpec((3, wide), lambda i: (0, i))]
+        + [whole] * 3,
         out_specs=pl.BlockSpec((2, both, 4 * own_width), lambda i: (i, 0, 0)),
         compiler_params=pltpu.CompilerParams(vmem_limit_bytes=VMEM_LIMIT),
-        cost_estimate=pl.CostEstimate(flops=8 * both * weights[0].size, bytes_accessed=lowered.size * 4, transcendentals=0),
+        cost_estimate=pl.CostEstimate(flops=2 * both * weights.size, bytes_accessed=lowered.size * 4, transcendentals=0),
         name="project",
-    )(lowered, grad_low, *weights, biases, *tables)
-
-
-def feed_kernel(grid, steps, low_ref, g_ref, we_ref, wc_ref, bias_ref, feed_ref, normed_ref, eb_ref, e2_ref, c2_ref, *refs):
+    )(lowered, grad_low, weights, biases, *tables)
+
+
+def unproject_kernel(grid, width, orders, col_ref, low_ref, g_ref, w_ref, feed_ref, normed_ref, last_ref, bias_ref, cos_ref, above_ref,
+                     below_ref, own_ref, theirs_ref, hb_ref, out_ref, *refs):
+    na, nb, nz = grid.na, grid.nb, grid.nz
+    kept, over_a, over_b, refs = refs[:4], refs[4], refs[5 : 4 + nb], refs[4 + nb :]
+    grad_ref, sending_ref, partial_ref, mine_ref, arrived_ref, split_sem, send_sem, recv_sem = refs
+    i = pl.program_id(0)
+    a, b, z, c = grid.here()
+    tokens = out_ref.shape[0]
+    other = grid.device(a, b, z, 1 - c)
+    own_rows = pl.ds(pl.multiple_of(c * tokens, tokens), tokens)
+    their_rows = pl.ds(pl.multiple_of((1 - c) * tokens, tokens), tokens)
+
+    def swap(k):
+        return [remote(sending_ref.at[k], theirs_ref.at[k], send_sem.at[k], recv_sem.at[k], other)]
+
+    def swap_out():
+        return [remote(partial_ref, arrived_ref, send_sem.at[4], recv_sem.at[4], other)]
+
+    def split(k):
+        grad = grad_ref.at[k]
+        if orders[k] == "ab":
+            found = [(grad.at[a], kept[k]), (grad.at[1 - a], over_a.at[k // 2])]
+        else:
+            found = [(grad.at[:, b], kept[k])]
+            found += [(grad.at[:, lax.rem(b + m, nb)], over_b[m - 1].at[k // 2]) for m in range(1, nb)]
+        return [pltpu.make_async_copy(src, dst, split_sem.at[k, n]) for n, (src, dst) in enumerate(found)]
+
+    def piece(n):
+        return jnp.concatenate([col_ref[m, :, n * width : (n + 1) * width] for m in range(nz)], axis=1)
+
+    def keep(k, grad):
+        grad_ref[k] = grad.astype(BF16).reshape(grad_ref.shape[1:])
+        start(split(k))
+
+    @pl.when(i == 0)
+    def _():
+        barrier = pltpu.get_barrier_semaphore()
+        pl.semaphore_signal(barrier, inc=1, device_id=other, device_id_type=MESH)
+        mine_ref[...] = piece(0)
+        partial_ref[...] = against(mine_ref[their_rows, :], w_ref[0]) + feed_ref[their_rows, :]
+        sending_ref[3] = normed_ref[their_rows, :].astype(BF16)
+        pl.semaphore_wait(barrier, 1)
+        start(swap_out())
+        start(swap(3))
+        own_ref[0] = normed_ref[own_rows, :]
+        out = against(mine_ref[own_rows, :], w_ref[0]) + feed_ref[own_rows, :] + last_ref[...] + bias_ref[...]
+        keep(3, inner(g_ref[...], mine_ref[...]))
+        finish(swap_out())
+        out_ref[...] = (out + arrived_ref[...]).astype(BF16)
+
+    for k in range(3):
+
+        @pl.when(i == k + 1)
+        def _(k=k):
+            grad = piece(k + 1).astype(F32)
+            if k < 2:
+                tables = [jnp.concatenate([t[...]] * (grad.shape[1] // 128), axis=1) for t in (cos_ref, above_ref, below_ref)]
+                grad = rotate(grad, tables, -1.0)
+            hb_ref[k : k + 1, :] = jnp.sum(grad, axis=0, keepdims=True)
+            mine_ref[...] = grad.astype(BF16)
+            sending_ref[k] = against(mine_ref[their_rows, :], w_ref[0]).astype(BF16)
+            start(swap(k))
+            own_ref[0] = against(mine_ref[own_rows, :], w_ref[0])
+            keep(k, inner(low_ref[0], mine_ref[...]))
+            if k == 2:
+                for n in range(4):
+                    finish(swap(n))
+                    finish(split(n))
+
+
+def unproject(grid, orders, collected, lowered, grad_low, weights, feed_part, normed_feed, last_stream, bias, tables, own_width, collective_id):
+    tokens, width = last_stream.shape
+    both, half = 2 * tokens, width // 2
+    na, nb, nz = grid.na, grid.nb, grid.nz
+    rows = width // (na * nb * nz)
+    whole = pl.BlockSpec(memory_space=pltpu.VMEM)
+    anywhere = pl.BlockSpec(memory_space=pl.ANY)
+    turn = lambda i: lax.rem(i + 3, 4)
+    split_shapes = [jax.ShapeDtypeStruct((nb if order == "ab" else na, nz, rows, half), BF16) for order in orders]
+    sent_shapes = [jax.ShapeDtypeStruct((2, nb, nz, rows, half), BF16)] + [jax.ShapeDtypeStruct((2, na, nz, rows, half), BF16)] * (nb - 1)
+    results = pl.pallas_call(
+        functools.partial(unproject_kernel, grid, own_width, orders),
+        grid=(4,),
+        out_shape=[
+            jax.ShapeDtypeStruct((4, tokens, width), F32),
+            jax.ShapeDtypeStruct((4, tokens, width), BF16),
+            jax.ShapeDtypeStruct((3, half), F32),
+            jax.ShapeDtypeStruct((tokens, width), BF16),
+        ]
+        + split_shapes
+        + sent_shapes,
+        in_specs=[
+            whole,
+            pl.BlockSpec((1, both, width), lambda i: (jnp.maximum(i - 1, 0), 0, 0)),
+            whole,
+            pl.BlockSpec((1, width, half), lambda i: (turn(i), 0, 0)),
+        ]
+        + [whole] * 7,
+        out_specs=[
+            pl.BlockSpec((1, tokens, width), lambda i: (turn(i), 0, 0)),
+            anywhere,
+            pl.BlockSpec((3, half), lambda i: (0, 0)),
+            pl.BlockSpec((tokens, width), lambda i: (0, 0)),
+        ]
+        + [anywhere] * (len(split_shapes) + len(sent_shapes)),
+        scratch_shapes=[
+            pltpu.VMEM((4, na, nb, nz, rows, half), BF16),
+            pltpu.VMEM((4, tokens, width), BF16),
+            pltpu.VMEM((tokens, width), F32),
+            pltpu.VMEM((both, half), BF16),
+            pltpu.VMEM((tokens, width), F32),
+            pltpu.SemaphoreType.DMA((4, nb + 1)),
+            pltpu.SemaphoreType.DMA((5,)),
+            pltpu.SemaphoreType.DMA((5,)),
+        ],
+        compiler_params=pltpu.CompilerParams(collective_id=collective_id, has_side_effects=True, vmem_limit_bytes=VMEM_LIMIT),
+        cost_estimate=pl.CostEstimate(flops=32 * both * width * half, bytes_accessed=40 * both * width, transcendentals=0),
+        name="unproject",
+    )(collected, lowered, grad_low, weights, feed_part, normed_feed, last_stream, bias, *tables)
+    own, theirs, head_bias, layer_out = results[:4]
+    return own, theirs, head_bias, layer_out, results[4:8], results[8:]
+
+
+def feed_kernel(grid, steps, low_ref, g_ref, we_ref, wc_ref, bias_ref, feed_ref, normed_ref, eb_ref, *refs):
+    nz = grid.nz
+    outs, refs = refs[:nz], refs[nz:]
     parts, refs = refs[: 2 * steps], refs[2 * steps :]
     first, second, refs = refs[: 2 * steps], refs[2 * steps : 4 * steps], refs[4 * steps :]
     send_sem, recv_sem, out_sem = refs
     i = pl.program_id(0)
     a, b, z, c = place = grid.here()
     orders = ["ab", "ba"] * steps
-    outs = (e2_ref, c2_ref)
 
     def copies(t, stage):
         if stage < 2:
             return fold_copies(grid, place, orders[t], stage, parts[t], first[t], second[t], (send_sem.at[t], recv_sem.at[t]))
         n = parts[t].shape[-1]
-        return [pltpu.make_async_copy(second[t].at[0], outs[t % 2].at[:, :, pl.ds((t // 2) * n, n)], out_sem.at[t])]
+        cols = pl.ds((t // 2) * n, n)
+        return [
+            pltpu.make_async_copy(second[t].at[0, lax.rem(z + k, nz)], outs[k].at[t % 2, :, cols], out_sem.at[t, k]) for k in range(nz)
+        ]
 
     def begin(u):
         for t in (2 * u, 2 * u + 1):
@@ -838,9 +980,8 @@
             jax.ShapeDtypeStruct((both, width), F32),
             jax.ShapeDtypeStruct((both, width), F32),
             jax.ShapeDtypeStruct((1, n * steps), F32),
-            jax.ShapeDtypeStruct((nz, rows, n * steps), BF16),
-            jax.ShapeDtypeStruct((nz, rows, n * steps), BF16),
-        ],
+        ]
+        + [jax.ShapeDtypeStruct((2, rows, n * steps), BF16)] * nz,
         in_specs=[
             pl.BlockSpec((1, both, width), lambda i: (3, 0, 0)),
             whole(both, width),
@@ -852,20 +993,19 @@
             whole(both, width),
             whole(both, width),
             cols(1),
-            pl.BlockSpec(memory_space=pl.ANY),
-            pl.BlockSpec(memory_space=pl.ANY),
-        ],
+        ]
+        + [pl.BlockSpec(memory_space=pl.ANY)] * nz,
         scratch_shapes=[pltpu.VMEM((na, nb, nz, rows, n), BF16)] * (2 * steps)
         + [f for _, f, _ in folds]
         + [s for _, _, s in folds]
-        + [sem, sem, pltpu.SemaphoreType.DMA((2 * steps,))],
+        + [sem, sem, pltpu.SemaphoreType.DMA((2 * steps, nz))],
         compiler_params=pltpu.CompilerParams(collective_id=collective_id, has_side_effects=True, vmem_limit_bytes=VMEM_LIMIT),
         cost_estimate=pl.CostEstimate(flops=12 * both * width * n * steps * 2, bytes_accessed=width * n * steps * 20, transcendentals=0),
         name="feed_forward",
     )(lowered, grad_low, weight_e, weight_c, bias)
 
 
-def attention_kernel(width, heads, tile, step, edge, length, x_ref, kdoc_ref, qdoc_ref, out_ref,
+def attention_kernel(width, heads, tile, step, edge, length, x_ref, qdoc_ref, out_ref, kdoc_ref,
                      s_ref, kt_ref, vt_ref, ot_ref, dqt_ref, dka_ref, dva_ref, top_ref):
     i = pl.program_id(0)
     tiles = length // tile
@@ -877,6 +1017,7 @@
         def turn(j, carry):
             at = pl.ds(pl.multiple_of(j * tile, tile), tile)
             kt_ref[:, at] = x_ref[at, width : 2 * width].T
+            kdoc_ref[at, :] = jnp.broadcast_to(qdoc_ref[:, at], (128, tile)).T
             vt_ref[:, at] = x_ref[at, 2 * width : 3 * width].T
             return carry
         lax.fori_loop(0, tiles, turn, 0)
@@ -975,22 +1116,21 @@
     width = heads * HEAD_DIM
     tile = step = 2 * edge
     pairs = length * length // 2 * heads
-    kdoc = jnp.broadcast_to(documents[:, None], (length, 128)); qdoc = documents[None, :]
     whole = lambda i: (0, 0)
     return pl.pallas_call(
         functools.partial(attention_kernel, width, heads, tile, step, edge, length),
         grid=(length // tile,),
         out_shape=jax.ShapeDtypeStruct((length, 4 * width), BF16),
-        in_specs=[pl.BlockSpec((length, 4 * width), whole), pl.BlockSpec((length, 128), whole), pl.BlockSpec((1, length), whole)],
+        in_specs=[pl.BlockSpec((length, 4 * width), whole), pl.BlockSpec((1, length), whole)],
         out_specs=pl.BlockSpec((length, 4 * width), whole),
         scratch_shapes=[
-            pltpu.VMEM((heads, length, tile), F32), pltpu.VMEM((width, length), BF16), pltpu.VMEM((width, length), BF16),
+            pltpu.VMEM((length, 128), F32), pltpu.VMEM((heads, length, tile), F32), pltpu.VMEM((width, length), BF16), pltpu.VMEM((width, length), BF16),
             pltpu.VMEM((width, tile), F32), pltpu.VMEM((width, tile), F32), pltpu.VMEM((length, width), F32), pltpu.VMEM((length, width), F32),
             pltpu.VMEM((heads, 8, tile), F32)],
         compiler_params=pltpu.CompilerParams(vmem_limit_bytes=VMEM_LIMIT),
         cost_estimate=pl.CostEstimate(flops=pairs * 64 * 2 * 6 * 4, bytes_accessed=length * width * 20, transcendentals=pairs),
         name="attention",
-    )(dealt, kdoc, qdoc)
+    )(dealt, documents)
 
 
 def on_device(
@@ -1013,12 +1153,13 @@
     contract,
     contract_bias,
 ):
-    n_seq, nz = grid.n_seq, grid.nz
+    n_dp, n_seq, nz = grid.n_dp, grid.n_seq, grid.nz
     tokens, width = history.shape[2], history.shape[3]
     hidden_width = expand.shape[1]
     half, hidden_half = width // 2, hidden_width // 2
     both = 2 * tokens
     length = documents.shape[1]
+    mix = mixer_bias.shape[0]
     heads = HEADS // n_seq
     own_width = heads * HEAD_DIM
     seq = lax.axis_index("seq")
@@ -1027,8 +1168,6 @@
     def take(array, start, size, axis=0):
         return lax.dynamic_slice_in_dim(array, start, size, axis)
 
-    gain = mixer_gain.astype(F32)[None]
-    stream_gain_full = stream_gain.astype(F32)
     pick = lambda base, n: (lambda core: base + core * n)
     parts = 4
     piece = hidden_half // parts
@@ -1037,112 +1176,69 @@
         base = lambda core, part=part: core * hidden_half + part * piece
         feed.append((2, base, 4, part * piece, piece, "ba"))
         feed.append((3, base, 5, part * piece, piece, "ab"))
-    lowered, grad_low, last_stream, mix_pre, coeffs, (weight_k, weight_v, weight_q, weight_o), started = mix_forward(
+    pairs = [[2 * part, 2 * part + 1] for part in range(parts)]
+    inner_t = mixer_inner.T
+    lowered, grad_low, last_stream, mix_pre, coeffs, tables, weights, started = mix_forward(
         grid,
         history,
         cotangent,
-        [gain, mixer_inner, mixer_outer, mixer_bias.astype(F32)[None], stream_gain_full, stream_bias.astype(F32)],
+        [mixer_gain[None], inner_t, mixer_outer, mixer_bias[None], stream_gain, stream_bias],
         [inbound_weight, outbound_weight, expand, contract],
         [
-            (0, pick(width, half), 0, 0, half, "ba"),
-            (0, pick(2 * width, half), 1, 0, half, "ab"),
-            (0, pick(0, half), 2, 0, half, "ba"),
+            (0, pick(width, half), 1, 0, half, "ba"),
+            (0, pick(2 * width, half), 2, 0, half, "ab"),
+            (0, pick(0, half), 0, 0, half, "ba"),
             (1, pick(0, half), 3, 0, half, "ab"),
         ]
         + feed,
         [[0, 1], [2, 3]],
-        [[4 + 2 * part, 5 + 2 * part] for part in range(parts)],
-        [half] * 4 + [hidden_half] * 2,
+        [[4 + n for n in pair] for pair in pairs],
+        [hidden_half] * 2,
         1,
     )
 
-    bias_in = inbound_bias.astype(F32).reshape(3, width)
-    positions = z * both + jnp.arange(both, dtype=jnp.int32)
-    tables = rotary_tables(positions, 128)
-    sent = project(
-        grid, lowered, grad_low, [weight_q, weight_k, weight_v, weight_o], take(bias_in, c * half, half, 1), tables, own_width
-    )
+    bias_in = take(inbound_bias.astype(F32).reshape(3, width), c * half, half, 1)
+    sent = project(grid, lowered, grad_low, weights, bias_in, tables, own_width)
     groups = [[2 * k + core for k in range(nz)] for core in range(2)]
     dealt = lax.all_to_all(sent, "seq", 0, 0, axis_index_groups=groups, tiled=True)
 
     started_e, started_c, _ = lax.optimization_barrier((*started, sent[0, 0]))
     chunks = [(0, None, n - 4, col, size, order) for _, _, n, col, size, order in feed]
-    pairs = [[2 * part, 2 * part + 1] for part in range(parts)]
-    weight_e, weight_c = gather(grid, [started_e, started_c], chunks, pairs, 3, "gather_feed")
+    weight_e, weight_c = gather(grid, [started_e, started_c], chunks, pairs, 2, "gather_feed")
     dealt, weight_e, weight_c = lax.optimization_barrier((dealt, weight_e, weight_c))
 
-    returned = attention(dealt.reshape(length, 4 * own_width), documents[0], heads, tokens).reshape(nz, both, 4 * own_width)
+    returned = attention(dealt.reshape(length, 4 * own_width), documents.astype(F32), heads, tokens)
+    returned = returned.reshape(nz, both, 4 * own_width)
     collected = lax.all_to_all(returned, "seq", 0, 0, axis_index_groups=groups, tiled=True)
 
     bias_e = take(expand_bias.astype(F32), c * hidden_half, hidden_half)[None]
     lowered_seen, _ = lax.optimization_barrier((lowered, returned[0, 0]))
     feed_part, normed_feed, expand_bias_part, *folded = feed_forward(
-        grid, lowered_seen, grad_low, weight_e, weight_c, bias_e, parts, 5
+        grid, lowered_seen, grad_low, weight_e, weight_c, bias_e, parts, 3
     )
 
-    pieces = [
-        jnp.concatenate([collected[m, :, k * own_width : (k + 1) * own_width] for m in range(nz)], axis=-1) for k in range(4)
-    ]
-    attended_low, value_low = pieces[0], pieces[3]
-    spread = [jnp.tile(t, (1, half // 128)) for t in tables]
-
-    def unturn(grad):
-        grad = grad.astype(F32)
-        up = jnp.roll(grad, -(ROT_DIMS // 2), axis=-1)
-        down = jnp.roll(grad, ROT_DIMS // 2, axis=-1)
-        return grad * spread[0] - (up * spread[1] + down * spread[2])
-
-    dq, dk = unturn(pieces[1]), unturn(pieces[2])
-    dq_low, dk_low, dv_low = dq.astype(BF16), dk.astype(BF16), value_low
-    head_bias_grads = jnp.stack([jnp.sum(x.astype(F32), axis=0) for x in (dq, dk, value_low)])
-
-    out_part = against(attended_low, weight_o) + feed_part
-    swap = [(s, s + 1 - 2 * (s % 2)) for s in range(n_seq)]
-    out_theirs = lax.ppermute(take(out_part, (1 - c) * tokens, tokens), "seq", swap)
-    out_own = take(out_part, c * tokens, tokens) + out_theirs
-    layer_out = (last_stream + (out_own + outbound_bias.astype(F32) + contract_bias.astype(F32))).astype(BF16)
-
-    normed_part = jnp.stack(
-        [
-            against(dq_low, weight_q),
-            against(dk_low, weight_k),
-            against(dv_low, weight_v),
-            normed_feed,
-        ]
+    def along_z(k):
+        return [(s, (s // 2 + k) % nz * 2 + s % 2) for s in range(n_seq)]
+
+    folded = [folded[0]] + [lax.ppermute(folded[k], "seq", along_z(k)) for k in range(1, nz)]
+
+    orders = ("ab", "ba", "ab", "ba")
+    bias_out = (outbound_bias.astype(F32) + contract_bias.astype(F32))[None]
+    normed_own, normed_theirs, head_bias_part, layer_out, kept, leaving = unproject(
+        grid, orders, collected, lowered, grad_low, weights, feed_part, normed_feed, last_stream, bias_out, tables, own_width, 4
     )
-    normed_theirs = lax.ppermute(take(normed_part, (1 - c) * tokens, tokens, 1).astype(BF16), "seq", swap)
-    normed_own = take(normed_part, c * tokens, tokens, 1)
-
-    chunks = [
-        (0, half, "ab", 0, pick(0, half)),
-        (1, half, "ba", 0, pick(width, half)),
-        (2, half, "ab", 0, pick(2 * width, half)),
-        (3, half, "ba", 1, pick(0, half)),
-        (4, hidden_half, "", 2, pick(0, hidden_half)),
-        (5, hidden_half, "", 3, pick(0, hidden_half)),
-    ]
-    history_grad, owned, small = mix_backward(
-        grid,
-        history,
-        normed_own,
-        normed_theirs,
-        cotangent,
-        mix_pre,
-        coeffs,
-        [gain, mixer_inner, mixer_outer, stream_gain_full],
-        [head_bias_grads, expand_bias_part],
-        [
-            inner(lowered[0], dq_low).astype(BF16),
-            inner(lowered[1], dk_low).astype(BF16),
-            inner(lowered[2], dv_low).astype(BF16),
-            inner(grad_low, attended_low).astype(BF16),
-        ],
-        folded,
-        chunks,
-        [[0, 1], [2, 3]],
-        [3 * width, width, hidden_width, hidden_width],
-        4,
+    nb = grid.nb
+    over_a = [(d, (d + nb) % n_dp) for d in range(n_dp)]
+    over_b = [[(d, d // nb * nb + (d + k) % nb) for d in range(n_dp)] for k in range(1, nb)]
+    came_a = lax.ppermute(leaving[0], "dp", over_a)
+    came_b = [lax.ppermute(x, "dp", perm) for x, perm in zip(leaving[1:], over_b)]
+
+    history_grad, *small = mix_backward(
+        history, normed_own, normed_theirs, cotangent, mix_pre, coeffs, [mixer_gain[None], inner_t, mixer_outer, stream_gain]
     )
+    smalls = [*small, head_bias_part, expand_bias_part]
+    summed, *owned = finish_sums(grid, orders, kept, [came_a, *came_b], folded, smalls, 5)
+    layer_out, *small, inbound_grad, outbound_grad, expand_grad, contract_grad = hand_over(summed, layer_out, owned, mix, hidden_width)
     gain_grad, inner_grad, outer_grad, bias_grad, stream_gain_grad, stream_bias_grad, in_bias_grad, out_bias_grad, expand_bias_grad = small
     return (
         layer_out[None],
@@ -1153,13 +1249,13 @@
         bias_grad.reshape(-1),
         stream_gain_grad,
         stream_bias_grad,
-        owned[0],
+        inbound_grad,
         in_bias_grad.reshape(3 * width),
-        owned[1],
+        outbound_grad,
         out_bias_grad.reshape(width),
-        owned[2],
+        expand_grad,
         expand_bias_grad.reshape(hidden_width),
-        owned[3],
+        contract_grad,
         out_bias_grad.reshape(width),
     )
 

time: 499 us -> 445 us (0.89)
  local copies, waits for them, and re-layouts: 55.6 us -> 8.81 us
  Pallas kernels: 390 us -> 412 us
  other arithmetic: 21.9 us -> 1.81 us
  matrix products: 14.8 us -> 0 us
  waiting for transfers between devices: 0.01 us -> 6.22 us
    unnamed x94 -> x27, local copies, waits for them, and re-layouts: 32 us -> 6.23 us
    pallas_call x1 -> x4, Pallas kernels: 89.5 us -> 108 us  [the longest x1 55.7 us: finish_sums(): pl.pallas_call(functools.partial(finish_kernel, grid, orders, len(kept)),...]
    dot_general x8 -> x0, matrix products: 14.8 us -> none  [the longest x4 8.12 us: inner(): lax.dot_general(left, right, (((0,), (0,)), ((), ())), preferred_element_...]
    another operation x2 -> x0, other arithmetic: 11.4 us -> none  [the longest x1 10.8 us: on_device(): jnp.stack([against(dq_low, weight_q), against(dk_low, weight_k), against(...]
    ppermute x2 -> x5, waiting for transfers between devices: 0.01 us -> 6.21 us  [the longest x3 6.21 us: on_device(): lax.ppermute(folded[k], 'seq', along_z(k))]
    ppermute x2 -> x5, starting transfers between devices: 0.56 us -> 6.05 us  [the longest x3 3.97 us: on_device(): lax.ppermute(folded[k], 'seq', along_z(k))]
  transfers between devices with their start and end apart: 4 -> 7, of which waited for: 0 -> 1; matrix products, arithmetic and copies ran while one was open for 5% -> 0% of each run, Pallas kernels for 32% -> 42%
where the time goes in v4:
time: 445 us; the launch traced here: 444 us
  Pallas kernels  412 us (93%)
  starting transfers between devices  14.9 us (3%)
  local copies, waits for them, and re-layouts  8.81 us (2%)
  waiting for transfers between devices  6.22 us (1%)
    pallas_call x1, Pallas kernels, mix_forward(): pl.pallas_call(functools.partial(mix_kernel, grid, rows, chunks, groups,...  85.8 us
    pallas_call x1, Pallas kernels, feed_forward(): pl.pallas_call(functools.partial(feed_kernel, grid, steps), grid=(steps,)...  85.4 us
    pallas_call x1, Pallas kernels, gather(): pl.pallas_call(functools.partial(gather_kernel, grid, chunks, groups, n),...  73 us
    pallas_call x1, Pallas kernels, finish_sums(): pl.pallas_call(functools.partial(finish_kernel, grid, orders, len(kept)),...  55.7 us
    pallas_call x1, Pallas kernels, attention(): pl.pallas_call(functools.partial(attention_kernel, width, heads, tile, st...  50.5 us
    pallas_call x1, Pallas kernels, mix_backward(): pl.pallas_call(unmix_kernel, grid=(tokens // block,), out_shape=[jax.Shap...  28.2 us
    pallas_call x1, Pallas kernels, unproject(): pl.pallas_call(functools.partial(unproject_kernel, grid, own_width, order...  21.1 us
    pallas_call x1, Pallas kernels, project(): pl.pallas_call(functools.partial(project_kernel, own_width), grid=(nz //...  9.01 us
  transfers between devices with their start and end apart: 7, of which 1 were waited for; matrix products, arithmetic and copies ran while one was open for 0% of the time, Pallas kernels for 42%

profile of v4, /device:TPU:0, one launch (start us, length us, event | category | flops | bytes accessed | tf_op | source)
XLA Modules:
  0.0 444.5 jit_solution(6760836510943038552)
XLA Ops:
  0.7 1.3 broadcast_in_dim.16.gain_ref
  1.9 0.7 reshape.90
  2.6 0.6 constant_dynamic-slice_fusion.bias_ref
  3.2 85.8 %mix_forward.1 = (bf16[4,2,384,1024]{3,2,1,0:T(8,128)(2,1)}, bf16[2,384,1024]{2,1,0:T(8,128)(2,1)}, f32[384,1024]{1,0:T(8,128)}, f32[384,36]{1,0:T(8,128)}, f32[...) custom-call(bf16[9,1,384,1024]{3,2,1,0:T(8,128)(2,1)} %h_ref.3, ...), custom_call_target="tpu_custom_call" | custom-call | flops 31457280 | bytes 141557760 | tf_op jit(solution)/shard_map/mix_forward/pallas_call | solution.py:425
  89.1 9.0 %project.1 = bf16[4,768,512]{2,1,0:T(8,128)(2,1)} custom-call(bf16[4,768,1024]{2,1,0:T(8,128)(2,1)} %bitcast.18, bf16[768,1024]{1,0:T(8,128)(2,1)} %bitcast.27, bf16[4,1024,512]{2,1,0:T(8,128)(2,1)} %bitcast.21, f32[3,512]{1,0:T(4,128)} %constant_dynamic-slice_fusion.bias_ref, f32[768,128]{1,0:T(8,128)} %get-tuple-element.81.cos_ref, ...), custom_call_target="tpu_custom_call" | custom-call | flops 3221225472 | bytes 12582912 | tf_op jit(solution)/shard_map/project/pallas_call | solution.py:758
  98.1 0.0 copy-start.7
  98.1 4.9 %all-to-all-start = ((bf16[4,768,512]{2,1,0:T(8,128)(2,1)}), bf16[4,768,512]{2,1,0:T(8,128)(2,1)S(1)}, u32[]{:S(2)}, u32[]{:S(2)}) async-start(bf16[4,768,512]{2,1,0:T(8,128)(2,1)} %project.1), calls=%async_computation | async-start | bytes 6291456 | tf_op jit(solution)/shard_map/all_to_all | solution.py:1203
  103.0 0.0 copy-done.7
  103.0 0.6 convert_element_type.13.qdoc_ref
  103.6 73.0 %gather_feed.1 = (bf16[2,2,4,64,2048]{4,3,2,1,0:T(8,128)(2,1)}, bf16[2,2,4,64,2048]{4,3,2,1,0:T(8,128)(2,1)}) custom-call(bf16[2,2,4,64,2048]{4,3,2,1,0:T(8,128)(2,1)} %get-tuple-element.86.refs_0_, bf16[2,2,4,64,2048]{4,3,2,1,0:T(8,128)(2,1)} %get-tuple-element.87.refs_1_), custom_call_target="tpu_custom_call", output_to_operand_aliasing={{0}: (0, {}), {1}: (1, {})} | custom-call | bytes 167772160 | tf_op jit(solution)/shard_map/gather_feed/pallas_call | solution.py:203
  176.5 0.0 all-to-all-done
  176.5 0.0 copy-start.1
  176.6 1.7 copy-done.1
  178.2 50.5 %attention.1 = bf16[3072,512]{1,0:T(8,128)(2,1)} custom-call(bf16[3072,512]{1,0:T(8,128)(2,1)} %bitcast.26, f32[1,3072]{1,0:T(1,128)} %convert_element_type.13.qdoc_ref), custom_call_target="tpu_custom_call" | custom-call | flops 28991029248 | bytes 7864320 | tf_op jit(solution)/shard_map/attention/pallas_call | solution.py:1120
  228.7 0.0 copy-start.8
  228.7 0.0 copy-start.9
  228.7 0.0 copy-start.10
  228.7 4.0 all-to-all-start.1
  232.7 0.0 copy-done.8
  232.7 0.6 dynamic-slice_convert_fusion
  233.3 0.0 copy-done.9
  233.3 0.0 copy-done.10
  233.3 0.6 convert_add_fusion
  233.9 85.4 %feed_forward.1 = (f32[768,1024]{1,0:T(8,128)}, f32[768,1024]{1,0:T(8,128)}, f32[1,2048]{1,0:T(1,128)}, bf16[2,64,2048]{2,1,0:T(8,128)(2,1)}, bf16[2,64,2048]{2,...) custom-call(bf16[4,768,1024]{2,1,0:T(8,128)(2,1)} %bitcast.19, bf16[768,1024]{1,0:T(8,128)(2,1)} %bitcast.28, ...), custom_call_target="tpu_custom_call" | custom-call | flops 38654705664 | bytes 41943040 | tf_op jit(solution)/shard_map/feed_forward/pallas_call | solution.py:976
  319.3 0.0 all-to-all-done.1.col_ref
  319.3 0.0 copy-start
  319.4 1.7 copy-done
  321.0 0.0 copy-start.12
  321.0 0.0 copy-start.11
  321.0 21.1 %unproject.1 = (f32[4,384,1024]{2,1,0:T(8,128)}, bf16[4,384,1024]{2,1,0:T(8,128)(2,1)}, f32[3,512]{1,0:T(4,128)}, bf16[384,1024]{1,0:T(8,128)(2,1)}, bf16[2,4,64...) custom-call(bf16[4,768,512]{2,1,0:T(8,128)(2,1)} %copy-done, ...), custom_call_target="tpu_custom_call" | custom-call | flops 12884901888 | bytes 31457280 | tf_op jit(solution)/shard_map/unproject/pallas_call | solution.py:852
  342.1 0.1 collective-permute-start
  342.2 2.0 collective-permute-start.1
  344.2 0.6 collective-permute-start.2
  344.8 0.0 copy-done.12
  344.8 1.9 collective-permute-start.3
  346.7 0.0 copy-done.11
  346.7 1.5 collective-permute-start.4
  348.2 28.2 %mix_backward.1 = (f32[9,1,384,1024]{3,2,1,0:T(8,128)}, f32[4,1024]{1,0:T(4,128)}, f32[4,1024]{1,0:T(4,128)}, f32[1,1024]{1,0:T(1,128)}, f32[36,1024]{1,0:T(8,12...) custom-call(bf16[9,1,384,1024]{3,2,1,0:T(8,128)(2,1)} %h_ref.3, ...), custom_call_target="tpu_custom_call" | custom-call | flops 393216000 | bytes 42467328 | tf_op jit(solution)/shard_map/mix_backward/pallas_call | solution.py:551
  376.4 0.0 collective-permute-done.2.refs_7_
  376.4 0.0 copy-start.4
  376.4 6.2 %collective-permute-done.3.refs_8_ = bf16[2,64,2048]{2,1,0:T(8,128)(2,1)S(1)} collective-permute-done((bf16[2,64,2048]{2,1,0:T(8,128)(2,1)S(1)}, bf16[2,64,2048]{2,1,0:T(8,128)(2,1)S(1)}, u32[]{:S(2)}, u32[]{:S(2)}) %collective-permute-start.3) | collective-permute-done | bytes 524320 | tf_op jit(solution)/shard_map/ppermute | solution.py:1223
  382.6 0.0 copy-start.5
  382.7 0.0 collective-permute-done.4.refs_9_
  382.7 0.0 copy-start.6
  382.7 0.0 collective-permute-done.refs_4_
  382.7 0.0 copy-start.2
  382.7 0.0 collective-permute-done.1.refs_5_
  382.7 0.0 copy-start.3
  382.7 0.0 copy-done.4
  382.7 0.7 copy-done.5
  383.4 0.2 copy-done.6
  383.6 0.4 copy-done.2
  384.0 0.3 copy-done.3
  384.3 55.7 %finish_sums.1 = (f32[512,128]{1,0:T(8,128)}, f32[32,3072]{1,0:T(8,128)}, f32[32,1024]{1,0:T(8,128)}, f32[32,4096]{1,0:T(8,128)}, f32[32,4096]{1,0:T(8,128)}) custom-call(bf16[2,4,64,512]{3,2,1,0:T(8,128)(2,1)} %get-tuple-element.96.refs_0_, bf16[2,4,64,512]{3,2,1,0:T(8,128)(2,1)} %get-tuple-element.97.refs_1_, ...), custom_call_target="tpu_custom_call" | custom-call | bytes 104857600 | tf_op jit(solution)/shard_map/finish_sums/pallas_call | solution.py:675
  440.0 3.2 hand_over.1
  443.2 1.3 copy.38
Async XLA Ops:
  98.1 4.9 %copy-start.7 = (s32[1,3072]{1,0:T(1,128)S(1)}, s32[1,3072]{1,0:T(1,128)}, u32[]{:S(2)}) copy-start(s32[1,3072]{1,0:T(1,128)} %param.18) | copy-start | bytes 36868
  98.1 78.4 %all-to-all-start = ((bf16[4,768,512]{2,1,0:T(8,128)(2,1)}), bf16[4,768,512]{2,1,0:T(8,128)(2,1)S(1)}, u32[]{:S(2)}, u32[]{:S(2)}) async-start(bf16[4,768,512]{2,1,0:T(8,128)(2,1)} %project.1), calls=%async_computation | async-start | bytes 6291456 | tf_op jit(solution)/shard_map/all_to_all | solution.py:1203
  176.5 1.7 copy-start.1
  228.7 4.0 copy-start.8
  228.7 4.7 %copy-start.9 = (bf16[1024]{0:T(1024)(128)(2,1)S(1)}, bf16[1024]{0:T(1024)(128)(2,1)}, u32[]{:S(2)}) copy-start(bf16[1024]{0:T(1024)(128)(2,1)} %param.33) | copy-start | bytes 6148
  228.7 4.7 %copy-start.10 = (bf16[1024]{0:T(1024)(128)(2,1)S(1)}, bf16[1024]{0:T(1024)(128)(2,1)}, u32[]{:S(2)}) copy-start(bf16[1024]{0:T(1024)(128)(2,1)} %param.29) | copy-start | bytes 6148
  228.7 90.6 %all-to-all-start.1 = ((bf16[4,768,512]{2,1,0:T(8,128)(2,1)}), bf16[4,768,512]{2,1,0:T(8,128)(2,1)S(1)}, u32[]{:S(2)}, u32[]{:S(2)}) async-start(bf16[4,768,512]{2,1,0:T(8,128)(2,1)} %bitcast.25), calls=%async_computation.1 | async-start | bytes 6291456 | tf_op jit(solution)/shard_map/all_to_all | solution.py:1212
  319.3 1.7 copy-start
  321.0 23.8 %copy-start.12 = (bf16[2,64,2048]{2,1,0:T(8,128)(2,1)S(1)}, bf16[2,64,2048]{2,1,0:T(8,128)(2,1)}, u32[]{:S(2)}) copy-start(bf16[2,64,2048]{2,1,0:T(8,128)(2,1)} %get-tuple-element.104) | copy-start | bytes 1572868
  321.0 25.7 %copy-start.11 = (bf16[2,64,2048]{2,1,0:T(8,128)(2,1)S(1)}, bf16[2,64,2048]{2,1,0:T(8,128)(2,1)}, u32[]{:S(2)}) copy-start(bf16[2,64,2048]{2,1,0:T(8,128)(2,1)} %get-tuple-element.105) | copy-start | bytes 1572868
  342.1 40.5 %collective-permute-start = (bf16[2,2,4,64,512]{4,3,2,1,0:T(8,128)(2,1)}, bf16[2,2,4,64,512]{4,3,2,1,0:T(8,128)(2,1)S(1)}, u32[]{:S(2)}, u32[]{:S(2)}) collective-permute-start(bf16[2,2,4,64,512]{4,3,2,1,0:T(8,128)(2,1)} %get-tuple-element.100), channel_id=1, source_target_pairs={{0,16},{8,24},{16,0},{24,8},{1,17},{9,25},{17,1},{25,9},{2,18},{10... | collective-permute-start | bytes 3145736 | tf_op jit(solution)/shard_map/ppermute | solution.py:1233
  342.2 40.5 %collective-permute-start.1 = (bf16[2,2,4,64,512]{4,3,2,1,0:T(8,128)(2,1)}, bf16[2,2,4,64,512]{4,3,2,1,0:T(8,128)(2,1)S(1)}, u32[]{:S(2)}, u32[]{:S(2)}) collective-permute-start(bf16[2,2,4,64,512]{4,3,2,1,0:T(8,128)(2,1)} %get-tuple-element.101), channel_id=1, source_target_pairs={{0,8},{8,0},{16,24},{24,16},{1,9},{9,1},{17,25},{25,17},{2,10},{10... | collective-permute-start | bytes 3145736 | tf_op jit(solution)/shard_map/ppermute | solution.py:1234
  344.2 32.2 %collective-permute-start.2 = (bf16[2,64,2048]{2,1,0:T(8,128)(2,1)}, bf16[2,64,2048]{2,1,0:T(8,128)(2,1)S(1)}, u32[]{:S(2)}, u32[]{:S(2)}) collective-permute-start(bf16[2,64,2048]{2,1,0:T(8,128)(2,1)} %get-tuple-element.103), channel_id=1, source_target_pairs={{0,2},{1,3},{2,4},{3,5},{4,6},{5,7},{6,0},{7,1},{8,10},{9,11},{10,... | collective-permute-start | bytes 1572872 | tf_op jit(solution)/shard_map/ppermute | solution.py:1223
  344.8 37.9 %collective-permute-start.3 = (bf16[2,64,2048]{2,1,0:T(8,128)(2,1)S(1)}, bf16[2,64,2048]{2,1,0:T(8,128)(2,1)S(1)}, u32[]{:S(2)}, u32[]{:S(2)}) collective-permute-start(bf16[2,64,2048]{2,1,0:T(8,128)(2,1)S(1)} %copy-done.12), channel_id=1, source_target_pairs={{0,4},{1,5},{2,6},{3,7},{4,0},{5,1},{6,2},{7,3},{8,12},{9,13},{10,... | collective-permute-start | bytes 1572872 | tf_op jit(solution)/shard_map/ppermute | solution.py:1223
  346.7 35.9 %collective-permute-start.4 = (bf16[2,64,2048]{2,1,0:T(8,128)(2,1)S(1)}, bf16[2,64,2048]{2,1,0:T(8,128)(2,1)S(1)}, u32[]{:S(2)}, u32[]{:S(2)}) collective-permute-start(bf16[2,64,2048]{2,1,0:T(8,128)(2,1)S(1)} %copy-done.11), channel_id=1, source_target_pairs={{0,6},{1,7},{2,0},{3,1},{4,2},{5,3},{6,4},{7,5},{8,14},{9,15},{10,... | collective-permute-start | bytes 1572872 | tf_op jit(solution)/shard_map/ppermute | solution.py:1223
  376.4 6.3 %copy-start.4 = (bf16[2,64,2048]{2,1,0:T(8,128)(2,1)}, bf16[2,64,2048]{2,1,0:T(8,128)(2,1)S(1)}, u32[]{:S(2)}) copy-start(bf16[2,64,2048]{2,1,0:T(8,128)(2,1)S(1)} %collective-permute-done.2.refs_7_) | copy-start | bytes 1572868
  382.6 0.8 copy-start.5
  382.7 1.0 copy-start.6
  382.7 1.3 copy-start.2
  382.7 1.6 copy-start.3

commit v5 on v4

--- a/solution.py
+++ b/solution.py
@@ -122,14 +122,33 @@
             theirs = self.ins[source].at[:, pl.ds(pl.multiple_of(base(1 - c), 128), n)]
             spot = out.at[a, b, z, pl.ds(pl.multiple_of(c * rows, rows), rows), cols]
             return [pltpu.make_async_copy(mine, spot, self.local_sem.at[t]), send(theirs, spot, 0, grid.device(a, b, z, 1 - c))]
-        if stage == 1:
-            block = out.at[a, b, z, :, cols]
-            return [send(block, block, k, grid.device(a, b, lax.rem(z + k, nz), c)) for k in range(1, nz)]
         if order[stage - 2] == "b":
             block = out.at[a, b, :, :, cols] if stage == 2 else out.at[:, b, :, :, cols]
-            return [send(block, block, nz + k - 1, grid.device(a, lax.rem(b + k, nb), z, c)) for k in range(1, nb)]
+            return [send(block, block, k, grid.device(a, lax.rem(b + k, nb), z, c)) for k in range(1, nb)]
         block = out.at[a, b, :, :, cols] if stage == 2 else out.at[a, :, :, :, cols]
-        return [send(block, block, nz + nb - 1, grid.device(1 - a, b, z, c))]
+        return [send(block, block, nb, grid.device(1 - a, b, z, c))]
+
+    def hop(self, t, step, begin):
+        a, b, z, c = self.place
+        nz, nb = self.grid.nz, self.grid.nb
+        _, _, result, col, n, _ = self.chunks[t]
+        out, cols = self.outs[result], pl.ds(col, n)
+        for side, way in enumerate((1, -1)):
+            slot = nb + 1 + side * (nz - 1) + step - 1
+            there, arriving = z + way, z - way * step
+            going = there - way * step
+            inside = (there >= 0) & (there < nz) & (going >= 0) & (going < nz)
+            coming = (arriving >= 0) & (arriving < nz)
+
+            def link(which, slot=slot, there=there):
+                block = out.at[a, b, which, :, cols]
+                return remote(block, block, self.send_sem.at[t, slot], self.recv_sem.at[t, slot], self.grid.device(a, b, there, c))
+
+            if begin:
+                pl.when(inside)(lambda link=link, going=going: link(going).start())
+            else:
+                pl.when(inside)(lambda link=link, going=going: link(going).wait_send())
+                pl.when(coming)(lambda link=link, arriving=arriving: link(arriving).wait_recv())
 
     def begin(self, group, stage):
         for t in group:
@@ -139,79 +158,47 @@
         for t in group:
             finish(self.copies(t, stage))
 
-    def events(self, whole, partial):
-        groups = whole + partial
+    def ticks(self, whole, partial):
+        groups, nz = whole + partial, self.grid.nz
+
+        def advance(u, at):
+            group = groups[u]
+            if at == 0:
+                self.end(group, 0)
+            elif at < nz:
+                for t in group:
+                    self.hop(t, at, False)
+            else:
+                self.end(group, 2)
+            for t in group:
+                if at < nz - 1:
+                    self.hop(t, at + 1, True)
+                elif u < len(whole):
+                    start(self.copies(t, 2 if at == nz - 1 else 3))
 
         def first():
             for group in groups:
                 self.begin(group, 0)
 
-        def second():
-            self.end(groups[0], 0)
-            self.begin(groups[0], 1)
-
-        def turn(u):
-            if u < len(groups):
-                self.end(groups[u], 1)
-                if u + 1 < len(groups):
-                    self.end(groups[u + 1], 0)
-                    self.begin(groups[u + 1], 1)
-                if u < len(whole):
-                    self.begin(groups[u], 2)
-            if 0 <= u - 1 < len(whole):
-                self.end(groups[u - 1], 2)
-                self.begin(groups[u - 1], 3)
-            if 0 <= u - 2 < len(whole):
-                self.end(groups[u - 2], 3)
-
-        turns = max(len(whole) + 2, len(groups))
-        return [first, second] + [functools.partial(turn, u) for u in range(turns)]
-
-    def late_events(self, groups):
-        def turn(u):
-            if u < len(groups):
-                self.begin(groups[u], 2)
-            if 0 <= u - 1 < len(groups):
-                self.end(groups[u - 1], 2)
-                self.begin(groups[u - 1], 3)
-            if 0 <= u - 2 < len(groups):
-                self.end(groups[u - 2], 3)
-
-        return [functools.partial(turn, u) for u in range(len(groups) + 2)]
-
-
-def gather_kernel(grid, chunks, groups, n, *refs):
-    outs = refs[n : 2 * n]
-    place = grid.here()
-    grid.greet(*place)
-    for event in Gathering(grid, place, None, chunks, None, outs, *refs[2 * n :]).late_events(groups):
-        event()
+        def tick(now):
+            for u in range(len(groups)):
+                if 0 <= now - u <= (nz if u < len(whole) else nz - 1):
+                    advance(u, now - u)
+
+        def last():
+            for group in whole:
+                self.end(group, 3)
+
+        return [first] + [functools.partial(tick, now) for now in range(len(groups) + nz)] + [last]
 
 
 def gather_sems(grid, chunks):
-    slots = grid.nz + grid.nb
+    slots = 2 * grid.nz + grid.nb - 1
     return [
         pltpu.SemaphoreType.DMA((len(chunks),)),
         pltpu.SemaphoreType.DMA((len(chunks), slots)),
         pltpu.SemaphoreType.DMA((len(chunks), slots)),
     ]
-
-
-def gather(grid, arrays, chunks, groups, collective_id, name):
-    n = len(arrays)
-    moved = sum(x.size for x in arrays) * 2
-    results = pl.pallas_call(
-        functools.partial(gather_kernel, grid, chunks, groups, n),
-        out_shape=[jax.ShapeDtypeStruct(x.shape, x.dtype) for x in arrays],
-        in_specs=[pl.BlockSpec(memory_space=pl.ANY)] * n,
-        out_specs=[pl.BlockSpec(memory_space=pl.ANY)] * n,
-        input_output_aliases={k: k for k in range(n)},
-        scratch_shapes=gather_sems(grid, chunks),
-        compiler_params=pltpu.CompilerParams(collective_id=collective_id, has_side_effects=True),
-        cost_estimate=pl.CostEstimate(flops=0, bytes_accessed=moved * 20, transcendentals=0),
-        name=name,
-    )(*arrays)
-    return [r.reshape(-1, r.shape[-1]) for r in results]
 
 
 def fold_copies(grid, place, order, stage, part, first, second, sems):
@@ -349,7 +336,7 @@
     a, b, z, c = place = grid.here()
     block = h_ref.shape[2]
     outs = [weights_ref.at[k] for k in range(4)] + list(outs)
-    events = Gathering(grid, place, rows, chunks, ins, outs, local_sem, send_sem, recv_sem).events(whole, partial)
+    events = Gathering(grid, place, rows, chunks, ins, outs, local_sem, send_sem, recv_sem).ticks(whole, partial)
     other = grid.device(a, b, z, 1 - c)
 
     def pair(k, src, dst):
@@ -367,9 +354,11 @@
         events[0]()
         start(grads())
 
-    @pl.when(i == 1)
-    def _():
-        events[1]()
+    for n, at in enumerate((0, 2, 3, 4)):
+
+        @pl.when(i == at)
+        def _(n=n):
+            events[n + 1]()
 
     @pl.when(i == 2)
     def _():
@@ -407,7 +396,7 @@
     @pl.when(i == steps - 1)
     def _():
         start(lowereds())
-        for event in events[2:]:
+        for event in events[5:]:
             event()
         finish(grads())
         finish(lowereds())
@@ -416,7 +405,7 @@
 def mix_forward(grid, history, cotangent, params, weights, chunks, groups, partial, widths, collective_id):
     hist, _, tokens, width = history.shape
     mix = params[1].shape[0]
-    block = 32
+    block = 64
     rows = weights[0].shape[0]
     whole = pl.BlockSpec(memory_space=pltpu.VMEM)
     anywhere = pl.BlockSpec(memory_space=pl.ANY)
@@ -542,7 +531,7 @@
 def mix_backward(history, own, theirs, cotangent, pre, coeffs, params):
     hist, _, tokens, width = history.shape
     mix = pre.shape[1]
-    block = 32
+    block = 64
     whole = pl.BlockSpec(memory_space=pltpu.VMEM)
     part = lambda n: pl.BlockSpec((block, n), lambda i: (i, 0))
     four = pl.BlockSpec((4, block, width), lambda i: (0, i, 0))
@@ -572,7 +561,7 @@
     nz = grid.nz
     kept, refs = refs[:n_kept], refs[n_kept:]
     came_a, came_b, refs = refs[:1], refs[1 : grid.nb], refs[grid.nb :]
-    folded, refs = refs[:nz], refs[nz:]
+    sums_refs, folded, refs = refs[:2], refs[2 : 2 + nz], refs[2 + nz :]
     sgg_ref, sbg_ref, gg_ref, ig_ref, og_ref, bg_ref, ob_ref, hb_ref, eb_ref = refs[:9]
     done_ref, outs, refs = refs[9], refs[10:14], refs[14:]
     first, second, third, final, refs = refs[:4], refs[4:8], refs[8:12], refs[12:18], refs[18:]
@@ -616,7 +605,7 @@
 
         lax.fori_loop(0, first[t].shape[1] * nz, step, 0)
     pl.semaphore_wait(pltpu.get_barrier_semaphore(), sums.count - 1)
-    for t in range(4):
+    for t in range(2):
         start(copies(t, 1))
 
     mine = sums.mine
@@ -641,10 +630,16 @@
         total = folded[0][t].astype(F32)
         for piece in folded[1:]:
             total = total + piece[t].astype(F32)
-        final[4 + t][...] = total.reshape(final[4 + t].shape)
+        at = 0
+        for piece in [ref[t] for ref in sums_refs] + [total]:
+            n = piece.shape[1]
+            final[4 + t][:, :, at : at + n] = piece.reshape(2, -1, n)
+            at += n
         start(copies(4 + t, 3))
     for t in range(4):
         finish(copies(t, 1))
+        if t < 2:
+            start(copies(t + 2, 1))
         fold_add(grid, place, orders[t], 1, None, first[t], second[t])
         start(copies(t, 2))
     sums.tell()
@@ -736,44 +731,94 @@
     )(summed, layer_out, *owned)
 
 
-def project_kernel(width, low_ref, g_ref, w_ref, bias_ref, cos_ref, above_ref, below_ref, sent_ref):
+def exchange_kernel(grid, width, chunks, groups, low_ref, g_ref, w_ref, bias_ref, cos_ref, above_ref, below_ref, _e, _c,
+                    dealt_ref, e_ref, c_ref, sent_ref, deal_send, deal_recv, local_sem, send_sem, recv_sem):
+    i, steps = pl.program_id(0), pl.num_programs(0)
+    a, b, z, c = place = grid.here()
+    nz = grid.nz
+    work = Gathering(grid, place, None, chunks, None, [e_ref, c_ref], local_sem, send_sem, recv_sem)
+
+    def link(to):
+        k = lax.rem(to - z + nz, nz)
+        return remote(sent_ref.at[to], dealt_ref.at[z], deal_send.at[k], deal_recv.at[k], grid.device(a, b, to, c))
+
+    def stay():
+        return pltpu.make_async_copy(sent_ref.at[z], dealt_ref.at[z], deal_send.at[0])
+
+    @pl.when(i == 0)
+    def _():
+        grid.greet(*place)
+        for group in groups:
+            work.begin(group, 2)
+
     wide = w_ref.shape[2]
-    reps = max(wide // 128, 1)
-    tables = [jnp.concatenate([t[...]] * reps, axis=1) for t in (cos_ref, above_ref, below_ref)]
+    each = wide // width
+    tables = [jnp.concatenate([t[...]] * max(wide // 128, 1), axis=1) for t in (cos_ref, above_ref, below_ref)]
     q = rotate(product(low_ref[0], w_ref[0]) + bias_ref[0:1, :], tables, 1.0)
     k = rotate(product(low_ref[1], w_ref[1]) + bias_ref[1:2, :], tables, 1.0)
     v = product(low_ref[2], w_ref[2]) + bias_ref[2:3, :]
     g = product(g_ref[...], w_ref[3])
     for n, x in enumerate((q, k, v, g)):
         x = x.astype(BF16)
-        for m in range(wide // width):
-            sent_ref[m, :, n * width : (n + 1) * width] = x[:, m * width : (m + 1) * width]
-
-
-def project(grid, lowered, grad_low, weights, biases, tables, own_width):
-    both = lowered.shape[1]
+        for m in range(each):
+            sent_ref[i * each + m, :, n * width : (n + 1) * width] = x[:, m * width : (m + 1) * width]
+    for m in range(each):
+        to = i * each + m
+        pl.when(to != z)(lambda to=to: link(to).start())
+        pl.when(to == z)(lambda: stay().start())
+
+    @pl.when(i == steps - 1)
+    def _():
+        for group in groups:
+            work.end(group, 2)
+            work.begin(group, 3)
+        for m in range(1, nz):
+            link(lax.rem(z + m, nz)).wait()
+        stay().wait()
+        for group in groups:
+            work.end(group, 3)
+
+
+def exchange(grid, lowered, grad_low, weights, biases, tables, started, chunks, groups, own_width, collective_id):
+    both, width = grad_low.shape
     nz = grid.nz
     wide = 2 * own_width
     whole = pl.BlockSpec(memory_space=pltpu.VMEM)
-    return pl.pallas_call(
-        functools.partial(project_kernel, own_width),
+    anywhere = pl.BlockSpec(memory_space=pl.ANY)
+    dealt, *full = pl.pallas_call(
+        functools.partial(exchange_kernel, grid, own_width, chunks, groups),
         grid=(nz // 2,),
-        out_shape=jax.ShapeDtypeStruct((nz, both, 4 * own_width), BF16),
-        in_specs=[whole, whole]
-        + [pl.BlockSpec((4, weights.shape[1], wide), lambda i: (0, 0, i)), pl.BlockSpec((3, wide), lambda i: (0, i))]
-        + [whole] * 3,
-        out_specs=pl.BlockSpec((2, both, 4 * own_width), lambda i: (i, 0, 0)),
-        compiler_params=pltpu.CompilerParams(vmem_limit_bytes=VMEM_LIMIT),
-        cost_estimate=pl.CostEstimate(flops=2 * both * weights.size, bytes_accessed=lowered.size * 4, transcendentals=0),
-        name="project",
-    )(lowered, grad_low, weights, biases, *tables)
-
-
-def unproject_kernel(grid, width, orders, col_ref, low_ref, g_ref, w_ref, feed_ref, normed_ref, last_ref, bias_ref, cos_ref, above_ref,
-                     below_ref, own_ref, theirs_ref, hb_ref, out_ref, *refs):
+        out_shape=[jax.ShapeDtypeStruct((nz, both, 4 * own_width), BF16)] + [jax.ShapeDtypeStruct(x.shape, x.dtype) for x in started],
+        in_specs=[
+            pl.BlockSpec((3, both, width), lambda i: (0, 0, 0)),
+            whole,
+            pl.BlockSpec((4, width, wide), lambda i: (0, 0, i)),
+            pl.BlockSpec((3, wide), lambda i: (0, i)),
+        ]
+        + [whole] * 3
+        + [anywhere] * 2,
+        out_specs=[anywhere] * 3,
+        input_output_aliases={7: 1, 8: 2},
+        scratch_shapes=[
+            pltpu.VMEM((nz, both, 4 * own_width), BF16),
+            pltpu.SemaphoreType.DMA((nz,)),
+            pltpu.SemaphoreType.DMA((nz,)),
+            *gather_sems(grid, chunks),
+        ],
+        compiler_params=pltpu.CompilerParams(collective_id=collective_id, has_side_effects=True, vmem_limit_bytes=VMEM_LIMIT),
+        cost_estimate=pl.CostEstimate(flops=2 * both * weights.size, bytes_accessed=weights.size * 60, transcendentals=0),
+        name="exchange",
+    )(lowered, grad_low, weights, biases, *tables, *started)
+    return dealt, [x.reshape(-1, x.shape[-1]) for x in full]
+
+
+def unproject_kernel(grid, width, orders, *all_refs):
+    mids, all_refs = all_refs[: grid.nz], all_refs[grid.nz :]
+    (col_ref, low_ref, g_ref, w_ref, feed_ref, normed_ref, last_ref, bias_ref, cos_ref, above_ref,
+     below_ref, own_ref, theirs_ref, hb_ref, out_ref, sum_ref, *refs) = all_refs
     na, nb, nz = grid.na, grid.nb, grid.nz
     kept, over_a, over_b, refs = refs[:4], refs[4], refs[5 : 4 + nb], refs[4 + nb :]
-    grad_ref, sending_ref, partial_ref, mine_ref, arrived_ref, split_sem, send_sem, recv_sem = refs
+    grad_ref, sending_ref, partial_ref, mine_ref, arrived_ref, along_ref, split_sem, send_sem, recv_sem, along_send, along_recv = refs
     i = pl.program_id(0)
     a, b, z, c = grid.here()
     tokens = out_ref.shape[0]
@@ -786,6 +831,12 @@
 
     def swap_out():
         return [remote(partial_ref, arrived_ref, send_sem.at[4], recv_sem.at[4], other)]
+
+    def along():
+        return [
+            remote(mids[k], along_ref.at[k - 1], along_send.at[k - 1], along_recv.at[k - 1], grid.device(a, b, lax.rem(z + k, nz), c))
+            for k in range(1, nz)
+        ]
 
     def split(k):
         grad = grad_ref.at[k]
@@ -805,12 +856,11 @@
 
     @pl.when(i == 0)
     def _():
-        barrier = pltpu.get_barrier_semaphore()
-        pl.semaphore_signal(barrier, inc=1, device_id=other, device_id_type=MESH)
+        grid.greet(a, b, z, c)
+        start(along())
         mine_ref[...] = piece(0)
         partial_ref[...] = against(mine_ref[their_rows, :], w_ref[0]) + feed_ref[their_rows, :]
         sending_ref[3] = normed_ref[their_rows, :].astype(BF16)
-        pl.semaphore_wait(barrier, 1)
         start(swap_out())
         start(swap(3))
         own_ref[0] = normed_ref[own_rows, :]
@@ -837,9 +887,14 @@
                 for n in range(4):
                     finish(swap(n))
                     finish(split(n))
-
-
-def unproject(grid, orders, collected, lowered, grad_low, weights, feed_part, normed_feed, last_stream, bias, tables, own_width, collective_id):
+                finish(along())
+                total = mids[0][...].astype(F32)
+                for n in range(nz - 1):
+                    total = total + along_ref[n].astype(F32)
+                sum_ref[...] = total
+
+
+def unproject(grid, orders, mids, collected, lowered, grad_low, weights, feed_part, normed_feed, last_stream, bias, tables, own_width, collective_id):
     tokens, width = last_stream.shape
     both, half = 2 * tokens, width // 2
     na, nb, nz = grid.na, grid.nb, grid.nz
@@ -857,10 +912,13 @@
             jax.ShapeDtypeStruct((4, tokens, width), BF16),
             jax.ShapeDtypeStruct((3, half), F32),
             jax.ShapeDtypeStruct((tokens, width), BF16),
+            jax.ShapeDtypeStruct(mids[0].shape, F32),
         ]
         + split_shapes
         + sent_shapes,
-        in_specs=[
+        in_specs=[whole]
+        + [anywhere] * (nz - 1)
+        + [
             whole,
             pl.BlockSpec((1, both, width), lambda i: (jnp.maximum(i - 1, 0), 0, 0)),
             whole,
@@ -872,6 +930,7 @@
             anywhere,
             pl.BlockSpec((3, half), lambda i: (0, 0)),
             pl.BlockSpec((tokens, width), lambda i: (0, 0)),
+            pl.BlockSpec(mids[0].shape, lambda i: (0, 0, 0)),
         ]
         + [anywhere] * (len(split_shapes) + len(sent_shapes)),
         scratch_shapes=[
@@ -880,24 +939,27 @@
             pltpu.VMEM((tokens, width), F32),
             pltpu.VMEM((both, half), BF16),
             pltpu.VMEM((tokens, width), F32),
+            pltpu.VMEM((nz - 1, *mids[0].shape), BF16),
             pltpu.SemaphoreType.DMA((4, nb + 1)),
             pltpu.SemaphoreType.DMA((5,)),
             pltpu.SemaphoreType.DMA((5,)),
+            pltpu.SemaphoreType.DMA((nz - 1,)),
+            pltpu.SemaphoreType.DMA((nz - 1,)),
         ],
         compiler_params=pltpu.CompilerParams(collective_id=collective_id, has_side_effects=True, vmem_limit_bytes=VMEM_LIMIT),
         cost_estimate=pl.CostEstimate(flops=32 * both * width * half, bytes_accessed=40 * both * width, transcendentals=0),
         name="unproject",
-    )(collected, lowered, grad_low, weights, feed_part, normed_feed, last_stream, bias, *tables)
-    own, theirs, head_bias, layer_out = results[:4]
-    return own, theirs, head_bias, layer_out, results[4:8], results[8:]
-
-
-def feed_kernel(grid, steps, low_ref, g_ref, we_ref, wc_ref, bias_ref, feed_ref, normed_ref, eb_ref, *refs):
+    )(*mids, collected, lowered, grad_low, weights, feed_part, normed_feed, last_stream, bias, *tables)
+    own, theirs, head_bias, layer_out, mid_sums = results[:5]
+    return own, theirs, head_bias, layer_out, mid_sums, results[5:9], results[9:]
+
+
+def feed_kernel(grid, steps, back_ref, low_ref, g_ref, we_ref, wc_ref, bias_ref, collected_ref, feed_ref, normed_ref, eb_ref, sum_ref, *refs):
     nz = grid.nz
-    outs, refs = refs[:nz], refs[nz:]
+    mids, outs, refs = refs[:nz], refs[nz : 2 * nz], refs[2 * nz :]
     parts, refs = refs[: 2 * steps], refs[2 * steps :]
     first, second, refs = refs[: 2 * steps], refs[2 * steps : 4 * steps], refs[4 * steps :]
-    send_sem, recv_sem, out_sem = refs
+    third, (send_sem, recv_sem, out_sem, back_send, back_recv) = refs[:2], refs[2:]
     i = pl.program_id(0)
     a, b, z, c = place = grid.here()
     orders = ["ab", "ba"] * steps
@@ -905,10 +967,14 @@
     def copies(t, stage):
         if stage < 2:
             return fold_copies(grid, place, orders[t], stage, parts[t], first[t], second[t], (send_sem.at[t], recv_sem.at[t]))
-        n = parts[t].shape[-1]
-        cols = pl.ds((t // 2) * n, n)
+        along = [lax.rem(z + k, nz) for k in range(nz)]
+        if t >= 2:
+            n = parts[t].shape[-1]
+            spot = outs if t >= 2 * steps - 2 else [mid.at[:, :, pl.ds((t // 2 - 1) * n, n)] for mid in mids]
+            return [pltpu.make_async_copy(second[t].at[0, along[k]], spot[k].at[t % 2], out_sem.at[t, k]) for k in range(nz)]
         return [
-            pltpu.make_async_copy(second[t].at[0, lax.rem(z + k, nz)], outs[k].at[t % 2, :, cols], out_sem.at[t, k]) for k in range(nz)
+            remote(second[t].at[0, along[k]], third[t].at[k - 1], send_sem.at[t, k], recv_sem.at[t, k], grid.device(a, b, along[k], c))
+            for k in range(1, nz)
         ]
 
     def begin(u):
@@ -922,16 +988,28 @@
                 own = parts[t].at[a] if orders[t] == "ab" else parts[t].at[:, b]
                 fold_add(grid, place, orders[t], stage, own, first[t], second[t])
                 start(copies(t, stage + 1))
+            elif u == 0:
+                total = second[t][0, z].astype(F32)
+                for k in range(nz - 1):
+                    total = total + third[t][k].astype(F32)
+                sum_ref[t % 2] = total
 
     def turn(u):
-        if u < steps:
-            end(u, 0)
-        if 0 <= u - 1 < steps:
-            end(u - 1, 1)
+        for stage in range(3):
+            if 0 <= u - stage < steps:
+                end(u - stage, stage)
+
+    def backs():
+        found = [pltpu.make_async_copy(back_ref.at[z], collected_ref.at[z], back_send.at[0])]
+        for k in range(1, nz):
+            to = lax.rem(z + k, nz)
+            found.append(remote(back_ref.at[to], collected_ref.at[z], back_send.at[k], back_recv.at[k], grid.device(a, b, to, c)))
+        return found
 
     @pl.when(i == 0)
     def _():
         grid.greet(*place)
+        start(backs())
         feed_ref[...] = jnp.zeros_like(feed_ref)
         normed_ref[...] = jnp.zeros_like(normed_ref)
 
@@ -957,13 +1035,12 @@
             if u >= 2:
                 turn(u - 2)
             if u == steps - 1:
-                for v in range(max(steps - 2, 0), steps + 1):
+                for v in range(max(steps - 2, 0), steps + 2):
                     turn(v)
-                for v in range(steps):
-                    end(v, 2)
-
-
-def feed_forward(grid, lowered, grad_low, weight_e, weight_c, bias, steps, collective_id):
+                finish(backs())
+
+
+def feed_forward(grid, returned, lowered, grad_low, weight_e, weight_c, bias, steps, collective_id):
     both, width = grad_low.shape
     n = weight_e.shape[1] // steps
     na, nb, nz = grid.na, grid.nb, grid.nz
@@ -977,12 +1054,16 @@
         functools.partial(feed_kernel, grid, steps),
         grid=(steps,),
         out_shape=[
+            jax.ShapeDtypeStruct(returned.shape, BF16),
             jax.ShapeDtypeStruct((both, width), F32),
             jax.ShapeDtypeStruct((both, width), F32),
             jax.ShapeDtypeStruct((1, n * steps), F32),
+            jax.ShapeDtypeStruct((2, rows, n), F32),
         ]
-        + [jax.ShapeDtypeStruct((2, rows, n * steps), BF16)] * nz,
+        + [jax.ShapeDtypeStruct((2, rows, n * (steps - 2)), BF16)] * nz
+        + [jax.ShapeDtypeStruct((2, rows, n), BF16)] * nz,
         in_specs=[
+            pl.BlockSpec(memory_space=pltpu.VMEM),
             pl.BlockSpec((1, both, width), lambda i: (3, 0, 0)),
             whole(both, width),
             cols(width),
@@ -990,19 +1071,22 @@
             cols(1),
         ],
         out_specs=[
+            pl.BlockSpec(memory_space=pl.ANY),
             whole(both, width),
             whole(both, width),
             cols(1),
+            whole(2, rows, n),
         ]
-        + [pl.BlockSpec(memory_space=pl.ANY)] * nz,
+        + [pl.BlockSpec(memory_space=pl.ANY)] * (2 * nz),
         scratch_shapes=[pltpu.VMEM((na, nb, nz, rows, n), BF16)] * (2 * steps)
         + [f for _, f, _ in folds]
         + [s for _, _, s in folds]
-        + [sem, sem, pltpu.SemaphoreType.DMA((2 * steps, nz))],
+        + [pltpu.VMEM((nz - 1, rows, n), BF16)] * 2
+        + [sem, sem, pltpu.SemaphoreType.DMA((2 * steps, nz)), pltpu.SemaphoreType.DMA((nz,)), pltpu.SemaphoreType.DMA((nz,))],
         compiler_params=pltpu.CompilerParams(collective_id=collective_id, has_side_effects=True, vmem_limit_bytes=VMEM_LIMIT),
         cost_estimate=pl.CostEstimate(flops=12 * both * width * n * steps * 2, bytes_accessed=width * n * steps * 20, transcendentals=0),
         name="feed_forward",
-    )(lowered, grad_low, weight_e, weight_c, bias)
+    )(returned, lowered, grad_low, weight_e, weight_c, bias)
 
 
 def attention_kernel(width, heads, tile, step, edge, length, x_ref, qdoc_ref, out_ref, kdoc_ref,
@@ -1176,7 +1260,7 @@
         base = lambda core, part=part: core * hidden_half + part * piece
         feed.append((2, base, 4, part * piece, piece, "ba"))
         feed.append((3, base, 5, part * piece, piece, "ab"))
-    pairs = [[2 * part, 2 * part + 1] for part in range(parts)]
+    pairs = [[4 + 2 * part, 5 + 2 * part] for part in range(parts)]
     inner_t = mixer_inner.T
     lowered, grad_low, last_stream, mix_pre, coeffs, tables, weights, started = mix_forward(
         grid,
@@ -1192,40 +1276,44 @@
         ]
         + feed,
         [[0, 1], [2, 3]],
-        [[4 + n for n in pair] for pair in pairs],
+        pairs,
         [hidden_half] * 2,
         1,
     )
 
     bias_in = take(inbound_bias.astype(F32).reshape(3, width), c * half, half, 1)
-    sent = project(grid, lowered, grad_low, weights, bias_in, tables, own_width)
-    groups = [[2 * k + core for k in range(nz)] for core in range(2)]
-    dealt = lax.all_to_all(sent, "seq", 0, 0, axis_index_groups=groups, tiled=True)
-
-    started_e, started_c, _ = lax.optimization_barrier((*started, sent[0, 0]))
     chunks = [(0, None, n - 4, col, size, order) for _, _, n, col, size, order in feed]
-    weight_e, weight_c = gather(grid, [started_e, started_c], chunks, pairs, 2, "gather_feed")
-    dealt, weight_e, weight_c = lax.optimization_barrier((dealt, weight_e, weight_c))
-
+    dealt, (weight_e, weight_c) = exchange(
+        grid,
+        lowered,
+        grad_low,
+        weights,
+        bias_in,
+        tables,
+        started,
+        chunks,
+        [[2 * part, 2 * part + 1] for part in range(parts)],
+        own_width,
+        2,
+    )
     returned = attention(dealt.reshape(length, 4 * own_width), documents.astype(F32), heads, tokens)
     returned = returned.reshape(nz, both, 4 * own_width)
-    collected = lax.all_to_all(returned, "seq", 0, 0, axis_index_groups=groups, tiled=True)
 
     bias_e = take(expand_bias.astype(F32), c * hidden_half, hidden_half)[None]
-    lowered_seen, _ = lax.optimization_barrier((lowered, returned[0, 0]))
-    feed_part, normed_feed, expand_bias_part, *folded = feed_forward(
-        grid, lowered_seen, grad_low, weight_e, weight_c, bias_e, parts, 3
+    collected, feed_part, normed_feed, expand_bias_part, feed_sums, *rest = feed_forward(
+        grid, returned, lowered, grad_low, weight_e, weight_c, bias_e, parts, 3
     )
 
     def along_z(k):
         return [(s, (s // 2 + k) % nz * 2 + s % 2) for s in range(n_seq)]
 
+    mids, folded = rest[:nz], rest[nz:]
     folded = [folded[0]] + [lax.ppermute(folded[k], "seq", along_z(k)) for k in range(1, nz)]
 
     orders = ("ab", "ba", "ab", "ba")
     bias_out = (outbound_bias.astype(F32) + contract_bias.astype(F32))[None]
-    normed_own, normed_theirs, head_bias_part, layer_out, kept, leaving = unproject(
-        grid, orders, collected, lowered, grad_low, weights, feed_part, normed_feed, last_stream, bias_out, tables, own_width, 4
+    normed_own, normed_theirs, head_bias_part, layer_out, mid_sums, kept, leaving = unproject(
+        grid, orders, mids, collected, lowered, grad_low, weights, feed_part, normed_feed, last_stream, bias_out, tables, own_width, 4
     )
     nb = grid.nb
     over_a = [(d, (d + nb) % n_dp) for d in range(n_dp)]
@@ -1237,7 +1325,7 @@
         history, normed_own, normed_theirs, cotangent, mix_pre, coeffs, [mixer_gain[None], inner_t, mixer_outer, stream_gain]
     )
     smalls = [*small, head_bias_part, expand_bias_part]
-    summed, *owned = finish_sums(grid, orders, kept, [came_a, *came_b], folded, smalls, 5)
+    summed, *owned = finish_sums(grid, orders, kept, [came_a, *came_b], [feed_sums, mid_sums, *folded], smalls, 5)
     layer_out, *small, inbound_grad, outbound_grad, expand_grad, contract_grad = hand_over(summed, layer_out, owned, mix, hidden_width)
     gain_grad, inner_grad, outer_grad, bias_grad, stream_gain_grad, stream_bias_grad, in_bias_grad, out_bias_grad, expand_bias_grad = small
     return (

time: 445 us -> 417 us (0.937)
  Pallas kernels: 412 us -> 397 us
  waiting for transfers between devices: 6.22 us -> 0.01 us
  starting transfers between devices: 14.9 us -> 8.98 us
    pallas_call x1, Pallas kernels: 85.8 us -> 71.3 us  [mix_forward(): pl.pallas_call(functools.partial(mix_kernel, grid, rows, chunks, groups,...]
    pallas_call x1, Pallas kernels: 85.4 us -> 94.9 us  [feed_forward(): pl.pallas_call(functools.partial(feed_kernel, grid, steps), grid=(steps,)...]
    pallas_call x1, Pallas kernels: 55.7 us -> 46.3 us  [finish_sums(): pl.pallas_call(functools.partial(finish_kernel, grid, orders, len(kept)),...]
    all_to_all x2 -> x0, starting transfers between devices: 8.88 us -> none  [the longest x1 4.87 us: on_device(): lax.all_to_all(sent, 'seq', 0, 0, axis_index_groups=groups, tiled=True)]
    pallas_call x1, Pallas kernels: 21.1 us -> 30 us  [unproject(): pl.pallas_call(functools.partial(unproject_kernel, grid, own_width, order...]
    ppermute x3, waiting for transfers between devices: 6.21 us -> 0.01 us  [on_device(): lax.ppermute(folded[k], 'seq', along_z(k))]
    pallas_call x2 -> x1, Pallas kernels: 82 us -> 75.8 us  [exchange(): pl.pallas_call(functools.partial(exchange_kernel, grid, own_width, chunks...]
  transfers between devices with their start and end apart: 7 -> 5, of which waited for: 1 -> 0; matrix products, arithmetic and copies ran while one was open for 0% -> 0% of each run, Pallas kernels for 42% -> 6%
where the time goes in v5:
time: 417 us; the launch traced here: 416 us
  Pallas kernels  397 us (95%)
  starting transfers between devices  8.98 us (2%)
  local copies, waits for them, and re-layouts  5.25 us (1%)
    pallas_call x1, Pallas kernels, feed_forward(): pl.pallas_call(functools.partial(feed_kernel, grid, steps), grid=(steps,)...  94.9 us
    pallas_call x1, Pallas kernels, exchange(): pl.pallas_call(functools.partial(exchange_kernel, grid, own_width, chunks...  75.8 us
    pallas_call x1, Pallas kernels, mix_forward(): pl.pallas_call(functools.partial(mix_kernel, grid, rows, chunks, groups,...  71.3 us
    pallas_call x1, Pallas kernels, attention(): pl.pallas_call(functools.partial(attention_kernel, width, heads, tile, st...  50.7 us
    pallas_call x1, Pallas kernels, finish_sums(): pl.pallas_call(functools.partial(finish_kernel, grid, orders, len(kept)),...  46.3 us
    pallas_call x1, Pallas kernels, unproject(): pl.pallas_call(functools.partial(unproject_kernel, grid, own_width, order...  30 us
    pallas_call x1, Pallas kernels, mix_backward(): pl.pallas_call(unmix_kernel, grid=(tokens // block,), out_shape=[jax.Shap...  25 us
  transfers between devices with their start and end apart: 5, of which 0 were waited for; matrix products, arithmetic and copies ran while one was open for 0% of the time, Pallas kernels for 6%

profile of v5, /device:TPU:0, one launch (start us, length us, event | category | flops | bytes accessed | tf_op | source)
XLA Modules:
  0.0 416.1 jit_solution(13546542760092442120)
XLA Ops:
  0.7 1.3 broadcast_in_dim.16.gain_ref
  1.9 1.3 convert_element_type.13.qdoc_ref
  3.3 0.7 reshape.90
  4.0 1.3 convert_add_fusion
  5.2 1.3 dynamic-slice_convert_fusion
  6.5 0.6 constant_dynamic-slice_fusion.bias_ref
  7.1 71.3 %mix_forward.1 = (bf16[4,2,384,1024]{3,2,1,0:T(8,128)(2,1)}, bf16[2,384,1024]{2,1,0:T(8,128)(2,1)}, f32[384,1024]{1,0:T(8,128)}, f32[384,36]{1,0:T(8,128)}, f32[...) custom-call(bf16[9,1,384,1024]{3,2,1,0:T(8,128)(2,1)} %h_ref.3, ...), custom_call_target="tpu_custom_call" | custom-call | flops 31457280 | bytes 141557760 | tf_op jit(solution)/shard_map/mix_forward/pallas_call | solution.py:414
  78.5 75.8 %exchange.1 = (bf16[4,768,512]{2,1,0:T(8,128)(2,1)}, bf16[2,2,4,64,2048]{4,3,2,1,0:T(8,128)(2,1)}, bf16[2,2,4,64,2048]{4,3,2,1,0:T(8,128)(2,1)}) custom-call(bf16[4,768,1024]{2,1,0:T(8,128)(2,1)} %bitcast.18, bf16[768,1024]{1,0:T(8,128)(2,1)} %bitcast.25, bf16[4,1024,512]{2,1,0:T(8,128)(2,1)} %bitcast.21, ...), custom_call_target="tpu_custom_call", output_to_operand_aliasing={{1}: (7, {}), {2}: (8, {})} | custom-call | flops 3221225472 | bytes 125829120 | tf_op jit(solution)/shard_map/exchange/pallas_call | solution.py:788
  154.3 50.7 %attention.1 = bf16[3072,512]{1,0:T(8,128)(2,1)} custom-call(bf16[3072,512]{1,0:T(8,128)(2,1)} %bitcast.35, f32[1,3072]{1,0:T(1,128)} %convert_element_type.13.qdoc_ref), custom_call_target="tpu_custom_call" | custom-call | flops 28991029248 | bytes 7864320 | tf_op jit(solution)/shard_map/attention/pallas_call | solution.py:1204
  204.9 94.9 %feed_forward.1 = (bf16[4,768,512]{2,1,0:T(8,128)(2,1)}, f32[768,1024]{1,0:T(8,128)}, f32[768,1024]{1,0:T(8,128)}, f32[1,2048]{1,0:T(1,128)}, f32[2,64,512]{2,1,...) custom-call(bf16[4,768,512]{2,1,0:T(8,128)(2,1)} %bitcast.42, ...), custom_call_target="tpu_custom_call" | custom-call | flops 38654705664 | bytes 41943040 | tf_op jit(solution)/shard_map/feed_forward/pallas_call | solution.py:1053
  299.8 0.0 copy-start.7
  299.9 0.0 copy-start.6
  299.9 0.0 copy-start.5
  299.9 30.0 %unproject.1 = (f32[4,384,1024]{2,1,0:T(8,128)}, bf16[4,384,1024]{2,1,0:T(8,128)(2,1)}, f32[3,512]{1,0:T(4,128)}, bf16[384,1024]{1,0:T(8,128)(2,1)}, f32[2,64,10...) custom-call(bf16[2,64,1024]{2,1,0:T(8,128)(2,1)} %get-tuple-element., ...), custom_call_target="tpu_custom_call" | custom-call | flops 12884901888 | bytes 31457280 | tf_op jit(solution)/shard_map/unproject/pallas_call | solution.py:907
  329.9 0.6 collective-permute-start
  330.5 1.5 collective-permute-start.1
  331.9 0.0 copy-done.7
  331.9 4.5 %collective-permute-start.2 = (bf16[2,64,512]{2,1,0:T(8,128)(2,1)S(1)}, bf16[2,64,512]{2,1,0:T(8,128)(2,1)S(1)}, u32[]{:S(2)}, u32[]{:S(2)}) collective-permute-start(bf16[2,64,512]{2,1,0:T(8,128)(2,1)S(1)} %copy-done.7), channel_id=1, source_target_pairs={{0,2},{1,3},{2,4},{3,5},{4,6},{5,7},{6,0},{7,1},{8,10},{9,11},{10,... | collective-permute-start | bytes 393224 | tf_op jit(solution)/shard_map/ppermute | solution.py:1311
  336.4 0.0 copy-done.6
  336.4 1.8 collective-permute-start.3
  338.2 0.0 copy-done.5
  338.2 0.7 collective-permute-start.4
  338.8 25.0 %mix_backward.1 = (f32[9,1,384,1024]{3,2,1,0:T(8,128)}, f32[4,1024]{1,0:T(4,128)}, f32[4,1024]{1,0:T(4,128)}, f32[1,1024]{1,0:T(1,128)}, f32[36,1024]{1,0:T(8,12...) custom-call(bf16[9,1,384,1024]{3,2,1,0:T(8,128)(2,1)} %h_ref.3, ...), custom_call_target="tpu_custom_call" | custom-call | flops 393216000 | bytes 42467328 | tf_op jit(solution)/shard_map/mix_backward/pallas_call | solution.py:540
  363.9 0.0 collective-permute-done.2.refs_9_
  363.9 0.0 copy-start.2
  363.9 0.0 collective-permute-done.3.refs_10_
  363.9 0.0 copy-start.3
  363.9 0.0 collective-permute-done.4.refs_11_
  363.9 0.0 copy-start.4
  363.9 0.0 collective-permute-done.refs_4_
  364.0 0.0 copy-start
  364.0 0.0 collective-permute-done.1.refs_5_
  364.0 0.0 copy-start.1
  364.0 0.6 copy-done.2
  364.6 0.0 copy-done.3
  364.6 0.0 copy-done.4
  364.6 0.4 copy-done
  365.0 0.4 copy-done.1
  365.4 46.3 %finish_sums.1 = (f32[512,128]{1,0:T(8,128)}, f32[32,3072]{1,0:T(8,128)}, f32[32,1024]{1,0:T(8,128)}, f32[32,4096]{1,0:T(8,128)}, f32[32,4096]{1,0:T(8,128)}) custom-call(bf16[2,4,64,512]{3,2,1,0:T(8,128)(2,1)} %get-tuple-element.100.refs_0_, bf16[2,4,64,512]{3,2,1,0:T(8,128)(2,1)} %get-tuple-element.101.refs_1_, ...), custom_call_target="tpu_custom_call" | custom-call | bytes 104857600 | tf_op jit(solution)/shard_map/finish_sums/pallas_call | solution.py:670
  411.6 3.2 hand_over.1
  414.8 1.3 copy.38
Async XLA Ops:
  299.8 32.1 %copy-start.7 = (bf16[2,64,512]{2,1,0:T(8,128)(2,1)S(1)}, bf16[2,64,512]{2,1,0:T(8,128)(2,1)}, u32[]{:S(2)}) copy-start(bf16[2,64,512]{2,1,0:T(8,128)(2,1)} %get-tuple-element.109) | copy-start | bytes 393220
  299.9 36.6 %copy-start.6 = (bf16[2,64,512]{2,1,0:T(8,128)(2,1)S(1)}, bf16[2,64,512]{2,1,0:T(8,128)(2,1)}, u32[]{:S(2)}) copy-start(bf16[2,64,512]{2,1,0:T(8,128)(2,1)} %get-tuple-element.110) | copy-start | bytes 393220
  299.9 38.3 %copy-start.5 = (bf16[2,64,512]{2,1,0:T(8,128)(2,1)S(1)}, bf16[2,64,512]{2,1,0:T(8,128)(2,1)}, u32[]{:S(2)}) copy-start(bf16[2,64,512]{2,1,0:T(8,128)(2,1)} %get-tuple-element.111) | copy-start | bytes 393220
  329.9 34.1 %collective-permute-start = (bf16[2,2,4,64,512]{4,3,2,1,0:T(8,128)(2,1)}, bf16[2,2,4,64,512]{4,3,2,1,0:T(8,128)(2,1)S(1)}, u32[]{:S(2)}, u32[]{:S(2)}) collective-permute-start(bf16[2,2,4,64,512]{4,3,2,1,0:T(8,128)(2,1)} %get-tuple-element.104), channel_id=1, source_target_pairs={{0,16},{8,24},{16,0},{24,8},{1,17},{9,25},{17,1},{25,9},{2,18},{10... | collective-permute-start | bytes 3145736 | tf_op jit(solution)/shard_map/ppermute | solution.py:1321
  330.5 33.5 %collective-permute-start.1 = (bf16[2,2,4,64,512]{4,3,2,1,0:T(8,128)(2,1)}, bf16[2,2,4,64,512]{4,3,2,1,0:T(8,128)(2,1)S(1)}, u32[]{:S(2)}, u32[]{:S(2)}) collective-permute-start(bf16[2,2,4,64,512]{4,3,2,1,0:T(8,128)(2,1)} %get-tuple-element.105), channel_id=1, source_target_pairs={{0,8},{8,0},{16,24},{24,16},{1,9},{9,1},{17,25},{25,17},{2,10},{10... | collective-permute-start | bytes 3145736 | tf_op jit(solution)/shard_map/ppermute | solution.py:1322
  331.9 31.9 %collective-permute-start.2 = (bf16[2,64,512]{2,1,0:T(8,128)(2,1)S(1)}, bf16[2,64,512]{2,1,0:T(8,128)(2,1)S(1)}, u32[]{:S(2)}, u32[]{:S(2)}) collective-permute-start(bf16[2,64,512]{2,1,0:T(8,128)(2,1)S(1)} %copy-done.7), channel_id=1, source_target_pairs={{0,2},{1,3},{2,4},{3,5},{4,6},{5,7},{6,0},{7,1},{8,10},{9,11},{10,... | collective-permute-start | bytes 393224 | tf_op jit(solution)/shard_map/ppermute | solution.py:1311
  336.4 27.5 %collective-permute-start.3 = (bf16[2,64,512]{2,1,0:T(8,128)(2,1)S(1)}, bf16[2,64,512]{2,1,0:T(8,128)(2,1)S(1)}, u32[]{:S(2)}, u32[]{:S(2)}) collective-permute-start(bf16[2,64,512]{2,1,0:T(8,128)(2,1)S(1)} %copy-done.6), channel_id=1, source_target_pairs={{0,4},{1,5},{2,6},{3,7},{4,0},{5,1},{6,2},{7,3},{8,12},{9,13},{10,... | collective-permute-start | bytes 393224 | tf_op jit(solution)/shard_map/ppermute | solution.py:1311
  338.2 25.8 %collective-permute-start.4 = (bf16[2,64,512]{2,1,0:T(8,128)(2,1)S(1)}, bf16[2,64,512]{2,1,0:T(8,128)(2,1)S(1)}, u32[]{:S(2)}, u32[]{:S(2)}) collective-permute-start(bf16[2,64,512]{2,1,0:T(8,128)(2,1)S(1)} %copy-done.5), channel_id=1, source_target_pairs={{0,6},{1,7},{2,0},{3,1},{4,2},{5,3},{6,4},{7,5},{8,14},{9,15},{10,... | collective-permute-start | bytes 393224 | tf_op jit(solution)/shard_map/ppermute | solution.py:1311
  363.9 0.7 copy-start.2
  363.9 0.7 copy-start.3
  363.9 0.7 copy-start.4
  364.0 1.0 copy-start
  364.0 1.4 copy-start.1

commit v6 on v5

--- a/solution.py
+++ b/solution.py
@@ -18,6 +18,7 @@
 F32 = jnp.float32
 BF16 = jnp.bfloat16
 VMEM_LIMIT = 56 * 1024 * 1024
+STEPS = 4
 
 
 def inner(left, right):
@@ -79,10 +80,9 @@
         pl.semaphore_wait(barrier, len(found))
 
 
-def remote(src, dst, send, recv, device):
-    return pltpu.make_async_remote_copy(
-        src_ref=src, dst_ref=dst, send_sem=send, recv_sem=recv, device_id=device, device_id_type=MESH
-    )
+def row(ref):
+    value = ref[...].astype(F32)
+    return jnp.concatenate([value[l : l + 1] for l in range(value.shape[0])], axis=1)
 
 
 def remote(src, dst, send, recv, device):
@@ -180,16 +180,18 @@
             for group in groups:
                 self.begin(group, 0)
 
+        enter = [u if u < len(whole) else len(whole) + (u - len(whole)) // 2 for u in range(len(groups))]
+
         def tick(now):
             for u in range(len(groups)):
-                if 0 <= now - u <= (nz if u < len(whole) else nz - 1):
-                    advance(u, now - u)
+                if 0 <= now - enter[u] <= (nz if u < len(whole) else nz - 1):
+                    advance(u, now - enter[u])
 
         def last():
             for group in whole:
                 self.end(group, 3)
 
-        return [first] + [functools.partial(tick, now) for now in range(len(groups) + nz)] + [last]
+        return [first] + [functools.partial(tick, now) for now in range(max(enter) + nz + 1)] + [last]
 
 
 def gather_sems(grid, chunks):
@@ -378,7 +380,7 @@
 
     last = h_ref[h_ref.shape[0] - 1, 0].astype(F32)
     r = lax.rsqrt(jnp.mean(last * last, axis=1, keepdims=True) + EPS)
-    scaled_low = (last * r * gain_ref[...].astype(F32)).astype(BF16)
+    scaled_low = (last * r * row(gain_ref)).astype(BF16)
     pre = against(scaled_low, inner_ref[...])
     pre_ref[...] = pre
     coeffs = product((pre * phi(pre)).astype(BF16), outer_ref[...]) + bias_ref[...].astype(F32)
@@ -504,7 +506,7 @@
     mpg = (against(cg_low, outer_ref[...]) * gelu_slope(pre)).astype(BF16)
     last = h_ref[hist - 1, 0].astype(F32)
     r = lax.rsqrt(jnp.mean(last * last, axis=1, keepdims=True) + EPS)
-    gain = gain_ref[...].astype(F32)
+    gain = row(gain_ref)
     scaled_ref[at, :] = (last * r * gain).astype(BF16)
     mpg_ref[at, :] = mpg
     hidden_ref[at, :] = (pre * phi(pre)).astype(BF16)
@@ -561,7 +563,7 @@
     nz = grid.nz
     kept, refs = refs[:n_kept], refs[n_kept:]
     came_a, came_b, refs = refs[:1], refs[1 : grid.nb], refs[grid.nb :]
-    sums_refs, folded, refs = refs[:2], refs[2 : 2 + nz], refs[2 + nz :]
+    sum_ref, folded, refs = refs[0], refs[1 : 1 + nz], refs[1 + nz :]
     sgg_ref, sbg_ref, gg_ref, ig_ref, og_ref, bg_ref, ob_ref, hb_ref, eb_ref = refs[:9]
     done_ref, outs, refs = refs[9], refs[10:14], refs[14:]
     first, second, third, final, refs = refs[:4], refs[4:8], refs[8:12], refs[12:18], refs[18:]
@@ -592,10 +594,8 @@
             pltpu.make_async_copy(final[t].at[c], spot, local_sem.at[t]),
         ]
 
-    sums.greet()
-    for t in range(4):
-
-        def step(i, carry, t=t):
+    def add_first(t):
+        def step(i, carry):
             o, j = i // nz, lax.rem(i, nz)
             total = kept[t][o, j].astype(F32)
             for piece in came_a if orders[t] == "ab" else came_b:
@@ -604,9 +604,15 @@
             return carry
 
         lax.fori_loop(0, first[t].shape[1] * nz, step, 0)
+
+    sums.greet()
+    add_first(0)
+    add_first(1)
     pl.semaphore_wait(pltpu.get_barrier_semaphore(), sums.count - 1)
     for t in range(2):
         start(copies(t, 1))
+    add_first(2)
+    add_first(3)
 
     mine = sums.mine
     mine[...] = jnp.zeros_like(mine)
@@ -631,7 +637,7 @@
         for piece in folded[1:]:
             total = total + piece[t].astype(F32)
         at = 0
-        for piece in [ref[t] for ref in sums_refs] + [total]:
+        for piece in (sum_ref[t], total):
             n = piece.shape[1]
             final[4 + t][:, :, at : at + n] = piece.reshape(2, -1, n)
             at += n
@@ -699,6 +705,7 @@
     wl, padded, hidden_rows = width // 128, -(-mix // 8) * 8, hidden_width // 256
     firsts, _ = small_rows(width, mix, hidden_width)
     placed_ref[...] = out_ref[...]
+    outs, again = outs[:4], outs[4]
     for src, dst in zip(owned, outs):
         dst[...] = src[...]
     for l in range(wl):
@@ -707,7 +714,7 @@
         small[1][:, lanes] = done[firsts[1] + l * padded : firsts[1] + l * padded + mix, :]
         small[4][:, lanes] = done[firsts[4] + 4 * l : firsts[4] + 4 * l + 4, :]
         small[5][:, lanes] = done[firsts[5] + 4 * l : firsts[5] + 4 * l + 4, :]
-        small[7][:, lanes] = done[firsts[7] + l : firsts[7] + l + 1, :]
+        small[7][:, lanes] = again[:, lanes] = done[firsts[7] + l : firsts[7] + l + 1, :]
     small[2][...] = done[firsts[2] : firsts[2] + mix, 0:mix]
     small[3][...] = done[firsts[3] : firsts[3] + 1, 0:mix]
     for l in range(3 * wl):
@@ -724,15 +731,16 @@
         functools.partial(hand_kernel, mix, hidden_width),
         out_shape=[jax.ShapeDtypeStruct(layer_out.shape, BF16)]
         + [jax.ShapeDtypeStruct(shape, F32) for shape in small]
-        + [jax.ShapeDtypeStruct(x.shape, F32) for x in owned],
+        + [jax.ShapeDtypeStruct(x.shape, F32) for x in owned]
+        + [jax.ShapeDtypeStruct((1, width), F32)],
         in_specs=[vmem] * 6,
-        out_specs=[vmem] * 14,
+        out_specs=[vmem] * 15,
         name="hand_over",
     )(summed, layer_out, *owned)
 
 
 def exchange_kernel(grid, width, chunks, groups, low_ref, g_ref, w_ref, bias_ref, cos_ref, above_ref, below_ref, _e, _c,
-                    dealt_ref, e_ref, c_ref, sent_ref, deal_send, deal_recv, local_sem, send_sem, recv_sem):
+                    dealt_ref, e_ref, c_ref, sent_ref, bias_full, deal_send, deal_recv, local_sem, send_sem, recv_sem):
     i, steps = pl.program_id(0), pl.num_programs(0)
     a, b, z, c = place = grid.here()
     nz = grid.nz
@@ -750,13 +758,20 @@
         grid.greet(*place)
         for group in groups:
             work.begin(group, 2)
+        bias_full[...] = bias_ref[...].astype(F32)
 
     wide = w_ref.shape[2]
     each = wide // width
     tables = [jnp.concatenate([t[...]] * max(wide // 128, 1), axis=1) for t in (cos_ref, above_ref, below_ref)]
-    q = rotate(product(low_ref[0], w_ref[0]) + bias_ref[0:1, :], tables, 1.0)
-    k = rotate(product(low_ref[1], w_ref[1]) + bias_ref[1:2, :], tables, 1.0)
-    v = product(low_ref[2], w_ref[2]) + bias_ref[2:3, :]
+    third = bias_full.shape[0] // 3
+
+    def bias(n):
+        first_row = n * third + c * (third // 2) + i * (wide // 128)
+        return jnp.concatenate([bias_full[pl.ds(first_row + l, 1), :] for l in range(wide // 128)], axis=1)
+
+    q = rotate(product(low_ref[0], w_ref[0]) + bias(0), tables, 1.0)
+    k = rotate(product(low_ref[1], w_ref[1]) + bias(1), tables, 1.0)
+    v = product(low_ref[2], w_ref[2]) + bias(2)
     g = product(g_ref[...], w_ref[3])
     for n, x in enumerate((q, k, v, g)):
         x = x.astype(BF16)
@@ -793,7 +808,7 @@
             pl.BlockSpec((3, both, width), lambda i: (0, 0, 0)),
             whole,
             pl.BlockSpec((4, width, wide), lambda i: (0, 0, i)),
-            pl.BlockSpec((3, wide), lambda i: (0, i)),
+            whole,
         ]
         + [whole] * 3
         + [anywhere] * 2,
@@ -801,6 +816,7 @@
         input_output_aliases={7: 1, 8: 2},
         scratch_shapes=[
             pltpu.VMEM((nz, both, 4 * own_width), BF16),
+            pltpu.VMEM(biases.shape, F32),
             pltpu.SemaphoreType.DMA((nz,)),
             pltpu.SemaphoreType.DMA((nz,)),
             *gather_sems(grid, chunks),
@@ -813,12 +829,15 @@
 
 
 def unproject_kernel(grid, width, orders, *all_refs):
-    mids, all_refs = all_refs[: grid.nz], all_refs[grid.nz :]
-    (col_ref, low_ref, g_ref, w_ref, feed_ref, normed_ref, last_ref, bias_ref, cos_ref, above_ref,
+    nz = grid.nz
+    mids, lates, last_parts, all_refs = all_refs[:nz], all_refs[nz : 2 * nz], all_refs[2 * nz : 2 * nz + 2], all_refs[2 * nz + 2 :]
+    (col_ref, low_ref, g_ref, w_ref, feed_ref, normed_ref, last_ref, bias_ref, bias2_ref, cos_ref, above_ref,
      below_ref, own_ref, theirs_ref, hb_ref, out_ref, sum_ref, *refs) = all_refs
-    na, nb, nz = grid.na, grid.nb, grid.nz
+    nb = grid.nb
+    lasts, refs = refs[:nz], refs[nz:]
     kept, over_a, over_b, refs = refs[:4], refs[4], refs[5 : 4 + nb], refs[4 + nb :]
-    grad_ref, sending_ref, partial_ref, mine_ref, arrived_ref, along_ref, split_sem, send_sem, recv_sem, along_send, along_recv = refs
+    grad_ref, sending_ref, partial_ref, mine_ref, arrived_ref, along_ref, split_sem, send_sem, recv_sem, along_send, along_recv = refs[:11]
+    keep_refs, firsts, seconds, (fold_send, fold_recv, late_sem) = refs[11:13], refs[13:15], refs[15:17], refs[17:]
     i = pl.program_id(0)
     a, b, z, c = grid.here()
     tokens = out_ref.shape[0]
@@ -837,6 +856,30 @@
             remote(mids[k], along_ref.at[k - 1], along_send.at[k - 1], along_recv.at[k - 1], grid.device(a, b, lax.rem(z + k, nz), c))
             for k in range(1, nz)
         ]
+
+    def fold(t, stage):
+        if stage < 2:
+            order = ("ab", "ba")[t]
+            found = fold_copies(grid, (a, b, z, c), order, stage, last_parts[t], firsts[t], seconds[t], (fold_send.at[t], fold_recv.at[t]))
+            if stage == 0:
+                kept_part = last_parts[t].at[a] if order == "ab" else last_parts[t].at[:, b]
+                found.append(pltpu.make_async_copy(kept_part, keep_refs[t], late_sem.at[t]))
+            return found
+        n = seconds[t].shape[-1]
+        return [
+            pltpu.make_async_copy(seconds[t].at[0, lax.rem(z + k, nz)], lasts[k].at[t, :, pl.ds(n, n)], late_sem.at[2 + t * nz + k])
+            for k in range(nz)
+        ]
+
+    def settle(stage):
+        for t in range(2):
+            finish(fold(t, stage))
+            fold_add(grid, (a, b, z, c), ("ab", "ba")[t], stage, keep_refs[t], firsts[t], seconds[t])
+            start(fold(t, stage + 1))
+
+    def place_lates():
+        n = lates[0].shape[-1]
+        return [pltpu.make_async_copy(lates[k], lasts[k].at[:, :, pl.ds(0, n)], late_sem.at[2 + 2 * nz + k]) for k in range(nz)]
 
     def split(k):
         grad = grad_ref.at[k]
@@ -857,14 +900,17 @@
     @pl.when(i == 0)
     def _():
         grid.greet(a, b, z, c)
+        for t in range(2):
+            start(fold(t, 0))
         start(along())
+        start(place_lates())
         mine_ref[...] = piece(0)
         partial_ref[...] = against(mine_ref[their_rows, :], w_ref[0]) + feed_ref[their_rows, :]
         sending_ref[3] = normed_ref[their_rows, :].astype(BF16)
         start(swap_out())
         start(swap(3))
         own_ref[0] = normed_ref[own_rows, :]
-        out = against(mine_ref[own_rows, :], w_ref[0]) + feed_ref[own_rows, :] + last_ref[...] + bias_ref[...]
+        out = against(mine_ref[own_rows, :], w_ref[0]) + feed_ref[own_rows, :] + last_ref[...] + (row(bias_ref) + row(bias2_ref))
         keep(3, inner(g_ref[...], mine_ref[...]))
         finish(swap_out())
         out_ref[...] = (out + arrived_ref[...]).astype(BF16)
@@ -873,6 +919,8 @@
 
         @pl.when(i == k + 1)
         def _(k=k):
+            if k == 2:
+                settle(0)
             grad = piece(k + 1).astype(F32)
             if k < 2:
                 tables = [jnp.concatenate([t[...]] * (grad.shape[1] // 128), axis=1) for t in (cos_ref, above_ref, below_ref)]
@@ -887,18 +935,24 @@
                 for n in range(4):
                     finish(swap(n))
                     finish(split(n))
+                settle(1)
                 finish(along())
                 total = mids[0][...].astype(F32)
                 for n in range(nz - 1):
                     total = total + along_ref[n].astype(F32)
                 sum_ref[...] = total
-
-
-def unproject(grid, orders, mids, collected, lowered, grad_low, weights, feed_part, normed_feed, last_stream, bias, tables, own_width, collective_id):
+                for t in range(2):
+                    finish(fold(t, 2))
+                finish(place_lates())
+
+
+def unproject(grid, orders, mids, lates, last_parts, collected, lowered, grad_low, weights, feed_part, normed_feed, last_stream, biases, tables, own_width, collective_id):
     tokens, width = last_stream.shape
     both, half = 2 * tokens, width // 2
     na, nb, nz = grid.na, grid.nb, grid.nz
     rows = width // (na * nb * nz)
+    n = lates[0].shape[-1]
+    folds = [fold_scratch(grid, order, rows, n) for order in ("ab", "ba")]
     whole = pl.BlockSpec(memory_space=pltpu.VMEM)
     anywhere = pl.BlockSpec(memory_space=pl.ANY)
     turn = lambda i: lax.rem(i + 3, 4)
@@ -914,17 +968,20 @@
             jax.ShapeDtypeStruct((tokens, width), BF16),
             jax.ShapeDtypeStruct(mids[0].shape, F32),
         ]
+        + [jax.ShapeDtypeStruct((2, rows, 2 * n), BF16)] * nz
         + split_shapes
         + sent_shapes,
         in_specs=[whole]
         + [anywhere] * (nz - 1)
+        + [whole] * nz
+        + [anywhere] * 2
         + [
             whole,
             pl.BlockSpec((1, both, width), lambda i: (jnp.maximum(i - 1, 0), 0, 0)),
             whole,
             pl.BlockSpec((1, width, half), lambda i: (turn(i), 0, 0)),
         ]
-        + [whole] * 7,
+        + [whole] * 8,
         out_specs=[
             pl.BlockSpec((1, tokens, width), lambda i: (turn(i), 0, 0)),
             anywhere,
@@ -932,7 +989,7 @@
             pl.BlockSpec((tokens, width), lambda i: (0, 0)),
             pl.BlockSpec(mids[0].shape, lambda i: (0, 0, 0)),
         ]
-        + [anywhere] * (len(split_shapes) + len(sent_shapes)),
+        + [anywhere] * (nz + len(split_shapes) + len(sent_shapes)),
         scratch_shapes=[
             pltpu.VMEM((4, na, nb, nz, rows, half), BF16),
             pltpu.VMEM((4, tokens, width), BF16),
@@ -945,21 +1002,29 @@
             pltpu.SemaphoreType.DMA((5,)),
             pltpu.SemaphoreType.DMA((nz - 1,)),
             pltpu.SemaphoreType.DMA((nz - 1,)),
+            *[o for o, _, _ in folds],
+            *[f for _, f, _ in folds],
+            *[f for _, _, f in folds],
+            pltpu.SemaphoreType.DMA((2, nz + nb)),
+            pltpu.SemaphoreType.DMA((2, nz + nb)),
+            pltpu.SemaphoreType.DMA((2 + 3 * nz,)),
         ],
         compiler_params=pltpu.CompilerParams(collective_id=collective_id, has_side_effects=True, vmem_limit_bytes=VMEM_LIMIT),
         cost_estimate=pl.CostEstimate(flops=32 * both * width * half, bytes_accessed=40 * both * width, transcendentals=0),
         name="unproject",
-    )(*mids, collected, lowered, grad_low, weights, feed_part, normed_feed, last_stream, bias, *tables)
+    )(*mids, *lates, *last_parts, collected, lowered, grad_low, weights, feed_part, normed_feed, last_stream, *biases, *tables)
     own, theirs, head_bias, layer_out, mid_sums = results[:5]
-    return own, theirs, head_bias, layer_out, mid_sums, results[5:9], results[9:]
-
-
-def feed_kernel(grid, steps, back_ref, low_ref, g_ref, we_ref, wc_ref, bias_ref, collected_ref, feed_ref, normed_ref, eb_ref, sum_ref, *refs):
+    lasts, results = results[5 : 5 + nz], results[5 + nz :]
+    return own, theirs, head_bias, layer_out, mid_sums, lasts, results[:4], results[4:]
+
+
+def feed_kernel(grid, steps, back_ref, low_ref, g_ref, we_ref, wc_ref, bias_ref, collected_ref, feed_ref, normed_ref, eb_ref, *refs):
     nz = grid.nz
-    mids, outs, refs = refs[:nz], refs[nz : 2 * nz], refs[2 * nz :]
+    groups = steps - 1
+    mids, outs, whole_outs, refs = refs[:nz], refs[nz : 2 * nz], refs[2 * nz : 2 * nz + 2], refs[2 * nz + 2 :]
     parts, refs = refs[: 2 * steps], refs[2 * steps :]
-    first, second, refs = refs[: 2 * steps], refs[2 * steps : 4 * steps], refs[4 * steps :]
-    third, (send_sem, recv_sem, out_sem, back_send, back_recv) = refs[:2], refs[2:]
+    first, second, refs = refs[: 2 * groups], refs[2 * groups : 4 * groups], refs[4 * groups :]
+    bias_full, send_sem, recv_sem, out_sem, back_send, back_recv = refs
     i = pl.program_id(0)
     a, b, z, c = place = grid.here()
     orders = ["ab", "ba"] * steps
@@ -968,14 +1033,14 @@
         if stage < 2:
             return fold_copies(grid, place, orders[t], stage, parts[t], first[t], second[t], (send_sem.at[t], recv_sem.at[t]))
         along = [lax.rem(z + k, nz) for k in range(nz)]
-        if t >= 2:
-            n = parts[t].shape[-1]
-            spot = outs if t >= 2 * steps - 2 else [mid.at[:, :, pl.ds((t // 2 - 1) * n, n)] for mid in mids]
-            return [pltpu.make_async_copy(second[t].at[0, along[k]], spot[k].at[t % 2], out_sem.at[t, k]) for k in range(nz)]
-        return [
-            remote(second[t].at[0, along[k]], third[t].at[k - 1], send_sem.at[t, k], recv_sem.at[t, k], grid.device(a, b, along[k], c))
-            for k in range(1, nz)
-        ]
+        u, n = t // 2, parts[t].shape[-1]
+        late = u == groups - 1
+        cols = pl.ds(0 if late else u * n, n)
+        spot = outs if late else mids
+        return [pltpu.make_async_copy(second[t].at[0, along[k]], spot[k].at[t % 2, :, cols], out_sem.at[t, k]) for k in range(nz)]
+
+    def last_parts():
+        return [pltpu.make_async_copy(parts[2 * groups + k], whole_outs[k], out_sem.at[2 * groups + k, 0]) for k in range(2)]
 
     def begin(u):
         for t in (2 * u, 2 * u + 1):
@@ -988,15 +1053,10 @@
                 own = parts[t].at[a] if orders[t] == "ab" else parts[t].at[:, b]
                 fold_add(grid, place, orders[t], stage, own, first[t], second[t])
                 start(copies(t, stage + 1))
-            elif u == 0:
-                total = second[t][0, z].astype(F32)
-                for k in range(nz - 1):
-                    total = total + third[t][k].astype(F32)
-                sum_ref[t % 2] = total
 
     def turn(u):
         for stage in range(3):
-            if 0 <= u - stage < steps:
+            if 0 <= u - stage < groups:
                 end(u - stage, stage)
 
     def backs():
@@ -1010,11 +1070,15 @@
     def _():
         grid.greet(*place)
         start(backs())
+        bias_full[...] = bias_ref[...].astype(F32)
         feed_ref[...] = jnp.zeros_like(feed_ref)
         normed_ref[...] = jnp.zeros_like(normed_ref)
 
     low, grad, expand, contract = low_ref[0], g_ref[...], we_ref[...], wc_ref[...]
-    expanded = product(low, expand) + bias_ref[...]
+    wide = expand.shape[1] // 128
+    first_row = c * (bias_full.shape[0] // 2) + i * wide
+    bias = jnp.concatenate([bias_full[pl.ds(first_row + l, 1), :] for l in range(wide)], axis=1)
+    expanded = product(low, expand) + bias
     share = phi(expanded)
     hidden = (expanded * share).astype(BF16)
     slope = share + expanded * jnp.exp(-0.5 * expanded * expanded) * (1.0 / math.sqrt(2.0 * math.pi))
@@ -1031,12 +1095,16 @@
         def _(u=u):
             parts[2 * u][...] = expand_grad.reshape(parts[2 * u].shape)
             parts[2 * u + 1][...] = hidden_grad.reshape(parts[2 * u + 1].shape)
-            begin(u)
+            if u < groups:
+                begin(u)
+            else:
+                start(last_parts())
             if u >= 2:
                 turn(u - 2)
             if u == steps - 1:
-                for v in range(max(steps - 2, 0), steps + 2):
+                for v in range(max(steps - 2, 0), groups + 2):
                     turn(v)
+                finish(last_parts())
                 finish(backs())
 
 
@@ -1058,30 +1126,29 @@
             jax.ShapeDtypeStruct((both, width), F32),
             jax.ShapeDtypeStruct((both, width), F32),
             jax.ShapeDtypeStruct((1, n * steps), F32),
-            jax.ShapeDtypeStruct((2, rows, n), F32),
         ]
         + [jax.ShapeDtypeStruct((2, rows, n * (steps - 2)), BF16)] * nz
-        + [jax.ShapeDtypeStruct((2, rows, n), BF16)] * nz,
+        + [jax.ShapeDtypeStruct((2, rows, n), BF16)] * nz
+        + [jax.ShapeDtypeStruct((na, nb, nz, rows, n), BF16)] * 2,
         in_specs=[
             pl.BlockSpec(memory_space=pltpu.VMEM),
             pl.BlockSpec((1, both, width), lambda i: (3, 0, 0)),
             whole(both, width),
             cols(width),
             cols(width),
-            cols(1),
+            whole(*bias.shape),
         ],
         out_specs=[
             pl.BlockSpec(memory_space=pl.ANY),
             whole(both, width),
             whole(both, width),
             cols(1),
-            whole(2, rows, n),
         ]
-        + [pl.BlockSpec(memory_space=pl.ANY)] * (2 * nz),
+        + [pl.BlockSpec(memory_space=pl.ANY)] * (2 * nz + 2),
         scratch_shapes=[pltpu.VMEM((na, nb, nz, rows, n), BF16)] * (2 * steps)
-        + [f for _, f, _ in folds]
-        + [s for _, _, s in folds]
-        + [pltpu.VMEM((nz - 1, rows, n), BF16)] * 2
+        + [f for _, f, _ in folds[:-2]]
+        + [s for _, _, s in folds[:-2]]
+        + [pltpu.VMEM(bias.shape, F32)]
         + [sem, sem, pltpu.SemaphoreType.DMA((2 * steps, nz)), pltpu.SemaphoreType.DMA((nz,)), pltpu.SemaphoreType.DMA((nz,))],
         compiler_params=pltpu.CompilerParams(collective_id=collective_id, has_side_effects=True, vmem_limit_bytes=VMEM_LIMIT),
         cost_estimate=pl.CostEstimate(flops=12 * both * width * n * steps * 2, bytes_accessed=width * n * steps * 20, transcendentals=0),
@@ -1089,7 +1156,7 @@
     )(returned, lowered, grad_low, weight_e, weight_c, bias)
 
 
-def attention_kernel(width, heads, tile, step, edge, length, x_ref, qdoc_ref, out_ref, kdoc_ref,
+def attention_kernel(width, heads, tile, edge, length, x_ref, qdoc_ref, out_ref, kdoc_ref,
                      s_ref, kt_ref, vt_ref, ot_ref, dqt_ref, dka_ref, dva_ref, top_ref):
     i = pl.program_id(0)
     tiles = length // tile
@@ -1101,7 +1168,7 @@
         def turn(j, carry):
             at = pl.ds(pl.multiple_of(j * tile, tile), tile)
             kt_ref[:, at] = x_ref[at, width : 2 * width].T
-            kdoc_ref[at, :] = jnp.broadcast_to(qdoc_ref[:, at], (128, tile)).T
+            kdoc_ref[at, :] = jnp.broadcast_to(qdoc_ref[:, at].astype(F32), (128, tile)).T
             vt_ref[:, at] = x_ref[at, 2 * width : 3 * width].T
             return carry
         lax.fori_loop(0, tiles, turn, 0)
@@ -1114,54 +1181,60 @@
     zero = jnp.zeros((), BF16)
     queries_t = [jnp.where(subs == h, query_t, zero) for h in range(heads)]
     grads_t = [jnp.where(subs == h, grad_t, zero) for h in range(heads)]
-    all_queries = jnp.concatenate([jnp.where(lanes == h, query, zero) for h in range(heads)], axis=0)
-    all_grads = jnp.concatenate([jnp.where(lanes == h, grad, zero) for h in range(heads)], axis=0)
-    qdoc = qdoc_ref[:, rows]
-    qpos = i * tile + lax.broadcasted_iota(jnp.int32, (step, tile), 1)
-    head_edge = -(-edge // step)
+    spread_queries = [jnp.where(lanes == h, query, zero) for h in range(heads)]
+    spread_grads = [jnp.where(lanes == h, grad, zero) for h in range(heads)]
+    qdoc = qdoc_ref[:, rows].astype(F32)
+    head_edge = -(-edge // tile)
     tail_edge = (length - edge) // tile
-    per = tile // step
-    count = (i + 1) * per
+    half = tile // 2
+    corners = [(0, half, 0), (half, half, half)]
     ot_ref[...] = jnp.zeros_like(ot_ref)
     dqt_ref[...] = jnp.zeros_like(dqt_ref)
     top_ref[...] = jnp.full_like(top_ref, NEG)
 
     def fold(x, f):
-        return f(x.reshape(step // 8, 8, tile), axis=0)
+        return f(x.reshape(x.shape[0] // 8, 8, x.shape[1]), axis=0)
+
+    def score(first, size, left, documents, causal):
+        at = pl.ds(pl.multiple_of(first, size), size)
+        keys = x_ref[at, width : 2 * width]
+        wide = tile - left
+        if documents:
+            allowed = jnp.concatenate([kdoc_ref[at, :]] * (wide // 128), axis=1) == qdoc[:, left:]
+        if causal:
+            allowed &= lax.broadcasted_iota(jnp.int32, (size, wide), 0) <= lax.broadcasted_iota(jnp.int32, (size, wide), 1)
+        for h in range(heads):
+            s = product(keys, queries_t[h][:, left:])
+            if documents:
+                s = jnp.where(allowed, s, NEG)
+            s_ref[h, at, left:] = s
+            top_ref[h, :, left:] = jnp.maximum(top_ref[h, :, left:], fold(s, jnp.max))
 
     def scores(j, carry):
-        at = pl.ds(pl.multiple_of(j * step, step), step)
-        checked = (j >= i * per) | (j < head_edge) | (i >= tail_edge)
-        def run(mask):
-            keys = x_ref[at, width : 2 * width]
-            if mask:
-                kdoc = jnp.concatenate([kdoc_ref[at, :]] * (tile // 128), axis=1)
-                kpos = j * step + lax.broadcasted_iota(jnp.int32, (step, tile), 0)
-                allowed = (kdoc == qdoc) & (kpos <= qpos)
-            for h in range(heads):
-                s = product(keys, queries_t[h])
-                if mask:
-                    s = jnp.where(allowed, s, NEG)
-                s_ref[h, at, :] = s
-                top_ref[h] = jnp.maximum(top_ref[h], fold(s, jnp.max))
-        pl.when(checked)(lambda: run(True))
-        pl.when(jnp.logical_not(checked))(lambda: run(False))
+        checked = (j < head_edge) | (i >= tail_edge)
+        pl.when(checked)(lambda: score(j * tile, tile, 0, True, False))
+        pl.when(jnp.logical_not(checked))(lambda: score(j * tile, tile, 0, False, False))
         return carry
-    lax.fori_loop(0, count, scores, 0)
+
+    lax.fori_loop(0, i, scores, 0)
+    for first, size, left in corners:
+        score(i * tile + first, size, left, True, True)
     tops = [jnp.max(top_ref[h], axis=0, keepdims=True) for h in range(heads)]
-
-    def weigh(j, totals):
-        at = pl.ds(pl.multiple_of(j * step, step), step)
-        new = []
+    top_ref[...] = jnp.zeros_like(top_ref)
+
+    def weigh(first, size, left):
+        at = pl.ds(pl.multiple_of(first, size), size)
         for h in range(heads):
             own = slice(h * HEAD_DIM, (h + 1) * HEAD_DIM)
-            weights = jnp.exp(s_ref[h, at, :] - tops[h])
-            s_ref[h, at, :] = weights
-            new.append(totals[h] + fold(weights, jnp.sum))
-            ot_ref[own, :] += product(vt_ref[own, at], weights.astype(BF16))
-        return new
-    totals = lax.fori_loop(0, count, weigh, [jnp.zeros((8, tile), F32)] * heads)
-    inverse = [1.0 / jnp.sum(t, axis=0, keepdims=True) for t in totals]
+            weights = jnp.exp(s_ref[h, at, left:] - tops[h][:, left:])
+            s_ref[h, at, left:] = weights
+            top_ref[h, :, left:] += fold(weights, jnp.sum)
+            ot_ref[own, left:] += product(vt_ref[own, at], weights.astype(BF16))
+
+    lax.fori_loop(0, i, lambda j, carry: (weigh(j * tile, tile, 0), carry)[1], 0)
+    for first, size, left in corners:
+        weigh(i * tile + first, size, left)
+    inverse = [1.0 / jnp.sum(top_ref[h], axis=0, keepdims=True) for h in range(heads)]
     grad_f = grad_t.astype(F32)
     deltas = []
     for h in range(heads):
@@ -1171,22 +1244,24 @@
         deltas.append(jnp.sum(value * grad_f[own], axis=0, keepdims=True))
     out_ref[rows, 0:width] = ot_ref[...].T.astype(BF16)
 
-    def back(j, carry):
-        at = pl.ds(pl.multiple_of(j * step, step), step)
+    def back(first, size, left):
+        at = pl.ds(pl.multiple_of(first, size), size)
         values = x_ref[at, 2 * width : 3 * width]
         probs_low, grads_low = [], []
         for h in range(heads):
             own = slice(h * HEAD_DIM, (h + 1) * HEAD_DIM)
-            probs_grad = product(values, grads_t[h])
-            probs = s_ref[h, at, :] * inverse[h]
-            scores_grad = (probs * (probs_grad - deltas[h])).astype(BF16)
+            probs_grad = product(values, grads_t[h][:, left:])
+            probs = s_ref[h, at, left:] * inverse[h][:, left:]
+            scores_grad = (probs * (probs_grad - deltas[h][:, left:])).astype(BF16)
             probs_low.append(probs.astype(BF16))
             grads_low.append(scores_grad)
-            dqt_ref[own, :] += product(kt_ref[own, at], scores_grad)
-        dva_ref[at, :] += product(jnp.concatenate(probs_low, axis=1), all_grads)
-        dka_ref[at, :] += product(jnp.concatenate(grads_low, axis=1), all_queries)
-        return carry
-    lax.fori_loop(0, count, back, 0)
+            dqt_ref[own, left:] += product(kt_ref[own, at], scores_grad)
+        dva_ref[at, :] += product(jnp.concatenate(probs_low, axis=1), jnp.concatenate([x[left:] for x in spread_grads], axis=0))
+        dka_ref[at, :] += product(jnp.concatenate(grads_low, axis=1), jnp.concatenate([x[left:] for x in spread_queries], axis=0))
+
+    lax.fori_loop(0, i, lambda j, carry: (back(j * tile, tile, 0), carry)[1], 0)
+    for first, size, left in corners:
+        back(i * tile + first, size, left)
     out_ref[rows, width : 2 * width] = (dqt_ref[...].T * scale).astype(BF16)
 
     @pl.when(i == tiles - 1)
@@ -1198,11 +1273,11 @@
 def attention(dealt, documents, heads, edge):
     length = dealt.shape[0]
     width = heads * HEAD_DIM
-    tile = step = 2 * edge
+    tile = 2 * edge
     pairs = length * length // 2 * heads
     whole = lambda i: (0, 0)
     return pl.pallas_call(
-        functools.partial(attention_kernel, width, heads, tile, step, edge, length),
+        functools.partial(attention_kernel, width, heads, tile, edge, length),
         grid=(length // tile,),
         out_shape=jax.ShapeDtypeStruct((length, 4 * width), BF16),
         in_specs=[pl.BlockSpec((length, 4 * width), whole), pl.BlockSpec((1, length), whole)],
@@ -1246,12 +1321,6 @@
     mix = mixer_bias.shape[0]
     heads = HEADS // n_seq
     own_width = heads * HEAD_DIM
-    seq = lax.axis_index("seq")
-    z, c = seq // 2, lax.rem(seq, 2)
-
-    def take(array, start, size, axis=0):
-        return lax.dynamic_slice_in_dim(array, start, size, axis)
-
     pick = lambda base, n: (lambda core: base + core * n)
     parts = 4
     piece = hidden_half // parts
@@ -1266,7 +1335,7 @@
         grid,
         history,
         cotangent,
-        [mixer_gain[None], inner_t, mixer_outer, mixer_bias[None], stream_gain, stream_bias],
+        [mixer_gain.reshape(-1, 128), inner_t, mixer_outer, mixer_bias[None], stream_gain, stream_bias],
         [inbound_weight, outbound_weight, expand, contract],
         [
             (0, pick(width, half), 1, 0, half, "ba"),
@@ -1281,14 +1350,13 @@
         1,
     )
 
-    bias_in = take(inbound_bias.astype(F32).reshape(3, width), c * half, half, 1)
     chunks = [(0, None, n - 4, col, size, order) for _, _, n, col, size, order in feed]
     dealt, (weight_e, weight_c) = exchange(
         grid,
         lowered,
         grad_low,
         weights,
-        bias_in,
+        inbound_bias.reshape(-1, 128),
         tables,
         started,
         chunks,
@@ -1296,25 +1364,22 @@
         own_width,
         2,
     )
-    returned = attention(dealt.reshape(length, 4 * own_width), documents.astype(F32), heads, tokens)
+    returned = attention(dealt.reshape(length, 4 * own_width), documents, heads, tokens)
     returned = returned.reshape(nz, both, 4 * own_width)
 
-    bias_e = take(expand_bias.astype(F32), c * hidden_half, hidden_half)[None]
-    collected, feed_part, normed_feed, expand_bias_part, feed_sums, *rest = feed_forward(
-        grid, returned, lowered, grad_low, weight_e, weight_c, bias_e, parts, 3
+    collected, feed_part, normed_feed, expand_bias_part, *rest = feed_forward(
+        grid, returned, lowered, grad_low, weight_e, weight_c, expand_bias.reshape(-1, 128), STEPS, 3
     )
 
-    def along_z(k):
-        return [(s, (s // 2 + k) % nz * 2 + s % 2) for s in range(n_seq)]
-
-    mids, folded = rest[:nz], rest[nz:]
-    folded = [folded[0]] + [lax.ppermute(folded[k], "seq", along_z(k)) for k in range(1, nz)]
-
     orders = ("ab", "ba", "ab", "ba")
-    bias_out = (outbound_bias.astype(F32) + contract_bias.astype(F32))[None]
-    normed_own, normed_theirs, head_bias_part, layer_out, mid_sums, kept, leaving = unproject(
-        grid, orders, mids, collected, lowered, grad_low, weights, feed_part, normed_feed, last_stream, bias_out, tables, own_width, 4
+    bias_out = [outbound_bias.reshape(-1, 128), contract_bias.reshape(-1, 128)]
+    mids, lates, last_parts = rest[:nz], rest[nz : 2 * nz], rest[2 * nz :]
+    normed_own, normed_theirs, head_bias_part, layer_out, mid_sums, lasts, kept, leaving = unproject(
+        grid, orders, mids, lates, last_parts, collected, lowered, grad_low, weights, feed_part, normed_feed, last_stream, bias_out, tables, own_width, 4
     )
+
+    along_z = [[(s, (s // 2 + k) % nz * 2 + s % 2) for s in range(n_seq)] for k in range(nz)]
+    folded = [lasts[0]] + [lax.ppermute(lasts[k], "seq", along_z[k]) for k in range(1, nz)]
     nb = grid.nb
     over_a = [(d, (d + nb) % n_dp) for d in range(n_dp)]
     over_b = [[(d, d // nb * nb + (d + k) % nb) for d in range(n_dp)] for k in range(1, nb)]
@@ -1322,11 +1387,11 @@
     came_b = [lax.ppermute(x, "dp", perm) for x, perm in zip(leaving[1:], over_b)]
 
     history_grad, *small = mix_backward(
-        history, normed_own, normed_theirs, cotangent, mix_pre, coeffs, [mixer_gain[None], inner_t, mixer_outer, stream_gain]
+        history, normed_own, normed_theirs, cotangent, mix_pre, coeffs, [mixer_gain.reshape(-1, 128), inner_t, mixer_outer, stream_gain]
     )
     smalls = [*small, head_bias_part, expand_bias_part]
-    summed, *owned = finish_sums(grid, orders, kept, [came_a, *came_b], [feed_sums, mid_sums, *folded], smalls, 5)
-    layer_out, *small, inbound_grad, outbound_grad, expand_grad, contract_grad = hand_over(summed, layer_out, owned, mix, hidden_width)
+    summed, *owned = finish_sums(grid, orders, kept, [came_a, *came_b], [mid_sums, *folded], smalls, 5)
+    layer_out, *small, inbound_grad, outbound_grad, expand_grad, contract_grad, again = hand_over(summed, layer_out, owned, mix, hidden_width)
     gain_grad, inner_grad, outer_grad, bias_grad, stream_gain_grad, stream_bias_grad, in_bias_grad, out_bias_grad, expand_bias_grad = small
     return (
         layer_out[None],
@@ -1344,7 +1409,7 @@
         expand_grad,
         expand_bias_grad.reshape(hidden_width),
         contract_grad,
-        out_bias_grad.reshape(width),
+        again.reshape(width),
     )
 
 

time: 417 us -> 392 us (0.940); the launches traced: 416 us -> 386 us
  Pallas kernels: 397 us -> 377 us
    pallas_call x1, Pallas kernels: 94.9 us -> 68.4 us  [feed_forward(): pl.pallas_call(functools.partial(feed_kernel, grid, steps), grid=(steps,)...]
    pallas_call x1, Pallas kernels: 30 us -> 40.3 us  [unproject(): pl.pallas_call(functools.partial(unproject_kernel, grid, own_width, order...]
where the time goes in v6:
time: 392 us; the launch traced here: 386 us
  Pallas kernels  377 us (96%)
  starting transfers between devices  6.84 us (2%)
    pallas_call x1, Pallas kernels, exchange(): pl.pallas_call(functools.partial(exchange_kernel, grid, own_width, chunks...  75.4 us
    pallas_call x1, Pallas kernels, mix_forward(): pl.pallas_call(functools.partial(mix_kernel, grid, rows, chunks, groups,...  69.2 us
    pallas_call x1, Pallas kernels, feed_forward(): pl.pallas_call(functools.partial(feed_kernel, grid, steps), grid=(steps,)...  68.4 us
    pallas_call x1, Pallas kernels, finish_sums(): pl.pallas_call(functools.partial(finish_kernel, grid, orders, len(kept)),...  47.9 us
    pallas_call x1, Pallas kernels, attention(): pl.pallas_call(functools.partial(attention_kernel, width, heads, tile, ed...  47.1 us
    pallas_call x1, Pallas kernels, unproject(): pl.pallas_call(functools.partial(unproject_kernel, grid, own_width, order...  40.3 us
    pallas_call x1, Pallas kernels, mix_backward(): pl.pallas_call(unmix_kernel, grid=(tokens // block,), out_shape=[jax.Shap...  25 us
  transfers between devices with their start and end apart: 5, of which 0 were waited for; matrix products, arithmetic and copies ran while one was open for 0% of the time, Pallas kernels for 6%

profile of v6, /device:TPU:0, one launch (start us, length us, event | category | flops | bytes accessed | tf_op | source)
XLA Modules:
  0.0 385.9 jit_solution(5858986527590362238)
XLA Ops:
  0.6 69.2 %mix_forward.1 = (bf16[4,2,384,1024]{3,2,1,0:T(8,128)(2,1)}, bf16[2,384,1024]{2,1,0:T(8,128)(2,1)}, f32[384,1024]{1,0:T(8,128)}, f32[384,36]{1,0:T(8,128)}, f32[...) custom-call(bf16[9,1,384,1024]{3,2,1,0:T(8,128)(2,1)} %h_ref.3, ...), custom_call_target="tpu_custom_call" | custom-call | flops 31457280 | bytes 141557760 | tf_op jit(solution)/shard_map/mix_forward/pallas_call | solution.py:416
  69.8 75.4 %exchange.1 = (bf16[4,768,512]{2,1,0:T(8,128)(2,1)}, bf16[2,2,4,64,2048]{4,3,2,1,0:T(8,128)(2,1)}, bf16[2,2,4,64,2048]{4,3,2,1,0:T(8,128)(2,1)}) custom-call(bf16[4,768,1024]{2,1,0:T(8,128)(2,1)} %bitcast.22, bf16[768,1024]{1,0:T(8,128)(2,1)} %bitcast.29, bf16[4,1024,512]{2,1,0:T(8,128)(2,1)} %bitcast.25, ...), custom_call_target="tpu_custom_call", output_to_operand_aliasing={{1}: (7, {}), {2}: (8, {})} | custom-call | flops 3221225472 | bytes 125829120 | tf_op jit(solution)/shard_map/exchange/pallas_call | solution.py:803
  145.2 47.1 %attention.1 = bf16[3072,512]{1,0:T(8,128)(2,1)} custom-call(bf16[3072,512]{1,0:T(8,128)(2,1)} %bitcast.38, s32[1,3072]{1,0:T(1,128)} %qdoc_ref.1), custom_call_target="tpu_custom_call" | custom-call | flops 28991029248 | bytes 7864320 | tf_op jit(solution)/shard_map/attention/pallas_call | solution.py:1279
  192.3 68.4 %feed_forward.1 = (bf16[4,768,512]{2,1,0:T(8,128)(2,1)}, f32[768,1024]{1,0:T(8,128)}, f32[768,1024]{1,0:T(8,128)}, f32[1,2048]{1,0:T(1,128)}, bf16[2,64,1024]{2,...) custom-call(bf16[4,768,512]{2,1,0:T(8,128)(2,1)} %bitcast.50, ...), custom_call_target="tpu_custom_call" | custom-call | flops 38654705664 | bytes 41943040 | tf_op jit(solution)/shard_map/feed_forward/pallas_call | solution.py:1121
  260.7 40.3 %unproject.1 = (f32[4,384,1024]{2,1,0:T(8,128)}, bf16[4,384,1024]{2,1,0:T(8,128)(2,1)}, f32[3,512]{1,0:T(4,128)}, bf16[384,1024]{1,0:T(8,128)(2,1)}, f32[2,64,10...) custom-call(bf16[2,64,1024]{2,1,0:T(8,128)(2,1)} %get-tuple-element., ...), custom_call_target="tpu_custom_call" | custom-call | flops 12884901888 | bytes 31457280 | tf_op jit(solution)/shard_map/unproject/pallas_call | solution.py:961
  301.0 0.4 collective-permute-start
  301.5 1.6 collective-permute-start.1
  303.1 1.5 collective-permute-start.2
  304.6 3.3 collective-permute-start.3
  307.9 0.0 collective-permute-start.4
  307.9 25.0 %mix_backward.1 = (f32[9,1,384,1024]{3,2,1,0:T(8,128)}, f32[4,1024]{1,0:T(4,128)}, f32[4,1024]{1,0:T(4,128)}, f32[1,1024]{1,0:T(1,128)}, f32[36,1024]{1,0:T(8,12...) custom-call(bf16[9,1,384,1024]{3,2,1,0:T(8,128)(2,1)} %h_ref.3, ...), custom_call_target="tpu_custom_call" | custom-call | flops 393216000 | bytes 42467328 | tf_op jit(solution)/shard_map/mix_backward/pallas_call | solution.py:542
  332.9 0.0 collective-permute-done.2.refs_8_
  332.9 0.0 copy-start.2
  332.9 0.0 collective-permute-done.3.refs_9_
  332.9 0.0 copy-start.3
  332.9 0.0 collective-permute-done.4.refs_10_
  332.9 0.0 copy-start.4
  332.9 0.0 collective-permute-done.refs_4_
  332.9 0.0 copy-start
  332.9 0.0 collective-permute-done.1.refs_5_
  333.0 0.0 copy-start.1
  333.0 0.6 copy-done.2
  333.6 0.1 copy-done.3
  333.7 0.1 copy-done.4
  333.7 0.4 copy-done
  334.1 0.4 copy-done.1
  334.5 47.9 %finish_sums.1 = (f32[512,128]{1,0:T(8,128)}, f32[32,3072]{1,0:T(8,128)}, f32[32,1024]{1,0:T(8,128)}, f32[32,4096]{1,0:T(8,128)}, f32[32,4096]{1,0:T(8,128)}) custom-call(bf16[2,4,64,512]{3,2,1,0:T(8,128)(2,1)} %get-tuple-element.112.refs_0_, bf16[2,4,64,512]{3,2,1,0:T(8,128)(2,1)} %get-tuple-element.113.refs_1_, ...), custom_call_target="tpu_custom_call" | custom-call | bytes 104857600 | tf_op jit(solution)/shard_map/finish_sums/pallas_call | solution.py:676
  382.4 3.2 hand_over.1
Async XLA Ops:
  301.0 31.9 %collective-permute-start = (bf16[2,2,4,64,512]{4,3,2,1,0:T(8,128)(2,1)}, bf16[2,2,4,64,512]{4,3,2,1,0:T(8,128)(2,1)S(1)}, u32[]{:S(2)}, u32[]{:S(2)}) collective-permute-start(bf16[2,2,4,64,512]{4,3,2,1,0:T(8,128)(2,1)} %get-tuple-element.116), channel_id=1, source_target_pairs={{0,16},{8,24},{16,0},{24,8},{1,17},{9,25},{17,1},{25,9},{2,18},{10... | collective-permute-start | bytes 3145736 | tf_op jit(solution)/shard_map/ppermute | solution.py:1386
  301.5 31.5 %collective-permute-start.1 = (bf16[2,2,4,64,512]{4,3,2,1,0:T(8,128)(2,1)}, bf16[2,2,4,64,512]{4,3,2,1,0:T(8,128)(2,1)S(1)}, u32[]{:S(2)}, u32[]{:S(2)}) collective-permute-start(bf16[2,2,4,64,512]{4,3,2,1,0:T(8,128)(2,1)} %get-tuple-element.117), channel_id=1, source_target_pairs={{0,8},{8,0},{16,24},{24,16},{1,9},{9,1},{17,25},{25,17},{2,10},{10... | collective-permute-start | bytes 3145736 | tf_op jit(solution)/shard_map/ppermute | solution.py:1387
  303.1 29.8 %collective-permute-start.2 = (bf16[2,64,1024]{2,1,0:T(8,128)(2,1)}, bf16[2,64,1024]{2,1,0:T(8,128)(2,1)S(1)}, u32[]{:S(2)}, u32[]{:S(2)}) collective-permute-start(bf16[2,64,1024]{2,1,0:T(8,128)(2,1)} %get-tuple-element.120), channel_id=1, source_target_pairs={{0,2},{1,3},{2,4},{3,5},{4,6},{5,7},{6,0},{7,1},{8,10},{9,11},{10,... | collective-permute-start | bytes 786440 | tf_op jit(solution)/shard_map/ppermute | solution.py:1382
  304.6 28.3 %collective-permute-start.3 = (bf16[2,64,1024]{2,1,0:T(8,128)(2,1)}, bf16[2,64,1024]{2,1,0:T(8,128)(2,1)S(1)}, u32[]{:S(2)}, u32[]{:S(2)}) collective-permute-start(bf16[2,64,1024]{2,1,0:T(8,128)(2,1)} %get-tuple-element.121), channel_id=1, source_target_pairs={{0,4},{1,5},{2,6},{3,7},{4,0},{5,1},{6,2},{7,3},{8,12},{9,13},{10,... | collective-permute-start | bytes 786440 | tf_op jit(solution)/shard_map/ppermute | solution.py:1382
  307.9 25.0 %collective-permute-start.4 = (bf16[2,64,1024]{2,1,0:T(8,128)(2,1)}, bf16[2,64,1024]{2,1,0:T(8,128)(2,1)S(1)}, u32[]{:S(2)}, u32[]{:S(2)}) collective-permute-start(bf16[2,64,1024]{2,1,0:T(8,128)(2,1)} %get-tuple-element.122), channel_id=1, source_target_pairs={{0,6},{1,7},{2,0},{3,1},{4,2},{5,3},{6,4},{7,5},{8,14},{9,15},{10,... | collective-permute-start | bytes 786440 | tf_op jit(solution)/shard_map/ppermute | solution.py:1382
  332.9 0.7 copy-start.2
  332.9 0.8 copy-start.3
  332.9 0.8 copy-start.4
  332.9 1.2 copy-start
  333.0 1.5 copy-start.1

commit v7 on v6

--- a/solution.py
+++ b/solution.py
@@ -316,9 +316,13 @@
         self.settle(self.done, 1)
 
 
+def spread_out(coeffs):
+    return [jnp.broadcast_to(coeffs[:, k : k + 1], (coeffs.shape[0], 128)) for k in range(coeffs.shape[1])]
+
+
 def blend(h_ref, coeffs, streams_ref):
-    hist, block, width = h_ref.shape[0], h_ref.shape[2], h_ref.shape[3]
-    spread = [jnp.broadcast_to(coeffs[:, k : k + 1], (block, 128)) for k in range(4 * hist)]
+    hist, width = h_ref.shape[0], h_ref.shape[3]
+    spread = spread_out(coeffs)
     for at in range(0, width, 128):
         lanes = slice(at, at + 128)
         inputs = [h_ref[j, 0, :, lanes].astype(F32) for j in range(hist)]
@@ -327,34 +331,78 @@
             for j in range(1, hist):
                 total = total + spread[c * hist + j] * inputs[j]
             streams_ref[c, :, lanes] = total
-    return spread
-
-
-def mix_kernel(grid, rows, chunks, whole, partial, h_ref, g_ref, gain_ref, inner_ref, outer_ref, bias_ref, sgain_ref, sbias_ref, *refs):
-    ins, (lowered_ref, gpair_ref, last_ref, pre_ref, coeffs_ref, cos_ref, above_ref, below_ref) = refs[:4], refs[4:12]
-    weights_ref, outs = refs[12], refs[13:15]
-    streams_ref, held_ref, local_sem, send_sem, recv_sem, pair_local, pair_send, pair_recv = refs[15:]
+
+
+def mix_kernel(grid, rows, chunks, whole, partial, own_width, h_ref, g_ref, gain_ref, inner_ref, outer_ref, bias_ref, sgain_ref, sbias_ref,
+               in_bias_ref, *refs):
+    ins, (lowered_ref, gpair_ref, kept_ref, pre_ref, coeffs_ref, cos_ref, above_ref, below_ref) = refs[:4], refs[4:12]
+    weights_ref, outs, dealt_ref, refs = refs[12], refs[13:15], refs[15], refs[16:]
+    streams_ref, full_ref, gfull_ref, held_ref, sent_ref, bias_full, local_sem, send_sem, recv_sem = refs[:9]
+    pair_local, pair_send, pair_recv, deal_send, deal_recv = refs[9:]
     i, steps = pl.program_id(0), pl.num_programs(0)
     a, b, z, c = place = grid.here()
     block = h_ref.shape[2]
     outs = [weights_ref.at[k] for k in range(4)] + list(outs)
-    events = Gathering(grid, place, rows, chunks, ins, outs, local_sem, send_sem, recv_sem).ticks(whole, partial)
+    work = Gathering(grid, place, rows, chunks, ins, outs, local_sem, send_sem, recv_sem)
+    events = work.ticks(whole, partial)
     other = grid.device(a, b, z, 1 - c)
-
-    def pair(k, src, dst):
+    nz = grid.nz
+
+    def swap_grads():
+        return [remote(g_ref.at[0], gfull_ref.at[c], pair_send.at[0], pair_recv.at[0], other)]
+
+    def swap_lowered():
+        return [remote(full_ref.at[:, c], full_ref.at[:, c], pair_send.at[1], pair_recv.at[1], other)]
+
+    def hand_out():
         return [
-            pltpu.make_async_copy(src, dst, pair_local.at[k]),
-            remote(src, dst, pair_send.at[k], pair_recv.at[k], other),
+            pltpu.make_async_copy(full_ref, lowered_ref, pair_local.at[0]),
+            pltpu.make_async_copy(gfull_ref, gpair_ref, pair_local.at[1]),
         ]
 
-    grads = lambda: pair(0, g_ref.at[0], gpair_ref.at[c])
-    lowereds = lambda: pair(1, held_ref, lowered_ref.at[:, c])
+    def fetch():
+        return [pltpu.make_async_copy(weights_ref, held_ref, pair_local.at[2])]
+
+    def link(to):
+        k = lax.rem(to - z + nz, nz)
+        return remote(sent_ref.at[to], dealt_ref.at[z], deal_send.at[k], deal_recv.at[k], grid.device(a, b, to, c))
+
+    def stay():
+        return pltpu.make_async_copy(sent_ref.at[z], dealt_ref.at[z], deal_send.at[0])
+
+    def project(n):
+        wide = 2 * own_width
+        turn = far_first(nz, z, n)
+        cols = pl.ds(pl.multiple_of(turn * wide, wide), wide)
+        both, width = 2 * full_ref.shape[2], full_ref.shape[3]
+        third = bias_full.shape[0] // 3
+        tables = [jnp.concatenate([t[...]] * (wide // 128), axis=1) for t in (cos_ref, above_ref, below_ref)]
+
+        def one(k):
+            inputs = gfull_ref[...] if k == 3 else full_ref[k]
+            found = product(inputs.reshape(both, width), held_ref[k, :, :, :, :, cols].reshape(width, wide))
+            if k == 3:
+                return found
+            first_row = k * third + c * (third // 2) + turn * (wide // 128)
+            found = found + jnp.concatenate([bias_full[pl.ds(first_row + l, 1), :] for l in range(wide // 128)], axis=1)
+            return rotate(found, tables, 1.0) if k < 2 else found
+
+        for k in range(4):
+            x = one(k).astype(BF16)
+            for m in range(2):
+                sent_ref[turn * 2 + m, :, k * own_width : (k + 1) * own_width] = x[:, m * own_width : (m + 1) * own_width]
+        for m in range(2):
+            to = turn * 2 + m
+            pl.when(to != z)(lambda to=to: link(to).start())
+            pl.when(to == z)(lambda: stay().start())
 
     @pl.when(i == 0)
     def _():
         grid.greet(*place)
         events[0]()
-        start(grads())
+        start(swap_grads())
+        gfull_ref[c] = g_ref[0]
+        bias_full[...] = in_bias_ref[...].astype(F32)
 
     for n, at in enumerate((0, 2, 3, 4)):
 
@@ -392,19 +440,43 @@
         centered = stream - jnp.mean(stream, axis=1, keepdims=True)
         rs = lax.rsqrt(jnp.mean(centered * centered, axis=1, keepdims=True) + EPS)
         gain, bias = sgain_ref[k : k + 1, :].astype(F32), sbias_ref[k : k + 1, :].astype(F32)
-        held_ref[k, at, :] = (centered * rs * gain + bias).astype(BF16)
-    last_ref[...] = streams_ref[3]
+        full_ref[k, c, at, :] = (centered * rs * gain + bias).astype(BF16)
+    kept_ref[...] = streams_ref[...]
 
     @pl.when(i == steps - 1)
     def _():
-        start(lowereds())
-        for event in events[5:]:
+        start(swap_lowered())
+        ready = len(whole) + nz - 1
+        for event in events[5 : 1 + ready + 1]:
             event()
-        finish(grads())
-        finish(lowereds())
-
-
-def mix_forward(grid, history, cotangent, params, weights, chunks, groups, partial, widths, collective_id):
+        events[-1]()
+        start(fetch())
+        finish(swap_grads())
+        finish(swap_lowered())
+        start(hand_out())
+        hopped = [u for u in range(len(partial)) if u // 2 + len(whole) + nz - 1 <= ready]
+        for u in hopped:
+            work.begin(partial[u], 2)
+        finish(fetch())
+        for n in range(nz // 2):
+            project(n)
+        for event in events[1 + ready + 1 : -1]:
+            event()
+        for u in range(len(partial)):
+            if u not in hopped:
+                work.begin(partial[u], 2)
+        for group in partial:
+            work.end(group, 2)
+            work.begin(group, 3)
+        for m in range(1, nz):
+            link(lax.rem(z + m, nz)).wait()
+        stay().wait()
+        finish(hand_out())
+        for group in partial:
+            work.end(group, 3)
+
+
+def mix_forward(grid, history, cotangent, params, weights, chunks, groups, partial, widths, own_width, collective_id):
     hist, _, tokens, width = history.shape
     mix = params[1].shape[0]
     block = 64
@@ -414,44 +486,52 @@
     part = lambda n: pl.BlockSpec((block, n), lambda i: (i, 0))
     chips = (grid.na, grid.nb, grid.nz, 2 * rows)
     results = pl.pallas_call(
-        functools.partial(mix_kernel, grid, rows, chunks, groups, partial),
+        functools.partial(mix_kernel, grid, rows, chunks, groups, partial, own_width),
         grid=(tokens // block,),
         out_shape=[
             jax.ShapeDtypeStruct((4, 2, tokens, width), BF16),
             jax.ShapeDtypeStruct((2, tokens, width), BF16),
-            jax.ShapeDtypeStruct((tokens, width), F32),
+            jax.ShapeDtypeStruct((4, tokens, width), F32),
             jax.ShapeDtypeStruct((tokens, mix), F32),
             jax.ShapeDtypeStruct((tokens, mix), F32),
         ]
         + [jax.ShapeDtypeStruct((2 * tokens, 128), F32)] * 3
         + [jax.ShapeDtypeStruct((4, *chips, width // 2), BF16)]
-        + [jax.ShapeDtypeStruct((*chips, w), BF16) for w in widths],
-        in_specs=[pl.BlockSpec((hist, 1, block, width), lambda i: (0, 0, i, 0))] + [whole] * 11,
-        out_specs=[anywhere, anywhere, part(width), part(mix), part(mix)]
+        + [jax.ShapeDtypeStruct((*chips, w), BF16) for w in widths]
+        + [jax.ShapeDtypeStruct((grid.nz, 2 * tokens, 4 * own_width), BF16)],
+        in_specs=[pl.BlockSpec((hist, 1, block, width), lambda i: (0, 0, i, 0))] + [whole] * 12,
+        out_specs=[anywhere, anywhere, pl.BlockSpec((4, block, width), lambda i: (0, i, 0)), part(mix), part(mix)]
         + [pl.BlockSpec((2 * tokens, 128), lambda i: (0, 0))] * 3
-        + [anywhere] * 3,
+        + [anywhere] * 4,
         scratch_shapes=[
             pltpu.VMEM((4, block, width), F32),
-            pltpu.VMEM((4, tokens, width), BF16),
+            pltpu.VMEM((4, 2, tokens, width), BF16),
+            pltpu.VMEM((2, tokens, width), BF16),
+            pltpu.VMEM((4, *chips, width // 2), BF16),
+            pltpu.VMEM((grid.nz, 2 * tokens, 4 * own_width), BF16),
+            pltpu.VMEM(params[-1].shape, F32),
             *gather_sems(grid, chunks),
+            pltpu.SemaphoreType.DMA((3,)),
             pltpu.SemaphoreType.DMA((2,)),
             pltpu.SemaphoreType.DMA((2,)),
-            pltpu.SemaphoreType.DMA((2,)),
+            pltpu.SemaphoreType.DMA((grid.nz,)),
+            pltpu.SemaphoreType.DMA((grid.nz,)),
         ],
         compiler_params=pltpu.CompilerParams(collective_id=collective_id, has_side_effects=True, vmem_limit_bytes=VMEM_LIMIT),
         cost_estimate=pl.CostEstimate(flops=tokens * width * 80, bytes_accessed=history.size * 40, transcendentals=0),
         name="mix_forward",
     )(history, cotangent, *params, *weights)
-    lowered, gpair, last, pre, coeffs = results[:5]
+    lowered, gpair, streams, pre, coeffs = results[:5]
     return (
         lowered.reshape(4, 2 * tokens, width),
         gpair.reshape(2 * tokens, width),
-        last,
+        streams,
         pre,
         coeffs,
         results[5:8],
         results[8].reshape(4, width, width // 2),
-        results[9:],
+        [x.reshape(-1, x.shape[-1]) for x in results[9:-1]],
+        results[-1],
     )
 
 
@@ -462,9 +542,9 @@
     return firsts, sum(sizes)
 
 
-def unmix_kernel(h_ref, own_ref, theirs_ref, g_ref, pre_ref, coeffs_ref, gain_ref, inner_ref, outer_ref, sgain_ref,
+def unmix_kernel(h_ref, streams_ref, own_ref, theirs_ref, g_ref, pre_ref, coeffs_ref, gain_ref, inner_ref, outer_ref, sgain_ref,
                  hist_ref, sgg_ref, sbg_ref, gg_ref, ig_ref, og_ref, bg_ref, ob_ref,
-                 streams_ref, sg_ref, scaled_ref, mpg_ref, hidden_ref, cgl_ref):
+                 sg_ref, scaled_ref, mpg_ref, hidden_ref, cgl_ref):
     i, steps = pl.program_id(0), pl.num_programs(0)
     hist, block, width = h_ref.shape[0], h_ref.shape[2], h_ref.shape[3]
     mix = 4 * hist
@@ -477,8 +557,7 @@
     def down(x):
         return jnp.sum(x, axis=0, keepdims=True)
 
-    coeffs = coeffs_ref[...]
-    spread = blend(h_ref, coeffs, streams_ref)
+    spread = spread_out(coeffs_ref[...])
     grad = g_ref[0].astype(F32)
     ob_ref[...] += down(grad)
     for k in range(4):
@@ -530,7 +609,7 @@
         og_ref[...] = inner(hidden_ref[...], cgl_ref[...])
 
 
-def mix_backward(history, own, theirs, cotangent, pre, coeffs, params):
+def mix_backward(history, streams, own, theirs, cotangent, pre, coeffs, params):
     hist, _, tokens, width = history.shape
     mix = pre.shape[1]
     block = 64
@@ -543,10 +622,9 @@
         unmix_kernel,
         grid=(tokens // block,),
         out_shape=[jax.ShapeDtypeStruct(history.shape, F32)] + [jax.ShapeDtypeStruct(shape, F32) for shape in small],
-        in_specs=[story, four, four, pl.BlockSpec((1, block, width), lambda i: (0, i, 0)), part(mix), part(mix)] + [whole] * 4,
+        in_specs=[story, four, four, four, pl.BlockSpec((1, block, width), lambda i: (0, i, 0)), part(mix), part(mix)] + [whole] * 4,
         out_specs=[story] + [pl.BlockSpec(shape, lambda i: (0, 0)) for shape in small],
         scratch_shapes=[
-            pltpu.VMEM((4, block, width), F32),
             pltpu.VMEM((4, block, width), F32),
             pltpu.VMEM((tokens, width), BF16),
             pltpu.VMEM((tokens, mix), BF16),
@@ -556,7 +634,7 @@
         compiler_params=pltpu.CompilerParams(vmem_limit_bytes=VMEM_LIMIT),
         cost_estimate=pl.CostEstimate(flops=tokens * width * 1000, bytes_accessed=history.size * 12, transcendentals=0),
         name="mix_backward",
-    )(history, own, theirs, cotangent, pre, coeffs, *params)
+    )(history, streams, own, theirs, cotangent, pre, coeffs, *params)
 
 
 def finish_kernel(grid, orders, n_kept, *refs):
@@ -614,6 +692,25 @@
     add_first(2)
     add_first(3)
 
+    for t in range(2):
+        total = folded[0][t].astype(F32)
+        for piece in folded[1:]:
+            total = total + piece[t].astype(F32)
+        at = 0
+        for piece in (sum_ref[t], total):
+            n = piece.shape[1]
+            final[4 + t][:, :, at : at + n] = piece.reshape(2, -1, n)
+            at += n
+        start(copies(4 + t, 3))
+    def second_step(t):
+        finish(copies(t, 1))
+        if t < 2:
+            start(copies(t + 2, 1))
+        fold_add(grid, place, orders[t], 1, None, first[t], second[t])
+        start(copies(t, 2))
+
+    second_step(0)
+    second_step(1)
     mine = sums.mine
     mine[...] = jnp.zeros_like(mine)
     for l in range(wl):
@@ -631,23 +728,8 @@
     for l in range(hidden_rows):
         mine[pl.ds(firsts[8] + c * hidden_rows + l, 1), :] = eb_ref[:, l * 128 : (l + 1) * 128]
     sums.deal()
-
-    for t in range(2):
-        total = folded[0][t].astype(F32)
-        for piece in folded[1:]:
-            total = total + piece[t].astype(F32)
-        at = 0
-        for piece in (sum_ref[t], total):
-            n = piece.shape[1]
-            final[4 + t][:, :, at : at + n] = piece.reshape(2, -1, n)
-            at += n
-        start(copies(4 + t, 3))
-    for t in range(4):
-        finish(copies(t, 1))
-        if t < 2:
-            start(copies(t + 2, 1))
-        fold_add(grid, place, orders[t], 1, None, first[t], second[t])
-        start(copies(t, 2))
+    second_step(2)
+    second_step(3)
     sums.tell()
     for t in range(4):
         finish(copies(t, 2))
@@ -739,93 +821,9 @@
     )(summed, layer_out, *owned)
 
 
-def exchange_kernel(grid, width, chunks, groups, low_ref, g_ref, w_ref, bias_ref, cos_ref, above_ref, below_ref, _e, _c,
-                    dealt_ref, e_ref, c_ref, sent_ref, bias_full, deal_send, deal_recv, local_sem, send_sem, recv_sem):
-    i, steps = pl.program_id(0), pl.num_programs(0)
-    a, b, z, c = place = grid.here()
-    nz = grid.nz
-    work = Gathering(grid, place, None, chunks, None, [e_ref, c_ref], local_sem, send_sem, recv_sem)
-
-    def link(to):
-        k = lax.rem(to - z + nz, nz)
-        return remote(sent_ref.at[to], dealt_ref.at[z], deal_send.at[k], deal_recv.at[k], grid.device(a, b, to, c))
-
-    def stay():
-        return pltpu.make_async_copy(sent_ref.at[z], dealt_ref.at[z], deal_send.at[0])
-
-    @pl.when(i == 0)
-    def _():
-        grid.greet(*place)
-        for group in groups:
-            work.begin(group, 2)
-        bias_full[...] = bias_ref[...].astype(F32)
-
-    wide = w_ref.shape[2]
-    each = wide // width
-    tables = [jnp.concatenate([t[...]] * max(wide // 128, 1), axis=1) for t in (cos_ref, above_ref, below_ref)]
-    third = bias_full.shape[0] // 3
-
-    def bias(n):
-        first_row = n * third + c * (third // 2) + i * (wide // 128)
-        return jnp.concatenate([bias_full[pl.ds(first_row + l, 1), :] for l in range(wide // 128)], axis=1)
-
-    q = rotate(product(low_ref[0], w_ref[0]) + bias(0), tables, 1.0)
-    k = rotate(product(low_ref[1], w_ref[1]) + bias(1), tables, 1.0)
-    v = product(low_ref[2], w_ref[2]) + bias(2)
-    g = product(g_ref[...], w_ref[3])
-    for n, x in enumerate((q, k, v, g)):
-        x = x.astype(BF16)
-        for m in range(each):
-            sent_ref[i * each + m, :, n * width : (n + 1) * width] = x[:, m * width : (m + 1) * width]
-    for m in range(each):
-        to = i * each + m
-        pl.when(to != z)(lambda to=to: link(to).start())
-        pl.when(to == z)(lambda: stay().start())
-
-    @pl.when(i == steps - 1)
-    def _():
-        for group in groups:
-            work.end(group, 2)
-            work.begin(group, 3)
-        for m in range(1, nz):
-            link(lax.rem(z + m, nz)).wait()
-        stay().wait()
-        for group in groups:
-            work.end(group, 3)
-
-
-def exchange(grid, lowered, grad_low, weights, biases, tables, started, chunks, groups, own_width, collective_id):
-    both, width = grad_low.shape
-    nz = grid.nz
-    wide = 2 * own_width
-    whole = pl.BlockSpec(memory_space=pltpu.VMEM)
-    anywhere = pl.BlockSpec(memory_space=pl.ANY)
-    dealt, *full = pl.pallas_call(
-        functools.partial(exchange_kernel, grid, own_width, chunks, groups),
-        grid=(nz // 2,),
-        out_shape=[jax.ShapeDtypeStruct((nz, both, 4 * own_width), BF16)] + [jax.ShapeDtypeStruct(x.shape, x.dtype) for x in started],
-        in_specs=[
-            pl.BlockSpec((3, both, width), lambda i: (0, 0, 0)),
-            whole,
-            pl.BlockSpec((4, width, wide), lambda i: (0, 0, i)),
-            whole,
-        ]
-        + [whole] * 3
-        + [anywhere] * 2,
-        out_specs=[anywhere] * 3,
-        input_output_aliases={7: 1, 8: 2},
-        scratch_shapes=[
-            pltpu.VMEM((nz, both, 4 * own_width), BF16),
-            pltpu.VMEM(biases.shape, F32),
-            pltpu.SemaphoreType.DMA((nz,)),
-            pltpu.SemaphoreType.DMA((nz,)),
-            *gather_sems(grid, chunks),
-        ],
-        compiler_params=pltpu.CompilerParams(collective_id=collective_id, has_side_effects=True, vmem_limit_bytes=VMEM_LIMIT),
-        cost_estimate=pl.CostEstimate(flops=2 * both * weights.size, bytes_accessed=weights.size * 60, transcendentals=0),
-        name="exchange",
-    )(lowered, grad_low, weights, biases, *tables, *started)
-    return dealt, [x.reshape(-1, x.shape[-1]) for x in full]
+def far_first(nz, z, i):
+    pairs = nz // 2
+    return lax.rem(i + pairs // 2 * (1 - z // pairs), pairs)
 
 
 def unproject_kernel(grid, width, orders, *all_refs):
@@ -910,7 +908,7 @@
         start(swap_out())
         start(swap(3))
         own_ref[0] = normed_ref[own_rows, :]
-        out = against(mine_ref[own_rows, :], w_ref[0]) + feed_ref[own_rows, :] + last_ref[...] + (row(bias_ref) + row(bias2_ref))
+        out = against(mine_ref[own_rows, :], w_ref[0]) + feed_ref[own_rows, :] + last_ref[0] + (row(bias_ref) + row(bias2_ref))
         keep(3, inner(g_ref[...], mine_ref[...]))
         finish(swap_out())
         out_ref[...] = (out + arrived_ref[...]).astype(BF16)
@@ -946,8 +944,8 @@
                 finish(place_lates())
 
 
-def unproject(grid, orders, mids, lates, last_parts, collected, lowered, grad_low, weights, feed_part, normed_feed, last_stream, biases, tables, own_width, collective_id):
-    tokens, width = last_stream.shape
+def unproject(grid, orders, mids, lates, last_parts, collected, lowered, grad_low, weights, feed_part, normed_feed, streams, biases, tables, own_width, collective_id):
+    _, tokens, width = streams.shape
     both, half = 2 * tokens, width // 2
     na, nb, nz = grid.na, grid.nb, grid.nz
     rows = width // (na * nb * nz)
@@ -981,7 +979,9 @@
             whole,
             pl.BlockSpec((1, width, half), lambda i: (turn(i), 0, 0)),
         ]
-        + [whole] * 8,
+        + [whole] * 2
+        + [pl.BlockSpec((1, tokens, width), lambda i: (3, 0, 0))]
+        + [whole] * 5,
         out_specs=[
             pl.BlockSpec((1, tokens, width), lambda i: (turn(i), 0, 0)),
             anywhere,
@@ -1012,7 +1012,7 @@
         compiler_params=pltpu.CompilerParams(collective_id=collective_id, has_side_effects=True, vmem_limit_bytes=VMEM_LIMIT),
         cost_estimate=pl.CostEstimate(flops=32 * both * width * half, bytes_accessed=40 * both * width, transcendentals=0),
         name="unproject",
-    )(*mids, *lates, *last_parts, collected, lowered, grad_low, weights, feed_part, normed_feed, last_stream, *biases, *tables)
+    )(*mids, *lates, *last_parts, collected, lowered, grad_low, weights, feed_part, normed_feed, streams, *biases, *tables)
     own, theirs, head_bias, layer_out, mid_sums = results[:5]
     lasts, results = results[5 : 5 + nz], results[5 + nz :]
     return own, theirs, head_bias, layer_out, mid_sums, lasts, results[:4], results[4:]
@@ -1331,11 +1331,11 @@
         feed.append((3, base, 5, part * piece, piece, "ab"))
     pairs = [[4 + 2 * part, 5 + 2 * part] for part in range(parts)]
     inner_t = mixer_inner.T
-    lowered, grad_low, last_stream, mix_pre, coeffs, tables, weights, started = mix_forward(
+    lowered, grad_low, streams, mix_pre, coeffs, tables, weights, (weight_e, weight_c), dealt = mix_forward(
         grid,
         history,
         cotangent,
-        [mixer_gain.reshape(-1, 128), inner_t, mixer_outer, mixer_bias[None], stream_gain, stream_bias],
+        [mixer_gain.reshape(-1, 128), inner_t, mixer_outer, mixer_bias[None], stream_gain, stream_bias, inbound_bias.reshape(-1, 128)],
         [inbound_weight, outbound_weight, expand, contract],
         [
             (0, pick(width, half), 1, 0, half, "ba"),
@@ -1347,23 +1347,10 @@
         [[0, 1], [2, 3]],
         pairs,
         [hidden_half] * 2,
+        own_width,
         1,
     )
 
-    chunks = [(0, None, n - 4, col, size, order) for _, _, n, col, size, order in feed]
-    dealt, (weight_e, weight_c) = exchange(
-        grid,
-        lowered,
-        grad_low,
-        weights,
-        inbound_bias.reshape(-1, 128),
-        tables,
-        started,
-        chunks,
-        [[2 * part, 2 * part + 1] for part in range(parts)],
-        own_width,
-        2,
-    )
     returned = attention(dealt.reshape(length, 4 * own_width), documents, heads, tokens)
     returned = returned.reshape(nz, both, 4 * own_width)
 
@@ -1375,7 +1362,7 @@
     bias_out = [outbound_bias.reshape(-1, 128), contract_bias.reshape(-1, 128)]
     mids, lates, last_parts = rest[:nz], rest[nz : 2 * nz], rest[2 * nz :]
     normed_own, normed_theirs, head_bias_part, layer_out, mid_sums, lasts, kept, leaving = unproject(
-        grid, orders, mids, lates, last_parts, collected, lowered, grad_low, weights, feed_part, normed_feed, last_stream, bias_out, tables, own_width, 4
+        grid, orders, mids, lates, last_parts, collected, lowered, grad_low, weights, feed_part, normed_feed, streams, bias_out, tables, own_width, 4
     )
 
     along_z = [[(s, (s // 2 + k) % nz * 2 + s % 2) for s in range(n_seq)] for k in range(nz)]
@@ -1387,7 +1374,7 @@
     came_b = [lax.ppermute(x, "dp", perm) for x, perm in zip(leaving[1:], over_b)]
 
     history_grad, *small = mix_backward(
-        history, normed_own, normed_theirs, cotangent, mix_pre, coeffs, [mixer_gain.reshape(-1, 128), inner_t, mixer_outer, stream_gain]
+        history, streams, normed_own, normed_theirs, cotangent, mix_pre, coeffs, [mixer_gain.reshape(-1, 128), inner_t, mixer_outer, stream_gain]
     )
     smalls = [*small, head_bias_part, expand_bias_part]
     summed, *owned = finish_sums(grid, orders, kept, [came_a, *came_b], [mid_sums, *folded], smalls, 5)

time: 392 us -> 388 us (0.990)
  Pallas kernels: 377 us -> 373 us
    pallas_call x1 -> x0, Pallas kernels: 75.4 us -> none  [exchange(): pl.pallas_call(functools.partial(exchange_kernel, grid, own_width, chunks...]
    pallas_call x1, Pallas kernels: 69.2 us -> 137 us  [mix_forward(): pl.pallas_call(functools.partial(mix_kernel, grid, rows, chunks, groups,...]
where the time goes in v7:
time: 388 us; the launch traced here: 382 us
  Pallas kernels  373 us (96%)
  starting transfers between devices  5.94 us (2%)
    pallas_call x1, Pallas kernels, mix_forward(): pl.pallas_call(functools.partial(mix_kernel, grid, rows, chunks, groups,...  137 us
    pallas_call x1, Pallas kernels, feed_forward(): pl.pallas_call(functools.partial(feed_kernel, grid, steps), grid=(steps,)...  71.4 us
    pallas_call x1, Pallas kernels, finish_sums(): pl.pallas_call(functools.partial(finish_kernel, grid, orders, len(kept)),...  51.6 us
    pallas_call x1, Pallas kernels, attention(): pl.pallas_call(functools.partial(attention_kernel, width, heads, tile, ed...  47.1 us
    pallas_call x1, Pallas kernels, unproject(): pl.pallas_call(functools.partial(unproject_kernel, grid, own_width, order...  41.1 us
    pallas_call x1, Pallas kernels, mix_backward(): pl.pallas_call(unmix_kernel, grid=(tokens // block,), out_shape=[jax.Shap...  21.6 us
  transfers between devices with their start and end apart: 5, of which 0 were waited for; matrix products, arithmetic and copies ran while one was open for 0% of the time, Pallas kernels for 6%

profile of v7, /device:TPU:0, one launch (start us, length us, event | category | flops | bytes accessed | tf_op | source)
XLA Modules:
  0.0 381.6 jit_solution(11618536118837944370)
XLA Ops:
  0.6 137.1 %mix_forward.1 = (bf16[4,2,384,1024]{3,2,1,0:T(8,128)(2,1)}, bf16[2,384,1024]{2,1,0:T(8,128)(2,1)}, f32[4,384,1024]{2,1,0:T(8,128)}, f32[384,36]{1,0:T(8,128)}, ...) custom-call(bf16[9,1,384,1024]{3,2,1,0:T(8,128)(2,1)} %h_ref.3, ...), custom_call_target="tpu_custom_call" | custom-call | flops 31457280 | bytes 141557760 | tf_op jit(solution)/shard_map/mix_forward/pallas_call | solution.py:488
  137.7 47.1 %attention.1 = bf16[3072,512]{1,0:T(8,128)(2,1)} custom-call(bf16[3072,512]{1,0:T(8,128)(2,1)} %bitcast.33, s32[1,3072]{1,0:T(1,128)} %qdoc_ref.1), custom_call_target="tpu_custom_call" | custom-call | flops 28991029248 | bytes 7864320 | tf_op jit(solution)/shard_map/attention/pallas_call | solution.py:1279
  184.8 71.4 %feed_forward.1 = (bf16[4,768,512]{2,1,0:T(8,128)(2,1)}, f32[768,1024]{1,0:T(8,128)}, f32[768,1024]{1,0:T(8,128)}, f32[1,2048]{1,0:T(1,128)}, bf16[2,64,1024]{2,...) custom-call(bf16[4,768,512]{2,1,0:T(8,128)(2,1)} %bitcast.47, ...), custom_call_target="tpu_custom_call" | custom-call | flops 38654705664 | bytes 41943040 | tf_op jit(solution)/shard_map/feed_forward/pallas_call | solution.py:1121
  256.3 41.1 %unproject.1 = (f32[4,384,1024]{2,1,0:T(8,128)}, bf16[4,384,1024]{2,1,0:T(8,128)(2,1)}, f32[3,512]{1,0:T(4,128)}, bf16[384,1024]{1,0:T(8,128)(2,1)}, f32[2,64,10...) custom-call(bf16[2,64,1024]{2,1,0:T(8,128)(2,1)} %get-tuple-element., ...), custom_call_target="tpu_custom_call" | custom-call | flops 12884901888 | bytes 31457280 | tf_op jit(solution)/shard_map/unproject/pallas_call | solution.py:959
  297.4 0.1 collective-permute-start
  297.4 2.0 collective-permute-start.1
  299.4 1.4 collective-permute-start.2
  300.8 2.5 collective-permute-start.3
  303.3 0.0 collective-permute-start.4
  303.3 21.6 %mix_backward.1 = (f32[9,1,384,1024]{3,2,1,0:T(8,128)}, f32[4,1024]{1,0:T(4,128)}, f32[4,1024]{1,0:T(4,128)}, f32[1,1024]{1,0:T(1,128)}, f32[36,1024]{1,0:T(8,12...) custom-call(bf16[9,1,384,1024]{3,2,1,0:T(8,128)(2,1)} %h_ref.3, ...), custom_call_target="tpu_custom_call" | custom-call | flops 393216000 | bytes 42467328 | tf_op jit(solution)/shard_map/mix_backward/pallas_call | solution.py:621
  324.9 0.0 collective-permute-done.2.refs_8_
  324.9 0.0 copy-start.2
  324.9 0.0 collective-permute-done.3.refs_9_
  324.9 0.0 copy-start.3
  324.9 0.0 collective-permute-done.4.refs_10_
  325.0 0.0 copy-start.4
  325.0 0.0 collective-permute-done.refs_4_
  325.0 0.0 copy-start
  325.0 0.0 collective-permute-done.1.refs_5_
  325.0 0.0 copy-start.1
  325.0 0.6 copy-done.2
  325.6 0.1 copy-done.3
  325.7 0.1 copy-done.4
  325.8 0.4 copy-done
  326.2 0.4 copy-done.1
  326.5 51.6 %finish_sums.1 = (f32[512,128]{1,0:T(8,128)}, f32[32,3072]{1,0:T(8,128)}, f32[32,1024]{1,0:T(8,128)}, f32[32,4096]{1,0:T(8,128)}, f32[32,4096]{1,0:T(8,128)}) custom-call(bf16[2,4,64,512]{3,2,1,0:T(8,128)(2,1)} %get-tuple-element.108.refs_0_, bf16[2,4,64,512]{3,2,1,0:T(8,128)(2,1)} %get-tuple-element.109.refs_1_, ...), custom_call_target="tpu_custom_call" | custom-call | bytes 104857600 | tf_op jit(solution)/shard_map/finish_sums/pallas_call | solution.py:758
  378.1 3.2 hand_over.1
Async XLA Ops:
  297.4 27.6 %collective-permute-start = (bf16[2,2,4,64,512]{4,3,2,1,0:T(8,128)(2,1)}, bf16[2,2,4,64,512]{4,3,2,1,0:T(8,128)(2,1)S(1)}, u32[]{:S(2)}, u32[]{:S(2)}) collective-permute-start(bf16[2,2,4,64,512]{4,3,2,1,0:T(8,128)(2,1)} %get-tuple-element.112), channel_id=1, source_target_pairs={{0,16},{8,24},{16,0},{24,8},{1,17},{9,25},{17,1},{25,9},{2,18},{10... | collective-permute-start | bytes 3145736 | tf_op jit(solution)/shard_map/ppermute | solution.py:1373
  297.4 27.6 %collective-permute-start.1 = (bf16[2,2,4,64,512]{4,3,2,1,0:T(8,128)(2,1)}, bf16[2,2,4,64,512]{4,3,2,1,0:T(8,128)(2,1)S(1)}, u32[]{:S(2)}, u32[]{:S(2)}) collective-permute-start(bf16[2,2,4,64,512]{4,3,2,1,0:T(8,128)(2,1)} %get-tuple-element.113), channel_id=1, source_target_pairs={{0,8},{8,0},{16,24},{24,16},{1,9},{9,1},{17,25},{25,17},{2,10},{10... | collective-permute-start | bytes 3145736 | tf_op jit(solution)/shard_map/ppermute | solution.py:1374
  299.4 25.5 %collective-permute-start.2 = (bf16[2,64,1024]{2,1,0:T(8,128)(2,1)}, bf16[2,64,1024]{2,1,0:T(8,128)(2,1)S(1)}, u32[]{:S(2)}, u32[]{:S(2)}) collective-permute-start(bf16[2,64,1024]{2,1,0:T(8,128)(2,1)} %get-tuple-element.116), channel_id=1, source_target_pairs={{0,2},{1,3},{2,4},{3,5},{4,6},{5,7},{6,0},{7,1},{8,10},{9,11},{10,... | collective-permute-start | bytes 786440 | tf_op jit(solution)/shard_map/ppermute | solution.py:1369
  300.8 24.1 %collective-permute-start.3 = (bf16[2,64,1024]{2,1,0:T(8,128)(2,1)}, bf16[2,64,1024]{2,1,0:T(8,128)(2,1)S(1)}, u32[]{:S(2)}, u32[]{:S(2)}) collective-permute-start(bf16[2,64,1024]{2,1,0:T(8,128)(2,1)} %get-tuple-element.117), channel_id=1, source_target_pairs={{0,4},{1,5},{2,6},{3,7},{4,0},{5,1},{6,2},{7,3},{8,12},{9,13},{10,... | collective-permute-start | bytes 786440 | tf_op jit(solution)/shard_map/ppermute | solution.py:1369
  303.3 21.6 %collective-permute-start.4 = (bf16[2,64,1024]{2,1,0:T(8,128)(2,1)}, bf16[2,64,1024]{2,1,0:T(8,128)(2,1)S(1)}, u32[]{:S(2)}, u32[]{:S(2)}) collective-permute-start(bf16[2,64,1024]{2,1,0:T(8,128)(2,1)} %get-tuple-element.118), channel_id=1, source_target_pairs={{0,6},{1,7},{2,0},{3,1},{4,2},{5,3},{6,4},{7,5},{8,14},{9,15},{10,... | collective-permute-start | bytes 786440 | tf_op jit(solution)/shard_map/ppermute | solution.py:1369
  324.9 0.7 copy-start.2
  324.9 0.8 copy-start.3
  325.0 0.8 copy-start.4
  325.0 1.2 copy-start
  325.0 1.5 copy-start.1

commit v8 on v7

--- a/solution.py
+++ b/solution.py
@@ -342,7 +342,7 @@
     i, steps = pl.program_id(0), pl.num_programs(0)
     a, b, z, c = place = grid.here()
     block = h_ref.shape[2]
-    outs = [weights_ref.at[k] for k in range(4)] + list(outs)
+    outs = [held_ref.at[k] for k in range(4)] + list(outs)
     work = Gathering(grid, place, rows, chunks, ins, outs, local_sem, send_sem, recv_sem)
     events = work.ticks(whole, partial)
     other = grid.device(a, b, z, 1 - c)
@@ -358,10 +358,8 @@
         return [
             pltpu.make_async_copy(full_ref, lowered_ref, pair_local.at[0]),
             pltpu.make_async_copy(gfull_ref, gpair_ref, pair_local.at[1]),
+            pltpu.make_async_copy(held_ref, weights_ref, pair_local.at[2]),
         ]
-
-    def fetch():
-        return [pltpu.make_async_copy(weights_ref, held_ref, pair_local.at[2])]
 
     def link(to):
         k = lax.rem(to - z + nz, nz)
@@ -404,7 +402,7 @@
         gfull_ref[c] = g_ref[0]
         bias_full[...] = in_bias_ref[...].astype(F32)
 
-    for n, at in enumerate((0, 2, 3, 4)):
+    for n, at in enumerate((0, 1, 2, 3, 5)):
 
         @pl.when(i == at)
         def _(n=n):
@@ -447,17 +445,15 @@
     def _():
         start(swap_lowered())
         ready = len(whole) + nz - 1
-        for event in events[5 : 1 + ready + 1]:
+        for event in events[6 : 1 + ready + 1]:
             event()
         events[-1]()
-        start(fetch())
         finish(swap_grads())
         finish(swap_lowered())
         start(hand_out())
         hopped = [u for u in range(len(partial)) if u // 2 + len(whole) + nz - 1 <= ready]
         for u in hopped:
             work.begin(partial[u], 2)
-        finish(fetch())
         for n in range(nz // 2):
             project(n)
         for event in events[1 + ready + 1 : -1]:
@@ -686,12 +682,28 @@
     sums.greet()
     add_first(0)
     add_first(1)
+    mine = sums.mine
+    mine[...] = jnp.zeros_like(mine)
+    for l in range(wl):
+        lanes = slice(l * 128, (l + 1) * 128)
+        mine[firsts[0] + l : firsts[0] + l + 1, :] = gg_ref[:, lanes]
+        mine[firsts[1] + l * padded : firsts[1] + l * padded + mix, :] = ig_ref[:, lanes]
+        mine[firsts[4] + 4 * l : firsts[4] + 4 * l + 4, :] = sgg_ref[:, lanes]
+        mine[firsts[5] + 4 * l : firsts[5] + 4 * l + 4, :] = sbg_ref[:, lanes]
+        mine[firsts[7] + l : firsts[7] + l + 1, :] = ob_ref[:, lanes]
+    mine[firsts[2] : firsts[2] + mix, 0:mix] = og_ref[...]
+    mine[firsts[3] : firsts[3] + 1, 0:mix] = bg_ref[...]
+    for k in range(3):
+        for l in range(wl // 2):
+            mine[pl.ds(firsts[6] + k * wl + c * (wl // 2) + l, 1), :] = hb_ref[k : k + 1, l * 128 : (l + 1) * 128]
+    for l in range(hidden_rows):
+        mine[pl.ds(firsts[8] + c * hidden_rows + l, 1), :] = eb_ref[:, l * 128 : (l + 1) * 128]
     pl.semaphore_wait(pltpu.get_barrier_semaphore(), sums.count - 1)
     for t in range(2):
         start(copies(t, 1))
+    sums.deal()
     add_first(2)
     add_first(3)
-
     for t in range(2):
         total = folded[0][t].astype(F32)
         for piece in folded[1:]:
@@ -709,27 +721,8 @@
         fold_add(grid, place, orders[t], 1, None, first[t], second[t])
         start(copies(t, 2))
 
-    second_step(0)
-    second_step(1)
-    mine = sums.mine
-    mine[...] = jnp.zeros_like(mine)
-    for l in range(wl):
-        lanes = slice(l * 128, (l + 1) * 128)
-        mine[firsts[0] + l : firsts[0] + l + 1, :] = gg_ref[:, lanes]
-        mine[firsts[1] + l * padded : firsts[1] + l * padded + mix, :] = ig_ref[:, lanes]
-        mine[firsts[4] + 4 * l : firsts[4] + 4 * l + 4, :] = sgg_ref[:, lanes]
-        mine[firsts[5] + 4 * l : firsts[5] + 4 * l + 4, :] = sbg_ref[:, lanes]
-        mine[firsts[7] + l : firsts[7] + l + 1, :] = ob_ref[:, lanes]
-    mine[firsts[2] : firsts[2] + mix, 0:mix] = og_ref[...]
-    mine[firsts[3] : firsts[3] + 1, 0:mix] = bg_ref[...]
-    for k in range(3):
-        for l in range(wl // 2):
-            mine[pl.ds(firsts[6] + k * wl + c * (wl // 2) + l, 1), :] = hb_ref[k : k + 1, l * 128 : (l + 1) * 128]
-    for l in range(hidden_rows):
-        mine[pl.ds(firsts[8] + c * hidden_rows + l, 1), :] = eb_ref[:, l * 128 : (l + 1) * 128]
-    sums.deal()
-    second_step(2)
-    second_step(3)
+    for t in range(4):
+        second_step(t)
     sums.tell()
     for t in range(4):
         finish(copies(t, 2))

time: 388 us -> 379 us (0.977)
  Pallas kernels: 373 us -> 364 us
    pallas_call x1, Pallas kernels: 71.4 us -> 67.1 us  [feed_forward(): pl.pallas_call(functools.partial(feed_kernel, grid, steps), grid=(steps,)...]
where the time goes in v8:
time: 379 us; the launch traced here: 373 us
  Pallas kernels  364 us (96%)
  starting transfers between devices  6.44 us (2%)
    pallas_call x1, Pallas kernels, mix_forward(): pl.pallas_call(functools.partial(mix_kernel, grid, rows, chunks, groups,...  136 us
    pallas_call x1, Pallas kernels, feed_forward(): pl.pallas_call(functools.partial(feed_kernel, grid, steps), grid=(steps,)...  67.1 us
    pallas_call x1, Pallas kernels, finish_sums(): pl.pallas_call(functools.partial(finish_kernel, grid, orders, len(kept)),...  48.2 us
    pallas_call x1, Pallas kernels, attention(): pl.pallas_call(functools.partial(attention_kernel, width, heads, tile, ed...  47.1 us
    pallas_call x1, Pallas kernels, unproject(): pl.pallas_call(functools.partial(unproject_kernel, grid, own_width, order...  39.9 us
    pallas_call x1, Pallas kernels, mix_backward(): pl.pallas_call(unmix_kernel, grid=(tokens // block,), out_shape=[jax.Shap...  21.6 us
  transfers between devices with their start and end apart: 5, of which 0 were waited for; matrix products, arithmetic and copies ran while one was open for 0% of the time, Pallas kernels for 6%

profile of v8, /device:TPU:0, one launch (start us, length us, event | category | flops | bytes accessed | tf_op | source)
XLA Modules:
  0.0 372.6 jit_solution(10017108676564860301)
XLA Ops:
  0.6 136.5 %mix_forward.1 = (bf16[4,2,384,1024]{3,2,1,0:T(8,128)(2,1)}, bf16[2,384,1024]{2,1,0:T(8,128)(2,1)}, f32[4,384,1024]{2,1,0:T(8,128)}, f32[384,36]{1,0:T(8,128)}, ...) custom-call(bf16[9,1,384,1024]{3,2,1,0:T(8,128)(2,1)} %h_ref.3, ...), custom_call_target="tpu_custom_call" | custom-call | flops 31457280 | bytes 141557760 | tf_op jit(solution)/shard_map/mix_forward/pallas_call | solution.py:484
  137.1 47.1 %attention.1 = bf16[3072,512]{1,0:T(8,128)(2,1)} custom-call(bf16[3072,512]{1,0:T(8,128)(2,1)} %bitcast.33, s32[1,3072]{1,0:T(1,128)} %qdoc_ref.1), custom_call_target="tpu_custom_call" | custom-call | flops 28991029248 | bytes 7864320 | tf_op jit(solution)/shard_map/attention/pallas_call | solution.py:1272
  184.2 67.1 %feed_forward.1 = (bf16[4,768,512]{2,1,0:T(8,128)(2,1)}, f32[768,1024]{1,0:T(8,128)}, f32[768,1024]{1,0:T(8,128)}, f32[1,2048]{1,0:T(1,128)}, bf16[2,64,1024]{2,...) custom-call(bf16[4,768,512]{2,1,0:T(8,128)(2,1)} %bitcast.47, ...), custom_call_target="tpu_custom_call" | custom-call | flops 38654705664 | bytes 41943040 | tf_op jit(solution)/shard_map/feed_forward/pallas_call | solution.py:1114
  251.3 39.9 %unproject.1 = (f32[4,384,1024]{2,1,0:T(8,128)}, bf16[4,384,1024]{2,1,0:T(8,128)(2,1)}, f32[3,512]{1,0:T(4,128)}, bf16[384,1024]{1,0:T(8,128)(2,1)}, f32[2,64,10...) custom-call(bf16[2,64,1024]{2,1,0:T(8,128)(2,1)} %get-tuple-element., ...), custom_call_target="tpu_custom_call" | custom-call | flops 12884901888 | bytes 31457280 | tf_op jit(solution)/shard_map/unproject/pallas_call | solution.py:952
  291.2 0.3 collective-permute-start
  291.5 1.8 collective-permute-start.1
  293.3 1.1 collective-permute-start.2
  294.4 3.3 collective-permute-start.3
  297.7 0.0 collective-permute-start.4
  297.7 21.6 %mix_backward.1 = (f32[9,1,384,1024]{3,2,1,0:T(8,128)}, f32[4,1024]{1,0:T(4,128)}, f32[4,1024]{1,0:T(4,128)}, f32[1,1024]{1,0:T(1,128)}, f32[36,1024]{1,0:T(8,12...) custom-call(bf16[9,1,384,1024]{3,2,1,0:T(8,128)(2,1)} %h_ref.3, ...), custom_call_target="tpu_custom_call" | custom-call | flops 393216000 | bytes 42467328 | tf_op jit(solution)/shard_map/mix_backward/pallas_call | solution.py:617
  319.3 0.0 collective-permute-done.2.refs_8_
  319.3 0.0 copy-start.2
  319.3 0.0 collective-permute-done.3.refs_9_
  319.3 0.0 copy-start.3
  319.3 0.0 collective-permute-done.4.refs_10_
  319.3 0.0 copy-start.4
  319.3 0.0 collective-permute-done.refs_4_
  319.3 0.0 copy-start
  319.3 0.0 collective-permute-done.1.refs_5_
  319.4 0.0 copy-start.1
  319.4 0.6 copy-done.2
  320.0 0.1 copy-done.3
  320.1 0.1 copy-done.4
  320.1 0.4 copy-done
  320.5 0.4 copy-done.1
  320.9 48.2 %finish_sums.1 = (f32[512,128]{1,0:T(8,128)}, f32[32,3072]{1,0:T(8,128)}, f32[32,1024]{1,0:T(8,128)}, f32[32,4096]{1,0:T(8,128)}, f32[32,4096]{1,0:T(8,128)}) custom-call(bf16[2,4,64,512]{3,2,1,0:T(8,128)(2,1)} %get-tuple-element.108.refs_0_, bf16[2,4,64,512]{3,2,1,0:T(8,128)(2,1)} %get-tuple-element.109.refs_1_, ...), custom_call_target="tpu_custom_call" | custom-call | bytes 104857600 | tf_op jit(solution)/shard_map/finish_sums/pallas_call | solution.py:751
  369.1 3.2 hand_over.1
Async XLA Ops:
  291.2 28.1 %collective-permute-start = (bf16[2,2,4,64,512]{4,3,2,1,0:T(8,128)(2,1)}, bf16[2,2,4,64,512]{4,3,2,1,0:T(8,128)(2,1)S(1)}, u32[]{:S(2)}, u32[]{:S(2)}) collective-permute-start(bf16[2,2,4,64,512]{4,3,2,1,0:T(8,128)(2,1)} %get-tuple-element.112), channel_id=1, source_target_pairs={{0,16},{8,24},{16,0},{24,8},{1,17},{9,25},{17,1},{25,9},{2,18},{10... | collective-permute-start | bytes 3145736 | tf_op jit(solution)/shard_map/ppermute | solution.py:1366
  291.5 27.8 %collective-permute-start.1 = (bf16[2,2,4,64,512]{4,3,2,1,0:T(8,128)(2,1)}, bf16[2,2,4,64,512]{4,3,2,1,0:T(8,128)(2,1)S(1)}, u32[]{:S(2)}, u32[]{:S(2)}) collective-permute-start(bf16[2,2,4,64,512]{4,3,2,1,0:T(8,128)(2,1)} %get-tuple-element.113), channel_id=1, source_target_pairs={{0,8},{8,0},{16,24},{24,16},{1,9},{9,1},{17,25},{25,17},{2,10},{10... | collective-permute-start | bytes 3145736 | tf_op jit(solution)/shard_map/ppermute | solution.py:1367
  293.3 26.0 %collective-permute-start.2 = (bf16[2,64,1024]{2,1,0:T(8,128)(2,1)}, bf16[2,64,1024]{2,1,0:T(8,128)(2,1)S(1)}, u32[]{:S(2)}, u32[]{:S(2)}) collective-permute-start(bf16[2,64,1024]{2,1,0:T(8,128)(2,1)} %get-tuple-element.116), channel_id=1, source_target_pairs={{0,2},{1,3},{2,4},{3,5},{4,6},{5,7},{6,0},{7,1},{8,10},{9,11},{10,... | collective-permute-start | bytes 786440 | tf_op jit(solution)/shard_map/ppermute | solution.py:1362
  294.4 24.9 %collective-permute-start.3 = (bf16[2,64,1024]{2,1,0:T(8,128)(2,1)}, bf16[2,64,1024]{2,1,0:T(8,128)(2,1)S(1)}, u32[]{:S(2)}, u32[]{:S(2)}) collective-permute-start(bf16[2,64,1024]{2,1,0:T(8,128)(2,1)} %get-tuple-element.117), channel_id=1, source_target_pairs={{0,4},{1,5},{2,6},{3,7},{4,0},{5,1},{6,2},{7,3},{8,12},{9,13},{10,... | collective-permute-start | bytes 786440 | tf_op jit(solution)/shard_map/ppermute | solution.py:1362
  297.7 21.6 %collective-permute-start.4 = (bf16[2,64,1024]{2,1,0:T(8,128)(2,1)}, bf16[2,64,1024]{2,1,0:T(8,128)(2,1)S(1)}, u32[]{:S(2)}, u32[]{:S(2)}) collective-permute-start(bf16[2,64,1024]{2,1,0:T(8,128)(2,1)} %get-tuple-element.118), channel_id=1, source_target_pairs={{0,6},{1,7},{2,0},{3,1},{4,2},{5,3},{6,4},{7,5},{8,14},{9,15},{10,... | collective-permute-start | bytes 786440 | tf_op jit(solution)/shard_map/ppermute | solution.py:1362
  319.3 0.7 copy-start.2
  319.3 0.8 copy-start.3
  319.3 0.8 copy-start.4
  319.3 1.2 copy-start
  319.4 1.5 copy-start.1

commit v9 on v8

--- a/solution.py
+++ b/solution.py
@@ -891,9 +891,9 @@
     @pl.when(i == 0)
     def _():
         grid.greet(a, b, z, c)
+        start(along())
         for t in range(2):
             start(fold(t, 0))
-        start(along())
         start(place_lates())
         mine_ref[...] = piece(0)
         partial_ref[...] = against(mine_ref[their_rows, :], w_ref[0]) + feed_ref[their_rows, :]
@@ -1124,7 +1124,7 @@
         + [jax.ShapeDtypeStruct((2, rows, n), BF16)] * nz
         + [jax.ShapeDtypeStruct((na, nb, nz, rows, n), BF16)] * 2,
         in_specs=[
-            pl.BlockSpec(memory_space=pltpu.VMEM),
+            pl.BlockSpec(memory_space=pl.ANY),
             pl.BlockSpec((1, both, width), lambda i: (3, 0, 0)),
             whole(both, width),
             cols(width),

time: 379 us -> 378 us (level)
  no operation moved by 1% of the time
where the time goes in v9:
time: 378 us; the launch traced here: 372 us
  Pallas kernels  363 us (96%)
  starting transfers between devices  6.44 us (2%)
    pallas_call x1, Pallas kernels, mix_forward(): pl.pallas_call(functools.partial(mix_kernel, grid, rows, chunks, groups,...  136 us
    pallas_call x1, Pallas kernels, feed_forward(): pl.pallas_call(functools.partial(feed_kernel, grid, steps), grid=(steps,)...  66.2 us
    pallas_call x1, Pallas kernels, finish_sums(): pl.pallas_call(functools.partial(finish_kernel, grid, orders, len(kept)),...  48.2 us
    pallas_call x1, Pallas kernels, attention(): pl.pallas_call(functools.partial(attention_kernel, width, heads, tile, ed...  47.1 us
    pallas_call x1, Pallas kernels, unproject(): pl.pallas_call(functools.partial(unproject_kernel, grid, own_width, order...  40.2 us
    pallas_call x1, Pallas kernels, mix_backward(): pl.pallas_call(unmix_kernel, grid=(tokens // block,), out_shape=[jax.Shap...  21.6 us
  transfers between devices with their start and end apart: 5, of which 0 were waited for; matrix products, arithmetic and copies ran while one was open for 0% of the time, Pallas kernels for 6%

profile of v9, /device:TPU:0, one launch (start us, length us, event | category | flops | bytes accessed | tf_op | source)
XLA Modules:
  0.0 371.9 jit_solution(1848806621751267906)
XLA Ops:
  0.6 136.5 %mix_forward.1 = (bf16[4,2,384,1024]{3,2,1,0:T(8,128)(2,1)}, bf16[2,384,1024]{2,1,0:T(8,128)(2,1)}, f32[4,384,1024]{2,1,0:T(8,128)}, f32[384,36]{1,0:T(8,128)}, ...) custom-call(bf16[9,1,384,1024]{3,2,1,0:T(8,128)(2,1)} %h_ref.3, ...), custom_call_target="tpu_custom_call" | custom-call | flops 31457280 | bytes 141557760 | tf_op jit(solution)/shard_map/mix_forward/pallas_call | solution.py:484
  137.1 47.1 %attention.1 = bf16[3072,512]{1,0:T(8,128)(2,1)} custom-call(bf16[3072,512]{1,0:T(8,128)(2,1)} %bitcast.33, s32[1,3072]{1,0:T(1,128)} %qdoc_ref.1), custom_call_target="tpu_custom_call" | custom-call | flops 28991029248 | bytes 7864320 | tf_op jit(solution)/shard_map/attention/pallas_call | solution.py:1272
  184.2 66.2 %feed_forward.1 = (bf16[4,768,512]{2,1,0:T(8,128)(2,1)}, f32[768,1024]{1,0:T(8,128)}, f32[768,1024]{1,0:T(8,128)}, f32[1,2048]{1,0:T(1,128)}, bf16[2,64,1024]{2,...) custom-call(bf16[4,768,512]{2,1,0:T(8,128)(2,1)} %bitcast.47, ...), custom_call_target="tpu_custom_call" | custom-call | flops 38654705664 | bytes 41943040 | tf_op jit(solution)/shard_map/feed_forward/pallas_call | solution.py:1114
  250.4 40.2 %unproject.1 = (f32[4,384,1024]{2,1,0:T(8,128)}, bf16[4,384,1024]{2,1,0:T(8,128)(2,1)}, f32[3,512]{1,0:T(4,128)}, bf16[384,1024]{1,0:T(8,128)(2,1)}, f32[2,64,10...) custom-call(bf16[2,64,1024]{2,1,0:T(8,128)(2,1)} %get-tuple-element., ...), custom_call_target="tpu_custom_call" | custom-call | flops 12884901888 | bytes 31457280 | tf_op jit(solution)/shard_map/unproject/pallas_call | solution.py:952
  290.5 0.3 collective-permute-start
  290.8 1.8 collective-permute-start.1
  292.6 1.1 collective-permute-start.2
  293.7 3.3 collective-permute-start.3
  297.0 0.0 collective-permute-start.4
  297.0 21.6 %mix_backward.1 = (f32[9,1,384,1024]{3,2,1,0:T(8,128)}, f32[4,1024]{1,0:T(4,128)}, f32[4,1024]{1,0:T(4,128)}, f32[1,1024]{1,0:T(1,128)}, f32[36,1024]{1,0:T(8,12...) custom-call(bf16[9,1,384,1024]{3,2,1,0:T(8,128)(2,1)} %h_ref.3, ...), custom_call_target="tpu_custom_call" | custom-call | flops 393216000 | bytes 42467328 | tf_op jit(solution)/shard_map/mix_backward/pallas_call | solution.py:617
  318.6 0.0 collective-permute-done.2.refs_8_
  318.6 0.0 copy-start.2
  318.6 0.0 collective-permute-done.3.refs_9_
  318.6 0.0 copy-start.3
  318.6 0.0 collective-permute-done.4.refs_10_
  318.6 0.0 copy-start.4
  318.6 0.0 collective-permute-done.refs_4_
  318.6 0.0 copy-start
  318.6 0.0 collective-permute-done.1.refs_5_
  318.7 0.0 copy-start.1
  318.7 0.6 copy-done.2
  319.3 0.1 copy-done.3
  319.4 0.1 copy-done.4
  319.4 0.4 copy-done
  319.8 0.4 copy-done.1
  320.2 48.2 %finish_sums.1 = (f32[512,128]{1,0:T(8,128)}, f32[32,3072]{1,0:T(8,128)}, f32[32,1024]{1,0:T(8,128)}, f32[32,4096]{1,0:T(8,128)}, f32[32,4096]{1,0:T(8,128)}) custom-call(bf16[2,4,64,512]{3,2,1,0:T(8,128)(2,1)} %get-tuple-element.108.refs_0_, bf16[2,4,64,512]{3,2,1,0:T(8,128)(2,1)} %get-tuple-element.109.refs_1_, ...), custom_call_target="tpu_custom_call" | custom-call | bytes 104857600 | tf_op jit(solution)/shard_map/finish_sums/pallas_call | solution.py:751
  368.4 3.2 hand_over.1
Async XLA Ops:
  290.5 28.1 %collective-permute-start = (bf16[2,2,4,64,512]{4,3,2,1,0:T(8,128)(2,1)}, bf16[2,2,4,64,512]{4,3,2,1,0:T(8,128)(2,1)S(1)}, u32[]{:S(2)}, u32[]{:S(2)}) collective-permute-start(bf16[2,2,4,64,512]{4,3,2,1,0:T(8,128)(2,1)} %get-tuple-element.112), channel_id=1, source_target_pairs={{0,16},{8,24},{16,0},{24,8},{1,17},{9,25},{17,1},{25,9},{2,18},{10... | collective-permute-start | bytes 3145736 | tf_op jit(solution)/shard_map/ppermute | solution.py:1366
  290.8 27.8 %collective-permute-start.1 = (bf16[2,2,4,64,512]{4,3,2,1,0:T(8,128)(2,1)}, bf16[2,2,4,64,512]{4,3,2,1,0:T(8,128)(2,1)S(1)}, u32[]{:S(2)}, u32[]{:S(2)}) collective-permute-start(bf16[2,2,4,64,512]{4,3,2,1,0:T(8,128)(2,1)} %get-tuple-element.113), channel_id=1, source_target_pairs={{0,8},{8,0},{16,24},{24,16},{1,9},{9,1},{17,25},{25,17},{2,10},{10... | collective-permute-start | bytes 3145736 | tf_op jit(solution)/shard_map/ppermute | solution.py:1367
  292.6 26.0 %collective-permute-start.2 = (bf16[2,64,1024]{2,1,0:T(8,128)(2,1)}, bf16[2,64,1024]{2,1,0:T(8,128)(2,1)S(1)}, u32[]{:S(2)}, u32[]{:S(2)}) collective-permute-start(bf16[2,64,1024]{2,1,0:T(8,128)(2,1)} %get-tuple-element.116), channel_id=1, source_target_pairs={{0,2},{1,3},{2,4},{3,5},{4,6},{5,7},{6,0},{7,1},{8,10},{9,11},{10,... | collective-permute-start | bytes 786440 | tf_op jit(solution)/shard_map/ppermute | solution.py:1362
  293.7 24.9 %collective-permute-start.3 = (bf16[2,64,1024]{2,1,0:T(8,128)(2,1)}, bf16[2,64,1024]{2,1,0:T(8,128)(2,1)S(1)}, u32[]{:S(2)}, u32[]{:S(2)}) collective-permute-start(bf16[2,64,1024]{2,1,0:T(8,128)(2,1)} %get-tuple-element.117), channel_id=1, source_target_pairs={{0,4},{1,5},{2,6},{3,7},{4,0},{5,1},{6,2},{7,3},{8,12},{9,13},{10,... | collective-permute-start | bytes 786440 | tf_op jit(solution)/shard_map/ppermute | solution.py:1362
  297.0 21.6 %collective-permute-start.4 = (bf16[2,64,1024]{2,1,0:T(8,128)(2,1)}, bf16[2,64,1024]{2,1,0:T(8,128)(2,1)S(1)}, u32[]{:S(2)}, u32[]{:S(2)}) collective-permute-start(bf16[2,64,1024]{2,1,0:T(8,128)(2,1)} %get-tuple-element.118), channel_id=1, source_target_pairs={{0,6},{1,7},{2,0},{3,1},{4,2},{5,3},{6,4},{7,5},{8,14},{9,15},{10,... | collective-permute-start | bytes 786440 | tf_op jit(solution)/shard_map/ppermute | solution.py:1362
  318.6 0.7 copy-start.2
  318.6 0.8 copy-start.3
  318.6 0.8 copy-start.4
  318.6 1.2 copy-start
  318.7 1.5 copy-start.1
